TPU v7x, 512 devices: a whole 4x4x16 slice. The times are simulated.
512 devices in a mesh: seq: 32 (over z_lo, y, core), clip: 16 (over z_hi, x).
Axes of the slice: x: 4, y: 4, z: 16 (z_hi: 4, z_lo: 4; z = z_hi * 4 + z_lo), core: 2. Of those that a mesh axis runs over, the one named last changes fastest.
Arguments:
- state: bfloat16 [3072, 4096], P(('clip', 'seq')), parts along dimension 0, may hold values from -5 to 5
- probe: bfloat16 [3072, 4096], P(('clip', 'seq')), parts along dimension 0, may hold values from -4 to 4
- norm_gain: float32 [4096], replicated, may hold values from 0.5 to 1.5
- head_maps: bfloat16 [32, 4096, 384], P('seq'), may hold values from -0.09375 to 0.09375
- query_gain: float32 [32, 128], P('seq'), may hold values from 0.5 to 1.5
- key_gain: float32 [32, 128], P('seq'), may hold values from 0.5 to 4
- out_map: bfloat16 [4096, 4096], P(None, 'seq'), may hold values from -0.09375 to 0.09375
- out_gate: float32 [4096], replicated, may hold values from 2 to 3
Outputs:
- next_state: bfloat16 [3072, 4096], P(('clip', 'seq')), parts along dimension 0
- density_change: float32 [16], P('clip'), parts along dimension 0
There are 16 independent parts, one for each index of `clip`. A program takes and returns all parts, laid end to end along the dimension named above; an argument that names none is the same for every part. Nothing has to cross between parts.
All inputs are finite; a program needn't handle non-finite values.
Results may differ from a plain program's by a relative error of at most 0.035.
Values may be sent and summed in bfloat16 or wider, within the bound.
No kernel may reach another device: no remote copies, remote signals or barrier semaphores. Data moves between devices by JAX's collectives and lax.ppermute only.
A program may use at most 64 MiB of HBM per device.

v0:
```python
import jax
import jax.numpy as jnp
from jax import lax
from jax.sharding import PartitionSpec as P

EPS = 1e-06
step_length = 0.5


def qk_norm(vals, tang, gain):
    recip = lax.rsqrt(jnp.mean(vals * vals, axis=-1, keepdims=True) + EPS)
    d_recip = -(recip**3) * jnp.mean(vals * tang, axis=-1, keepdims=True)
    return (vals * recip * gain, (tang * recip + vals * d_recip) * gain)


def local_heads(proj, d_proj, query_gain, key_gain):
    total = proj.shape[0]
    heads = proj.shape[1]
    width = proj.shape[2] // 3
    query, d_query = qk_norm(proj[..., :width], d_proj[..., :width], query_gain[None])
    keys, d_keys = qk_norm(
        proj[..., width : 2 * width], d_proj[..., width : 2 * width], key_gain[None]
    )
    q_b = query.astype(jnp.bfloat16)
    dq_b = d_query.astype(jnp.bfloat16)
    k_b = keys.astype(jnp.bfloat16)
    dk_b = d_keys.astype(jnp.bfloat16)
    v_b = proj[..., 2 * width :].astype(jnp.bfloat16)
    dv_b = d_proj[..., 2 * width :].astype(jnp.bfloat16)
    block = min(512, total)
    count = total // block
    scale = width ** (-0.5)

    def one_block(index):
        scores = jnp.einsum("qhd,khd->hqk", q_b, k_b, preferred_element_type=jnp.float32) * scale
        expo = jnp.exp(scores)
        probs = expo / jnp.sum(expo, axis=-1, keepdims=True)
        d_scores = (
            jnp.einsum("qhd,khd->hqk", dq_b, k_b, preferred_element_type=jnp.float32)
            + jnp.einsum("qhd,khd->hqk", q_b, dk_b, preferred_element_type=jnp.float32)
        ) * scale
        d_probs = probs * (d_scores - jnp.sum(probs * d_scores, axis=-1, keepdims=True))
        probs_b = probs.astype(jnp.bfloat16)
        d_probs_b = d_probs.astype(jnp.bfloat16)
        attended = jnp.einsum("hqk,khd->qhd", probs_b, v_b, preferred_element_type=jnp.float32)
        d_attended = jnp.einsum(
            "hqk,khd->qhd", d_probs_b, v_b, preferred_element_type=jnp.float32
        ) + jnp.einsum("hqk,khd->qhd", probs_b, dv_b, preferred_element_type=jnp.float32)
        return (attended.astype(jnp.bfloat16), d_attended.astype(jnp.bfloat16))

    attended, d_attended = lax.map(one_block, jnp.arange(count))
    return (attended.reshape(total, heads * width), d_attended.reshape(total, heads * width))


def normalize(xf, probe_rows, norm_gain):
    recip = lax.rsqrt(jnp.mean(xf * xf, axis=-1, keepdims=True) + EPS)
    d_recip = -(recip**3) * jnp.mean(xf * probe_rows, axis=-1, keepdims=True)
    normed = (xf * recip * norm_gain).astype(jnp.bfloat16)
    d_normed = ((probe_rows * recip + xf * d_recip) * norm_gain).astype(jnp.bfloat16)
    return jnp.stack([normed, d_normed])


def project_rows(stacked, head_maps):
    return jnp.einsum("std,hde->sthe", stacked, head_maps, preferred_element_type=jnp.float32)


def per_device(state, probe, norm_gain, head_maps, query_gain, key_gain, out_map, out_gate):
    tok_rows = state.shape[0]
    columns = out_map.shape[1]
    offset = lax.axis_index("seq") * columns
    gate_cols = lax.dynamic_slice_in_dim(out_gate, offset, columns)
    start_f = state.astype(jnp.float32)
    probe_f = probe.astype(jnp.float32)
    total = tok_rows * lax.axis_size("seq")

    def add_heads(piece):
        return jnp.einsum("str,rc->stc", piece, out_map, preferred_element_type=jnp.float32)

    def evaluate(current):
        stacked = normalize(current.astype(jnp.float32), probe_f, norm_gain)
        proj_both = project_rows(lax.all_gather(stacked, "seq", axis=1, tiled=True), head_maps)
        attended, d_attended = local_heads(proj_both[0], proj_both[1], query_gain, key_gain)
        both = jnp.stack([attended, d_attended])
        mapped = add_heads(lax.all_gather(both, "seq", axis=2, tiled=True))
        fields = (gate_cols * mapped).astype(jnp.bfloat16)
        back = lax.all_to_all(fields, "seq", split_axis=1, concat_axis=2, tiled=True)
        back = lax.optimization_barrier(back)
        velocity = back[0].astype(jnp.float32)
        tangent = back[1].astype(jnp.float32)
        return (velocity, jnp.sum(probe_f * tangent))

    first, trace_first = evaluate(state)
    middle = (start_f + step_length * first).astype(jnp.bfloat16)
    second, trace_second = evaluate(middle)
    next_state = (start_f + 0.5 * step_length * (first + second)).astype(jnp.bfloat16)
    total_trace = lax.psum(trace_first + trace_second, "seq")
    change = -0.5 * step_length * total_trace / total
    return (next_state, jnp.reshape(change, (1,)))


def solution(mesh):
    placed = (
        P(("clip", "seq"), None),
        P(("clip", "seq"), None),
        P(),
        P("seq", None, None),
        P("seq", None),
        P("seq", None),
        P(None, "seq"),
        P(),
    )
    return jax.shard_map(
        per_device,
        mesh=mesh,
        in_specs=placed,
        out_specs=(P(("clip", "seq"), None), P("clip")),
        check_vma=False,
    )
```

profile of v0, /device:TPU:1, one launch (start us, length us, event | category | flops | bytes accessed | tf_op | source)
XLA Modules:
  0.0 422.4 jit_solution(1007990683232927042)
XLA Ops:
  7.2 1.2 fusion.29
  8.4 1.0 fusion.46
  9.5 0.7 copy.20
  10.3 72.6 %all-gather.5.cloned.1.call-done = bf16[2,192,4096]{2,0,1:T(2,128)(2,1)} async-done(((bf16[2,6,4096]{2,0,1:T(2,128)(2,1)}), bf16[2,192,4096]{2,0,1:T(2,128)(2,1)}) %all-gather.5.cloned.1.call-update) | async-done | bytes 3145744 | tf_op jit(solution)/shard_map/all_gather | solution.py:81
  82.9 5.5 %fusion.2 = f32[2,192,384]{2,1,0:T(8,128)S(1)} fusion(bf16[1,4096,384]{2,1,0:T(8,128)(2,1)S(1)} %copy-done, bf16[2,192,4096]{2,0,1:T(2,128)(2,1)} %all-gather.5.cloned.1.call-done), kind=kOutput, calls=%fused_computation.2 | convolution fusion | flops 1207959552 | bytes 6881280 | tf_op jit(solution)/shard_map/std,hde->sthe/dot_general | solution.py:64
  88.7 0.3 fusion.111
  89.0 0.3 fusion.52
  89.2 0.2 fusion.14
  89.5 0.3 multiply_reduce_fusion.1
  90.1 0.2 fusion.17
  90.3 0.6 pad_maximum_fusion.2
  91.0 0.8 dynamic_slice.3
  91.8 70.9 %all-gather.7.cloned.1.call-done = bf16[2,192,4096]{2,1,0:T(8,128)(2,1)} async-done(((bf16[2,192,128]{2,1,0:T(8,128)(2,1)}), bf16[2,192,4096]{2,1,0:T(8,128)(2,1)}) %all-gather.7.cloned.1.call-update) | async-done | bytes 3145744 | tf_op jit(solution)/shard_map/all_gather | solution.py:84
  162.7 3.1 fusion.10
  166.0 13.2 %all_to_all.36 = bf16[2,192,128]{2,0,1:T(2,128)(2,1)S(1)} all-to-all(bf16[2,192,128]{2,0,1:T(2,128)(2,1)S(1)} %copy.22), channel_id=1, replica_groups=mesh['seq'=32,'clip'=16] {'seq'}, dimensions={1} | all-to-all | bytes 196608 | tf_op jit(solution)/shard_map/all_to_all | solution.py:86
  179.9 0.7 copy.25
  180.9 64.8 %all-gather.9.cloned.1.call-done = bf16[2,192,4096]{2,0,1:T(2,128)(2,1)} async-done(((bf16[2,6,4096]{2,0,1:T(2,128)(2,1)}), bf16[2,192,4096]{2,0,1:T(2,128)(2,1)}) %all-gather.9.cloned.1.call-update) | async-done | bytes 3145744 | tf_op jit(solution)/shard_map/all_gather | solution.py:81
  245.7 5.5 %fusion = f32[2,192,384]{2,1,0:T(8,128)S(1)} fusion(bf16[1,4096,384]{2,1,0:T(8,128)(2,1)S(1)} %copy-done, bf16[2,192,4096]{2,0,1:T(2,128)(2,1)} %all-gather.9.cloned.1.call-done), kind=kOutput, calls=%fused_computation | convolution fusion | flops 1207959552 | bytes 6881280 | tf_op jit(solution)/shard_map/std,hde->sthe/dot_general | solution.py:64
  251.5 0.3 fusion.112
  251.8 0.3 fusion.59
  252.0 0.2 fusion.15
  252.3 0.3 multiply_reduce_fusion
  252.6 0.2 fusion.42
  252.9 0.2 fusion.16
  253.1 0.6 pad_maximum_fusion.3
  253.8 71.8 %all-gather.11.cloned.1.call-done = bf16[2,192,4096]{2,1,0:T(8,128)(2,1)} async-done(((bf16[2,192,128]{2,1,0:T(8,128)(2,1)}), bf16[2,192,4096]{2,1,0:T(8,128)(2,1)}) %all-gather.11.cloned.1.call-update) | async-done | bytes 3145744 | tf_op jit(solution)/shard_map/all_gather | solution.py:84
  325.5 3.1 fusion.11
  328.8 13.2 %all_to_all.37 = bf16[2,192,128]{2,0,1:T(2,128)(2,1)S(1)} all-to-all(bf16[2,192,128]{2,0,1:T(2,128)(2,1)S(1)} %copy.27), channel_id=1, replica_groups=mesh['seq'=32,'clip'=16] {'seq'}, dimensions={1} | all-to-all | bytes 196608 | tf_op jit(solution)/shard_map/all_to_all | solution.py:86
  342.1 0.8 fusion.110
  342.8 0.7 fusion.40
  344.9 1.6 fusion.36
  346.5 67.6 %psum.7 = f32[]{:T(128)} all-reduce(f32[]{:T(128)S(6)} %add.148), channel_id=1, replica_groups=mesh['seq'=32,'clip'=16] {'seq'}, use_global_device_ids=true, to_apply=%region_18.0 | all-reduce | flops 1 | bytes 8 | tf_op jit(solution)/shard_map/psum | solution.py:96
  (39 shorter events, 2.2 us)
Async XLA Ops:
  7.2 75.7 %copy-start = (bf16[1,4096,384]{2,1,0:T(8,128)(2,1)S(1)}, bf16[1,4096,384]{2,1,0:T(8,128)(2,1)}, u32[]{:S(2)}) copy-start(bf16[1,4096,384]{2,1,0:T(8,128)(2,1)} %param.11) | copy-start | bytes 9437188
  7.2 75.7 %all-gather.5.cloned.1.call-start = ((), (), s32[]{:S(2)}) async-start(), calls=%async_computation.2 | async-start | bytes 3244032 | tf_op jit(solution)/shard_map/all_gather | solution.py:81
  10.2 78.4 %copy-start.4 = (f32[1,128]{1,0:T(1,128)S(1)}, f32[1,128]{1,0:T(1,128)}, u32[]{:S(2)}) copy-start(f32[1,128]{1,0:T(1,128)} %param.13) | copy-start | bytes 1540
  10.3 78.4 %copy-start.5 = (f32[1,128]{1,0:T(1,128)S(1)}, f32[1,128]{1,0:T(1,128)}, u32[]{:S(2)}) copy-start(f32[1,128]{1,0:T(1,128)} %param.12) | copy-start | bytes 1540
  10.3 152.5 %all-gather.7.cloned.1.call-start = ((), (), s32[]{:S(2)}) async-start(), calls=%async_computation.3 | async-start | bytes 3244032 | tf_op jit(solution)/shard_map/all_gather | solution.py:84
  90.0 89.4 %copy-start.1 = (bf16[6,4096]{1,0:T(8,128)(2,1)S(1)}, bf16[6,4096]{1,0:T(8,128)(2,1)}, u32[]{:S(2)}) copy-start(bf16[6,4096]{1,0:T(8,128)(2,1)} %param.9) | copy-start | bytes 147460
  90.1 89.4 %copy-start.2 = (bf16[6,4096]{1,0:T(8,128)(2,1)S(1)}, bf16[6,4096]{1,0:T(8,128)(2,1)}, u32[]{:S(2)}) copy-start(bf16[6,4096]{1,0:T(8,128)(2,1)} %param.8) | copy-start | bytes 147460
  90.1 89.7 %copy-start.3 = (f32[4096]{0:T(1024)S(1)}, f32[4096]{0:T(1024)}, u32[]{:S(2)}) copy-start(f32[4096]{0:T(1024)} %param.10) | copy-start | bytes 49156
  91.0 154.7 %all-gather.9.cloned.1.call-start = ((), (), s32[]{:S(2)}) async-start(), calls=%async_computation.4 | async-start | bytes 3244032 | tf_op jit(solution)/shard_map/all_gather | solution.py:81
  180.6 144.9 %all-gather.11.cloned.1.call-start = ((), (), s32[]{:S(2)}) async-start(), calls=%async_computation.5 | async-start | bytes 3244032 | tf_op jit(solution)/shard_map/all_gather | solution.py:84
Sparse Core Ops, SparseCore 0:
  10.4 72.4 all-gather.4
  91.1 71.5 all-gather.6
  180.8 64.9 all-gather.8
  253.9 71.5 all-gather.10
where the time goes:
time: 423 us; the launch traced here: 422 us
  waiting for transfers between devices  280 us (66%)
  blocking collectives  94 us (22%)
  matrix products  20.4 us (5%)
  between operations  17.1 us (4%)
  other arithmetic  6.93 us (2%)
    all_gather x2, waiting for transfers between devices, evaluate(): mapped = add_heads(lax.all_gather(both, 'seq', axis=2, tiled=True))  143 us
    all_gather x2, waiting for transfers between devices, evaluate(): lax.all_gather(stacked, 'seq', axis=1, tiled=True)  137 us
    psum x1, blocking collectives, per_device(): total_trace = lax.psum(trace_first + trace_second, 'seq')  67.6 us
    all_to_all x2, blocking collectives, evaluate(): lax.all_to_all(fields, 'seq', split_axis=1, concat_axis=2, tiled=True)  26.4 us
    dot_general x2, matrix products, project_rows(): jnp.einsum('std,hde->sthe', stacked, head_maps, preferred_element_type=jn...  10.9 us
  transfers between devices with their start and end apart: 4, of which 4 were waited for; matrix products, arithmetic and copies ran while one was open for 0% of the time, Pallas kernels for 0%

commit v1 on v0

v1 whole, which is shorter than its diff:
```python
import jax
import jax.numpy as jnp
from jax import lax
from jax.experimental import pallas as pl
from jax.experimental.pallas import tpu as pltpu
from jax.sharding import Mesh, PartitionSpec as P

EPS = 1e-06
STEP = 0.5
SEQ = ("z", "y", "c")
BF = jnp.bfloat16
F32 = jnp.float32
NT = (((1,), (1,)), ((), ()))
TOK = 192
SCALE = 128 ** (-0.5)


def dot(a, b):
    return jnp.dot(a, b, preferred_element_type=F32)


def dot_nt(a, b):
    return lax.dot_general(a, b, NT, preferred_element_type=F32)


def row_mean(v):
    return jnp.mean(v, axis=-1, keepdims=True)


def call(kernel, out_shape, n_scalar, *args):
    in_specs = [pl.BlockSpec(memory_space=pltpu.SMEM)] * n_scalar
    for a in args[n_scalar:]:
        if isinstance(a, tuple):
            in_specs.append(pl.BlockSpec(memory_space=pl.ANY))
        else:
            in_specs.append(pl.BlockSpec(memory_space=pltpu.VMEM))
    flat = [a[0] if isinstance(a, tuple) else a for a in args]
    multi = isinstance(out_shape, (tuple, list))
    vmem = pl.BlockSpec(memory_space=pltpu.VMEM)
    return pl.pallas_call(
        kernel,
        out_shape=out_shape,
        in_specs=in_specs,
        out_specs=[vmem] * len(out_shape) if multi else vmem,
        compiler_params=pltpu.CompilerParams(vmem_limit_bytes=28 * 1024 * 1024),
    )(*flat)


def shape(dims, kind=BF):
    return jax.ShapeDtypeStruct(dims, kind)


def selectors(first_row_token, rows):
    packed = lax.broadcasted_iota(jnp.int32, (TOK, rows), 1)
    token = lax.broadcasted_iota(jnp.int32, (TOK, rows), 0)
    slot = packed & 7
    base = first_row_token(packed)
    one = jnp.ones((TOK, rows), F32)
    zero = jnp.zeros((TOK, rows), F32)
    main = jnp.where((token == base + slot) & (slot < 6), one, zero).astype(BF)
    rest = [
        jnp.where((token == base + m + 3 * (slot - 6)) & (slot >= 6), one, zero).astype(BF)
        for m in range(3)
    ]
    return main, rest


def pieces(main, rest, chunk_of):
    tail = None
    for m in range(3):
        chunk = chunk_of(m)
        part = dot(rest[m], chunk)
        tail = part if tail is None else tail + part
        yield m * 1024, dot(main, chunk)
    yield 3072, tail


def qkv_norm(proj, q_gain, k_gain):
    query, key, val = proj[:, :128], proj[:, 128:256], proj[:, 256:]
    rq = lax.rsqrt(row_mean(query * query) + EPS)
    rk = lax.rsqrt(row_mean(key * key) + EPS)
    qn = (query * rq * q_gain).astype(BF)
    kn = (key * rk * k_gain).astype(BF)
    return query, key, rq, rk, qn, kn, val.astype(BF)


def probabilities(qn, kn):
    expo = jnp.exp(dot_nt(qn, kn) * SCALE)
    return expo / jnp.sum(expo, axis=-1, keepdims=True)


def attend(proj, q_gain, k_gain):
    _, _, _, _, qn, kn, val = qkv_norm(proj, q_gain, k_gain)
    return dot(probabilities(qn, kn).astype(BF), val).astype(BF)


def attend_tangent(proj, d_proj, q_gain, k_gain):
    query, key, rq, rk, qn, kn, val = qkv_norm(proj, q_gain, k_gain)
    dq, dk, dv = d_proj[:, :128], d_proj[:, 128:256], d_proj[:, 256:].astype(BF)
    drq = -(rq * rq * rq) * row_mean(query * dq)
    drk = -(rk * rk * rk) * row_mean(key * dk)
    dqn = ((dq * rq + query * drq) * q_gain).astype(BF)
    dkn = ((dk * rk + key * drk) * k_gain).astype(BF)
    probs = probabilities(qn, kn)
    ds = (dot_nt(dqn, kn) + dot_nt(qn, dkn)) * SCALE
    d_probs = probs * (ds - jnp.sum(probs * ds, axis=-1, keepdims=True))
    return dot(d_probs.astype(BF), val) + dot(probs.astype(BF), dv)


def tangent_of(raw, sum_sq, sum_sp, probe_proj, q_gain, k_gain):
    recip = lax.rsqrt(sum_sq[:, :1] * (1.0 / 4096) + EPS)
    d_recip = -(recip * recip * recip) * (sum_sp * (1.0 / 4096))
    proj = raw * recip
    d_proj = probe_proj * recip + raw * d_recip
    return attend_tangent(proj, d_proj, q_gain, k_gain)


def first_kernel(
    meta, xa, xb, maps, gain, q_gain, k_gain, att_ref, xc_ref, col_ref, raw_ref, sq_ref
):
    core = meta[0]

    def token_base(packed):
        inner = packed & 127
        other = packed >> 7
        z = (inner >> 3) & 3
        y = inner >> 5
        c = jnp.where(other == 0, core, 1 - core)
        return (z * 8 + y * 2 + c) * 6

    main, rest = selectors(token_base, 256)
    raw = jnp.zeros((TOK, 384), F32)
    sum_sq = jnp.zeros((TOK, 1), F32)
    chunk_of = lambda m: jnp.concatenate(
        [xa[:, m * 1024 : (m + 1) * 1024], xb[:, m * 1024 : (m + 1) * 1024]], axis=0
    )
    for start, x in pieces(main, rest, chunk_of):
        sum_sq = sum_sq + jnp.sum(x * x, axis=-1, keepdims=True)
        scaled = (x * gain[:, start : start + 1024]).astype(BF)
        raw = raw + dot(scaled, maps[start : start + 1024, :])
        for b in range(8):
            xc_ref[start // 128 + b] = x[:, b * 128 : (b + 1) * 128].astype(BF)
    recip = lax.rsqrt(sum_sq * (1.0 / 4096) + EPS)
    att = attend(raw * recip, q_gain[...], k_gain[...])
    for i in range(4):
        att_ref[i] = att
    col_ref[...] = xc_ref[meta[1]]
    raw_ref[...] = raw
    sq_ref[...] = jnp.broadcast_to(sum_sq, (TOK, 128))


def out_product(core, own, oth, out_map):
    total = jnp.zeros((TOK, 128), F32)
    for side, c in ((own, core), (oth, 1 - core)):
        for y in range(4):
            for z in (0, 2):
                b = y * 4 + z
                left = jnp.concatenate([side[b], side[b + 1]], axis=1)
                right = jnp.concatenate(
                    [out_map[z * 8 + y * 2 + c], out_map[z * 8 + 8 + y * 2 + c]], axis=0
                )
                total = total + dot(left, right)
    return total


def middle_kernel(meta, own, oth, out_map, gate, col, vel_ref, mid_ref):
    vel = (gate[...] * out_product(meta[0], own, oth, out_map)).astype(BF)
    vel_ref[...] = vel
    mid = (col[...].astype(F32) + STEP * vel.astype(F32)).astype(BF)
    for i in range(4):
        mid_ref[i] = mid


def second_kernel(meta, own, oth, maps, gain, q_gain, k_gain, att_ref, raw_ref, sq_ref):
    core = meta[0]
    raw = jnp.zeros((TOK, 384), F32)
    sum_sq = jnp.zeros((TOK, 1), F32)
    for side, c in ((own, core), (oth, 1 - core)):
        squares = jnp.zeros((TOK, 128), F32)
        for y in range(4):
            for z in (0, 2):
                b = y * 4 + z
                h0 = z * 8 + y * 2 + c
                left = side[b].astype(F32)
                right = side[b + 1].astype(F32)
                squares = squares + left * left + right * right
                scaled = jnp.concatenate(
                    [(left * gain[h0]).astype(BF), (right * gain[h0 + 8]).astype(BF)], axis=1
                )
                rows = jnp.concatenate([maps[h0], maps[h0 + 8]], axis=0)
                raw = raw + dot(scaled, rows)
        sum_sq = sum_sq + jnp.sum(squares, axis=-1, keepdims=True)
    recip = lax.rsqrt(sum_sq * (1.0 / 4096) + EPS)
    att = attend(raw * recip, q_gain[...], k_gain[...])
    for i in range(4):
        att_ref[i] = att
    raw_ref[...] = raw
    sq_ref[...] = jnp.broadcast_to(sum_sq, (TOK, 128))


def probe_kernel(
    meta, packed, xc, raw1, sq1, maps, out_map, gain, gate, q_gain, k_gain, after,
    pc_ref, pp_ref, datt_ref, back_ref,
):
    main, rest = selectors(lambda row: (row >> 3) * 6, 256)
    proj = jnp.zeros((TOK, 384), F32)
    dots = jnp.zeros((TOK, 128), F32)
    for start, x in pieces(main, rest, lambda m: packed[:, m * 1024 : (m + 1) * 1024]):
        scaled = (x * gain[:, start : start + 1024]).astype(BF)
        proj = proj + dot(scaled, maps[start : start + 1024, :])
        for b in range(8):
            piece = x[:, b * 128 : (b + 1) * 128]
            dots = dots + piece * xc[start // 128 + b].astype(F32)
            pc_ref[start // 128 + b] = piece.astype(BF)
    pp_ref[...] = proj
    sum_sp = jnp.sum(dots, axis=-1, keepdims=True)
    datt_ref[...] = tangent_of(raw1[...], sq1[...], sum_sp, proj, q_gain[...], k_gain[...])
    weighted = (pc_ref[meta[1]].astype(F32) * gate[...]).astype(BF)
    for h in range(32):
        back_ref[h] = dot_nt(weighted, out_map[h]).astype(back_ref.dtype)


def tangent_kernel(meta, own, oth, pc, raw2, sq2, pp, datt1, q_gain, k_gain, datt_ref):
    core = meta[0]
    dots = jnp.zeros((TOK, 128), F32)
    for side, c in ((own, core), (oth, 1 - core)):
        for y in range(4):
            for z in range(4):
                probe = pc[z * 8 + y * 2 + c].astype(F32)
                dots = dots + side[y * 4 + z].astype(F32) * probe
    sum_sp = jnp.sum(dots, axis=-1, keepdims=True)
    datt_ref[...] = datt1[...] + tangent_of(
        raw2[...], sq2[...], sum_sp, pp[...], q_gain[...], k_gain[...]
    )


def last_kernel(meta, own, oth, out_map, gate, col, vel1, datt, back, out_ref):
    vel = (gate[...] * out_product(meta[0], own, oth, out_map)).astype(BF)
    both = vel1[...].astype(F32) + vel.astype(F32)
    new = (col[...].astype(F32) + 0.5 * STEP * both).astype(BF)
    row = lax.broadcasted_iota(jnp.int32, (256, TOK), 0)
    token = lax.broadcasted_iota(jnp.int32, (256, TOK), 1)
    hit = (token == (row >> 3) * 6 + (row & 7)) & ((row & 7) < 6)
    place = jnp.where(hit, jnp.ones((256, TOK), F32), jnp.zeros((256, TOK), F32)).astype(BF)
    spread = dot(place, new)
    partial = jnp.sum(datt[...] * back[...].astype(F32), axis=0, keepdims=True)
    trace = jnp.sum(partial, axis=1, keepdims=True)
    high = trace.astype(BF).astype(F32)
    mid = (trace - high).astype(BF).astype(F32)
    low = trace - high - mid
    lane = lax.broadcasted_iota(jnp.int32, (1, 128), 1)
    coded = jnp.where(lane == 0, high, jnp.where(lane == 1, mid, jnp.where(lane == 2, low, 0.0)))
    slot = lax.broadcasted_iota(jnp.int32, (256, 128), 0) & 7
    out_ref[...] = jnp.where(slot == 6, coded, spread).astype(BF)


def land_kernel(got, next_ref, change_ref):
    total = jnp.zeros((8, 128), F32)
    for j in range(32):
        block = got[j]
        next_ref[:, j * 128 : (j + 1) * 128] = block[:6]
        total = total + block.astype(F32)
    trace = jnp.sum(total[6:7, :], axis=1, keepdims=True)
    change_ref[...] = jnp.broadcast_to(-0.5 * STEP * trace / TOK, (1, 128))


def spread(copies, rows, lanes):
    a = lax.all_to_all(copies.reshape(4 * rows, lanes), "z", 0, 0, tiled=True)
    b = lax.all_to_all(jnp.tile(a, (4, 1)), "y", 0, 0, tiled=True)
    return a, b


def swap(block):
    return lax.ppermute(block, "c", [(0, 1), (1, 0)])


def pack(rows):
    return jnp.concatenate([rows[:, :3072], rows[:, 3072:].reshape(2, 3072)], axis=0)


def per_device(state, probe, norm_gain, head_maps, query_gain, key_gain, out_map, out_gate):
    core = lax.axis_index("c")
    place = lax.axis_index(SEQ)
    meta = jnp.stack([core, place]).astype(jnp.int32)
    gate = lax.dynamic_slice_in_dim(out_gate, place * 128, 128).reshape(1, 128)
    maps = head_maps.reshape(4096, 384)
    maps_blocks = head_maps.reshape(32, 128, 384)
    out_blocks = out_map.reshape(32, 128, 128)
    gain = norm_gain.reshape(1, 4096)
    gain_blocks = norm_gain.reshape(32, 1, 128)

    packed_probe = lax.all_gather(pack(probe), SEQ, axis=0, tiled=True)
    _, own = spread(jnp.broadcast_to(pack(state)[None], (4, 8, 3072)), 8, 3072)
    att1, xc, col, raw1, sq1 = call(
        first_kernel,
        [shape((4, TOK, 128)), shape((32, TOK, 128)), shape((TOK, 128)), shape((TOK, 384), F32), shape((TOK, 128), F32)],
        1, meta, own, swap(own), maps, gain, query_gain, key_gain,
    )

    def gathered(copies):
        a, b = spread(copies, TOK, 128)
        other = swap(b)
        return a, b.reshape(16, TOK, 128), other.reshape(16, TOK, 128)

    _, own1, oth1 = gathered(att1)
    vel1, mid = call(
        middle_kernel, [shape((TOK, 128)), shape((4, TOK, 128))],
        1, meta, own1, oth1, out_blocks, gate, col,
    )
    early, own_m, oth_m = gathered(mid)
    pc, pp, datt1, back = call(
        probe_kernel,
        [shape((32, TOK, 128)), shape((TOK, 384), F32), shape((TOK, 128), F32), shape((32, TOK, 128), F32)],
        1, meta, packed_probe, xc, raw1, sq1, maps, out_blocks, gain, gate, query_gain, key_gain, (early,),
    )
    adjoint = lax.psum_scatter(back, SEQ, scatter_dimension=0, tiled=False)
    att2, raw2, sq2 = call(
        second_kernel,
        [shape((4, TOK, 128)), shape((TOK, 384), F32), shape((TOK, 128), F32)],
        1, meta, own_m, oth_m, maps_blocks, gain_blocks, query_gain, key_gain,
    )
    datt = call(
        tangent_kernel, shape((TOK, 128), F32),
        1, meta, own_m, oth_m, pc, raw2, sq2, pp, datt1, query_gain, key_gain,
    )
    _, own2, oth2 = gathered(att2)
    columns = call(
        last_kernel, shape((256, 128)),
        1, meta, own2, oth2, out_blocks, gate, col, vel1, datt, adjoint,
    )
    got = lax.all_to_all(columns, SEQ, 0, 0, tiled=True).reshape(32, 8, 128)
    next_state, change = call(land_kernel, [shape((6, 4096)), shape((1, 128), F32)], 0, got)
    return next_state, change[0, :1]


def solution(mesh):
    split = Mesh(mesh.devices.reshape(4, 4, 2, 4, 4), ("z", "y", "c", "w", "x"))
    rows = P(("w", "x", "z", "y", "c"), None)
    return jax.shard_map(
        per_device,
        mesh=split,
        in_specs=(rows, rows, P(), P(SEQ, None, None), P(SEQ, None), P(SEQ, None), P(None, SEQ), P()),
        out_specs=(rows, P(("w", "x"))),
        check_vma=False,
    )
```

time: 423 us -> 296 us (0.70)
  waiting for transfers between devices: 280 us -> 126 us
  starting transfers between devices: 0.34 us -> 28.3 us
  matrix products: 20.4 us -> 0 us
  Pallas kernels: 0 us -> 15.5 us
  local copies, waits for them, and re-layouts: 3.45 us -> 16.8 us
  other arithmetic: 6.93 us -> 0.76 us
    all_gather x4 -> x1, waiting for transfers between devices: 280 us -> 18 us  [per_device(): packed_probe = lax.all_gather(pack(probe), SEQ, axis=0, tiled=True)]
    reduce_scatter x0 -> x1, waiting for transfers between devices: none -> 94.4 us  [per_device(): adjoint = lax.psum_scatter(back, SEQ, scatter_dimension=0, tiled=False)]
    psum x1 -> x0, blocking collectives: 67.6 us -> none  [per_device(): total_trace = lax.psum(trace_first + trace_second, 'seq')]
    all_to_all x2 -> x7, blocking collectives: 26.4 us -> 92.8 us  [the longest x3 45.2 us: spread(): b = lax.all_to_all(jnp.tile(a, (4, 1)), 'y', 0, 0, tiled=True)]
    dot_general x16 -> x0, matrix products: 20.4 us -> none  [the longest x2 10.9 us: project_rows(): jnp.einsum('std,hde->sthe', stacked, head_maps, preferred_element_type=jn...]
    ppermute x0 -> x4, starting transfers between devices: none -> 20 us  [swap(): return lax.ppermute(block, 'c', [(0, 1), (1, 0)])]
    pallas_call x0 -> x7, Pallas kernels: none -> 15.5 us  [call(): pl.pallas_call(kernel, out_shape=out_shape, in_specs=in_specs, out_specs=...]
    unnamed x12 -> x46, local copies, waits for them, and re-layouts: 0.04 us -> 13.8 us
  transfers between devices with their start and end apart: 4 -> 8, of which waited for: 4 -> 7; matrix products, arithmetic and copies ran while one was open for 0% -> 0% of each run, Pallas kernels for 0% -> 3%
where the time goes in v1:
time: 296 us; the launch traced here: 295 us
  waiting for transfers between devices  126 us (43%)
  blocking collectives  92.8 us (31%)
  starting transfers between devices  28.3 us (10%)
  local copies, waits for them, and re-layouts  16.8 us (6%)
  Pallas kernels  15.5 us (5%)
  between operations  14.3 us (5%)
    reduce_scatter x1, waiting for transfers between devices, per_device(): adjoint = lax.psum_scatter(back, SEQ, scatter_dimension=0, tiled=False)  94.4 us
    all_to_all x3, blocking collectives, spread(): b = lax.all_to_all(jnp.tile(a, (4, 1)), 'y', 0, 0, tiled=True)  45.2 us
    all_to_all x3, blocking collectives, spread(): a = lax.all_to_all(copies.reshape(4 * rows, lanes), 'z', 0, 0, tiled=True)  32.2 us
    ppermute x4, starting transfers between devices, swap(): return lax.ppermute(block, 'c', [(0, 1), (1, 0)])  20 us
    all_gather x1, waiting for transfers between devices, per_device(): packed_probe = lax.all_gather(pack(probe), SEQ, axis=0, tiled=True)  18 us
    pallas_call x7, Pallas kernels, call(): pl.pallas_call(kernel, out_shape=out_shape, in_specs=in_specs, out_specs=...  15.5 us
    all_to_all x1, blocking collectives, per_device(): got = lax.all_to_all(columns, SEQ, 0, 0, tiled=True).reshape(32, 8, 128)  15.4 us
    unnamed x46, local copies, waits for them, and re-layouts  13.8 us
  transfers between devices with their start and end apart: 8, of which 7 were waited for; matrix products, arithmetic and copies ran while one was open for 0% of the time, Pallas kernels for 3%

profile of v1, /device:TPU:1, one launch (start us, length us, event | category | flops | bytes accessed | tf_op | source)
XLA Modules:
  0.0 294.9 jit_solution(9449047618976339087)
XLA Ops:
  8.9 12.2 %all_to_all.67 = bf16[4,8,3072]{2,1,0:T(8,128)(2,1)S(1)} all-to-all(bf16[4,8,3072]{2,1,0:T(8,128)(2,1)S(1)} %broadcast_in_dim.2), channel_id=1, replica_groups=mesh['z'=4,'y'=4,'c'=2,'w'=4,'x'=4] {'z'}, dimensions={0} | all-to-all | bytes 393216 | tf_op jit(solution)/shard_map/all_to_all | solution.py:268
  22.0 4.2 %all-to-all-start.1 = ((bf16[4,32,3072]{2,1,0:T(8,128)(2,1)}), bf16[4,32,3072]{2,1,0:T(8,128)(2,1)}, u32[]{:S(2)}, u32[]{:S(2)}) async-start(bf16[4,32,3072]{2,1,0:T(8,128)(2,1)} %tile.17), calls=%async_computation.1 | async-start | bytes 1572864 | tf_op jit(solution)/shard_map/all_to_all | solution.py:269
  26.3 8.4 %all-to-all-done.1 = bf16[4,32,3072]{2,1,0:T(8,128)(2,1)} async-done(((bf16[4,32,3072]{2,1,0:T(8,128)(2,1)}), bf16[4,32,3072]{2,1,0:T(8,128)(2,1)}, u32[]{:S(2)}, u32[]{:S(2)}) %all-to-all-start.1) | async-done | bytes 786464 | tf_op jit(solution)/shard_map/all_to_all | solution.py:269
  34.7 7.1 %collective-permute-start = (bf16[128,3072]{1,0:T(8,128)(2,1)}, bf16[128,3072]{1,0:T(8,128)(2,1)}, u32[]{:S(2)}, u32[]{:S(2)}) collective-permute-start(bf16[128,3072]{1,0:T(8,128)(2,1)} %bitcast.3.xa), channel_id=1, source_target_pairs={{0,16},{16,0},{1,17},{17,1},{2,18},{18,2},{3,19},{19,3},{4,20},{20... | collective-permute-start | bytes 2359304 | tf_op jit(solution)/shard_map/ppermute | solution.py:274
  42.6 1.5 collective-permute-done.xb
  44.0 3.6 %shard_map.95 = (bf16[4,192,128]{2,1,0:T(8,128)(2,1)S(1)}, bf16[32,192,128]{2,1,0:T(8,128)(2,1)S(1)}, bf16[192,128]{1,0:T(8,128)(2,1)S(1)}, f32[192,384]{1,0:T(8,128)S(1)}, f32[192,128]{1,0:T(8,128)S(1)}) custom-call(s32[2]{0:T(128)S(1)} %pad_add_fusion.meta, bf16[128,3072]{1,0:T(8,128)(2,1)} %bitcast.3.xa, bf16[128,3072]{1,0:T(8,128)(2,1)} %collective-permute-done.xb, ...), custom_call_target="tpu_custom_call" | custom-call | tf_op jit(solution)/shard_map/pallas_call | solution.py:40
  47.6 1.2 copy-done.9
  49.5 9.7 %all_to_all.68 = bf16[4,192,128]{2,1,0:T(8,128)(2,1)S(1)} all-to-all(bf16[4,192,128]{2,1,0:T(8,128)(2,1)S(1)} %get-tuple-element.18), channel_id=1, replica_groups=mesh['z'=4,'y'=4,'c'=2,'w'=4,'x'=4] {'z'}, dimensions={0} | all-to-all | bytes 393216 | tf_op jit(solution)/shard_map/all_to_all | solution.py:268
  59.3 14.8 %all_to_all.69 = bf16[4,768,128]{2,1,0:T(8,128)(2,1)} all-to-all(bf16[4,768,128]{2,1,0:T(8,128)(2,1)S(1)} %tile.19), channel_id=1, replica_groups=mesh['z'=4,'y'=4,'c'=2,'w'=4,'x'=4] {'y'}, dimensions={0} | all-to-all | bytes 1572864 | tf_op jit(solution)/shard_map/all_to_all | solution.py:269
  74.2 5.2 %collective-permute-start.1 = (bf16[3072,128]{1,0:T(8,128)(2,1)}, bf16[3072,128]{1,0:T(8,128)(2,1)}, u32[]{:S(2)}, u32[]{:S(2)}) collective-permute-start(bf16[3072,128]{1,0:T(8,128)(2,1)} %bitcast.8), channel_id=1, source_target_pairs={{0,16},{16,0},{1,17},{17,1},{2,18},{18,2},{3,19},{19,3},{4,20},{20... | collective-permute-start | bytes 2359304 | tf_op jit(solution)/shard_map/ppermute | solution.py:274
  79.5 2.2 collective-permute-done.1
  81.6 1.2 copy-done.2
  82.9 2.6 shard_map.96
  86.1 4.1 %all-to-all-start.4 = ((bf16[4,192,128]{2,1,0:T(8,128)(2,1)}), bf16[4,192,128]{2,1,0:T(8,128)(2,1)S(1)}, u32[]{:S(2)}, u32[]{:S(2)}) async-start(bf16[4,192,128]{2,1,0:T(8,128)(2,1)} %get-tuple-element.20), calls=%async_computation.4 | async-start | bytes 393216 | tf_op jit(solution)/shard_map/all_to_all | solution.py:268
  90.3 18.0 %all-gather.2.cloned.1.call-done.packed = bf16[256,3072]{1,0:T(8,128)(2,1)} async-done(((bf16[8,3072]{1,0:T(8,128)(2,1)}), bf16[256,3072]{1,0:T(8,128)(2,1)}) %all-gather.2.cloned.1.call-update) | async-done | bytes 1572880 | tf_op jit(solution)/shard_map/all_gather | solution.py:292
  108.3 1.2 copy-done.3
  109.5 1.4 copy-done.8
  110.9 1.4 copy-done.10
  113.3 3.5 %shard_map.98 = (bf16[32,192,128]{2,1,0:T(8,128)(2,1)S(1)}, f32[192,384]{1,0:T(8,128)S(1)}, f32[192,128]{1,0:T(8,128)S(1)}, f32[32,192,128]{2,1,0:T(8,128)S(1)}) custom-call(s32[2]{0:T(128)S(1)} %pad_add_fusion.meta, bf16[256,3072]{1,0:T(8,128)(2,1)S(1)} %copy-done.8, bf16[32,192,128]{2,1,0:T(8,128)(2,1)S(1)} %copy-done.10, f32[192,384]{1,0:T(8,128)S(1)} %copy-done.12, ...), custom_call_target="tpu_custom_call" | custom-call | tf_op jit(solution)/shard_map/pallas_call | solution.py:40
  116.8 1.6 copy-done.5
  118.4 1.1 copy-done.6
  121.1 15.4 %all_to_all.70 = bf16[4,768,128]{2,1,0:T(8,128)(2,1)S(1)} all-to-all(bf16[4,768,128]{2,1,0:T(8,128)(2,1)S(1)} %tile.41), channel_id=1, replica_groups=mesh['z'=4,'y'=4,'c'=2,'w'=4,'x'=4] {'y'}, dimensions={0} | all-to-all | bytes 1572864 | tf_op jit(solution)/shard_map/all_to_all | solution.py:269
  136.4 3.3 %collective-permute-start.2 = (bf16[3072,128]{1,0:T(8,128)(2,1)S(1)}, bf16[3072,128]{1,0:T(8,128)(2,1)S(1)}, u32[]{:S(2)}, u32[]{:S(2)}) collective-permute-start(bf16[3072,128]{1,0:T(8,128)(2,1)S(1)} %bitcast.33), channel_id=1, source_target_pairs={{0,16},{16,0},{1,17},{17,1},{2,18},{18,2},{3,19},{19,3},{4,20},{20... | collective-permute-start | bytes 2359304 | tf_op jit(solution)/shard_map/ppermute | solution.py:274
  139.8 1.9 collective-permute-done.2
  141.7 2.0 shard_map.97
  143.7 10.3 %all_to_all.71 = bf16[4,192,128]{2,1,0:T(8,128)(2,1)S(1)} all-to-all(bf16[4,192,128]{2,1,0:T(8,128)(2,1)S(1)} %get-tuple-element.21), channel_id=1, replica_groups=mesh['z'=4,'y'=4,'c'=2,'w'=4,'x'=4] {'z'}, dimensions={0} | all-to-all | bytes 393216 | tf_op jit(solution)/shard_map/all_to_all | solution.py:268
  154.2 15.0 %all_to_all.72 = bf16[4,768,128]{2,1,0:T(8,128)(2,1)S(1)} all-to-all(bf16[4,768,128]{2,1,0:T(8,128)(2,1)S(1)} %tile.43), channel_id=1, replica_groups=mesh['z'=4,'y'=4,'c'=2,'w'=4,'x'=4] {'y'}, dimensions={0} | all-to-all | bytes 1572864 | tf_op jit(solution)/shard_map/all_to_all | solution.py:269
  169.2 4.3 %collective-permute-start.3 = (bf16[3072,128]{1,0:T(8,128)(2,1)S(1)}, bf16[3072,128]{1,0:T(8,128)(2,1)S(1)}, u32[]{:S(2)}, u32[]{:S(2)}) collective-permute-start(bf16[3072,128]{1,0:T(8,128)(2,1)S(1)} %bitcast.36), channel_id=1, source_target_pairs={{0,16},{16,0},{1,17},{17,1},{2,18},{18,2},{3,19},{19,3},{4,20},{20... | collective-permute-start | bytes 2359304 | tf_op jit(solution)/shard_map/ppermute | solution.py:274
  173.6 1.7 shard_map.99.datt
  175.4 94.4 %reduce-scatter.2.cloned.1.call-done = f32[1,192,128]{2,1,0:T(8,128)} async-done(((f32[32,192,128]{2,1,0:T(8,128)}), f32[1,192,128]{2,1,0:T(8,128)}) %reduce-scatter.2.cloned.1.call-update) | async-done | bytes 98320 | tf_op jit(solution)/shard_map/reduce_scatter | solution.py:316
  270.7 1.3 shard_map.100
  272.1 15.4 %all_to_all.73.got = bf16[32,8,128]{2,1,0:T(8,128)(2,1)S(1)} all-to-all(bf16[32,8,128]{2,1,0:T(8,128)(2,1)S(1)} %bitcast.43), channel_id=1, replica_groups=mesh['z'=4,'y'=4,'c'=2,'w'=4,'x'=4] {'z','y','c'}, dimensions={0} | all-to-all | bytes 131072 | tf_op jit(solution)/shard_map/all_to_all | solution.py:331
  (63 shorter events, 9.1 us)
Async XLA Ops:
  7.2 72.2 %copy-start = (f32[4096]{0:T(1024)S(1)}, f32[4096]{0:T(1024)}, u32[]{:S(2)}) copy-start(f32[4096]{0:T(1024)} %param.15) | copy-start | bytes 49156
  8.8 17.5 %slice-start.1 = ((bf16[6,4096]{1,0:T(8,128)(2,1)}), bf16[6,1024]{1,0:T(8,128)(2,1)S(1)}, s32[]{:S(2)}) async-start(bf16[6,4096]{1,0:T(8,128)(2,1)} %param.9), calls=%async_computation.13 | async-start | bytes 32768 | tf_op jit(solution)/shard_map/slice | solution.py:278
  8.8 33.0 %slice-start = ((bf16[6,4096]{1,0:T(8,128)(2,1)}), bf16[6,3072]{1,0:T(8,128)(2,1)S(1)}, s32[]{:S(2)}) async-start(bf16[6,4096]{1,0:T(8,128)(2,1)} %param.9), calls=%async_computation.12 | async-start | bytes 98304 | tf_op jit(solution)/shard_map/slice | solution.py:278
  8.8 35.2 %copy-start.1 = (bf16[1,4096,384]{2,1,0:T(8,128)(2,1)S(1)}, bf16[1,4096,384]{2,1,0:T(8,128)(2,1)}, u32[]{:S(2)}) copy-start(bf16[1,4096,384]{2,1,0:T(8,128)(2,1)} %param.11) | copy-start | bytes 9437188
  8.8 35.2 %copy-start.15 = (f32[4096]{0:T(1024)S(1)}, f32[4096]{0:T(1024)}, u32[]{:S(2)}) copy-start(f32[4096]{0:T(1024)} %param.10) | copy-start | bytes 49156
  8.8 35.2 %copy-start.21 = (f32[1,128]{1,0:T(1,128)S(1)}, f32[1,128]{1,0:T(1,128)}, u32[]{:S(2)}) copy-start(f32[1,128]{1,0:T(1,128)} %q_gain.7) | copy-start | bytes 1540
  8.9 35.2 %copy-start.22 = (f32[1,128]{1,0:T(1,128)S(1)}, f32[1,128]{1,0:T(1,128)}, u32[]{:S(2)}) copy-start(f32[1,128]{1,0:T(1,128)} %k_gain.7) | copy-start | bytes 1540
  22.0 12.7 %all-to-all-start.1 = ((bf16[4,32,3072]{2,1,0:T(8,128)(2,1)}), bf16[4,32,3072]{2,1,0:T(8,128)(2,1)}, u32[]{:S(2)}, u32[]{:S(2)}) async-start(bf16[4,32,3072]{2,1,0:T(8,128)(2,1)} %tile.17), calls=%async_computation.1 | async-start | bytes 1572864 | tf_op jit(solution)/shard_map/all_to_all | solution.py:269
  26.2 82.0 %all-gather.2.cloned.1.call-start = ((), (), s32[]{:S(2)}) async-start(), calls=%async_computation.10 | async-start | bytes 1622016 | tf_op jit(solution)/shard_map/all_gather | solution.py:292
  34.7 9.3 %collective-permute-start = (bf16[128,3072]{1,0:T(8,128)(2,1)}, bf16[128,3072]{1,0:T(8,128)(2,1)}, u32[]{:S(2)}, u32[]{:S(2)}) collective-permute-start(bf16[128,3072]{1,0:T(8,128)(2,1)} %bitcast.3.xa), channel_id=1, source_target_pairs={{0,16},{16,0},{1,17},{17,1},{2,18},{18,2},{3,19},{19,3},{4,20},{20... | collective-permute-start | bytes 2359304 | tf_op jit(solution)/shard_map/ppermute | solution.py:274
  47.6 1.2 copy-start.9
  48.8 0.7 copy-start.11
  74.2 7.5 %collective-permute-start.1 = (bf16[3072,128]{1,0:T(8,128)(2,1)}, bf16[3072,128]{1,0:T(8,128)(2,1)}, u32[]{:S(2)}, u32[]{:S(2)}) collective-permute-start(bf16[3072,128]{1,0:T(8,128)(2,1)} %bitcast.8), channel_id=1, source_target_pairs={{0,16},{16,0},{1,17},{17,1},{2,18},{18,2},{3,19},{19,3},{4,20},{20... | collective-permute-start | bytes 2359304 | tf_op jit(solution)/shard_map/ppermute | solution.py:274
  81.6 1.2 copy-start.2
  86.1 22.1 %all-to-all-start.4 = ((bf16[4,192,128]{2,1,0:T(8,128)(2,1)}), bf16[4,192,128]{2,1,0:T(8,128)(2,1)S(1)}, u32[]{:S(2)}, u32[]{:S(2)}) async-start(bf16[4,192,128]{2,1,0:T(8,128)(2,1)} %get-tuple-element.20), calls=%async_computation.4 | async-start | bytes 393216 | tf_op jit(solution)/shard_map/all_to_all | solution.py:268
  90.2 179.6 %reduce-scatter.2.cloned.1.call-start = ((), (), s32[]{:S(2)}) async-start(), calls=%async_computation.11 | async-start | bytes 3244032 | tf_op jit(solution)/shard_map/reduce_scatter | solution.py:316
  108.3 1.2 copy-start.3
  109.5 1.4 copy-start.8
  110.9 1.4 copy-start.10
  112.3 1.0 copy-start.12
  116.8 1.6 copy-start.5
  118.4 1.1 copy-start.6
  119.6 0.7 copy-start.13
  120.3 0.6 copy-start.17
  136.4 5.2 %collective-permute-start.2 = (bf16[3072,128]{1,0:T(8,128)(2,1)S(1)}, bf16[3072,128]{1,0:T(8,128)(2,1)S(1)}, u32[]{:S(2)}, u32[]{:S(2)}) collective-permute-start(bf16[3072,128]{1,0:T(8,128)(2,1)S(1)} %bitcast.33), channel_id=1, source_target_pairs={{0,16},{16,0},{1,17},{17,1},{2,18},{18,2},{3,19},{19,3},{4,20},{20... | collective-permute-start | bytes 2359304 | tf_op jit(solution)/shard_map/ppermute | solution.py:274
  143.7 29.8 %copy-start.7 = (bf16[32,192,128]{2,1,0:T(8,128)(2,1)S(1)}, bf16[32,192,128]{2,1,0:T(8,128)(2,1)}, u32[]{:S(2)}) copy-start(bf16[32,192,128]{2,1,0:T(8,128)(2,1)} %copy-done.6) | copy-start | bytes 4718596
  143.7 29.8 %copy-start.14 = (f32[192,384]{1,0:T(8,128)S(1)}, f32[192,384]{1,0:T(8,128)}, u32[]{:S(2)}) copy-start(f32[192,384]{1,0:T(8,128)} %copy-done.13) | copy-start | bytes 884740
  143.7 29.8 %copy-start.18 = (f32[192,128]{1,0:T(8,128)S(1)}, f32[192,128]{1,0:T(8,128)}, u32[]{:S(2)}) copy-start(f32[192,128]{1,0:T(8,128)} %copy-done.17) | copy-start | bytes 294916
  169.2 6.2 %collective-permute-start.3 = (bf16[3072,128]{1,0:T(8,128)(2,1)S(1)}, bf16[3072,128]{1,0:T(8,128)(2,1)S(1)}, u32[]{:S(2)}, u32[]{:S(2)}) collective-permute-start(bf16[3072,128]{1,0:T(8,128)(2,1)S(1)} %bitcast.36), channel_id=1, source_target_pairs={{0,16},{16,0},{1,17},{17,1},{2,18},{18,2},{3,19},{19,3},{4,20},{20... | collective-permute-start | bytes 2359304 | tf_op jit(solution)/shard_map/ppermute | solution.py:274
  173.6 96.3 %copy-start.4 = (bf16[4096,128]{1,0:T(8,128)(2,1)S(1)}, bf16[4096,128]{1,0:T(8,128)(2,1)}, u32[]{:S(2)}) copy-start(bf16[4096,128]{1,0:T(8,128)(2,1)} %param.14) | copy-start | bytes 3145732
  173.6 96.2 %copy-start.20 = (bf16[192,128]{1,0:T(8,128)(2,1)S(1)}, bf16[192,128]{1,0:T(8,128)(2,1)}, u32[]{:S(2)}) copy-start(bf16[192,128]{1,0:T(8,128)(2,1)} %copy-done.19) | copy-start | bytes 147460
  269.8 0.9 copy-start.16
  (1 other events, 0.6 us)
Sparse Core Ops, SparseCore 0:
  42.6 65.6 all-gather.1
  121.1 148.6 reduce-scatter.1

commit v2 on v1

v2 whole, which is shorter than its diff:
```python
import jax
import jax.numpy as jnp
from jax import lax
from jax.experimental import pallas as pl
from jax.experimental.pallas import tpu as pltpu
from jax.sharding import Mesh, PartitionSpec as P

EPS = 1e-06
STEP = 0.5
SEQ = ("z", "y", "c")
BF = jnp.bfloat16
F32 = jnp.float32
NT = (((1,), (1,)), ((), ()))
TOK = 192
SCALE = 128 ** (-0.5)


def dot(a, b):
    return jnp.dot(a, b, preferred_element_type=F32)


def dot_nt(a, b):
    return lax.dot_general(a, b, NT, preferred_element_type=F32)


def row_mean(v):
    return jnp.mean(v, axis=-1, keepdims=True)


HELD = [pltpu.VMEM((32, TOK, 128), BF)]


def call(kernel, out_shape, n_scalar, *args, scratch=()):
    in_specs = [pl.BlockSpec(memory_space=pltpu.SMEM)] * n_scalar
    for a in args[n_scalar:]:
        if isinstance(a, tuple):
            in_specs.append(pl.BlockSpec(memory_space=pl.ANY))
        else:
            in_specs.append(pl.BlockSpec(memory_space=pltpu.VMEM))
    flat = [a[0] if isinstance(a, tuple) else a for a in args]
    multi = isinstance(out_shape, (tuple, list))
    vmem = pl.BlockSpec(memory_space=pltpu.VMEM)
    return pl.pallas_call(
        kernel,
        out_shape=out_shape,
        in_specs=in_specs,
        out_specs=[vmem] * len(out_shape) if multi else vmem,
        scratch_shapes=scratch,
        compiler_params=pltpu.CompilerParams(vmem_limit_bytes=20 * 1024 * 1024),
    )(*flat)


def shape(dims, kind=BF):
    return jax.ShapeDtypeStruct(dims, kind)


def selectors(first_row_token, rows):
    packed = lax.broadcasted_iota(jnp.int32, (TOK, rows), 1)
    token = lax.broadcasted_iota(jnp.int32, (TOK, rows), 0)
    slot = packed & 7
    base = first_row_token(packed)
    one = jnp.ones((TOK, rows), F32)
    zero = jnp.zeros((TOK, rows), F32)
    main = jnp.where((token == base + slot) & (slot < 6), one, zero).astype(BF)
    rest = [
        jnp.where((token == base + m + 3 * (slot - 6)) & (slot >= 6), one, zero).astype(BF)
        for m in range(3)
    ]
    return main, rest


def pieces(main, rest, chunk_of):
    tail = None
    for m in range(3):
        chunk = chunk_of(m)
        part = dot(rest[m], chunk)
        tail = part if tail is None else tail + part
        yield m * 1024, dot(main, chunk)
    yield 3072, tail


def qkv_norm(proj, q_gain, k_gain):
    query, key, val = proj[:, :128], proj[:, 128:256], proj[:, 256:]
    rq = lax.rsqrt(row_mean(query * query) + EPS)
    rk = lax.rsqrt(row_mean(key * key) + EPS)
    qn = (query * rq * q_gain).astype(BF)
    kn = (key * rk * k_gain).astype(BF)
    return query, key, rq, rk, qn, kn, val.astype(BF)


def probabilities(qn, kn):
    expo = jnp.exp(dot_nt(qn, kn) * SCALE)
    return expo / jnp.sum(expo, axis=-1, keepdims=True)


def attend(proj, q_gain, k_gain):
    _, _, _, _, qn, kn, val = qkv_norm(proj, q_gain, k_gain)
    return dot(probabilities(qn, kn).astype(BF), val).astype(BF)


def attend_tangent(proj, d_proj, q_gain, k_gain):
    query, key, rq, rk, qn, kn, val = qkv_norm(proj, q_gain, k_gain)
    dq, dk, dv = d_proj[:, :128], d_proj[:, 128:256], d_proj[:, 256:].astype(BF)
    drq = -(rq * rq * rq) * row_mean(query * dq)
    drk = -(rk * rk * rk) * row_mean(key * dk)
    dqn = ((dq * rq + query * drq) * q_gain).astype(BF)
    dkn = ((dk * rk + key * drk) * k_gain).astype(BF)
    probs = probabilities(qn, kn)
    ds = (dot_nt(dqn, kn) + dot_nt(qn, dkn)) * SCALE
    d_probs = probs * (ds - jnp.sum(probs * ds, axis=-1, keepdims=True))
    probs = probs.astype(BF)
    return dot(probs, val).astype(BF), dot(d_probs.astype(BF), val) + dot(probs, dv)


def pack_kernel(state, probe, state_ref, probe_ref):
    for source, write in ((state, None), (probe, probe_ref)):
        main = source[:, :3072]
        sixth = jnp.concatenate([source[q : q + 1, 3072:] for q in range(3)], axis=1)
        seventh = jnp.concatenate([source[q : q + 1, 3072:] for q in range(3, 6)], axis=1)
        whole = jnp.concatenate([main, sixth, seventh], axis=0)
        if write is None:
            for i in range(4):
                state_ref[i] = whole
        else:
            write[:, :3072] = whole
            write[:, 3072:] = whole


def core_order(core):
    def first_token(packed):
        inner = packed & 127
        z = (inner >> 3) & 3
        y = inner >> 5
        c = jnp.where((packed >> 7) == 0, core, 1 - core)
        return (z * 8 + y * 2 + c) * 6

    return first_token


def unpack_state(core, xa, xb, held):
    main, rest = selectors(core_order(core), 256)
    squares = jnp.zeros((TOK, 128), F32)

    def chunk_of(m):
        cols = slice(m * 1024, (m + 1) * 1024)
        return jnp.concatenate([xa[:, cols], xb[:, cols]], axis=0)

    for start, x in pieces(main, rest, chunk_of):
        for b in range(8):
            piece = x[:, b * 128 : (b + 1) * 128]
            squares = squares + piece * piece
            held[start // 128 + b] = piece.astype(BF)
    return lax.rsqrt(row_sum(squares) * (1.0 / 4096) + EPS)


def row_sum(v):
    return jnp.sum(v, axis=-1, keepdims=True)


def first_kernel(meta, xa, xb, maps, gain, q_gain, k_gain, att_ref, col_ref, held):
    recip = unpack_state(meta[0], xa, xb, held)
    proj = jnp.zeros((TOK, 384), F32)
    for h in range(0, 32, 2):
        left = (held[h].astype(F32) * recip * gain[h]).astype(BF)
        right = (held[h + 1].astype(F32) * recip * gain[h + 1]).astype(BF)
        rows = jnp.concatenate([maps[h], maps[h + 1]], axis=0)
        proj = proj + dot(jnp.concatenate([left, right], axis=1), rows)
    att = attend(proj, q_gain[...], k_gain[...])
    for i in range(4):
        att_ref[i] = att
    col_ref[...] = held[meta[1]]


def blocks(core, own, oth):
    for side, c in ((own, core), (oth, 1 - core)):
        for y in range(4):
            for z in (0, 2):
                yield side, y * 4 + z, z * 8 + y * 2 + c


def out_product(core, own, oth, out_map):
    total = jnp.zeros((own.shape[1], 128), F32)
    for side, b, h in blocks(core, own, oth):
        left = jnp.concatenate([side[b], side[b + 1]], axis=1)
        right = jnp.concatenate([out_map[h], out_map[h + 8]], axis=0)
        total = total + dot(left, right)
    return total


def middle_kernel(meta, own, oth, out_map, gate, col, vel_ref, mid_ref):
    vel = (gate[...] * out_product(meta[0], own, oth, out_map)).astype(BF)
    vel_ref[...] = vel
    mid = (col[...].astype(F32) + STEP * vel.astype(F32)).astype(BF)
    for i in range(4):
        mid_ref[i] = mid


def both_rows(x, probe, recip, d_recip, gain):
    normed = (x * recip * gain).astype(BF)
    d_normed = ((probe * recip + x * d_recip) * gain).astype(BF)
    return jnp.concatenate([normed, d_normed], axis=0)


def tangent_kernel(
    meta, xa, xb, packed, maps, gain, q_gain, k_gain, after, probe_ref, datt_ref, held
):
    recip = unpack_state(meta[0], xa, xb, held)
    main, rest = selectors(lambda row: (row >> 3) * 6, 256)
    dots = jnp.zeros((TOK, 128), F32)
    for start, x in pieces(main, rest, lambda m: packed[:, m * 1024 : (m + 1) * 1024]):
        for b in range(8):
            piece = x[:, b * 128 : (b + 1) * 128]
            dots = dots + piece * held[start // 128 + b].astype(F32)
            probe_ref[start // 128 + b] = piece.astype(BF)
    d_recip = -(recip * recip * recip) * (row_sum(dots) * (1.0 / 4096))
    proj = jnp.zeros((2 * TOK, 384), F32)
    for h in range(0, 32, 2):
        pair = [
            both_rows(held[i].astype(F32), probe_ref[i].astype(F32), recip, d_recip, gain[i])
            for i in (h, h + 1)
        ]
        rows = jnp.concatenate([maps[h], maps[h + 1]], axis=0)
        proj = proj + dot(jnp.concatenate(pair, axis=1), rows)
    datt_ref[...] = attend_tangent(proj[:TOK], proj[TOK:], q_gain[...], k_gain[...])[1]


def second_kernel(meta, own, oth, probe, maps, gain, q_gain, k_gain, datt1, both_ref):
    core = meta[0]
    squares = jnp.zeros((TOK, 128), F32)
    dots = jnp.zeros((TOK, 128), F32)
    for side, b, h in blocks(core, own, oth):
        for i in range(2):
            x = side[b + i].astype(F32)
            squares = squares + x * x
            dots = dots + x * probe[h + 8 * i].astype(F32)
    recip = lax.rsqrt(row_sum(squares) * (1.0 / 4096) + EPS)
    d_recip = -(recip * recip * recip) * (row_sum(dots) * (1.0 / 4096))
    proj = jnp.zeros((2 * TOK, 384), F32)
    for side, b, h in blocks(core, own, oth):
        pair = [
            both_rows(
                side[b + i].astype(F32), probe[h + 8 * i].astype(F32), recip, d_recip, gain[h + 8 * i]
            )
            for i in range(2)
        ]
        rows = jnp.concatenate([maps[h], maps[h + 8]], axis=0)
        proj = proj + dot(jnp.concatenate(pair, axis=1), rows)
    att, d_att = attend_tangent(proj[:TOK], proj[TOK:], q_gain[...], k_gain[...])
    d_both = (d_att + datt1[...]).astype(BF)
    for i in range(4):
        both_ref[i, :TOK] = att
        both_ref[i, TOK:] = d_both


def last_kernel(meta, own, oth, out_map, gate, col, vel1, probe, out_ref):
    mapped = gate[...] * out_product(meta[0], own, oth, out_map)
    both = vel1[...].astype(F32) + mapped[:TOK].astype(BF).astype(F32)
    new = (col[...].astype(F32) + 0.5 * STEP * both).astype(BF)
    row = lax.broadcasted_iota(jnp.int32, (256, TOK), 0)
    token = lax.broadcasted_iota(jnp.int32, (256, TOK), 1)
    hit = (token == (row >> 3) * 6 + (row & 7)) & ((row & 7) < 6)
    place = jnp.where(hit, jnp.ones((256, TOK), F32), jnp.zeros((256, TOK), F32)).astype(BF)
    laid = dot(place, new)
    terms = mapped[TOK:] * probe[meta[1]].astype(F32)
    trace = row_sum(jnp.sum(terms, axis=0, keepdims=True))
    high = trace.astype(BF).astype(F32)
    mid = (trace - high).astype(BF).astype(F32)
    low = trace - high - mid
    lane = lax.broadcasted_iota(jnp.int32, (1, 128), 1)
    coded = jnp.where(lane == 0, high, jnp.where(lane == 1, mid, jnp.where(lane == 2, low, 0.0)))
    slot = lax.broadcasted_iota(jnp.int32, (256, 128), 0) & 7
    out_ref[...] = jnp.where(slot == 6, coded, laid).astype(BF)


def land_kernel(got, next_ref, change_ref):
    total = jnp.zeros((8, 128), F32)
    for j in range(32):
        block = got[j]
        next_ref[:, j * 128 : (j + 1) * 128] = block[:6]
        total = total + block.astype(F32)
    change_ref[...] = jnp.broadcast_to(-0.5 * STEP * row_sum(total[6:7, :]) / TOK, (1, 128))


def spread(copies):
    n, rows, lanes = copies.shape
    a = lax.all_to_all(copies.reshape(n * rows, lanes), "z", 0, 0, tiled=True)
    return a, lax.all_to_all(jnp.tile(a, (4, 1)), "y", 0, 0, tiled=True)


def swap(block):
    return lax.ppermute(block, "c", [(0, 1), (1, 0)])


def gathered(copies):
    rows = copies.shape[1]
    early, own = spread(copies)
    other = swap(own)
    return early, own.reshape(16, rows, 128), other.reshape(16, rows, 128)


def per_device(state, probe, norm_gain, head_maps, query_gain, key_gain, out_map, out_gate):
    place = lax.axis_index(SEQ)
    meta = jnp.stack([lax.axis_index("c"), place]).astype(jnp.int32)
    gate = lax.dynamic_slice_in_dim(out_gate, place * 128, 128).reshape(1, 128)
    maps = head_maps.reshape(32, 128, 384)
    outs = out_map.reshape(32, 128, 128)
    gain = norm_gain.reshape(32, 1, 128)

    packed_state, packed_probe = call(
        pack_kernel, [shape((4, 8, 3072)), shape((8, 6144))], 0, state, probe
    )
    probe_all = lax.all_gather(packed_probe, SEQ, axis=0, tiled=True)
    _, own = spread(packed_state)
    oth = swap(own)
    att1, col = call(
        first_kernel, [shape((4, TOK, 128)), shape((TOK, 128))],
        1, meta, own, oth, maps, gain, query_gain, key_gain, scratch=HELD,
    )
    _, own1, oth1 = gathered(att1)
    vel1, mid = call(
        middle_kernel, [shape((TOK, 128)), shape((4, TOK, 128))],
        1, meta, own1, oth1, outs, gate, col,
    )
    early, own_m, oth_m = gathered(mid)
    probe_blocks, datt1 = call(
        tangent_kernel, [shape((32, TOK, 128)), shape((TOK, 128), F32)],
        1, meta, own, oth, probe_all, maps, gain, query_gain, key_gain, (early,), scratch=HELD,
    )
    both = call(
        second_kernel, shape((4, 2 * TOK, 128)),
        1, meta, own_m, oth_m, probe_blocks, maps, gain, query_gain, key_gain, datt1,
    )
    _, own2, oth2 = gathered(both)
    columns = call(
        last_kernel, shape((256, 128)),
        1, meta, own2, oth2, outs, gate, col, vel1, probe_blocks,
    )
    got = lax.all_to_all(columns, SEQ, 0, 0, tiled=True).reshape(32, 8, 128)
    next_state, change = call(land_kernel, [shape((6, 4096)), shape((1, 128), F32)], 0, got)
    return next_state, change[0, :1]


def solution(mesh):
    split = Mesh(mesh.devices.reshape(4, 4, 2, 4, 4), ("z", "y", "c", "w", "x"))
    rows = P(("w", "x", "z", "y", "c"), None)
    return jax.shard_map(
        per_device,
        mesh=split,
        in_specs=(rows, rows, P(), P(SEQ, None, None), P(SEQ, None), P(SEQ, None), P(None, SEQ), P()),
        out_specs=(rows, P(("w", "x"))),
        check_vma=False,
    )
```

time: 296 us -> 193 us (0.65)
  waiting for transfers between devices: 126 us -> 7.36 us
  blocking collectives: 92.8 us -> 126 us
  local copies, waits for them, and re-layouts: 16.8 us -> 5.36 us
  starting transfers between devices: 28.3 us -> 21.2 us
  Pallas kernels: 15.5 us -> 18.5 us
    reduce_scatter x1 -> x0, waiting for transfers between devices: 94.4 us -> none  [per_device(): adjoint = lax.psum_scatter(back, SEQ, scatter_dimension=0, tiled=False)]
    all_to_all x6 -> x8, blocking collectives: 77.4 us -> 114 us  [the longest x4 67 us: spread(): return (a, lax.all_to_all(jnp.tile(a, (4, 1)), 'y', 0, 0, tiled=True))]
    all_gather x1, waiting for transfers between devices: 18 us -> 0.02 us  [per_device(): probe_all = lax.all_gather(packed_probe, SEQ, axis=0, tiled=True)]
    unnamed x46 -> x20, local copies, waits for them, and re-layouts: 13.8 us -> 4.81 us
    all_to_all x2 -> x0, waiting for transfers between devices: 8.41 us -> none  [the longest x1 8.41 us: spread(): b = lax.all_to_all(jnp.tile(a, (4, 1)), 'y', 0, 0, tiled=True)]
    all_to_all x2 -> x0, starting transfers between devices: 8.36 us -> none  [the longest x1 4.24 us: spread(): b = lax.all_to_all(jnp.tile(a, (4, 1)), 'y', 0, 0, tiled=True)]
    all_to_all x1, blocking collectives: 15.4 us -> 11.5 us  [per_device(): got = lax.all_to_all(columns, SEQ, 0, 0, tiled=True).reshape(32, 8, 128)]
    pallas_call x7, Pallas kernels: 15.5 us -> 18.5 us  [call(): pl.pallas_call(kernel, out_shape=out_shape, in_specs=in_specs, out_specs=...]
  transfers between devices with their start and end apart: 8 -> 5, of which waited for: 7 -> 3; matrix products, arithmetic and copies ran while one was open for 0% -> 0% of each run, Pallas kernels for 3% -> 6%
where the time goes in v2:
time: 193 us; the launch traced here: 192 us
  blocking collectives  126 us (65%)
  starting transfers between devices  21.2 us (11%)
  Pallas kernels  18.5 us (10%)
  between operations  14.2 us (7%)
  waiting for transfers between devices  7.36 us (4%)
  local copies, waits for them, and re-layouts  5.36 us (3%)
    all_to_all x4, blocking collectives, spread(): return (a, lax.all_to_all(jnp.tile(a, (4, 1)), 'y', 0, 0, tiled=True))  67 us
    all_to_all x4, blocking collectives, spread(): a = lax.all_to_all(copies.reshape(n * rows, lanes), 'z', 0, 0, tiled=True)  47.1 us
    ppermute x4, starting transfers between devices, swap(): return lax.ppermute(block, 'c', [(0, 1), (1, 0)])  21.1 us
    pallas_call x7, Pallas kernels, call(): pl.pallas_call(kernel, out_shape=out_shape, in_specs=in_specs, out_specs=...  18.5 us
    all_to_all x1, blocking collectives, per_device(): got = lax.all_to_all(columns, SEQ, 0, 0, tiled=True).reshape(32, 8, 128)  11.5 us
    ppermute x4, waiting for transfers between devices, swap(): return lax.ppermute(block, 'c', [(0, 1), (1, 0)])  7.32 us
    unnamed x20, local copies, waits for them, and re-layouts  4.81 us
  transfers between devices with their start and end apart: 5, of which 3 were waited for; matrix products, arithmetic and copies ran while one was open for 0% of the time, Pallas kernels for 6%

profile of v2, /device:TPU:1, one launch (start us, length us, event | category | flops | bytes accessed | tf_op | source)
XLA Modules:
  0.0 192.3 jit_solution(14423440247562550773)
XLA Ops:
  7.2 0.8 copy-done.6
  8.1 0.8 copy-done.7
  8.9 0.7 shard_map.95
  9.6 12.0 %all_to_all.67 = bf16[4,8,3072]{2,1,0:T(8,128)(2,1)S(1)} all-to-all(bf16[4,8,3072]{2,1,0:T(8,128)(2,1)S(1)} %get-tuple-element.12), channel_id=1, replica_groups=mesh['z'=4,'y'=4,'c'=2,'w'=4,'x'=4] {'z'}, dimensions={0} | all-to-all | bytes 393216 | tf_op jit(solution)/shard_map/all_to_all | solution.py:286
  21.7 13.3 %all_to_all.68 = bf16[4,32,3072]{2,1,0:T(8,128)(2,1)} all-to-all(bf16[4,32,3072]{2,1,0:T(8,128)(2,1)S(1)} %tile.17), channel_id=1, replica_groups=mesh['z'=4,'y'=4,'c'=2,'w'=4,'x'=4] {'y'}, dimensions={0} | all-to-all | bytes 1572864 | tf_op jit(solution)/shard_map/all_to_all | solution.py:287
  35.1 7.6 %collective-permute-start = (bf16[128,3072]{1,0:T(8,128)(2,1)}, bf16[128,3072]{1,0:T(8,128)(2,1)}, u32[]{:S(2)}, u32[]{:S(2)}) collective-permute-start(bf16[128,3072]{1,0:T(8,128)(2,1)} %bitcast.3.xa), channel_id=1, source_target_pairs={{0,16},{16,0},{1,17},{17,1},{2,18},{18,2},{3,19},{19,3},{4,20},{20... | collective-permute-start | bytes 2359304 | tf_op jit(solution)/shard_map/ppermute | solution.py:291
  42.7 0.1 pad_add_fusion.meta
  42.8 2.2 %collective-permute-done.xb = bf16[128,3072]{1,0:T(8,128)(2,1)} collective-permute-done((bf16[128,3072]{1,0:T(8,128)(2,1)}, bf16[128,3072]{1,0:T(8,128)(2,1)}, u32[]{:S(2)}, u32[]{:S(2)}) %collective-permute-start) | collective-permute-done | bytes 786464 | tf_op jit(solution)/shard_map/ppermute | solution.py:291
  45.0 3.7 %shard_map.96 = (bf16[4,192,128]{2,1,0:T(8,128)(2,1)S(1)}, bf16[192,128]{1,0:T(8,128)(2,1)S(1)}) custom-call(s32[2]{0:T(128)S(1)} %pad_add_fusion.meta, bf16[128,3072]{1,0:T(8,128)(2,1)} %bitcast.3.xa, bf16[128,3072]{1,0:T(8,128)(2,1)} %collective-permute-done.xb, bf16[32,128,384]{2,1,0:T(8,128)(2,1)S(1)} %bitcast.24, f32[32,1,128]{2,1,0:T(1,128)S(1)} %bitcast.35, ...), custom_call_target="tpu_custom_call" | custom-call | tf_op jit(solution)/shard_map/pallas_call | solution.py:43
  48.7 10.8 %all_to_all.69 = bf16[4,192,128]{2,1,0:T(8,128)(2,1)S(1)} all-to-all(bf16[4,192,128]{2,1,0:T(8,128)(2,1)S(1)} %get-tuple-element.13), channel_id=1, replica_groups=mesh['z'=4,'y'=4,'c'=2,'w'=4,'x'=4] {'z'}, dimensions={0} | all-to-all | bytes 393216 | tf_op jit(solution)/shard_map/all_to_all | solution.py:286
  59.4 0.1 tile.19
  59.5 18.4 %all_to_all.70 = bf16[4,768,128]{2,1,0:T(8,128)(2,1)} all-to-all(bf16[4,768,128]{2,1,0:T(8,128)(2,1)S(1)} %tile.19), channel_id=1, replica_groups=mesh['z'=4,'y'=4,'c'=2,'w'=4,'x'=4] {'y'}, dimensions={0} | all-to-all | bytes 1572864 | tf_op jit(solution)/shard_map/all_to_all | solution.py:287
  78.0 4.3 %collective-permute-start.1 = (bf16[3072,128]{1,0:T(8,128)(2,1)}, bf16[3072,128]{1,0:T(8,128)(2,1)}, u32[]{:S(2)}, u32[]{:S(2)}) collective-permute-start(bf16[3072,128]{1,0:T(8,128)(2,1)} %bitcast.8), channel_id=1, source_target_pairs={{0,16},{16,0},{1,17},{17,1},{2,18},{18,2},{3,19},{19,3},{4,20},{20... | collective-permute-start | bytes 2359304 | tf_op jit(solution)/shard_map/ppermute | solution.py:291
  82.3 0.1 dynamic-slice_bitcast_fusion.gate
  82.4 2.1 %collective-permute-done.1 = bf16[3072,128]{1,0:T(8,128)(2,1)} collective-permute-done((bf16[3072,128]{1,0:T(8,128)(2,1)}, bf16[3072,128]{1,0:T(8,128)(2,1)}, u32[]{:S(2)}, u32[]{:S(2)}) %collective-permute-start.1) | collective-permute-done | bytes 786464 | tf_op jit(solution)/shard_map/ppermute | solution.py:291
  84.6 1.2 copy-done.2
  85.8 2.0 %shard_map.97 = (bf16[192,128]{1,0:T(8,128)(2,1)S(1)}, bf16[4,192,128]{2,1,0:T(8,128)(2,1)S(1)}) custom-call(s32[2]{0:T(128)S(1)} %pad_add_fusion.meta, bf16[16,192,128]{2,1,0:T(8,128)(2,1)} %bitcast.7.own, bf16[16,192,128]{2,1,0:T(8,128)(2,1)} %bitcast.9.oth, bf16[32,128,128]{2,1,0:T(8,128)(2,1)S(1)} %bitcast.29, ...), custom_call_target="tpu_custom_call" | custom-call | tf_op jit(solution)/shard_map/pallas_call | solution.py:43
  87.7 9.0 %all_to_all.71 = bf16[4,192,128]{2,1,0:T(8,128)(2,1)S(1)} all-to-all(bf16[4,192,128]{2,1,0:T(8,128)(2,1)S(1)} %get-tuple-element.15), channel_id=1, replica_groups=mesh['z'=4,'y'=4,'c'=2,'w'=4,'x'=4] {'z'}, dimensions={0} | all-to-all | bytes 393216 | tf_op jit(solution)/shard_map/all_to_all | solution.py:286
  96.8 0.1 tile.41
  96.9 13.1 %all_to_all.72 = bf16[4,768,128]{2,1,0:T(8,128)(2,1)} all-to-all(bf16[4,768,128]{2,1,0:T(8,128)(2,1)S(1)} %tile.41), channel_id=1, replica_groups=mesh['z'=4,'y'=4,'c'=2,'w'=4,'x'=4] {'y'}, dimensions={0} | all-to-all | bytes 1572864 | tf_op jit(solution)/shard_map/all_to_all | solution.py:287
  109.9 5.2 %collective-permute-start.2 = (bf16[3072,128]{1,0:T(8,128)(2,1)}, bf16[3072,128]{1,0:T(8,128)(2,1)}, u32[]{:S(2)}, u32[]{:S(2)}) collective-permute-start(bf16[3072,128]{1,0:T(8,128)(2,1)} %bitcast.14), channel_id=1, source_target_pairs={{0,16},{16,0},{1,17},{17,1},{2,18},{18,2},{3,19},{19,3},{4,20},{20... | collective-permute-start | bytes 2359304 | tf_op jit(solution)/shard_map/ppermute | solution.py:291
  115.2 1.9 copy-done.4
  117.0 5.5 %shard_map.98 = (bf16[32,192,128]{2,1,0:T(8,128)(2,1)S(1)}, f32[192,128]{1,0:T(8,128)S(1)}) custom-call(s32[2]{0:T(128)S(1)} %pad_add_fusion.meta, bf16[128,3072]{1,0:T(8,128)(2,1)} %bitcast.3.xa, bf16[128,3072]{1,0:T(8,128)(2,1)} %collective-permute-done.xb, bf16[256,6144]{1,0:T(8,128)(2,1)S(1)} %copy-done.4, bf16[32,128,384]{2,1,0:T(8,128)(2,1)S(1)} %bitcast.25, ...), custom_call_target="tpu_custom_call" | custom-call | tf_op jit(solution)/shard_map/pallas_call | solution.py:43
  122.5 4.4 %shard_map.99 = bf16[4,384,128]{2,1,0:T(8,128)(2,1)S(1)} custom-call(s32[2]{0:T(128)S(1)} %pad_add_fusion.meta, bf16[16,192,128]{2,1,0:T(8,128)(2,1)} %bitcast.13.own, bf16[16,192,128]{2,1,0:T(8,128)(2,1)} %bitcast.15.oth, bf16[32,192,128]{2,1,0:T(8,128)(2,1)S(1)} %get-tuple-element.17.probe, bf16[32,128,384]{2,1,0:T(8,128)(2,1)S(1)} %bitcast.26, ...), custom_call_target="tpu_custom_call" | custom-call | tf_op jit(solution)/shard_map/pallas_call | solution.py:43
  126.9 15.3 %all_to_all.73 = bf16[4,384,128]{2,1,0:T(8,128)(2,1)S(1)} all-to-all(bf16[4,384,128]{2,1,0:T(8,128)(2,1)S(1)} %shard_map.99), channel_id=1, replica_groups=mesh['z'=4,'y'=4,'c'=2,'w'=4,'x'=4] {'z'}, dimensions={0} | all-to-all | bytes 786432 | tf_op jit(solution)/shard_map/all_to_all | solution.py:286
  142.3 0.2 tile.43
  142.5 22.2 %all_to_all.74 = bf16[4,1536,128]{2,1,0:T(8,128)(2,1)S(1)} all-to-all(bf16[4,1536,128]{2,1,0:T(8,128)(2,1)S(1)} %tile.43), channel_id=1, replica_groups=mesh['z'=4,'y'=4,'c'=2,'w'=4,'x'=4] {'y'}, dimensions={0} | all-to-all | bytes 3145728 | tf_op jit(solution)/shard_map/all_to_all | solution.py:287
  164.7 3.9 %collective-permute-start.3 = (bf16[6144,128]{1,0:T(8,128)(2,1)S(1)}, bf16[6144,128]{1,0:T(8,128)(2,1)S(1)}, u32[]{:S(2)}, u32[]{:S(2)}) collective-permute-start(bf16[6144,128]{1,0:T(8,128)(2,1)S(1)} %bitcast.27), channel_id=1, source_target_pairs={{0,16},{16,0},{1,17},{17,1},{2,18},{18,2},{3,19},{19,3},{4,20},{20... | collective-permute-start | bytes 4718600 | tf_op jit(solution)/shard_map/ppermute | solution.py:291
  168.6 3.0 %collective-permute-done.3 = bf16[6144,128]{1,0:T(8,128)(2,1)S(1)} collective-permute-done((bf16[6144,128]{1,0:T(8,128)(2,1)S(1)}, bf16[6144,128]{1,0:T(8,128)(2,1)S(1)}, u32[]{:S(2)}, u32[]{:S(2)}) %collective-permute-start.3) | collective-permute-done | bytes 1572896 | tf_op jit(solution)/shard_map/ppermute | solution.py:291
  171.6 1.7 shard_map.100
  173.4 11.5 %all_to_all.75.got = bf16[32,8,128]{2,1,0:T(8,128)(2,1)S(1)} all-to-all(bf16[32,8,128]{2,1,0:T(8,128)(2,1)S(1)} %bitcast.34), channel_id=1, replica_groups=mesh['z'=4,'y'=4,'c'=2,'w'=4,'x'=4] {'z','y','c'}, dimensions={0} | all-to-all | bytes 131072 | tf_op jit(solution)/shard_map/all_to_all | solution.py:338
  184.8 0.6 shard_map.101
  (21 shorter events, 0.2 us)
Async XLA Ops:
  7.2 75.2 %copy-start = (f32[4096]{0:T(1024)S(1)}, f32[4096]{0:T(1024)}, u32[]{:S(2)}) copy-start(f32[4096]{0:T(1024)} %param.15) | copy-start | bytes 49156
  7.2 108.0 %all-gather.2.cloned.1.call-start = ((), (), s32[]{:S(2)}) async-start(), calls=%async_computation.9 | async-start | bytes 3244032 | tf_op jit(solution)/shard_map/all_gather | solution.py:312
  7.2 0.8 copy-start.6
  8.1 0.8 copy-start.7
  8.9 36.1 %copy-start.1 = (bf16[1,4096,384]{2,1,0:T(8,128)(2,1)S(1)}, bf16[1,4096,384]{2,1,0:T(8,128)(2,1)}, u32[]{:S(2)}) copy-start(bf16[1,4096,384]{2,1,0:T(8,128)(2,1)} %param.11) | copy-start | bytes 9437188
  9.6 35.4 %copy-start.5 = (f32[4096]{0:T(1024)S(1)}, f32[4096]{0:T(1024)}, u32[]{:S(2)}) copy-start(f32[4096]{0:T(1024)} %param.10) | copy-start | bytes 49156
  9.6 35.4 %copy-start.8 = (f32[1,128]{1,0:T(1,128)S(1)}, f32[1,128]{1,0:T(1,128)}, u32[]{:S(2)}) copy-start(f32[1,128]{1,0:T(1,128)} %q_gain.5) | copy-start | bytes 1540
  9.6 35.4 %copy-start.9 = (f32[1,128]{1,0:T(1,128)S(1)}, f32[1,128]{1,0:T(1,128)}, u32[]{:S(2)}) copy-start(f32[1,128]{1,0:T(1,128)} %k_gain.5) | copy-start | bytes 1540
  35.1 9.9 %collective-permute-start = (bf16[128,3072]{1,0:T(8,128)(2,1)}, bf16[128,3072]{1,0:T(8,128)(2,1)}, u32[]{:S(2)}, u32[]{:S(2)}) collective-permute-start(bf16[128,3072]{1,0:T(8,128)(2,1)} %bitcast.3.xa), channel_id=1, source_target_pairs={{0,16},{16,0},{1,17},{17,1},{2,18},{18,2},{3,19},{19,3},{4,20},{20... | collective-permute-start | bytes 2359304 | tf_op jit(solution)/shard_map/ppermute | solution.py:291
  78.0 6.6 %collective-permute-start.1 = (bf16[3072,128]{1,0:T(8,128)(2,1)}, bf16[3072,128]{1,0:T(8,128)(2,1)}, u32[]{:S(2)}, u32[]{:S(2)}) collective-permute-start(bf16[3072,128]{1,0:T(8,128)(2,1)} %bitcast.8), channel_id=1, source_target_pairs={{0,16},{16,0},{1,17},{17,1},{2,18},{18,2},{3,19},{19,3},{4,20},{20... | collective-permute-start | bytes 2359304 | tf_op jit(solution)/shard_map/ppermute | solution.py:291
  84.6 1.2 copy-start.2
  109.9 12.6 %collective-permute-start.2 = (bf16[3072,128]{1,0:T(8,128)(2,1)}, bf16[3072,128]{1,0:T(8,128)(2,1)}, u32[]{:S(2)}, u32[]{:S(2)}) collective-permute-start(bf16[3072,128]{1,0:T(8,128)(2,1)} %bitcast.14), channel_id=1, source_target_pairs={{0,16},{16,0},{1,17},{17,1},{2,18},{18,2},{3,19},{19,3},{4,20},{20... | collective-permute-start | bytes 2359304 | tf_op jit(solution)/shard_map/ppermute | solution.py:291
  115.1 1.9 copy-start.4
  142.5 29.2 %copy-start.3 = (bf16[4096,128]{1,0:T(8,128)(2,1)S(1)}, bf16[4096,128]{1,0:T(8,128)(2,1)}, u32[]{:S(2)}) copy-start(bf16[4096,128]{1,0:T(8,128)(2,1)} %param.14) | copy-start | bytes 3145732
  164.7 7.0 %collective-permute-start.3 = (bf16[6144,128]{1,0:T(8,128)(2,1)S(1)}, bf16[6144,128]{1,0:T(8,128)(2,1)S(1)}, u32[]{:S(2)}, u32[]{:S(2)}) collective-permute-start(bf16[6144,128]{1,0:T(8,128)(2,1)S(1)} %bitcast.27), channel_id=1, source_target_pairs={{0,16},{16,0},{1,17},{17,1},{2,18},{18,2},{3,19},{19,3},{4,20},{20... | collective-permute-start | bytes 4718600 | tf_op jit(solution)/shard_map/ppermute | solution.py:291
Sparse Core Ops, SparseCore 0:
  10.2 76.1 all-gather.1

commit v3 on v2

--- a/solution.py
+++ b/solution.py
@@ -252,32 +252,62 @@
         both_ref[i, TOK:] = d_both
 
 
-def last_kernel(meta, own, oth, out_map, gate, col, vel1, probe, out_ref):
-    mapped = gate[...] * out_product(meta[0], own, oth, out_map)
-    both = vel1[...].astype(F32) + mapped[:TOK].astype(BF).astype(F32)
-    new = (col[...].astype(F32) + 0.5 * STEP * both).astype(BF)
+def last_kernel(meta, own, oth, out_maps, gates, vel1, probe, out_ref, rows, sem):
+    core, place, plane = meta[0], meta[1], meta[2]
+    copy = pltpu.make_async_copy(out_maps.at[:, pl.ds(plane * 8, 8)], rows, sem)
+    copy.start()
     row = lax.broadcasted_iota(jnp.int32, (256, TOK), 0)
     token = lax.broadcasted_iota(jnp.int32, (256, TOK), 1)
     hit = (token == (row >> 3) * 6 + (row & 7)) & ((row & 7) < 6)
-    place = jnp.where(hit, jnp.ones((256, TOK), F32), jnp.zeros((256, TOK), F32)).astype(BF)
-    laid = dot(place, new)
-    terms = mapped[TOK:] * probe[meta[1]].astype(F32)
-    trace = row_sum(jnp.sum(terms, axis=0, keepdims=True))
+    lay = jnp.where(hit, jnp.ones((256, TOK), F32), jnp.zeros((256, TOK), F32)).astype(BF)
+    left = []
+    for y in range(4):
+        mine = own[y]
+        other = oth[y]
+        first = jnp.where(core == 0, mine, other)
+        second = jnp.where(core == 0, other, mine)
+        left.append(jnp.concatenate([first, second], axis=1))
+    in_plane = place - plane * 8
+    copy.wait()
+    trace = jnp.zeros((1, 128), F32)
+    laid = []
+    for z in range(4):
+        mapped = jnp.zeros((2 * TOK, 128), F32)
+        for y in range(4):
+            right = jnp.concatenate([rows[z, y * 2], rows[z, y * 2 + 1]], axis=0)
+            mapped = mapped + dot(left[y], right)
+        column = z * 8 + in_plane
+        mapped = mapped * gates[column]
+        terms = mapped[TOK:] * probe[column].astype(F32)
+        trace = trace + jnp.sum(terms, axis=0, keepdims=True)
+        vel = vel1[...].astype(F32)
+        part = mapped[:TOK] + jnp.where(plane == z, vel, jnp.zeros_like(vel))
+        laid.append(dot(lay, part.astype(BF)))
+    trace = row_sum(trace)
     high = trace.astype(BF).astype(F32)
     mid = (trace - high).astype(BF).astype(F32)
     low = trace - high - mid
     lane = lax.broadcasted_iota(jnp.int32, (1, 128), 1)
     coded = jnp.where(lane == 0, high, jnp.where(lane == 1, mid, jnp.where(lane == 2, low, 0.0)))
     slot = lax.broadcasted_iota(jnp.int32, (256, 128), 0) & 7
-    out_ref[...] = jnp.where(slot == 6, coded, laid).astype(BF)
-
-
-def land_kernel(got, next_ref, change_ref):
+    for z in range(4):
+        block = jnp.where(slot == 6, coded, laid[z]) if z == 0 else laid[z]
+        out_ref[:, z * 128 : (z + 1) * 128] = block.astype(BF)
+
+
+def land_kernel(got, state, next_ref, change_ref):
     total = jnp.zeros((8, 128), F32)
-    for j in range(32):
-        block = got[j]
-        next_ref[:, j * 128 : (j + 1) * 128] = block[:6]
-        total = total + block.astype(F32)
+    for j in range(8):
+        sums = got[j].astype(F32)
+        total = total + sums[:, :128]
+        for z in range(1, 4):
+            block = got[z * 8 + j].astype(F32)
+            total = total + block[:, :128]
+            sums = sums + block
+        for z in range(4):
+            cols = slice((z * 8 + j) * 128, (z * 8 + j + 1) * 128)
+            both = sums[:6, z * 128 : (z + 1) * 128]
+            next_ref[:, cols] = (state[:, cols].astype(F32) + 0.5 * STEP * both).astype(BF)
     change_ref[...] = jnp.broadcast_to(-0.5 * STEP * row_sum(total[6:7, :]) / TOK, (1, 128))
 
 
@@ -300,7 +330,7 @@
 
 def per_device(state, probe, norm_gain, head_maps, query_gain, key_gain, out_map, out_gate):
     place = lax.axis_index(SEQ)
-    meta = jnp.stack([lax.axis_index("c"), place]).astype(jnp.int32)
+    meta = jnp.stack([lax.axis_index("c"), place, lax.axis_index("z")]).astype(jnp.int32)
     gate = lax.dynamic_slice_in_dim(out_gate, place * 128, 128).reshape(1, 128)
     maps = head_maps.reshape(32, 128, 384)
     outs = out_map.reshape(32, 128, 128)
@@ -321,22 +351,32 @@
         middle_kernel, [shape((TOK, 128)), shape((4, TOK, 128))],
         1, meta, own1, oth1, outs, gate, col,
     )
-    early, own_m, oth_m = gathered(mid)
+    late_map, mid = lax.optimization_barrier((out_map, mid))
+    all_outs = lax.all_gather(late_map, "z", axis=0, tiled=False)
+    _, own_m = spread(mid)
     probe_blocks, datt1 = call(
         tangent_kernel, [shape((32, TOK, 128)), shape((TOK, 128), F32)],
-        1, meta, own, oth, probe_all, maps, gain, query_gain, key_gain, (early,), scratch=HELD,
-    )
+        1, meta, own, oth, probe_all, maps, gain, query_gain, key_gain, (mid,), scratch=HELD,
+    )
+    own_m, datt1 = lax.optimization_barrier((own_m, datt1))
+    oth_m = swap(own_m).reshape(16, TOK, 128)
+    own_m = own_m.reshape(16, TOK, 128)
     both = call(
         second_kernel, shape((4, 2 * TOK, 128)),
         1, meta, own_m, oth_m, probe_blocks, maps, gain, query_gain, key_gain, datt1,
     )
-    _, own2, oth2 = gathered(both)
+    own2 = lax.all_to_all(both.reshape(8 * TOK, 128), "y", 0, 0, tiled=True)
+    oth2 = swap(own2)
     columns = call(
-        last_kernel, shape((256, 128)),
-        1, meta, own2, oth2, outs, gate, col, vel1, probe_blocks,
-    )
-    got = lax.all_to_all(columns, SEQ, 0, 0, tiled=True).reshape(32, 8, 128)
-    next_state, change = call(land_kernel, [shape((6, 4096)), shape((1, 128), F32)], 0, got)
+        last_kernel, shape((256, 512)),
+        1, meta, own2.reshape(4, 2 * TOK, 128), oth2.reshape(4, 2 * TOK, 128),
+        (all_outs.reshape(4, 32, 128, 128),), out_gate.reshape(32, 1, 128), vel1, probe_blocks,
+        scratch=[pltpu.VMEM((4, 8, 128, 128), BF), pltpu.SemaphoreType.DMA],
+    )
+    got = lax.all_to_all(columns, SEQ, 0, 0, tiled=True).reshape(32, 8, 512)
+    next_state, change = call(
+        land_kernel, [shape((6, 4096)), shape((1, 128), F32)], 0, got, state
+    )
     return next_state, change[0, :1]
 
 

time: 193 us -> 210 us (1.088)
  waiting for transfers between devices: 7.36 us -> 46.5 us
  blocking collectives: 126 us -> 91.4 us
  local copies, waits for them, and re-layouts: 5.36 us -> 12.4 us
  starting transfers between devices: 21.2 us -> 24.9 us
    all_gather x0 -> x1, waiting for transfers between devices: none -> 37.5 us  [per_device(): all_outs = lax.all_gather(late_map, 'z', axis=0, tiled=False)]
    all_to_all x4 -> x2, blocking collectives: 67 us -> 31.5 us  [spread(): return (a, lax.all_to_all(jnp.tile(a, (4, 1)), 'y', 0, 0, tiled=True))]
    all_to_all x1 -> x2, blocking collectives: 11.5 us -> 28 us  [the longest x1 18 us: per_device(): got = lax.all_to_all(columns, SEQ, 0, 0, tiled=True).reshape(32, 8, 512)]
    all_to_all x4 -> x3, blocking collectives: 47.1 us -> 31.9 us  [spread(): a = lax.all_to_all(copies.reshape(n * rows, lanes), 'z', 0, 0, tiled=True)]
    unnamed x20 -> x28, local copies, waits for them, and re-layouts: 4.81 us -> 11.1 us
    all_to_all x0 -> x1, starting transfers between devices: none -> 4.2 us  [spread(): return (a, lax.all_to_all(jnp.tile(a, (4, 1)), 'y', 0, 0, tiled=True))]
  transfers between devices with their start and end apart: 5 -> 7, of which waited for: 3 -> 6; matrix products, arithmetic and copies ran while one was open for 0% -> 1% of each run, Pallas kernels for 6% -> 7%
where the time goes in v3:
time: 210 us; the launch traced here: 209 us
  blocking collectives  91.4 us (44%)
  waiting for transfers between devices  46.5 us (22%)
  starting transfers between devices  24.9 us (12%)
  Pallas kernels  19.8 us (9%)
  between operations  14.2 us (7%)
  local copies, waits for them, and re-layouts  12.4 us (6%)
    all_gather x1, waiting for transfers between devices, per_device(): all_outs = lax.all_gather(late_map, 'z', axis=0, tiled=False)  37.5 us
    all_to_all x3, blocking collectives, spread(): a = lax.all_to_all(copies.reshape(n * rows, lanes), 'z', 0, 0, tiled=True)  31.9 us
    all_to_all x2, blocking collectives, spread(): return (a, lax.all_to_all(jnp.tile(a, (4, 1)), 'y', 0, 0, tiled=True))  31.5 us
    ppermute x4, starting transfers between devices, swap(): return lax.ppermute(block, 'c', [(0, 1), (1, 0)])  20.6 us
    pallas_call x7, Pallas kernels, call(): pl.pallas_call(kernel, out_shape=out_shape, in_specs=in_specs, out_specs=...  19.8 us
    all_to_all x1, blocking collectives, per_device(): got = lax.all_to_all(columns, SEQ, 0, 0, tiled=True).reshape(32, 8, 512)  18 us
    unnamed x28, local copies, waits for them, and re-layouts  11.1 us
    all_to_all x1, blocking collectives, per_device(): own2 = lax.all_to_all(both.reshape(8 * TOK, 128), 'y', 0, 0, tiled=True)  10.1 us
  transfers between devices with their start and end apart: 7, of which 6 were waited for; matrix products, arithmetic and copies ran while one was open for 1% of the time, Pallas kernels for 7%

profile of v3, /device:TPU:1, one launch (start us, length us, event | category | flops | bytes accessed | tf_op | source)
XLA Modules:
  0.0 209.3 jit_solution(9875266049853555204)
XLA Ops:
  7.2 1.0 copy-done.7
  8.2 0.8 copy-done.10
  9.8 11.9 %all_to_all.62 = bf16[4,8,3072]{2,1,0:T(8,128)(2,1)S(1)} all-to-all(bf16[4,8,3072]{2,1,0:T(8,128)(2,1)S(1)} %get-tuple-element.16), channel_id=1, replica_groups=mesh['z'=4,'y'=4,'c'=2,'w'=4,'x'=4] {'z'}, dimensions={0} | all-to-all | bytes 393216 | tf_op jit(solution)/shard_map/all_to_all | solution.py:316
  21.8 13.3 %all_to_all.63 = bf16[4,32,3072]{2,1,0:T(8,128)(2,1)} all-to-all(bf16[4,32,3072]{2,1,0:T(8,128)(2,1)S(1)} %tile.13), channel_id=1, replica_groups=mesh['z'=4,'y'=4,'c'=2,'w'=4,'x'=4] {'y'}, dimensions={0} | all-to-all | bytes 1572864 | tf_op jit(solution)/shard_map/all_to_all | solution.py:317
  35.1 7.7 %collective-permute-start = (bf16[128,3072]{1,0:T(8,128)(2,1)}, bf16[128,3072]{1,0:T(8,128)(2,1)}, u32[]{:S(2)}, u32[]{:S(2)}) collective-permute-start(bf16[128,3072]{1,0:T(8,128)(2,1)} %bitcast.4.xa), channel_id=1, source_target_pairs={{0,16},{16,0},{1,17},{17,1},{2,18},{18,2},{3,19},{19,3},{4,20},{20... | collective-permute-start | bytes 2359304 | tf_op jit(solution)/shard_map/ppermute | solution.py:321
  42.9 2.1 %collective-permute-done.xb = bf16[128,3072]{1,0:T(8,128)(2,1)} collective-permute-done((bf16[128,3072]{1,0:T(8,128)(2,1)}, bf16[128,3072]{1,0:T(8,128)(2,1)}, u32[]{:S(2)}, u32[]{:S(2)}) %collective-permute-start) | collective-permute-done | bytes 786464 | tf_op jit(solution)/shard_map/ppermute | solution.py:321
  45.0 3.7 %shard_map.96 = (bf16[4,192,128]{2,1,0:T(8,128)(2,1)S(1)}, bf16[192,128]{1,0:T(8,128)(2,1)S(1)}) custom-call(s32[3]{0:T(128)S(1)} %pad_add_fusion.meta, bf16[128,3072]{1,0:T(8,128)(2,1)} %bitcast.4.xa, bf16[128,3072]{1,0:T(8,128)(2,1)} %collective-permute-done.xb, bf16[32,128,384]{2,1,0:T(8,128)(2,1)S(1)} %bitcast.25, f32[32,1,128]{2,1,0:T(1,128)S(1)} %bitcast.34, ...), custom_call_target="tpu_custom_call" | custom-call | tf_op jit(solution)/shard_map/pallas_call | solution.py:43
  48.7 10.8 %all_to_all.64 = bf16[4,192,128]{2,1,0:T(8,128)(2,1)S(1)} all-to-all(bf16[4,192,128]{2,1,0:T(8,128)(2,1)S(1)} %get-tuple-element.17), channel_id=1, replica_groups=mesh['z'=4,'y'=4,'c'=2,'w'=4,'x'=4] {'z'}, dimensions={0} | all-to-all | bytes 393216 | tf_op jit(solution)/shard_map/all_to_all | solution.py:316
  59.6 18.1 %all_to_all.65 = bf16[4,768,128]{2,1,0:T(8,128)(2,1)} all-to-all(bf16[4,768,128]{2,1,0:T(8,128)(2,1)S(1)} %tile.30), channel_id=1, replica_groups=mesh['z'=4,'y'=4,'c'=2,'w'=4,'x'=4] {'y'}, dimensions={0} | all-to-all | bytes 1572864 | tf_op jit(solution)/shard_map/all_to_all | solution.py:317
  77.8 4.4 %collective-permute-start.1 = (bf16[3072,128]{1,0:T(8,128)(2,1)}, bf16[3072,128]{1,0:T(8,128)(2,1)}, u32[]{:S(2)}, u32[]{:S(2)}) collective-permute-start(bf16[3072,128]{1,0:T(8,128)(2,1)} %bitcast.9), channel_id=1, source_target_pairs={{0,16},{16,0},{1,17},{17,1},{2,18},{18,2},{3,19},{19,3},{4,20},{20... | collective-permute-start | bytes 2359304 | tf_op jit(solution)/shard_map/ppermute | solution.py:321
  82.2 2.1 %collective-permute-done.1 = bf16[3072,128]{1,0:T(8,128)(2,1)} collective-permute-done((bf16[3072,128]{1,0:T(8,128)(2,1)}, bf16[3072,128]{1,0:T(8,128)(2,1)}, u32[]{:S(2)}, u32[]{:S(2)}) %collective-permute-start.1) | collective-permute-done | bytes 786464 | tf_op jit(solution)/shard_map/ppermute | solution.py:321
  84.4 1.2 copy-done.4
  85.6 1.9 shard_map.97
  87.6 9.2 %all_to_all.66 = bf16[4,192,128]{2,1,0:T(8,128)(2,1)S(1)} all-to-all(bf16[4,192,128]{2,1,0:T(8,128)(2,1)S(1)} %get-tuple-element.20.after), channel_id=1, replica_groups=mesh['z'=4,'y'=4,'c'=2,'w'=4,'x'=4] {'z'}, dimensions={0} | all-to-all | bytes 393216 | tf_op jit(solution)/shard_map/all_to_all | solution.py:316
  96.8 1.0 tile.32
  97.8 4.2 %all-to-all-start.5 = ((bf16[4,768,128]{2,1,0:T(8,128)(2,1)}), bf16[4,768,128]{2,1,0:T(8,128)(2,1)}, u32[]{:S(2)}, u32[]{:S(2)}) async-start(bf16[4,768,128]{2,1,0:T(8,128)(2,1)} %tile.32), calls=%async_computation.5 | async-start | bytes 1572864 | tf_op jit(solution)/shard_map/all_to_all | solution.py:317
  102.1 1.9 copy-done.6
  103.9 5.6 %shard_map.98 = (bf16[32,192,128]{2,1,0:T(8,128)(2,1)S(1)}, f32[192,128]{1,0:T(8,128)S(1)}) custom-call(s32[3]{0:T(128)S(1)} %pad_add_fusion.meta, bf16[128,3072]{1,0:T(8,128)(2,1)} %bitcast.4.xa, bf16[128,3072]{1,0:T(8,128)(2,1)} %collective-permute-done.xb, bf16[256,6144]{1,0:T(8,128)(2,1)S(1)} %copy-done.6, bf16[32,128,384]{2,1,0:T(8,128)(2,1)S(1)} %bitcast.26, ...), custom_call_target="tpu_custom_call" | custom-call | tf_op jit(solution)/shard_map/pallas_call | solution.py:43
  109.6 1.2 copy-done.1
  110.8 1.2 all-to-all-done.5
  111.9 5.3 %collective-permute-start.2 = (bf16[3072,128]{1,0:T(8,128)(2,1)}, bf16[3072,128]{1,0:T(8,128)(2,1)S(1)}, u32[]{:S(2)}, u32[]{:S(2)}) collective-permute-start(bf16[3072,128]{1,0:T(8,128)(2,1)} %bitcast.14), channel_id=1, source_target_pairs={{0,16},{16,0},{1,17},{17,1},{2,18},{18,2},{3,19},{19,3},{4,20},{20... | collective-permute-start | bytes 2359304 | tf_op jit(solution)/shard_map/ppermute | solution.py:321
  117.2 2.1 %collective-permute-done.2 = bf16[3072,128]{1,0:T(8,128)(2,1)S(1)} collective-permute-done((bf16[3072,128]{1,0:T(8,128)(2,1)}, bf16[3072,128]{1,0:T(8,128)(2,1)S(1)}, u32[]{:S(2)}, u32[]{:S(2)}) %collective-permute-start.2) | collective-permute-done | bytes 786464 | tf_op jit(solution)/shard_map/ppermute | solution.py:321
  119.3 1.4 copy-done.2
  120.8 4.2 %shard_map.99 = bf16[4,384,128]{2,1,0:T(8,128)(2,1)S(1)} custom-call(s32[3]{0:T(128)S(1)} %pad_add_fusion.meta, bf16[16,192,128]{2,1,0:T(8,128)(2,1)} %bitcast.15.own, bf16[16,192,128]{2,1,0:T(8,128)(2,1)S(1)} %bitcast.32, bf16[32,192,128]{2,1,0:T(8,128)(2,1)S(1)} %copy-done.2, bf16[32,128,384]{2,1,0:T(8,128)(2,1)S(1)} %bitcast.27, ...), custom_call_target="tpu_custom_call" | custom-call | tf_op jit(solution)/shard_map/pallas_call | solution.py:43
  124.9 10.1 %all_to_all.67.own = bf16[4,384,128]{2,1,0:T(8,128)(2,1)S(1)} all-to-all(bf16[4,384,128]{2,1,0:T(8,128)(2,1)S(1)} %shard_map.99), channel_id=1, replica_groups=mesh['z'=4,'y'=4,'c'=2,'w'=4,'x'=4] {'y'}, dimensions={0} | all-to-all | bytes 786432 | tf_op jit(solution)/shard_map/all_to_all | solution.py:368
  135.0 3.3 %collective-permute-start.3 = (bf16[1536,128]{1,0:T(8,128)(2,1)S(1)}, bf16[1536,128]{1,0:T(8,128)(2,1)S(1)}, u32[]{:S(2)}, u32[]{:S(2)}) collective-permute-start(bf16[1536,128]{1,0:T(8,128)(2,1)S(1)} %bitcast.30), channel_id=1, source_target_pairs={{0,16},{16,0},{1,17},{17,1},{2,18},{18,2},{3,19},{19,3},{4,20},{20... | collective-permute-start | bytes 1179656 | tf_op jit(solution)/shard_map/ppermute | solution.py:321
  138.2 1.3 collective-permute-done.3
  139.6 37.5 %all-gather.6.cloned.1.call-done = bf16[16384,128]{1,0:T(8,128)(2,1)} async-done(((bf16[4096,128]{1,0:T(8,128)(2,1)}), bf16[16384,128]{1,0:T(8,128)(2,1)}) %all-gather.6.cloned.1.call-update) | async-done | bytes 4194320 | tf_op jit(solution)/shard_map/all_gather | solution.py:355
  177.1 1.4 copy-done.3
  178.5 2.2 %copy-done.5 = bf16[16384,128]{1,0:T(8,128)(2,1)S(1)} copy-done((bf16[16384,128]{1,0:T(8,128)(2,1)S(1)}, bf16[16384,128]{1,0:T(8,128)(2,1)}, u32[]{:S(2)}) %copy-start.5) | copy-done | bytes 4194328
  180.7 3.1 %shard_map.100 = bf16[256,512]{1,0:T(8,128)(2,1)S(1)} custom-call(s32[3]{0:T(128)S(1)} %pad_add_fusion.meta, bf16[4,384,128]{2,1,0:T(8,128)(2,1)S(1)} %all_to_all.67.own, bf16[4,384,128]{2,1,0:T(8,128)(2,1)S(1)} %bitcast.33, bf16[4,32,128,128]{3,2,1,0:T(8,128)(2,1)S(1)} %bitcast.29, f32[32,1,128]{2,1,0:T(1,128)S(1)} %bitcast.37, ...), custom_call_target="tpu_custom_call" | custom-call | tf_op jit(solution)/shard_map/pallas_call | solution.py:43
  183.8 18.0 %all_to_all.68.got = bf16[32,8,512]{2,1,0:T(8,128)(2,1)S(1)} all-to-all(bf16[32,8,512]{2,1,0:T(8,128)(2,1)S(1)} %bitcast.31), channel_id=1, replica_groups=mesh['z'=4,'y'=4,'c'=2,'w'=4,'x'=4] {'z','y','c'}, dimensions={0} | all-to-all | bytes 524288 | tf_op jit(solution)/shard_map/all_to_all | solution.py:376
  (31 shorter events, 1.8 us)
Async XLA Ops:
  7.2 37.8 %copy-start = (bf16[1,4096,384]{2,1,0:T(8,128)(2,1)S(1)}, bf16[1,4096,384]{2,1,0:T(8,128)(2,1)}, u32[]{:S(2)}) copy-start(bf16[1,4096,384]{2,1,0:T(8,128)(2,1)} %param.11) | copy-start | bytes 9437188
  7.2 94.9 %all-gather.4.cloned.1.call-start = ((), (), s32[]{:S(2)}) async-start(), calls=%async_computation.8 | async-start | bytes 3244032 | tf_op jit(solution)/shard_map/all_gather | solution.py:342
  7.2 1.0 copy-start.7
  8.2 0.8 copy-start.10
  9.1 35.9 %copy-start.9 = (f32[4096]{0:T(1024)S(1)}, f32[4096]{0:T(1024)}, u32[]{:S(2)}) copy-start(f32[4096]{0:T(1024)} %param.10) | copy-start | bytes 49156
  9.1 35.9 %copy-start.12 = (f32[1,128]{1,0:T(1,128)S(1)}, f32[1,128]{1,0:T(1,128)}, u32[]{:S(2)}) copy-start(f32[1,128]{1,0:T(1,128)} %q_gain.5) | copy-start | bytes 1540
  9.1 36.0 %copy-start.13 = (f32[1,128]{1,0:T(1,128)S(1)}, f32[1,128]{1,0:T(1,128)}, u32[]{:S(2)}) copy-start(f32[1,128]{1,0:T(1,128)} %k_gain.5) | copy-start | bytes 1540
  9.7 167.3 %all-gather.6.cloned.1.call-start = ((), (), s32[]{:S(2)}) async-start(), calls=%async_computation.9 | async-start | bytes 5242880 | tf_op jit(solution)/shard_map/all_gather | solution.py:355
  35.1 9.9 %collective-permute-start = (bf16[128,3072]{1,0:T(8,128)(2,1)}, bf16[128,3072]{1,0:T(8,128)(2,1)}, u32[]{:S(2)}, u32[]{:S(2)}) collective-permute-start(bf16[128,3072]{1,0:T(8,128)(2,1)} %bitcast.4.xa), channel_id=1, source_target_pairs={{0,16},{16,0},{1,17},{17,1},{2,18},{18,2},{3,19},{19,3},{4,20},{20... | collective-permute-start | bytes 2359304 | tf_op jit(solution)/shard_map/ppermute | solution.py:321
  45.0 37.1 %copy-start.11 = (f32[4096]{0:T(1024)S(1)}, f32[4096]{0:T(1024)}, u32[]{:S(2)}) copy-start(f32[4096]{0:T(1024)} %param.15) | copy-start | bytes 49156
  77.8 6.6 %collective-permute-start.1 = (bf16[3072,128]{1,0:T(8,128)(2,1)}, bf16[3072,128]{1,0:T(8,128)(2,1)}, u32[]{:S(2)}, u32[]{:S(2)}) collective-permute-start(bf16[3072,128]{1,0:T(8,128)(2,1)} %bitcast.9), channel_id=1, source_target_pairs={{0,16},{16,0},{1,17},{17,1},{2,18},{18,2},{3,19},{19,3},{4,20},{20... | collective-permute-start | bytes 2359304 | tf_op jit(solution)/shard_map/ppermute | solution.py:321
  84.4 1.2 copy-start.4
  97.8 14.1 %all-to-all-start.5 = ((bf16[4,768,128]{2,1,0:T(8,128)(2,1)}), bf16[4,768,128]{2,1,0:T(8,128)(2,1)}, u32[]{:S(2)}, u32[]{:S(2)}) async-start(bf16[4,768,128]{2,1,0:T(8,128)(2,1)} %tile.32), calls=%async_computation.5 | async-start | bytes 1572864 | tf_op jit(solution)/shard_map/all_to_all | solution.py:317
  102.1 1.9 copy-start.6
  109.6 1.2 copy-start.1
  111.9 7.4 %collective-permute-start.2 = (bf16[3072,128]{1,0:T(8,128)(2,1)}, bf16[3072,128]{1,0:T(8,128)(2,1)S(1)}, u32[]{:S(2)}, u32[]{:S(2)}) collective-permute-start(bf16[3072,128]{1,0:T(8,128)(2,1)} %bitcast.14), channel_id=1, source_target_pairs={{0,16},{16,0},{1,17},{17,1},{2,18},{18,2},{3,19},{19,3},{4,20},{20... | collective-permute-start | bytes 2359304 | tf_op jit(solution)/shard_map/ppermute | solution.py:321
  119.3 1.4 copy-start.2
  135.0 4.6 %collective-permute-start.3 = (bf16[1536,128]{1,0:T(8,128)(2,1)S(1)}, bf16[1536,128]{1,0:T(8,128)(2,1)S(1)}, u32[]{:S(2)}, u32[]{:S(2)}) collective-permute-start(bf16[1536,128]{1,0:T(8,128)(2,1)S(1)} %bitcast.30), channel_id=1, source_target_pairs={{0,16},{16,0},{1,17},{17,1},{2,18},{18,2},{3,19},{19,3},{4,20},{20... | collective-permute-start | bytes 1179656 | tf_op jit(solution)/shard_map/ppermute | solution.py:321
  177.1 1.4 copy-start.3
  178.5 2.2 %copy-start.5 = (bf16[16384,128]{1,0:T(8,128)(2,1)S(1)}, bf16[16384,128]{1,0:T(8,128)(2,1)}, u32[]{:S(2)}) copy-start(bf16[16384,128]{1,0:T(8,128)(2,1)} %all-gather.6.cloned.1.call-done) | copy-start | bytes 12582916
  180.7 21.0 %copy-start.8 = (bf16[6,4096]{1,0:T(8,128)(2,1)S(1)}, bf16[6,4096]{1,0:T(8,128)(2,1)}, u32[]{:S(2)}) copy-start(bf16[6,4096]{1,0:T(8,128)(2,1)} %state.3) | copy-start | bytes 147460
Sparse Core Ops, SparseCore 0:
  10.2 75.5 all-gather.3
  87.9 89.1 all-gather.5

commit v4 on v3

--- a/solution.py
+++ b/solution.py
@@ -252,36 +252,31 @@
         both_ref[i, TOK:] = d_both
 
 
-def last_kernel(meta, own, oth, out_maps, gates, vel1, probe, out_ref, rows, sem):
-    core, place, plane = meta[0], meta[1], meta[2]
-    copy = pltpu.make_async_copy(out_maps.at[:, pl.ds(plane * 8, 8)], rows, sem)
-    copy.start()
+def last_kernel(meta, own, oth, rows, gates, vel1, probe, out_ref):
+    core, plane, slab = meta[0], meta[2], meta[3]
     row = lax.broadcasted_iota(jnp.int32, (256, TOK), 0)
     token = lax.broadcasted_iota(jnp.int32, (256, TOK), 1)
     hit = (token == (row >> 3) * 6 + (row & 7)) & ((row & 7) < 6)
     lay = jnp.where(hit, jnp.ones((256, TOK), F32), jnp.zeros((256, TOK), F32)).astype(BF)
     left = []
-    for y in range(4):
-        mine = own[y]
-        other = oth[y]
+    for z in range(4):
+        mine, other = own[z], oth[z]
         first = jnp.where(core == 0, mine, other)
         second = jnp.where(core == 0, other, mine)
         left.append(jnp.concatenate([first, second], axis=1))
-    in_plane = place - plane * 8
-    copy.wait()
     trace = jnp.zeros((1, 128), F32)
     laid = []
-    for z in range(4):
+    for y in range(4):
         mapped = jnp.zeros((2 * TOK, 128), F32)
-        for y in range(4):
-            right = jnp.concatenate([rows[z, y * 2], rows[z, y * 2 + 1]], axis=0)
-            mapped = mapped + dot(left[y], right)
-        column = z * 8 + in_plane
+        for z in range(4):
+            right = jnp.concatenate([rows[y, z * 2], rows[y, z * 2 + 1]], axis=0)
+            mapped = mapped + dot(left[z], right)
+        column = slab * 8 + y * 2 + core
         mapped = mapped * gates[column]
         terms = mapped[TOK:] * probe[column].astype(F32)
         trace = trace + jnp.sum(terms, axis=0, keepdims=True)
         vel = vel1[...].astype(F32)
-        part = mapped[:TOK] + jnp.where(plane == z, vel, jnp.zeros_like(vel))
+        part = mapped[:TOK] + jnp.where(plane == y, vel, jnp.zeros_like(vel))
         laid.append(dot(lay, part.astype(BF)))
     trace = row_sum(trace)
     high = trace.astype(BF).astype(F32)
@@ -290,24 +285,25 @@
     lane = lax.broadcasted_iota(jnp.int32, (1, 128), 1)
     coded = jnp.where(lane == 0, high, jnp.where(lane == 1, mid, jnp.where(lane == 2, low, 0.0)))
     slot = lax.broadcasted_iota(jnp.int32, (256, 128), 0) & 7
-    for z in range(4):
-        block = jnp.where(slot == 6, coded, laid[z]) if z == 0 else laid[z]
-        out_ref[:, z * 128 : (z + 1) * 128] = block.astype(BF)
+    for y in range(4):
+        block = jnp.where(slot == 6, coded, laid[y]) if y == 0 else laid[y]
+        out_ref[:, y * 128 : (y + 1) * 128] = block.astype(BF)
 
 
 def land_kernel(got, state, next_ref, change_ref):
     total = jnp.zeros((8, 128), F32)
-    for j in range(8):
-        sums = got[j].astype(F32)
-        total = total + sums[:, :128]
-        for z in range(1, 4):
-            block = got[z * 8 + j].astype(F32)
-            total = total + block[:, :128]
-            sums = sums + block
-        for z in range(4):
-            cols = slice((z * 8 + j) * 128, (z * 8 + j + 1) * 128)
-            both = sums[:6, z * 128 : (z + 1) * 128]
-            next_ref[:, cols] = (state[:, cols].astype(F32) + 0.5 * STEP * both).astype(BF)
+    for z in range(4):
+        for c in range(2):
+            sums = jnp.zeros((8, 512), F32)
+            for y in range(4):
+                block = got[z * 8 + y * 2 + c].astype(F32)
+                total = total + block[:, :128]
+                sums = sums + block
+            for y in range(4):
+                j = z * 8 + y * 2 + c
+                cols = slice(j * 128, (j + 1) * 128)
+                both = sums[:6, y * 128 : (y + 1) * 128]
+                next_ref[:, cols] = (state[:, cols].astype(F32) + 0.5 * STEP * both).astype(BF)
     change_ref[...] = jnp.broadcast_to(-0.5 * STEP * row_sum(total[6:7, :]) / TOK, (1, 128))
 
 
@@ -330,7 +326,8 @@
 
 def per_device(state, probe, norm_gain, head_maps, query_gain, key_gain, out_map, out_gate):
     place = lax.axis_index(SEQ)
-    meta = jnp.stack([lax.axis_index("c"), place, lax.axis_index("z")]).astype(jnp.int32)
+    meta = [lax.axis_index("c"), place, lax.axis_index("y"), lax.axis_index("z")]
+    meta = jnp.stack(meta).astype(jnp.int32)
     gate = lax.dynamic_slice_in_dim(out_gate, place * 128, 128).reshape(1, 128)
     maps = head_maps.reshape(32, 128, 384)
     outs = out_map.reshape(32, 128, 128)
@@ -351,27 +348,27 @@
         middle_kernel, [shape((TOK, 128)), shape((4, TOK, 128))],
         1, meta, own1, oth1, outs, gate, col,
     )
-    late_map, mid = lax.optimization_barrier((out_map, mid))
-    all_outs = lax.all_gather(late_map, "z", axis=0, tiled=False)
     _, own_m = spread(mid)
+    late_map, own_m = lax.optimization_barrier((out_map, own_m))
+    by_plane = late_map.reshape(4, 4, 256, 128).transpose(1, 0, 2, 3).reshape(4096, 128)
+    plane_outs = lax.all_to_all(by_plane, "y", 0, 0, tiled=True)
     probe_blocks, datt1 = call(
         tangent_kernel, [shape((32, TOK, 128)), shape((TOK, 128), F32)],
         1, meta, own, oth, probe_all, maps, gain, query_gain, key_gain, (mid,), scratch=HELD,
     )
-    own_m, datt1 = lax.optimization_barrier((own_m, datt1))
     oth_m = swap(own_m).reshape(16, TOK, 128)
     own_m = own_m.reshape(16, TOK, 128)
     both = call(
         second_kernel, shape((4, 2 * TOK, 128)),
         1, meta, own_m, oth_m, probe_blocks, maps, gain, query_gain, key_gain, datt1,
     )
-    own2 = lax.all_to_all(both.reshape(8 * TOK, 128), "y", 0, 0, tiled=True)
+    both, plane_outs = lax.optimization_barrier((both, plane_outs))
+    own2 = lax.all_to_all(both.reshape(8 * TOK, 128), "z", 0, 0, tiled=True)
     oth2 = swap(own2)
     columns = call(
         last_kernel, shape((256, 512)),
         1, meta, own2.reshape(4, 2 * TOK, 128), oth2.reshape(4, 2 * TOK, 128),
-        (all_outs.reshape(4, 32, 128, 128),), out_gate.reshape(32, 1, 128), vel1, probe_blocks,
-        scratch=[pltpu.VMEM((4, 8, 128, 128), BF), pltpu.SemaphoreType.DMA],
+        plane_outs.reshape(4, 8, 128, 128), out_gate.reshape(32, 1, 128), vel1, probe_blocks,
     )
     got = lax.all_to_all(columns, SEQ, 0, 0, tiled=True).reshape(32, 8, 512)
     next_state, change = call(

time: 210 us -> 187 us (0.89)
  waiting for transfers between devices: 46.5 us -> 6.55 us
  blocking collectives: 91.4 us -> 106 us
    all_gather x1 -> x0, waiting for transfers between devices: 37.5 us -> none  [per_device(): all_outs = lax.all_gather(late_map, 'z', axis=0, tiled=False)]
    all_to_all x2 -> x3, blocking collectives: 31.5 us -> 43.7 us  [spread(): return (a, lax.all_to_all(jnp.tile(a, (4, 1)), 'y', 0, 0, tiled=True))]
    all_to_all x1, blocking collectives: 10.1 us -> 14.1 us  [per_device(): own2 = lax.all_to_all(both.reshape(8 * TOK, 128), 'z', 0, 0, tiled=True)]
    ppermute x4, waiting for transfers between devices: 7.71 us -> 4.94 us  [swap(): return lax.ppermute(block, 'c', [(0, 1), (1, 0)])]
    all_to_all x1, blocking collectives: 18 us -> 15.3 us  [per_device(): got = lax.all_to_all(columns, SEQ, 0, 0, tiled=True).reshape(32, 8, 512)]
    unnamed x28 -> x38, local copies, waits for them, and re-layouts: 11.1 us -> 10.4 us
  transfers between devices with their start and end apart: 7 -> 6, of which waited for: 6 -> 4; matrix products, arithmetic and copies ran while one was open for 1% -> 1% of each run, Pallas kernels for 7% -> 8%
where the time goes in v4:
time: 187 us; the launch traced here: 186 us
  blocking collectives  106 us (57%)
  starting transfers between devices  26.2 us (14%)
  Pallas kernels  20.3 us (11%)
  between operations  14.2 us (8%)
  local copies, waits for them, and re-layouts  12.5 us (7%)
  waiting for transfers between devices  6.55 us (4%)
    all_to_all x3, blocking collectives, spread(): return (a, lax.all_to_all(jnp.tile(a, (4, 1)), 'y', 0, 0, tiled=True))  43.7 us
    all_to_all x3, blocking collectives, spread(): a = lax.all_to_all(copies.reshape(n * rows, lanes), 'z', 0, 0, tiled=True)  32.6 us
    ppermute x4, starting transfers between devices, swap(): return lax.ppermute(block, 'c', [(0, 1), (1, 0)])  21.9 us
    pallas_call x7, Pallas kernels, call(): pl.pallas_call(kernel, out_shape=out_shape, in_specs=in_specs, out_specs=...  20.3 us
    all_to_all x1, blocking collectives, per_device(): got = lax.all_to_all(columns, SEQ, 0, 0, tiled=True).reshape(32, 8, 512)  15.3 us
    all_to_all x1, blocking collectives, per_device(): own2 = lax.all_to_all(both.reshape(8 * TOK, 128), 'z', 0, 0, tiled=True)  14.1 us
    unnamed x38, local copies, waits for them, and re-layouts  10.4 us
    ppermute x4, waiting for transfers between devices, swap(): return lax.ppermute(block, 'c', [(0, 1), (1, 0)])  4.94 us
  transfers between devices with their start and end apart: 6, of which 4 were waited for; matrix products, arithmetic and copies ran while one was open for 1% of the time, Pallas kernels for 8%

profile of v4, /device:TPU:1, one launch (start us, length us, event | category | flops | bytes accessed | tf_op | source)
XLA Modules:
  0.0 185.6 jit_solution(17488762292703732022)
XLA Ops:
  7.2 1.0 copy-done.5
  8.2 0.8 copy-done.8
  9.8 11.9 %all_to_all.74 = bf16[4,8,3072]{2,1,0:T(8,128)(2,1)S(1)} all-to-all(bf16[4,8,3072]{2,1,0:T(8,128)(2,1)S(1)} %get-tuple-element.16), channel_id=1, replica_groups=mesh['z'=4,'y'=4,'c'=2,'w'=4,'x'=4] {'z'}, dimensions={0} | all-to-all | bytes 393216 | tf_op jit(solution)/shard_map/all_to_all | solution.py:312
  21.7 13.3 %all_to_all.75 = bf16[4,32,3072]{2,1,0:T(8,128)(2,1)} all-to-all(bf16[4,32,3072]{2,1,0:T(8,128)(2,1)S(1)} %tile.13), channel_id=1, replica_groups=mesh['z'=4,'y'=4,'c'=2,'w'=4,'x'=4] {'y'}, dimensions={0} | all-to-all | bytes 1572864 | tf_op jit(solution)/shard_map/all_to_all | solution.py:313
  35.0 7.7 %collective-permute-start = (bf16[128,3072]{1,0:T(8,128)(2,1)}, bf16[128,3072]{1,0:T(8,128)(2,1)}, u32[]{:S(2)}, u32[]{:S(2)}) collective-permute-start(bf16[128,3072]{1,0:T(8,128)(2,1)} %bitcast.5.xa), channel_id=1, source_target_pairs={{0,16},{16,0},{1,17},{17,1},{2,18},{18,2},{3,19},{19,3},{4,20},{20... | collective-permute-start | bytes 2359304 | tf_op jit(solution)/shard_map/ppermute | solution.py:317
  42.8 2.1 %collective-permute-done.xb = bf16[128,3072]{1,0:T(8,128)(2,1)} collective-permute-done((bf16[128,3072]{1,0:T(8,128)(2,1)}, bf16[128,3072]{1,0:T(8,128)(2,1)}, u32[]{:S(2)}, u32[]{:S(2)}) %collective-permute-start) | collective-permute-done | bytes 786464 | tf_op jit(solution)/shard_map/ppermute | solution.py:317
  45.0 3.7 %shard_map.96 = (bf16[4,192,128]{2,1,0:T(8,128)(2,1)S(1)}, bf16[192,128]{1,0:T(8,128)(2,1)S(1)}) custom-call(s32[4]{0:T(128)S(1)} %pad_add_fusion.meta, bf16[128,3072]{1,0:T(8,128)(2,1)} %bitcast.5.xa, bf16[128,3072]{1,0:T(8,128)(2,1)} %collective-permute-done.xb, bf16[32,128,384]{2,1,0:T(8,128)(2,1)S(1)} %bitcast.31, f32[32,1,128]{2,1,0:T(1,128)S(1)} %bitcast.39, ...), custom_call_target="tpu_custom_call" | custom-call | tf_op jit(solution)/shard_map/pallas_call | solution.py:43
  48.7 11.0 %all_to_all.76 = bf16[4,192,128]{2,1,0:T(8,128)(2,1)S(1)} all-to-all(bf16[4,192,128]{2,1,0:T(8,128)(2,1)S(1)} %get-tuple-element.17), channel_id=1, replica_groups=mesh['z'=4,'y'=4,'c'=2,'w'=4,'x'=4] {'z'}, dimensions={0} | all-to-all | bytes 393216 | tf_op jit(solution)/shard_map/all_to_all | solution.py:312
  59.8 17.3 %all_to_all.77 = bf16[4,768,128]{2,1,0:T(8,128)(2,1)} all-to-all(bf16[4,768,128]{2,1,0:T(8,128)(2,1)S(1)} %tile.30), channel_id=1, replica_groups=mesh['z'=4,'y'=4,'c'=2,'w'=4,'x'=4] {'y'}, dimensions={0} | all-to-all | bytes 1572864 | tf_op jit(solution)/shard_map/all_to_all | solution.py:313
  77.1 4.8 %collective-permute-start.1 = (bf16[3072,128]{1,0:T(8,128)(2,1)}, bf16[3072,128]{1,0:T(8,128)(2,1)}, u32[]{:S(2)}, u32[]{:S(2)}) collective-permute-start(bf16[3072,128]{1,0:T(8,128)(2,1)} %bitcast.10), channel_id=1, source_target_pairs={{0,16},{16,0},{1,17},{17,1},{2,18},{18,2},{3,19},{19,3},{4,20},{20... | collective-permute-start | bytes 2359304 | tf_op jit(solution)/shard_map/ppermute | solution.py:317
  82.0 0.8 dynamic-slice_bitcast_fusion.gate
  82.8 1.5 collective-permute-done.1
  84.2 1.2 copy-done.3
  85.5 2.0 %shard_map.97 = (bf16[192,128]{1,0:T(8,128)(2,1)S(1)}, bf16[4,192,128]{2,1,0:T(8,128)(2,1)S(1)}) custom-call(s32[4]{0:T(128)S(1)} %pad_add_fusion.meta, bf16[16,192,128]{2,1,0:T(8,128)(2,1)} %bitcast.9.own, bf16[16,192,128]{2,1,0:T(8,128)(2,1)} %bitcast.11.oth, bf16[32,128,128]{2,1,0:T(8,128)(2,1)S(1)} %bitcast.34, ...), custom_call_target="tpu_custom_call" | custom-call | tf_op jit(solution)/shard_map/pallas_call | solution.py:43
  87.4 9.6 %all_to_all.78 = bf16[4,192,128]{2,1,0:T(8,128)(2,1)S(1)} all-to-all(bf16[4,192,128]{2,1,0:T(8,128)(2,1)S(1)} %get-tuple-element.19.after), channel_id=1, replica_groups=mesh['z'=4,'y'=4,'c'=2,'w'=4,'x'=4] {'z'}, dimensions={0} | all-to-all | bytes 393216 | tf_op jit(solution)/shard_map/all_to_all | solution.py:312
  97.2 13.0 %all_to_all.79 = bf16[4,768,128]{2,1,0:T(8,128)(2,1)} all-to-all(bf16[4,768,128]{2,1,0:T(8,128)(2,1)S(1)} %tile.32), channel_id=1, replica_groups=mesh['z'=4,'y'=4,'c'=2,'w'=4,'x'=4] {'y'}, dimensions={0} | all-to-all | bytes 1572864 | tf_op jit(solution)/shard_map/all_to_all | solution.py:313
  110.2 5.2 %collective-permute-start.2 = (bf16[3072,128]{1,0:T(8,128)(2,1)}, bf16[3072,128]{1,0:T(8,128)(2,1)}, u32[]{:S(2)}, u32[]{:S(2)}) collective-permute-start(bf16[3072,128]{1,0:T(8,128)(2,1)} %bitcast.15), channel_id=1, source_target_pairs={{0,16},{16,0},{1,17},{17,1},{2,18},{18,2},{3,19},{19,3},{4,20},{20... | collective-permute-start | bytes 2359304 | tf_op jit(solution)/shard_map/ppermute | solution.py:317
  115.4 1.1 copy.10
  116.5 4.2 %all-to-all-start.6 = ((bf16[4,1024,128]{2,1,0:T(8,128)(2,1)}), bf16[4,1024,128]{2,1,0:T(8,128)(2,1)}, u32[]{:S(2)}, u32[]{:S(2)}) async-start(bf16[4,1024,128]{2,1,0:T(8,128)(2,1)} %bitcast.43), calls=%async_computation.6 | async-start | bytes 2097152 | tf_op jit(solution)/shard_map/all_to_all | solution.py:354
  120.8 1.9 %copy-done.4 = bf16[256,6144]{1,0:T(8,128)(2,1)S(1)} copy-done((bf16[256,6144]{1,0:T(8,128)(2,1)S(1)}, bf16[256,6144]{1,0:T(8,128)(2,1)}, u32[]{:S(2)}) %copy-start.4) | copy-done | bytes 3145752
  122.7 5.5 %shard_map.98 = (bf16[32,192,128]{2,1,0:T(8,128)(2,1)S(1)}, f32[192,128]{1,0:T(8,128)S(1)}) custom-call(s32[4]{0:T(128)S(1)} %pad_add_fusion.meta, bf16[128,3072]{1,0:T(8,128)(2,1)} %bitcast.5.xa, bf16[128,3072]{1,0:T(8,128)(2,1)} %collective-permute-done.xb, bf16[256,6144]{1,0:T(8,128)(2,1)S(1)} %copy-done.4, bf16[32,128,384]{2,1,0:T(8,128)(2,1)S(1)} %bitcast.32, ...), custom_call_target="tpu_custom_call" | custom-call | tf_op jit(solution)/shard_map/pallas_call | solution.py:43
  129.0 4.4 %shard_map.99 = bf16[4,384,128]{2,1,0:T(8,128)(2,1)S(1)} custom-call(s32[4]{0:T(128)S(1)} %copy-done.12, bf16[16,192,128]{2,1,0:T(8,128)(2,1)} %bitcast.16.own, bf16[16,192,128]{2,1,0:T(8,128)(2,1)} %bitcast.17.oth, bf16[32,192,128]{2,1,0:T(8,128)(2,1)S(1)} %get-tuple-element.22.probe, bf16[32,128,384]{2,1,0:T(8,128)(2,1)S(1)} %bitcast.33, ...), custom_call_target="tpu_custom_call" | custom-call | tf_op jit(solution)/shard_map/pallas_call | solution.py:43
  133.3 1.2 copy-done.1
  134.5 1.6 all-to-all-done.6
  136.1 14.1 %all_to_all.80.own = bf16[4,384,128]{2,1,0:T(8,128)(2,1)S(1)} all-to-all(bf16[4,384,128]{2,1,0:T(8,128)(2,1)S(1)} %shard_map.99), channel_id=1, replica_groups=mesh['z'=4,'y'=4,'c'=2,'w'=4,'x'=4] {'z'}, dimensions={0} | all-to-all | bytes 786432 | tf_op jit(solution)/shard_map/all_to_all | solution.py:366
  150.2 4.2 %collective-permute-start.3 = (bf16[1536,128]{1,0:T(8,128)(2,1)S(1)}, bf16[1536,128]{1,0:T(8,128)(2,1)S(1)}, u32[]{:S(2)}, u32[]{:S(2)}) collective-permute-start(bf16[1536,128]{1,0:T(8,128)(2,1)S(1)} %bitcast.36), channel_id=1, source_target_pairs={{0,16},{16,0},{1,17},{17,1},{2,18},{18,2},{3,19},{19,3},{4,20},{20... | collective-permute-start | bytes 1179656 | tf_op jit(solution)/shard_map/ppermute | solution.py:317
  154.4 1.3 collective-permute-done.3
  155.8 1.4 copy-done.2
  157.2 0.8 copy-done.10
  158.6 0.7 copy-done.14
  159.3 3.4 %shard_map.100 = bf16[256,512]{1,0:T(8,128)(2,1)S(1)} custom-call(s32[4]{0:T(128)S(1)} %copy-done.13, bf16[4,384,128]{2,1,0:T(8,128)(2,1)S(1)} %all_to_all.80.own, bf16[4,384,128]{2,1,0:T(8,128)(2,1)S(1)} %bitcast.38, bf16[4,8,128,128]{3,2,1,0:T(8,128)(2,1)} %bitcast.24.rows, f32[32,1,128]{2,1,0:T(1,128)S(1)} %bitcast.42, bf16[192,128]{1,0:T(8,128)(2,1)S(1)} %copy-done.10, ...), custom_call_target="tpu_custom_call" | custom-call | tf_op jit(solution)/shard_map/pallas_call | solution.py:43
  162.8 15.3 %all_to_all.81.got = bf16[32,8,512]{2,1,0:T(8,128)(2,1)S(1)} all-to-all(bf16[32,8,512]{2,1,0:T(8,128)(2,1)S(1)} %bitcast.37), channel_id=1, replica_groups=mesh['z'=4,'y'=4,'c'=2,'w'=4,'x'=4] {'z','y','c'}, dimensions={0} | all-to-all | bytes 524288 | tf_op jit(solution)/shard_map/all_to_all | solution.py:373
  (40 shorter events, 3.1 us)
Async XLA Ops:
  7.2 37.8 %copy-start = (bf16[1,4096,384]{2,1,0:T(8,128)(2,1)S(1)}, bf16[1,4096,384]{2,1,0:T(8,128)(2,1)}, u32[]{:S(2)}) copy-start(bf16[1,4096,384]{2,1,0:T(8,128)(2,1)} %param.11) | copy-start | bytes 9437188
  7.2 113.6 %all-gather.2.cloned.1.call-start = ((), (), s32[]{:S(2)}) async-start(), calls=%async_computation.9 | async-start | bytes 3244032 | tf_op jit(solution)/shard_map/all_gather | solution.py:339
  7.2 1.0 copy-start.5
  8.2 0.8 copy-start.8
  9.1 35.9 %copy-start.7 = (f32[4096]{0:T(1024)S(1)}, f32[4096]{0:T(1024)}, u32[]{:S(2)}) copy-start(f32[4096]{0:T(1024)} %param.10) | copy-start | bytes 49156
  9.1 35.9 %copy-start.15 = (f32[1,128]{1,0:T(1,128)S(1)}, f32[1,128]{1,0:T(1,128)}, u32[]{:S(2)}) copy-start(f32[1,128]{1,0:T(1,128)} %q_gain.5) | copy-start | bytes 1540
  9.1 35.9 %copy-start.17 = (f32[1,128]{1,0:T(1,128)S(1)}, f32[1,128]{1,0:T(1,128)}, u32[]{:S(2)}) copy-start(f32[1,128]{1,0:T(1,128)} %k_gain.5) | copy-start | bytes 1540
  35.0 9.9 %collective-permute-start = (bf16[128,3072]{1,0:T(8,128)(2,1)}, bf16[128,3072]{1,0:T(8,128)(2,1)}, u32[]{:S(2)}, u32[]{:S(2)}) collective-permute-start(bf16[128,3072]{1,0:T(8,128)(2,1)} %bitcast.5.xa), channel_id=1, source_target_pairs={{0,16},{16,0},{1,17},{17,1},{2,18},{18,2},{3,19},{19,3},{4,20},{20... | collective-permute-start | bytes 2359304 | tf_op jit(solution)/shard_map/ppermute | solution.py:317
  42.8 78.0 %copy-start.11 = (s32[4]{0:T(128)}, s32[4]{0:T(128)S(1)}, u32[]{:S(2)}) copy-start(s32[4]{0:T(128)S(1)} %pad_add_fusion.meta) | copy-start | bytes 52
  77.1 7.1 %collective-permute-start.1 = (bf16[3072,128]{1,0:T(8,128)(2,1)}, bf16[3072,128]{1,0:T(8,128)(2,1)}, u32[]{:S(2)}, u32[]{:S(2)}) collective-permute-start(bf16[3072,128]{1,0:T(8,128)(2,1)} %bitcast.10), channel_id=1, source_target_pairs={{0,16},{16,0},{1,17},{17,1},{2,18},{18,2},{3,19},{19,3},{4,20},{20... | collective-permute-start | bytes 2359304 | tf_op jit(solution)/shard_map/ppermute | solution.py:317
  84.2 1.2 copy-start.3
  87.4 29.1 %copy-start.9 = (bf16[192,128]{1,0:T(8,128)(2,1)}, bf16[192,128]{1,0:T(8,128)(2,1)S(1)}, u32[]{:S(2)}) copy-start(bf16[192,128]{1,0:T(8,128)(2,1)S(1)} %get-tuple-element.27.vel1) | copy-start | bytes 147460
  110.2 18.0 %collective-permute-start.2 = (bf16[3072,128]{1,0:T(8,128)(2,1)}, bf16[3072,128]{1,0:T(8,128)(2,1)}, u32[]{:S(2)}, u32[]{:S(2)}) collective-permute-start(bf16[3072,128]{1,0:T(8,128)(2,1)} %bitcast.15), channel_id=1, source_target_pairs={{0,16},{16,0},{1,17},{17,1},{2,18},{18,2},{3,19},{19,3},{4,20},{20... | collective-permute-start | bytes 2359304 | tf_op jit(solution)/shard_map/ppermute | solution.py:317
  116.5 19.6 %all-to-all-start.6 = ((bf16[4,1024,128]{2,1,0:T(8,128)(2,1)}), bf16[4,1024,128]{2,1,0:T(8,128)(2,1)}, u32[]{:S(2)}, u32[]{:S(2)}) async-start(bf16[4,1024,128]{2,1,0:T(8,128)(2,1)} %bitcast.43), calls=%async_computation.6 | async-start | bytes 2097152 | tf_op jit(solution)/shard_map/all_to_all | solution.py:354
  120.8 1.9 %copy-start.4 = (bf16[256,6144]{1,0:T(8,128)(2,1)S(1)}, bf16[256,6144]{1,0:T(8,128)(2,1)}, u32[]{:S(2)}) copy-start(bf16[256,6144]{1,0:T(8,128)(2,1)} %all-gather.2.cloned.1.call-done.packed) | copy-start | bytes 9437188
  122.7 5.6 %copy-start.16 = (f32[1,128]{1,0:T(1,128)S(1)}, f32[1,128]{1,0:T(1,128)}, u32[]{:S(2)}) copy-start(f32[1,128]{1,0:T(1,128)} %q_gain.5) | copy-start | bytes 1540
  122.7 5.6 %copy-start.18 = (f32[1,128]{1,0:T(1,128)S(1)}, f32[1,128]{1,0:T(1,128)}, u32[]{:S(2)}) copy-start(f32[1,128]{1,0:T(1,128)} %k_gain.5) | copy-start | bytes 1540
  128.3 0.7 copy-start.12
  133.3 1.2 copy-start.1
  134.5 43.6 %copy-start.6 = (bf16[6,4096]{1,0:T(8,128)(2,1)S(1)}, bf16[6,4096]{1,0:T(8,128)(2,1)}, u32[]{:S(2)}) copy-start(bf16[6,4096]{1,0:T(8,128)(2,1)} %state.3) | copy-start | bytes 147460
  150.2 5.5 %collective-permute-start.3 = (bf16[1536,128]{1,0:T(8,128)(2,1)S(1)}, bf16[1536,128]{1,0:T(8,128)(2,1)S(1)}, u32[]{:S(2)}, u32[]{:S(2)}) collective-permute-start(bf16[1536,128]{1,0:T(8,128)(2,1)S(1)} %bitcast.36), channel_id=1, source_target_pairs={{0,16},{16,0},{1,17},{17,1},{2,18},{18,2},{3,19},{19,3},{4,20},{20... | collective-permute-start | bytes 1179656 | tf_op jit(solution)/shard_map/ppermute | solution.py:317
  155.8 1.4 copy-start.2
  157.2 0.8 copy-start.10
  158.0 0.7 copy-start.13
  158.6 0.7 copy-start.14
Sparse Core Ops, SparseCore 0:
  10.2 75.9 all-gather.1

commit v5 on v4

--- a/solution.py
+++ b/solution.py
@@ -27,14 +27,32 @@
     return jnp.mean(v, axis=-1, keepdims=True)
 
 
-HELD = [pltpu.VMEM((32, TOK, 128), BF)]
-
-
-def call(kernel, out_shape, n_scalar, *args, scratch=()):
+HELD = pltpu.VMEM((32, TOK, 128), BF)
+MAPS = pltpu.VMEM((32, 128, 384), BF)
+
+
+FULL = 60
+LAST = 51
+MIDDLE = 51
+SECOND = 51
+
+
+def sems(n):
+    return pltpu.SemaphoreType.DMA((n,))
+
+
+def fetch(sem, *pairs):
+    copies = [pltpu.make_async_copy(a, b, sem.at[i]) for i, (a, b) in enumerate(pairs)]
+    for copy in copies:
+        copy.start()
+    return copies
+
+
+def call(kernel, out_shape, n_scalar, *args, scratch=(), vmem_mib=20):
     in_specs = [pl.BlockSpec(memory_space=pltpu.SMEM)] * n_scalar
     for a in args[n_scalar:]:
         if isinstance(a, tuple):
-            in_specs.append(pl.BlockSpec(memory_space=pl.ANY))
+            in_specs.append(pl.BlockSpec(memory_space=pltpu.HBM))
         else:
             in_specs.append(pl.BlockSpec(memory_space=pltpu.VMEM))
     flat = [a[0] if isinstance(a, tuple) else a for a in args]
@@ -46,7 +64,7 @@
         in_specs=in_specs,
         out_specs=[vmem] * len(out_shape) if multi else vmem,
         scratch_shapes=scratch,
-        compiler_params=pltpu.CompilerParams(vmem_limit_bytes=20 * 1024 * 1024),
+        compiler_params=pltpu.CompilerParams(vmem_limit_bytes=vmem_mib * 1024 * 1024),
     )(*flat)
 
 
@@ -112,15 +130,17 @@
     return dot(probs, val).astype(BF), dot(d_probs.astype(BF), val) + dot(probs, dv)
 
 
-def pack_kernel(state, probe, state_ref, probe_ref):
-    for source, write in ((state, None), (probe, probe_ref)):
+def pack_kernel(state_hbm, probe_hbm, state_ref, probe_ref, state, probe, sem):
+    copies = fetch(sem, (state_hbm, state), (probe_hbm, probe))
+    for i, (source, write) in enumerate(((state, None), (probe, probe_ref))):
+        copies[i].wait()
         main = source[:, :3072]
         sixth = jnp.concatenate([source[q : q + 1, 3072:] for q in range(3)], axis=1)
         seventh = jnp.concatenate([source[q : q + 1, 3072:] for q in range(3, 6)], axis=1)
         whole = jnp.concatenate([main, sixth, seventh], axis=0)
         if write is None:
-            for i in range(4):
-                state_ref[i] = whole
+            for n in range(4):
+                state_ref[n] = whole
         else:
             write[:, :3072] = whole
             write[:, 3072:] = whole
@@ -157,8 +177,12 @@
     return jnp.sum(v, axis=-1, keepdims=True)
 
 
-def first_kernel(meta, xa, xb, maps, gain, q_gain, k_gain, att_ref, col_ref, held):
+def first_kernel(
+    meta, xa, xb, maps_hbm, gain, q_gain, k_gain, att_ref, col_ref, held, maps, sem
+):
+    copies = fetch(sem, (maps_hbm, maps))
     recip = unpack_state(meta[0], xa, xb, held)
+    copies[0].wait()
     proj = jnp.zeros((TOK, 384), F32)
     for h in range(0, 32, 2):
         left = (held[h].astype(F32) * recip * gain[h]).astype(BF)
@@ -187,8 +211,11 @@
     return total
 
 
-def middle_kernel(meta, own, oth, out_map, gate, col, vel_ref, mid_ref):
-    vel = (gate[...] * out_product(meta[0], own, oth, out_map)).astype(BF)
+def middle_kernel(meta, own, oth, out_hbm, gates, col, vel_ref, mid_ref, out_map, sem):
+    copies = fetch(sem, (out_hbm, out_map))
+    gate = gates[meta[1]]
+    copies[0].wait()
+    vel = (gate * out_product(meta[0], own, oth, out_map)).astype(BF)
     vel_ref[...] = vel
     mid = (col[...].astype(F32) + STEP * vel.astype(F32)).astype(BF)
     for i in range(4):
@@ -202,10 +229,17 @@
 
 
 def tangent_kernel(
-    meta, xa, xb, packed, maps, gain, q_gain, k_gain, after, probe_ref, datt_ref, held
+    meta, xa_hbm, xb_hbm, packed_hbm, maps_hbm, gain, q_gain, k_gain, after, probe_ref, datt_ref,
+    held, xa, xb, packed, maps, sem,
 ):
+    copies = fetch(
+        sem, (xa_hbm, xa), (xb_hbm, xb), (packed_hbm.at[:, :3072], packed), (maps_hbm, maps)
+    )
+    copies[0].wait()
+    copies[1].wait()
     recip = unpack_state(meta[0], xa, xb, held)
     main, rest = selectors(lambda row: (row >> 3) * 6, 256)
+    copies[2].wait()
     dots = jnp.zeros((TOK, 128), F32)
     for start, x in pieces(main, rest, lambda m: packed[:, m * 1024 : (m + 1) * 1024]):
         for b in range(8):
@@ -213,6 +247,7 @@
             dots = dots + piece * held[start // 128 + b].astype(F32)
             probe_ref[start // 128 + b] = piece.astype(BF)
     d_recip = -(recip * recip * recip) * (row_sum(dots) * (1.0 / 4096))
+    copies[3].wait()
     proj = jnp.zeros((2 * TOK, 384), F32)
     for h in range(0, 32, 2):
         pair = [
@@ -224,8 +259,11 @@
     datt_ref[...] = attend_tangent(proj[:TOK], proj[TOK:], q_gain[...], k_gain[...])[1]
 
 
-def second_kernel(meta, own, oth, probe, maps, gain, q_gain, k_gain, datt1, both_ref):
+def second_kernel(
+    meta, own, oth, probe, maps_hbm, gain, q_gain, k_gain, datt1, both_ref, maps, sem
+):
     core = meta[0]
+    copies = fetch(sem, (maps_hbm, maps))
     squares = jnp.zeros((TOK, 128), F32)
     dots = jnp.zeros((TOK, 128), F32)
     for side, b, h in blocks(core, own, oth):
@@ -235,6 +273,7 @@
             dots = dots + x * probe[h + 8 * i].astype(F32)
     recip = lax.rsqrt(row_sum(squares) * (1.0 / 4096) + EPS)
     d_recip = -(recip * recip * recip) * (row_sum(dots) * (1.0 / 4096))
+    copies[0].wait()
     proj = jnp.zeros((2 * TOK, 384), F32)
     for side, b, h in blocks(core, own, oth):
         pair = [
@@ -252,8 +291,10 @@
         both_ref[i, TOK:] = d_both
 
 
-def last_kernel(meta, own, oth, rows, gates, vel1, probe, out_ref):
+def last_kernel(meta, own, oth, rows_hbm, gates, vel_hbm, probe_hbm, out_ref, rows, vel1, probe, sem):
     core, plane, slab = meta[0], meta[2], meta[3]
+    columns = [(probe_hbm.at[slab * 8 + y * 2 + core], probe.at[y]) for y in range(4)]
+    copies = fetch(sem, (rows_hbm, rows), (vel_hbm, vel1), *columns)
     row = lax.broadcasted_iota(jnp.int32, (256, TOK), 0)
     token = lax.broadcasted_iota(jnp.int32, (256, TOK), 1)
     hit = (token == (row >> 3) * 6 + (row & 7)) & ((row & 7) < 6)
@@ -264,6 +305,8 @@
         first = jnp.where(core == 0, mine, other)
         second = jnp.where(core == 0, other, mine)
         left.append(jnp.concatenate([first, second], axis=1))
+    for copy in copies:
+        copy.wait()
     trace = jnp.zeros((1, 128), F32)
     laid = []
     for y in range(4):
@@ -273,7 +316,7 @@
             mapped = mapped + dot(left[z], right)
         column = slab * 8 + y * 2 + core
         mapped = mapped * gates[column]
-        terms = mapped[TOK:] * probe[column].astype(F32)
+        terms = mapped[TOK:] * probe[y].astype(F32)
         trace = trace + jnp.sum(terms, axis=0, keepdims=True)
         vel = vel1[...].astype(F32)
         part = mapped[:TOK] + jnp.where(plane == y, vel, jnp.zeros_like(vel))
@@ -328,25 +371,27 @@
     place = lax.axis_index(SEQ)
     meta = [lax.axis_index("c"), place, lax.axis_index("y"), lax.axis_index("z")]
     meta = jnp.stack(meta).astype(jnp.int32)
-    gate = lax.dynamic_slice_in_dim(out_gate, place * 128, 128).reshape(1, 128)
+    gates = out_gate.reshape(32, 1, 128)
     maps = head_maps.reshape(32, 128, 384)
     outs = out_map.reshape(32, 128, 128)
     gain = norm_gain.reshape(32, 1, 128)
 
     packed_state, packed_probe = call(
-        pack_kernel, [shape((4, 8, 3072)), shape((8, 6144))], 0, state, probe
+        pack_kernel, [shape((4, 8, 3072)), shape((8, 6144))], 0, (state,), (probe,),
+        scratch=[pltpu.VMEM((6, 4096), BF), pltpu.VMEM((6, 4096), BF), sems(2)], vmem_mib=FULL,
     )
     probe_all = lax.all_gather(packed_probe, SEQ, axis=0, tiled=True)
     _, own = spread(packed_state)
     oth = swap(own)
     att1, col = call(
         first_kernel, [shape((4, TOK, 128)), shape((TOK, 128))],
-        1, meta, own, oth, maps, gain, query_gain, key_gain, scratch=HELD,
+        1, meta, own, oth, (maps,), gain, query_gain, key_gain, scratch=[HELD, MAPS, sems(1)],
     )
     _, own1, oth1 = gathered(att1)
     vel1, mid = call(
         middle_kernel, [shape((TOK, 128)), shape((4, TOK, 128))],
-        1, meta, own1, oth1, outs, gate, col,
+        1, meta, own1, oth1, (outs,), gates, col,
+        scratch=[pltpu.VMEM((32, 128, 128), BF), sems(1)], vmem_mib=MIDDLE,
     )
     _, own_m = spread(mid)
     late_map, own_m = lax.optimization_barrier((out_map, own_m))
@@ -354,13 +399,19 @@
     plane_outs = lax.all_to_all(by_plane, "y", 0, 0, tiled=True)
     probe_blocks, datt1 = call(
         tangent_kernel, [shape((32, TOK, 128)), shape((TOK, 128), F32)],
-        1, meta, own, oth, probe_all, maps, gain, query_gain, key_gain, (mid,), scratch=HELD,
+        1, meta, (own,), (oth,), (probe_all,), (maps,), gain, query_gain, key_gain, (mid,),
+        scratch=[
+            HELD, pltpu.VMEM((128, 3072), BF), pltpu.VMEM((128, 3072), BF),
+            pltpu.VMEM((256, 3072), BF), MAPS, sems(4),
+        ],
+        vmem_mib=FULL,
     )
     oth_m = swap(own_m).reshape(16, TOK, 128)
     own_m = own_m.reshape(16, TOK, 128)
     both = call(
         second_kernel, shape((4, 2 * TOK, 128)),
-        1, meta, own_m, oth_m, probe_blocks, maps, gain, query_gain, key_gain, datt1,
+        1, meta, own_m, oth_m, probe_blocks, (maps,), gain, query_gain, key_gain, datt1,
+        scratch=[MAPS, sems(1)], vmem_mib=SECOND,
     )
     both, plane_outs = lax.optimization_barrier((both, plane_outs))
     own2 = lax.all_to_all(both.reshape(8 * TOK, 128), "z", 0, 0, tiled=True)
@@ -368,7 +419,12 @@
     columns = call(
         last_kernel, shape((256, 512)),
         1, meta, own2.reshape(4, 2 * TOK, 128), oth2.reshape(4, 2 * TOK, 128),
-        plane_outs.reshape(4, 8, 128, 128), out_gate.reshape(32, 1, 128), vel1, probe_blocks,
+        (plane_outs.reshape(4, 8, 128, 128),), gates, (vel1,), (probe_blocks,),
+        scratch=[
+            pltpu.VMEM((4, 8, 128, 128), BF), pltpu.VMEM((TOK, 128), BF),
+            pltpu.VMEM((4, TOK, 128), BF), sems(6),
+        ],
+        vmem_mib=LAST,
     )
     got = lax.all_to_all(columns, SEQ, 0, 0, tiled=True).reshape(32, 8, 512)
     next_state, change = call(

time: 187 us -> 178 us (0.952)
  local copies, waits for them, and re-layouts: 12.5 us -> 2.31 us
  Pallas kernels: 20.3 us -> 24.3 us
  blocking collectives: 106 us -> 104 us
    unnamed x38 -> x28, local copies, waits for them, and re-layouts: 10.4 us -> 0.96 us
    pallas_call x7, Pallas kernels: 20.3 us -> 24.3 us  [call(): pl.pallas_call(kernel, out_shape=out_shape, in_specs=in_specs, out_specs=...]
    all_to_all x3, blocking collectives: 43.7 us -> 41.3 us  [spread(): return (a, lax.all_to_all(jnp.tile(a, (4, 1)), 'y', 0, 0, tiled=True))]
  transfers between devices with their start and end apart: 6 -> 6, of which waited for: 4 -> 4; matrix products, arithmetic and copies ran while one was open for 1% -> 1% of each run, Pallas kernels for 8% -> 10%
where the time goes in v5:
time: 178 us; the launch traced here: 177 us
  blocking collectives  104 us (58%)
  starting transfers between devices  25.6 us (14%)
  Pallas kernels  24.3 us (14%)
  between operations  14.3 us (8%)
  waiting for transfers between devices  6.74 us (4%)
  local copies, waits for them, and re-layouts  2.31 us (1%)
    all_to_all x3, blocking collectives, spread(): return (a, lax.all_to_all(jnp.tile(a, (4, 1)), 'y', 0, 0, tiled=True))  41.3 us
    all_to_all x3, blocking collectives, spread(): a = lax.all_to_all(copies.reshape(n * rows, lanes), 'z', 0, 0, tiled=True)  33.1 us
    pallas_call x7, Pallas kernels, call(): pl.pallas_call(kernel, out_shape=out_shape, in_specs=in_specs, out_specs=...  24.3 us
    ppermute x4, starting transfers between devices, swap(): return lax.ppermute(block, 'c', [(0, 1), (1, 0)])  22.1 us
    all_to_all x1, blocking collectives, per_device(): got = lax.all_to_all(columns, SEQ, 0, 0, tiled=True).reshape(32, 8, 512)  15.5 us
    all_to_all x1, blocking collectives, per_device(): own2 = lax.all_to_all(both.reshape(8 * TOK, 128), 'z', 0, 0, tiled=True)  14.1 us
    ppermute x4, waiting for transfers between devices, swap(): return lax.ppermute(block, 'c', [(0, 1), (1, 0)])  5.36 us
  transfers between devices with their start and end apart: 6, of which 4 were waited for; matrix products, arithmetic and copies ran while one was open for 1% of the time, Pallas kernels for 10%

profile of v5, /device:TPU:1, one launch (start us, length us, event | category | flops | bytes accessed | tf_op | source)
XLA Modules:
  0.0 177.4 jit_solution(13956839094952706397)
XLA Ops:
  7.2 0.0 all-gather.2.cloned.1.call-start
  7.3 1.8 shard_map.95
  9.1 12.1 %all_to_all.74 = bf16[4,8,3072]{2,1,0:T(8,128)(2,1)S(1)} all-to-all(bf16[4,8,3072]{2,1,0:T(8,128)(2,1)} %get-tuple-element.16), channel_id=1, replica_groups=mesh['z'=4,'y'=4,'c'=2,'w'=4,'x'=4] {'z'}, dimensions={0} | all-to-all | bytes 393216 | tf_op jit(solution)/shard_map/all_to_all | solution.py:355
  21.2 0.1 tile.13
  21.2 12.5 %all_to_all.75 = bf16[4,32,3072]{2,1,0:T(8,128)(2,1)} all-to-all(bf16[4,32,3072]{2,1,0:T(8,128)(2,1)S(1)} %tile.13), channel_id=1, replica_groups=mesh['z'=4,'y'=4,'c'=2,'w'=4,'x'=4] {'y'}, dimensions={0} | all-to-all | bytes 1572864 | tf_op jit(solution)/shard_map/all_to_all | solution.py:356
  33.7 8.4 %collective-permute-start = (bf16[128,3072]{1,0:T(8,128)(2,1)}, bf16[128,3072]{1,0:T(8,128)(2,1)}, u32[]{:S(2)}, u32[]{:S(2)}) collective-permute-start(bf16[128,3072]{1,0:T(8,128)(2,1)} %bitcast.5.xa.xa_hbm), channel_id=1, source_target_pairs={{0,16},{16,0},{1,17},{17,1},{2,18},{18,2},{3,19},{19,3},{4,20},{20... | collective-permute-start | bytes 2359304 | tf_op jit(solution)/shard_map/ppermute | solution.py:360
  42.1 0.1 pad_add_fusion.meta
  42.2 2.1 %collective-permute-done.xb.xb_hbm = bf16[128,3072]{1,0:T(8,128)(2,1)} collective-permute-done((bf16[128,3072]{1,0:T(8,128)(2,1)}, bf16[128,3072]{1,0:T(8,128)(2,1)}, u32[]{:S(2)}, u32[]{:S(2)}) %collective-permute-start) | collective-permute-done | bytes 786464 | tf_op jit(solution)/shard_map/ppermute | solution.py:360
  44.4 4.1 %shard_map.96 = (bf16[4,192,128]{2,1,0:T(8,128)(2,1)S(1)}, bf16[192,128]{1,0:T(8,128)(2,1)S(1)}) custom-call(s32[4]{0:T(128)S(1)} %pad_add_fusion.meta, bf16[128,3072]{1,0:T(8,128)(2,1)} %bitcast.5.xa.xa_hbm, bf16[128,3072]{1,0:T(8,128)(2,1)} %collective-permute-done.xb.xb_hbm, bf16[32,128,384]{2,1,0:T(8,128)(2,1)S(1)} %bitcast.31, ...), custom_call_target="tpu_custom_call" | custom-call | tf_op jit(solution)/shard_map/pallas_call | solution.py:61
  48.5 12.4 %all_to_all.76 = bf16[4,192,128]{2,1,0:T(8,128)(2,1)S(1)} all-to-all(bf16[4,192,128]{2,1,0:T(8,128)(2,1)S(1)} %get-tuple-element.17), channel_id=1, replica_groups=mesh['z'=4,'y'=4,'c'=2,'w'=4,'x'=4] {'z'}, dimensions={0} | all-to-all | bytes 393216 | tf_op jit(solution)/shard_map/all_to_all | solution.py:355
  60.8 0.1 tile.30
  60.9 16.6 %all_to_all.77 = bf16[4,768,128]{2,1,0:T(8,128)(2,1)S(1)} all-to-all(bf16[4,768,128]{2,1,0:T(8,128)(2,1)S(1)} %tile.30), channel_id=1, replica_groups=mesh['z'=4,'y'=4,'c'=2,'w'=4,'x'=4] {'y'}, dimensions={0} | all-to-all | bytes 1572864 | tf_op jit(solution)/shard_map/all_to_all | solution.py:356
  77.5 4.2 %collective-permute-start.1 = (bf16[3072,128]{1,0:T(8,128)(2,1)S(1)}, bf16[3072,128]{1,0:T(8,128)(2,1)S(1)}, u32[]{:S(2)}, u32[]{:S(2)}) collective-permute-start(bf16[3072,128]{1,0:T(8,128)(2,1)S(1)} %bitcast.37), channel_id=1, source_target_pairs={{0,16},{16,0},{1,17},{17,1},{2,18},{18,2},{3,19},{19,3},{4,20},{20... | collective-permute-start | bytes 2359304 | tf_op jit(solution)/shard_map/ppermute | solution.py:360
  81.7 1.9 %collective-permute-done.1 = bf16[3072,128]{1,0:T(8,128)(2,1)S(1)} collective-permute-done((bf16[3072,128]{1,0:T(8,128)(2,1)S(1)}, bf16[3072,128]{1,0:T(8,128)(2,1)S(1)}, u32[]{:S(2)}, u32[]{:S(2)}) %collective-permute-start.1) | collective-permute-done | bytes 786464 | tf_op jit(solution)/shard_map/ppermute | solution.py:360
  83.6 1.2 shard_map.97
  84.9 8.6 %all_to_all.78 = bf16[4,192,128]{2,1,0:T(8,128)(2,1)S(1)} all-to-all(bf16[4,192,128]{2,1,0:T(8,128)(2,1)S(1)} %get-tuple-element.19.after), channel_id=1, replica_groups=mesh['z'=4,'y'=4,'c'=2,'w'=4,'x'=4] {'z'}, dimensions={0} | all-to-all | bytes 393216 | tf_op jit(solution)/shard_map/all_to_all | solution.py:355
  93.5 0.1 tile.32
  93.6 12.2 %all_to_all.79 = bf16[4,768,128]{2,1,0:T(8,128)(2,1)S(1)} all-to-all(bf16[4,768,128]{2,1,0:T(8,128)(2,1)S(1)} %tile.32), channel_id=1, replica_groups=mesh['z'=4,'y'=4,'c'=2,'w'=4,'x'=4] {'y'}, dimensions={0} | all-to-all | bytes 1572864 | tf_op jit(solution)/shard_map/all_to_all | solution.py:356
  105.8 5.3 %collective-permute-start.2 = (bf16[3072,128]{1,0:T(8,128)(2,1)S(1)}, bf16[3072,128]{1,0:T(8,128)(2,1)S(1)}, u32[]{:S(2)}, u32[]{:S(2)}) collective-permute-start(bf16[3072,128]{1,0:T(8,128)(2,1)S(1)} %bitcast.35), channel_id=1, source_target_pairs={{0,16},{16,0},{1,17},{17,1},{2,18},{18,2},{3,19},{19,3},{4,20},{20... | collective-permute-start | bytes 2359304 | tf_op jit(solution)/shard_map/ppermute | solution.py:360
  111.1 1.1 copy.10
  112.2 3.5 %all-to-all-start.6 = ((bf16[4,1024,128]{2,1,0:T(8,128)(2,1)}), bf16[4,1024,128]{2,1,0:T(8,128)(2,1)S(1)}, u32[]{:S(2)}, u32[]{:S(2)}) async-start(bf16[4,1024,128]{2,1,0:T(8,128)(2,1)} %bitcast.49), calls=%async_computation.6 | async-start | bytes 2097152 | tf_op jit(solution)/shard_map/all_to_all | solution.py:399
  115.8 0.0 all-gather.2.cloned.1.call-done.packed_hbm
  115.8 7.2 %shard_map.98 = (bf16[32,192,128]{2,1,0:T(8,128)(2,1)}, f32[192,128]{1,0:T(8,128)}) custom-call(s32[4]{0:T(128)} %copy-done.8, bf16[128,3072]{1,0:T(8,128)(2,1)} %bitcast.5.xa.xa_hbm, bf16[128,3072]{1,0:T(8,128)(2,1)} %collective-permute-done.xb.xb_hbm, bf16[256,6144]{1,0:T(8,128)(2,1)} %all-gather.2.cloned.1.call-done.packed_hbm, ...), custom_call_target="tpu_custom_call" | custom-call | tf_op jit(solution)/shard_map/pallas_call | solution.py:61
  123.0 0.9 copy-done.6
  123.9 5.7 %shard_map.99 = bf16[4,384,128]{2,1,0:T(8,128)(2,1)S(1)} custom-call(s32[4]{0:T(128)S(1)} %copy-done.9, bf16[16,192,128]{2,1,0:T(8,128)(2,1)S(1)} %bitcast.36, bf16[16,192,128]{2,1,0:T(8,128)(2,1)S(1)} %bitcast.41, bf16[32,192,128]{2,1,0:T(8,128)(2,1)} %get-tuple-element.22.probe.probe_hbm, bf16[32,128,384]{2,1,0:T(8,128)(2,1)} %bitcast.30, ...), custom_call_target="tpu_custom_call" | custom-call | tf_op jit(solution)/shard_map/pallas_call | solution.py:61
  129.6 1.3 all-to-all-done.6
  130.9 14.1 %all_to_all.80.own = bf16[4,384,128]{2,1,0:T(8,128)(2,1)S(1)} all-to-all(bf16[4,384,128]{2,1,0:T(8,128)(2,1)S(1)} %shard_map.99), channel_id=1, replica_groups=mesh['z'=4,'y'=4,'c'=2,'w'=4,'x'=4] {'z'}, dimensions={0} | all-to-all | bytes 786432 | tf_op jit(solution)/shard_map/all_to_all | solution.py:417
  145.1 4.2 %collective-permute-start.3 = (bf16[1536,128]{1,0:T(8,128)(2,1)S(1)}, bf16[1536,128]{1,0:T(8,128)(2,1)S(1)}, u32[]{:S(2)}, u32[]{:S(2)}) collective-permute-start(bf16[1536,128]{1,0:T(8,128)(2,1)S(1)} %bitcast.39), channel_id=1, source_target_pairs={{0,16},{16,0},{1,17},{17,1},{2,18},{18,2},{3,19},{19,3},{4,20},{20... | collective-permute-start | bytes 1179656 | tf_op jit(solution)/shard_map/ppermute | solution.py:360
  149.3 1.3 collective-permute-done.3
  150.6 3.8 %shard_map.100 = bf16[256,512]{1,0:T(8,128)(2,1)S(1)} custom-call(s32[4]{0:T(128)S(1)} %copy-done.9, bf16[4,384,128]{2,1,0:T(8,128)(2,1)S(1)} %all_to_all.80.own, bf16[4,384,128]{2,1,0:T(8,128)(2,1)S(1)} %bitcast.43, bf16[4,8,128,128]{3,2,1,0:T(8,128)(2,1)S(1)} %bitcast.34, f32[32,1,128]{2,1,0:T(1,128)S(1)} %bitcast.48, ...), custom_call_target="tpu_custom_call" | custom-call | tf_op jit(solution)/shard_map/pallas_call | solution.py:61
  154.4 15.5 %all_to_all.81.got = bf16[32,8,512]{2,1,0:T(8,128)(2,1)S(1)} all-to-all(bf16[32,8,512]{2,1,0:T(8,128)(2,1)S(1)} %bitcast.40), channel_id=1, replica_groups=mesh['z'=4,'y'=4,'c'=2,'w'=4,'x'=4] {'z','y','c'}, dimensions={0} | all-to-all | bytes 524288 | tf_op jit(solution)/shard_map/all_to_all | solution.py:429
  169.9 0.7 shard_map.101
  (29 shorter events, 0.1 us)
Async XLA Ops:
  7.2 37.2 %copy-start.12 = (f32[1,128]{1,0:T(1,128)S(1)}, f32[1,128]{1,0:T(1,128)}, u32[]{:S(2)}) copy-start(f32[1,128]{1,0:T(1,128)} %k_gain.5) | copy-start | bytes 1540
  7.2 37.2 %copy-start.10 = (f32[1,128]{1,0:T(1,128)S(1)}, f32[1,128]{1,0:T(1,128)}, u32[]{:S(2)}) copy-start(f32[1,128]{1,0:T(1,128)} %q_gain.5) | copy-start | bytes 1540
  7.2 37.2 %copy-start = (bf16[1,4096,384]{2,1,0:T(8,128)(2,1)S(1)}, bf16[1,4096,384]{2,1,0:T(8,128)(2,1)}, u32[]{:S(2)}) copy-start(bf16[1,4096,384]{2,1,0:T(8,128)(2,1)} %param.11) | copy-start | bytes 9437188
  7.2 37.1 %copy-start.4 = (f32[4096]{0:T(1024)S(1)}, f32[4096]{0:T(1024)}, u32[]{:S(2)}) copy-start(f32[4096]{0:T(1024)} %param.10) | copy-start | bytes 49156
  7.2 108.6 %all-gather.2.cloned.1.call-start = ((), (), s32[]{:S(2)}) async-start(), calls=%async_computation.9 | async-start | bytes 3244032 | tf_op jit(solution)/shard_map/all_gather | solution.py:383
  33.7 10.6 %collective-permute-start = (bf16[128,3072]{1,0:T(8,128)(2,1)}, bf16[128,3072]{1,0:T(8,128)(2,1)}, u32[]{:S(2)}, u32[]{:S(2)}) collective-permute-start(bf16[128,3072]{1,0:T(8,128)(2,1)} %bitcast.5.xa.xa_hbm), channel_id=1, source_target_pairs={{0,16},{16,0},{1,17},{17,1},{2,18},{18,2},{3,19},{19,3},{4,20},{20... | collective-permute-start | bytes 2359304 | tf_op jit(solution)/shard_map/ppermute | solution.py:360
  42.2 41.4 %copy-start.8 = (s32[4]{0:T(128)}, s32[4]{0:T(128)S(1)}, u32[]{:S(2)}) copy-start(s32[4]{0:T(128)S(1)} %pad_add_fusion.meta) | copy-start | bytes 52
  44.3 39.3 %copy-start.1 = (bf16[4096,128]{1,0:T(8,128)(2,1)S(1)}, bf16[4096,128]{1,0:T(8,128)(2,1)}, u32[]{:S(2)}) copy-start(bf16[4096,128]{1,0:T(8,128)(2,1)} %param.14) | copy-start | bytes 3145732
  44.4 39.3 %copy-start.7 = (f32[4096]{0:T(1024)S(1)}, f32[4096]{0:T(1024)}, u32[]{:S(2)}) copy-start(f32[4096]{0:T(1024)} %param.15) | copy-start | bytes 49156
  77.5 6.1 %collective-permute-start.1 = (bf16[3072,128]{1,0:T(8,128)(2,1)S(1)}, bf16[3072,128]{1,0:T(8,128)(2,1)S(1)}, u32[]{:S(2)}, u32[]{:S(2)}) collective-permute-start(bf16[3072,128]{1,0:T(8,128)(2,1)S(1)} %bitcast.37), channel_id=1, source_target_pairs={{0,16},{16,0},{1,17},{17,1},{2,18},{18,2},{3,19},{19,3},{4,20},{20... | collective-permute-start | bytes 2359304 | tf_op jit(solution)/shard_map/ppermute | solution.py:360
  84.9 27.4 %copy-start.2 = (bf16[4,192,128]{2,1,0:T(8,128)(2,1)}, bf16[4,192,128]{2,1,0:T(8,128)(2,1)S(1)}, u32[]{:S(2)}) copy-start(bf16[4,192,128]{2,1,0:T(8,128)(2,1)S(1)} %get-tuple-element.19.after) | copy-start | bytes 589828
  105.8 17.2 %collective-permute-start.2 = (bf16[3072,128]{1,0:T(8,128)(2,1)S(1)}, bf16[3072,128]{1,0:T(8,128)(2,1)S(1)}, u32[]{:S(2)}, u32[]{:S(2)}) collective-permute-start(bf16[3072,128]{1,0:T(8,128)(2,1)S(1)} %bitcast.35), channel_id=1, source_target_pairs={{0,16},{16,0},{1,17},{17,1},{2,18},{18,2},{3,19},{19,3},{4,20},{20... | collective-permute-start | bytes 2359304 | tf_op jit(solution)/shard_map/ppermute | solution.py:360
  112.2 18.7 %all-to-all-start.6 = ((bf16[4,1024,128]{2,1,0:T(8,128)(2,1)}), bf16[4,1024,128]{2,1,0:T(8,128)(2,1)S(1)}, u32[]{:S(2)}, u32[]{:S(2)}) async-start(bf16[4,1024,128]{2,1,0:T(8,128)(2,1)} %bitcast.49), calls=%async_computation.6 | async-start | bytes 2097152 | tf_op jit(solution)/shard_map/all_to_all | solution.py:399
  115.7 7.3 %copy-start.5 = (f32[4096]{0:T(1024)S(1)}, f32[4096]{0:T(1024)}, u32[]{:S(2)}) copy-start(f32[4096]{0:T(1024)} %param.10) | copy-start | bytes 49156
  115.7 7.3 %copy-start.9 = (s32[4]{0:T(128)S(1)}, s32[4]{0:T(128)}, u32[]{:S(2)}) copy-start(s32[4]{0:T(128)} %copy-done.8) | copy-start | bytes 52
  115.8 7.3 %copy-start.11 = (f32[1,128]{1,0:T(1,128)S(1)}, f32[1,128]{1,0:T(1,128)}, u32[]{:S(2)}) copy-start(f32[1,128]{1,0:T(1,128)} %q_gain.5) | copy-start | bytes 1540
  115.8 7.2 %copy-start.13 = (f32[1,128]{1,0:T(1,128)S(1)}, f32[1,128]{1,0:T(1,128)}, u32[]{:S(2)}) copy-start(f32[1,128]{1,0:T(1,128)} %k_gain.5) | copy-start | bytes 1540
  123.0 0.9 copy-start.6
  129.6 40.3 %copy-start.3 = (bf16[6,4096]{1,0:T(8,128)(2,1)S(1)}, bf16[6,4096]{1,0:T(8,128)(2,1)}, u32[]{:S(2)}) copy-start(bf16[6,4096]{1,0:T(8,128)(2,1)} %state.1) | copy-start | bytes 147460
  145.1 5.5 %collective-permute-start.3 = (bf16[1536,128]{1,0:T(8,128)(2,1)S(1)}, bf16[1536,128]{1,0:T(8,128)(2,1)S(1)}, u32[]{:S(2)}, u32[]{:S(2)}) collective-permute-start(bf16[1536,128]{1,0:T(8,128)(2,1)S(1)} %bitcast.39), channel_id=1, source_target_pairs={{0,16},{16,0},{1,17},{17,1},{2,18},{18,2},{3,19},{19,3},{4,20},{20... | collective-permute-start | bytes 1179656 | tf_op jit(solution)/shard_map/ppermute | solution.py:360
Sparse Core Ops, SparseCore 0:
  10.2 76.4 all-gather.1

commit v6 on v5

--- a/solution.py
+++ b/solution.py
@@ -29,6 +29,7 @@
 
 HELD = pltpu.VMEM((32, TOK, 128), BF)
 MAPS = pltpu.VMEM((32, 128, 384), BF)
+ROWS = pltpu.VMEM((4, 8, 128, 128), BF)
 
 
 FULL = 60
@@ -202,20 +203,31 @@
                 yield side, y * 4 + z, z * 8 + y * 2 + c
 
 
-def out_product(core, own, oth, out_map):
-    total = jnp.zeros((own.shape[1], 128), F32)
-    for side, b, h in blocks(core, own, oth):
-        left = jnp.concatenate([side[b], side[b + 1]], axis=1)
-        right = jnp.concatenate([out_map[h], out_map[h + 8]], axis=0)
-        total = total + dot(left, right)
-    return total
-
-
-def middle_kernel(meta, own, oth, out_hbm, gates, col, vel_ref, mid_ref, out_map, sem):
-    copies = fetch(sem, (out_hbm, out_map))
-    gate = gates[meta[1]]
-    copies[0].wait()
-    vel = (gate * out_product(meta[0], own, oth, out_map)).astype(BF)
+def plane_products(core, own, oth, rows):
+    left = []
+    for z in range(4):
+        mine, other = own[z], oth[z]
+        first = jnp.where(core == 0, mine, other)
+        second = jnp.where(core == 0, other, mine)
+        left.append(jnp.concatenate([first, second], axis=1))
+    for y in range(4):
+        mapped = None
+        for z in range(4):
+            right = jnp.concatenate([rows[y, z * 2], rows[y, z * 2 + 1]], axis=0)
+            part = dot(left[z], right)
+            mapped = part if mapped is None else mapped + part
+        yield y, mapped
+
+
+def plane_kernel(meta, own, oth, rows_hbm, part_ref, rows, sem):
+    fetch(sem, (rows_hbm, rows))[0].wait()
+    for y, mapped in plane_products(meta[0], own, oth, rows):
+        part_ref[y] = mapped
+
+
+def middle_kernel(meta, parts, gates, col, vel_ref, mid_ref):
+    total = (parts[0] + parts[1]) + (parts[2] + parts[3])
+    vel = (gates[meta[1]] * total).astype(BF)
     vel_ref[...] = vel
     mid = (col[...].astype(F32) + STEP * vel.astype(F32)).astype(BF)
     for i in range(4):
@@ -299,21 +311,11 @@
     token = lax.broadcasted_iota(jnp.int32, (256, TOK), 1)
     hit = (token == (row >> 3) * 6 + (row & 7)) & ((row & 7) < 6)
     lay = jnp.where(hit, jnp.ones((256, TOK), F32), jnp.zeros((256, TOK), F32)).astype(BF)
-    left = []
-    for z in range(4):
-        mine, other = own[z], oth[z]
-        first = jnp.where(core == 0, mine, other)
-        second = jnp.where(core == 0, other, mine)
-        left.append(jnp.concatenate([first, second], axis=1))
     for copy in copies:
         copy.wait()
     trace = jnp.zeros((1, 128), F32)
     laid = []
-    for y in range(4):
-        mapped = jnp.zeros((2 * TOK, 128), F32)
-        for z in range(4):
-            right = jnp.concatenate([rows[y, z * 2], rows[y, z * 2 + 1]], axis=0)
-            mapped = mapped + dot(left[z], right)
+    for y, mapped in plane_products(core, own, oth, rows):
         column = slab * 8 + y * 2 + core
         mapped = mapped * gates[column]
         terms = mapped[TOK:] * probe[y].astype(F32)
@@ -360,20 +362,12 @@
     return lax.ppermute(block, "c", [(0, 1), (1, 0)])
 
 
-def gathered(copies):
-    rows = copies.shape[1]
-    early, own = spread(copies)
-    other = swap(own)
-    return early, own.reshape(16, rows, 128), other.reshape(16, rows, 128)
-
-
 def per_device(state, probe, norm_gain, head_maps, query_gain, key_gain, out_map, out_gate):
     place = lax.axis_index(SEQ)
     meta = [lax.axis_index("c"), place, lax.axis_index("y"), lax.axis_index("z")]
     meta = jnp.stack(meta).astype(jnp.int32)
     gates = out_gate.reshape(32, 1, 128)
     maps = head_maps.reshape(32, 128, 384)
-    outs = out_map.reshape(32, 128, 128)
     gain = norm_gain.reshape(32, 1, 128)
 
     packed_state, packed_probe = call(
@@ -382,21 +376,29 @@
     )
     probe_all = lax.all_gather(packed_probe, SEQ, axis=0, tiled=True)
     _, own = spread(packed_state)
+    by_plane = out_map.reshape(4, 4, 256, 128).transpose(1, 0, 2, 3).reshape(4096, 128)
+    by_plane, own = lax.optimization_barrier((by_plane, own))
+    plane_outs = lax.all_to_all(by_plane, "y", 0, 0, tiled=True)
     oth = swap(own)
     att1, col = call(
         first_kernel, [shape((4, TOK, 128)), shape((TOK, 128))],
         1, meta, own, oth, (maps,), gain, query_gain, key_gain, scratch=[HELD, MAPS, sems(1)],
     )
-    _, own1, oth1 = gathered(att1)
+    att1, plane_outs = lax.optimization_barrier((att1, plane_outs))
+    plane_outs = plane_outs.reshape(4, 8, 128, 128)
+    own1 = lax.all_to_all(att1.reshape(4 * TOK, 128), "z", 0, 0, tiled=True)
+    oth1 = swap(own1)
+    parts = call(
+        plane_kernel, shape((4, TOK, 128), F32),
+        1, meta, own1.reshape(4, TOK, 128), oth1.reshape(4, TOK, 128), (plane_outs,),
+        scratch=[ROWS, sems(1)], vmem_mib=MIDDLE,
+    )
+    parts = lax.all_to_all(parts.reshape(4 * TOK, 128), "y", 0, 0, tiled=True)
     vel1, mid = call(
         middle_kernel, [shape((TOK, 128)), shape((4, TOK, 128))],
-        1, meta, own1, oth1, (outs,), gates, col,
-        scratch=[pltpu.VMEM((32, 128, 128), BF), sems(1)], vmem_mib=MIDDLE,
+        1, meta, parts.reshape(4, TOK, 128), gates, col, vmem_mib=MIDDLE,
     )
     _, own_m = spread(mid)
-    late_map, own_m = lax.optimization_barrier((out_map, own_m))
-    by_plane = late_map.reshape(4, 4, 256, 128).transpose(1, 0, 2, 3).reshape(4096, 128)
-    plane_outs = lax.all_to_all(by_plane, "y", 0, 0, tiled=True)
     probe_blocks, datt1 = call(
         tangent_kernel, [shape((32, TOK, 128)), shape((TOK, 128), F32)],
         1, meta, (own,), (oth,), (probe_all,), (maps,), gain, query_gain, key_gain, (mid,),
@@ -406,6 +408,7 @@
         ],
         vmem_mib=FULL,
     )
+    own_m, datt1 = lax.optimization_barrier((own_m, datt1))
     oth_m = swap(own_m).reshape(16, TOK, 128)
     own_m = own_m.reshape(16, TOK, 128)
     both = call(
@@ -413,15 +416,14 @@
         1, meta, own_m, oth_m, probe_blocks, (maps,), gain, query_gain, key_gain, datt1,
         scratch=[MAPS, sems(1)], vmem_mib=SECOND,
     )
-    both, plane_outs = lax.optimization_barrier((both, plane_outs))
     own2 = lax.all_to_all(both.reshape(8 * TOK, 128), "z", 0, 0, tiled=True)
     oth2 = swap(own2)
     columns = call(
         last_kernel, shape((256, 512)),
         1, meta, own2.reshape(4, 2 * TOK, 128), oth2.reshape(4, 2 * TOK, 128),
-        (plane_outs.reshape(4, 8, 128, 128),), gates, (vel1,), (probe_blocks,),
+        (plane_outs,), gates, (vel1,), (probe_blocks,),
         scratch=[
-            pltpu.VMEM((4, 8, 128, 128), BF), pltpu.VMEM((TOK, 128), BF),
+            ROWS, pltpu.VMEM((TOK, 128), BF),
             pltpu.VMEM((4, TOK, 128), BF), sems(6),
         ],
         vmem_mib=LAST,

time: 178 us -> 182 us (1.022)
  blocking collectives: 104 us -> 70.9 us
  waiting for transfers between devices: 6.74 us -> 27.8 us
  starting transfers between devices: 25.6 us -> 36.8 us
  local copies, waits for them, and re-layouts: 2.31 us -> 5.24 us
    all_to_all x3 -> x2, blocking collectives: 41.3 us -> 20.7 us  [the longest x1 10.5 us: per_device(): own1 = lax.all_to_all(att1.reshape(4 * TOK, 128), 'z', 0, 0, tiled=True)]
    all_to_all x1, waiting for transfers between devices: 1.34 us -> 15.6 us  [per_device(): plane_outs = lax.all_to_all(by_plane, 'y', 0, 0, tiled=True)]
    all_to_all x3 -> x2, blocking collectives: 33.1 us -> 20.2 us  [spread(): a = lax.all_to_all(copies.reshape(n * rows, lanes), 'z', 0, 0, tiled=True)]
    all_to_all x0 -> x2, starting transfers between devices: none -> 8.01 us  [spread(): return (a, lax.all_to_all(jnp.tile(a, (4, 1)), 'y', 0, 0, tiled=True))]
    all_to_all x0 -> x2, waiting for transfers between devices: none -> 7.96 us  [spread(): return (a, lax.all_to_all(jnp.tile(a, (4, 1)), 'y', 0, 0, tiled=True))]
    ppermute x4, starting transfers between devices: 22.1 us -> 24.5 us  [swap(): return lax.ppermute(block, 'c', [(0, 1), (1, 0)])]
    pallas_call x7 -> x8, Pallas kernels: 24.3 us -> 26.1 us  [call(): pl.pallas_call(kernel, out_shape=out_shape, in_specs=in_specs, out_specs=...]
  transfers between devices with their start and end apart: 6 -> 8, of which waited for: 4 -> 6; matrix products, arithmetic and copies ran while one was open for 1% -> 2% of each run, Pallas kernels for 10% -> 8%
where the time goes in v6:
time: 182 us; the launch traced here: 181 us
  blocking collectives  70.9 us (39%)
  starting transfers between devices  36.8 us (20%)
  waiting for transfers between devices  27.8 us (15%)
  Pallas kernels  26.1 us (14%)
  between operations  14.3 us (8%)
  local copies, waits for them, and re-layouts  5.24 us (3%)
    pallas_call x8, Pallas kernels, call(): pl.pallas_call(kernel, out_shape=out_shape, in_specs=in_specs, out_specs=...  26.1 us
    ppermute x4, starting transfers between devices, swap(): return lax.ppermute(block, 'c', [(0, 1), (1, 0)])  24.5 us
    all_to_all x2, blocking collectives, spread(): a = lax.all_to_all(copies.reshape(n * rows, lanes), 'z', 0, 0, tiled=True)  20.2 us
    all_to_all x1, waiting for transfers between devices, per_device(): plane_outs = lax.all_to_all(by_plane, 'y', 0, 0, tiled=True)  15.6 us
    all_to_all x1, blocking collectives, per_device(): own2 = lax.all_to_all(both.reshape(8 * TOK, 128), 'z', 0, 0, tiled=True)  15.3 us
    all_to_all x1, blocking collectives, per_device(): got = lax.all_to_all(columns, SEQ, 0, 0, tiled=True).reshape(32, 8, 512)  14.8 us
    all_to_all x1, blocking collectives, per_device(): own1 = lax.all_to_all(att1.reshape(4 * TOK, 128), 'z', 0, 0, tiled=True)  10.5 us
    all_to_all x1, blocking collectives, per_device(): parts = lax.all_to_all(parts.reshape(4 * TOK, 128), 'y', 0, 0, tiled=True)  10.2 us
  transfers between devices with their start and end apart: 8, of which 6 were waited for; matrix products, arithmetic and copies ran while one was open for 2% of the time, Pallas kernels for 8%

profile of v6, /device:TPU:1, one launch (start us, length us, event | category | flops | bytes accessed | tf_op | source)
XLA Modules:
  0.0 181.2 jit_solution(17418371756730353940)
XLA Ops:
  7.2 1.6 shard_map.95
  8.9 12.1 %all_to_all.75 = bf16[4,8,3072]{2,1,0:T(8,128)(2,1)S(1)} all-to-all(bf16[4,8,3072]{2,1,0:T(8,128)(2,1)} %get-tuple-element.18), channel_id=1, replica_groups=mesh['z'=4,'y'=4,'c'=2,'w'=4,'x'=4] {'z'}, dimensions={0} | all-to-all | bytes 393216 | tf_op jit(solution)/shard_map/all_to_all | solution.py:357
  21.0 1.0 tile.9
  22.0 4.5 %all-to-all-start.1 = ((bf16[4,32,3072]{2,1,0:T(8,128)(2,1)}), bf16[4,32,3072]{2,1,0:T(8,128)(2,1)}, u32[]{:S(2)}, u32[]{:S(2)}) async-start(bf16[4,32,3072]{2,1,0:T(8,128)(2,1)} %tile.9), calls=%async_computation.1 | async-start | bytes 1572864 | tf_op jit(solution)/shard_map/all_to_all | solution.py:358
  26.5 2.3 %copy.10 = bf16[4,4,256,128]{3,2,1,0:T(8,128)(2,1)} copy(bf16[4,4,256,128]{3,2,0,1:T(8,128)(2,1)} %bitcast.44) | data formatting | bytes 2097152 | tf_op jit(solution)/shard_map/transpose | solution.py:379
  28.8 6.2 %all-to-all-done.1 = bf16[4,32,3072]{2,1,0:T(8,128)(2,1)} async-done(((bf16[4,32,3072]{2,1,0:T(8,128)(2,1)}), bf16[4,32,3072]{2,1,0:T(8,128)(2,1)}, u32[]{:S(2)}, u32[]{:S(2)}) %all-to-all-start.1) | async-done | bytes 786464 | tf_op jit(solution)/shard_map/all_to_all | solution.py:358
  34.9 10.2 %collective-permute-start = (bf16[128,3072]{1,0:T(8,128)(2,1)}, bf16[128,3072]{1,0:T(8,128)(2,1)}, u32[]{:S(2)}, u32[]{:S(2)}) collective-permute-start(bf16[128,3072]{1,0:T(8,128)(2,1)} %bitcast.8.xa.xa_hbm), channel_id=1, source_target_pairs={{0,16},{16,0},{1,17},{17,1},{2,18},{18,2},{3,19},{19,3},{4,20},{20... | collective-permute-start | bytes 2359304 | tf_op jit(solution)/shard_map/ppermute | solution.py:362
  45.1 4.3 %all-to-all-start.2 = ((bf16[4,1024,128]{2,1,0:T(8,128)(2,1)}), bf16[4,1024,128]{2,1,0:T(8,128)(2,1)}, u32[]{:S(2)}, u32[]{:S(2)}) async-start(bf16[4,1024,128]{2,1,0:T(8,128)(2,1)} %bitcast.43), calls=%async_computation.2 | async-start | bytes 2097152 | tf_op jit(solution)/shard_map/all_to_all | solution.py:381
  49.4 0.1 pad_add_fusion.meta
  49.5 4.0 %shard_map.96 = (bf16[4,192,128]{2,1,0:T(8,128)(2,1)S(1)}, bf16[192,128]{1,0:T(8,128)(2,1)S(1)}) custom-call(s32[4]{0:T(128)S(1)} %pad_add_fusion.meta, bf16[128,3072]{1,0:T(8,128)(2,1)} %bitcast.8.xa.xa_hbm, bf16[128,3072]{1,0:T(8,128)(2,1)} %collective-permute-done.xb.xb_hbm, bf16[32,128,384]{2,1,0:T(8,128)(2,1)S(1)} %bitcast.29, ...), custom_call_target="tpu_custom_call" | custom-call | tf_op jit(solution)/shard_map/pallas_call | solution.py:62
  53.5 15.6 %all-to-all-done.2 = bf16[4,1024,128]{2,1,0:T(8,128)(2,1)} async-done(((bf16[4,1024,128]{2,1,0:T(8,128)(2,1)}), bf16[4,1024,128]{2,1,0:T(8,128)(2,1)}, u32[]{:S(2)}, u32[]{:S(2)}) %all-to-all-start.2) | async-done | bytes 1048608 | tf_op jit(solution)/shard_map/all_to_all | solution.py:381
  69.1 10.5 %all_to_all.76.own = bf16[4,192,128]{2,1,0:T(8,128)(2,1)S(1)} all-to-all(bf16[4,192,128]{2,1,0:T(8,128)(2,1)S(1)} %get-tuple-element.22), channel_id=1, replica_groups=mesh['z'=4,'y'=4,'c'=2,'w'=4,'x'=4] {'z'}, dimensions={0} | all-to-all | bytes 393216 | tf_op jit(solution)/shard_map/all_to_all | solution.py:389
  79.6 5.0 %collective-permute-start.1 = (bf16[768,128]{1,0:T(8,128)(2,1)S(1)}, bf16[768,128]{1,0:T(8,128)(2,1)S(1)}, u32[]{:S(2)}, u32[]{:S(2)}) collective-permute-start(bf16[768,128]{1,0:T(8,128)(2,1)S(1)} %bitcast.35), channel_id=1, source_target_pairs={{0,16},{16,0},{1,17},{17,1},{2,18},{18,2},{3,19},{19,3},{4,20},{20... | collective-permute-start | bytes 589832 | tf_op jit(solution)/shard_map/ppermute | solution.py:362
  84.5 1.0 collective-permute-done.1
  85.6 2.3 %shard_map.97 = f32[4,192,128]{2,1,0:T(8,128)S(1)} custom-call(s32[4]{0:T(128)S(1)} %pad_add_fusion.meta, bf16[4,192,128]{2,1,0:T(8,128)(2,1)S(1)} %all_to_all.76.own, bf16[4,192,128]{2,1,0:T(8,128)(2,1)S(1)} %bitcast.37, bf16[4,8,128,128]{3,2,1,0:T(8,128)(2,1)} %bitcast.15.rows_hbm), custom_call_target="tpu_custom_call" | custom-call | tf_op jit(solution)/shard_map/pallas_call | solution.py:62
  87.9 10.2 %all_to_all.77.parts = f32[4,192,128]{2,1,0:T(8,128)S(1)} all-to-all(f32[4,192,128]{2,1,0:T(8,128)S(1)} %shard_map.97), channel_id=1, replica_groups=mesh['z'=4,'y'=4,'c'=2,'w'=4,'x'=4] {'y'}, dimensions={0} | all-to-all | bytes 786432 | tf_op jit(solution)/shard_map/all_to_all | solution.py:396
  98.1 0.6 shard_map.98
  98.7 8.1 %all_to_all.78 = bf16[4,192,128]{2,1,0:T(8,128)(2,1)S(1)} all-to-all(bf16[4,192,128]{2,1,0:T(8,128)(2,1)S(1)} %get-tuple-element.25.after), channel_id=1, replica_groups=mesh['z'=4,'y'=4,'c'=2,'w'=4,'x'=4] {'z'}, dimensions={0} | all-to-all | bytes 393216 | tf_op jit(solution)/shard_map/all_to_all | solution.py:357
  106.8 1.0 tile.21
  107.8 3.5 %all-to-all-start.6 = ((bf16[4,768,128]{2,1,0:T(8,128)(2,1)}), bf16[4,768,128]{2,1,0:T(8,128)(2,1)S(1)}, u32[]{:S(2)}, u32[]{:S(2)}) async-start(bf16[4,768,128]{2,1,0:T(8,128)(2,1)} %tile.21), calls=%async_computation.6 | async-start | bytes 1572864 | tf_op jit(solution)/shard_map/all_to_all | solution.py:358
  111.4 7.2 %shard_map.99 = (bf16[32,192,128]{2,1,0:T(8,128)(2,1)}, f32[192,128]{1,0:T(8,128)}) custom-call(s32[4]{0:T(128)} %copy-done.7, bf16[128,3072]{1,0:T(8,128)(2,1)} %bitcast.8.xa.xa_hbm, bf16[128,3072]{1,0:T(8,128)(2,1)} %collective-permute-done.xb.xb_hbm, bf16[256,6144]{1,0:T(8,128)(2,1)} %all-gather.2.cloned.1.call-done.packed_hbm, ...), custom_call_target="tpu_custom_call" | custom-call | tf_op jit(solution)/shard_map/pallas_call | solution.py:62
  118.6 1.8 all-to-all-done.6
  120.4 6.0 %collective-permute-start.2 = (bf16[3072,128]{1,0:T(8,128)(2,1)S(1)}, bf16[3072,128]{1,0:T(8,128)(2,1)S(1)}, u32[]{:S(2)}, u32[]{:S(2)}) collective-permute-start(bf16[3072,128]{1,0:T(8,128)(2,1)S(1)} %bitcast.30), channel_id=1, source_target_pairs={{0,16},{16,0},{1,17},{17,1},{2,18},{18,2},{3,19},{19,3},{4,20},{20... | collective-permute-start | bytes 2359304 | tf_op jit(solution)/shard_map/ppermute | solution.py:362
  126.4 1.9 %collective-permute-done.2 = bf16[3072,128]{1,0:T(8,128)(2,1)S(1)} collective-permute-done((bf16[3072,128]{1,0:T(8,128)(2,1)S(1)}, bf16[3072,128]{1,0:T(8,128)(2,1)S(1)}, u32[]{:S(2)}, u32[]{:S(2)}) %collective-permute-start.2) | collective-permute-done | bytes 786464 | tf_op jit(solution)/shard_map/ppermute | solution.py:362
  128.4 0.9 copy-done.5
  129.2 5.7 %shard_map.100 = bf16[4,384,128]{2,1,0:T(8,128)(2,1)S(1)} custom-call(s32[4]{0:T(128)S(1)} %copy-done.8, bf16[16,192,128]{2,1,0:T(8,128)(2,1)S(1)} %bitcast.31, bf16[16,192,128]{2,1,0:T(8,128)(2,1)S(1)} %bitcast.34, bf16[32,192,128]{2,1,0:T(8,128)(2,1)} %get-tuple-element.29.probe.probe_hbm, bf16[32,128,384]{2,1,0:T(8,128)(2,1)} %bitcast.28, ...), custom_call_target="tpu_custom_call" | custom-call | tf_op jit(solution)/shard_map/pallas_call | solution.py:62
  135.0 15.3 %all_to_all.79.own = bf16[4,384,128]{2,1,0:T(8,128)(2,1)S(1)} all-to-all(bf16[4,384,128]{2,1,0:T(8,128)(2,1)S(1)} %shard_map.100), channel_id=1, replica_groups=mesh['z'=4,'y'=4,'c'=2,'w'=4,'x'=4] {'z'}, dimensions={0} | all-to-all | bytes 786432 | tf_op jit(solution)/shard_map/all_to_all | solution.py:419
  150.2 3.3 %collective-permute-start.3 = (bf16[1536,128]{1,0:T(8,128)(2,1)S(1)}, bf16[1536,128]{1,0:T(8,128)(2,1)S(1)}, u32[]{:S(2)}, u32[]{:S(2)}) collective-permute-start(bf16[1536,128]{1,0:T(8,128)(2,1)S(1)} %bitcast.32), channel_id=1, source_target_pairs={{0,16},{16,0},{1,17},{17,1},{2,18},{18,2},{3,19},{19,3},{4,20},{20... | collective-permute-start | bytes 1179656 | tf_op jit(solution)/shard_map/ppermute | solution.py:362
  153.5 1.3 collective-permute-done.3
  154.9 4.0 %shard_map.101 = bf16[256,512]{1,0:T(8,128)(2,1)S(1)} custom-call(s32[4]{0:T(128)S(1)} %copy-done.8, bf16[4,384,128]{2,1,0:T(8,128)(2,1)S(1)} %all_to_all.79.own, bf16[4,384,128]{2,1,0:T(8,128)(2,1)S(1)} %bitcast.36, bf16[4,8,128,128]{3,2,1,0:T(8,128)(2,1)} %bitcast.15.rows_hbm, f32[32,1,128]{2,1,0:T(1,128)S(1)} %bitcast.42, ...), custom_call_target="tpu_custom_call" | custom-call | tf_op jit(solution)/shard_map/pallas_call | solution.py:62
  158.9 14.8 %all_to_all.80.got = bf16[32,8,512]{2,1,0:T(8,128)(2,1)S(1)} all-to-all(bf16[32,8,512]{2,1,0:T(8,128)(2,1)S(1)} %bitcast.33), channel_id=1, replica_groups=mesh['z'=4,'y'=4,'c'=2,'w'=4,'x'=4] {'z','y','c'}, dimensions={0} | all-to-all | bytes 524288 | tf_op jit(solution)/shard_map/all_to_all | solution.py:431
  173.7 0.7 shard_map.102
  (29 shorter events, 0.1 us)
Async XLA Ops:
  7.2 104.2 %all-gather.2.cloned.1.call-start = ((), (), s32[]{:S(2)}) async-start(), calls=%async_computation.9 | async-start | bytes 3244032 | tf_op jit(solution)/shard_map/all_gather | solution.py:377
  21.9 27.6 %copy-start = (bf16[1,4096,384]{2,1,0:T(8,128)(2,1)S(1)}, bf16[1,4096,384]{2,1,0:T(8,128)(2,1)}, u32[]{:S(2)}) copy-start(bf16[1,4096,384]{2,1,0:T(8,128)(2,1)} %param.11) | copy-start | bytes 9437188
  21.9 27.6 %copy-start.3 = (f32[4096]{0:T(1024)S(1)}, f32[4096]{0:T(1024)}, u32[]{:S(2)}) copy-start(f32[4096]{0:T(1024)} %param.10) | copy-start | bytes 49156
  21.9 27.6 %copy-start.9 = (f32[1,128]{1,0:T(1,128)S(1)}, f32[1,128]{1,0:T(1,128)}, u32[]{:S(2)}) copy-start(f32[1,128]{1,0:T(1,128)} %q_gain.5) | copy-start | bytes 1540
  22.0 27.6 %copy-start.11 = (f32[1,128]{1,0:T(1,128)S(1)}, f32[1,128]{1,0:T(1,128)}, u32[]{:S(2)}) copy-start(f32[1,128]{1,0:T(1,128)} %k_gain.5) | copy-start | bytes 1540
  22.0 13.0 %all-to-all-start.1 = ((bf16[4,32,3072]{2,1,0:T(8,128)(2,1)}), bf16[4,32,3072]{2,1,0:T(8,128)(2,1)}, u32[]{:S(2)}, u32[]{:S(2)}) async-start(bf16[4,32,3072]{2,1,0:T(8,128)(2,1)} %tile.9), calls=%async_computation.1 | async-start | bytes 1572864 | tf_op jit(solution)/shard_map/all_to_all | solution.py:358
  34.9 14.6 %collective-permute-start = (bf16[128,3072]{1,0:T(8,128)(2,1)}, bf16[128,3072]{1,0:T(8,128)(2,1)}, u32[]{:S(2)}, u32[]{:S(2)}) collective-permute-start(bf16[128,3072]{1,0:T(8,128)(2,1)} %bitcast.8.xa.xa_hbm), channel_id=1, source_target_pairs={{0,16},{16,0},{1,17},{17,1},{2,18},{18,2},{3,19},{19,3},{4,20},{20... | collective-permute-start | bytes 2359304 | tf_op jit(solution)/shard_map/ppermute | solution.py:362
  45.1 23.9 %all-to-all-start.2 = ((bf16[4,1024,128]{2,1,0:T(8,128)(2,1)}), bf16[4,1024,128]{2,1,0:T(8,128)(2,1)}, u32[]{:S(2)}, u32[]{:S(2)}) async-start(bf16[4,1024,128]{2,1,0:T(8,128)(2,1)} %bitcast.43), calls=%async_computation.2 | async-start | bytes 2097152 | tf_op jit(solution)/shard_map/all_to_all | solution.py:381
  49.5 48.6 %copy-start.7 = (s32[4]{0:T(128)}, s32[4]{0:T(128)S(1)}, u32[]{:S(2)}) copy-start(s32[4]{0:T(128)S(1)} %pad_add_fusion.meta) | copy-start | bytes 52
  49.5 48.6 %copy-start.6 = (f32[4096]{0:T(1024)S(1)}, f32[4096]{0:T(1024)}, u32[]{:S(2)}) copy-start(f32[4096]{0:T(1024)} %param.15) | copy-start | bytes 49156
  79.6 6.0 %collective-permute-start.1 = (bf16[768,128]{1,0:T(8,128)(2,1)S(1)}, bf16[768,128]{1,0:T(8,128)(2,1)S(1)}, u32[]{:S(2)}, u32[]{:S(2)}) collective-permute-start(bf16[768,128]{1,0:T(8,128)(2,1)S(1)} %bitcast.35), channel_id=1, source_target_pairs={{0,16},{16,0},{1,17},{17,1},{2,18},{18,2},{3,19},{19,3},{4,20},{20... | collective-permute-start | bytes 589832 | tf_op jit(solution)/shard_map/ppermute | solution.py:362
  98.7 12.7 %copy-start.1 = (bf16[4,192,128]{2,1,0:T(8,128)(2,1)}, bf16[4,192,128]{2,1,0:T(8,128)(2,1)S(1)}, u32[]{:S(2)}) copy-start(bf16[4,192,128]{2,1,0:T(8,128)(2,1)S(1)} %get-tuple-element.25.after) | copy-start | bytes 589828
  107.8 12.6 %all-to-all-start.6 = ((bf16[4,768,128]{2,1,0:T(8,128)(2,1)}), bf16[4,768,128]{2,1,0:T(8,128)(2,1)S(1)}, u32[]{:S(2)}, u32[]{:S(2)}) async-start(bf16[4,768,128]{2,1,0:T(8,128)(2,1)} %tile.21), calls=%async_computation.6 | async-start | bytes 1572864 | tf_op jit(solution)/shard_map/all_to_all | solution.py:358
  111.3 17.0 %copy-start.4 = (f32[4096]{0:T(1024)S(1)}, f32[4096]{0:T(1024)}, u32[]{:S(2)}) copy-start(f32[4096]{0:T(1024)} %param.10) | copy-start | bytes 49156
  111.3 17.0 %copy-start.8 = (s32[4]{0:T(128)S(1)}, s32[4]{0:T(128)}, u32[]{:S(2)}) copy-start(s32[4]{0:T(128)} %copy-done.7) | copy-start | bytes 52
  111.4 17.0 %copy-start.10 = (f32[1,128]{1,0:T(1,128)S(1)}, f32[1,128]{1,0:T(1,128)}, u32[]{:S(2)}) copy-start(f32[1,128]{1,0:T(1,128)} %q_gain.5) | copy-start | bytes 1540
  111.4 17.0 %copy-start.12 = (f32[1,128]{1,0:T(1,128)S(1)}, f32[1,128]{1,0:T(1,128)}, u32[]{:S(2)}) copy-start(f32[1,128]{1,0:T(1,128)} %k_gain.5) | copy-start | bytes 1540
  120.4 7.9 %collective-permute-start.2 = (bf16[3072,128]{1,0:T(8,128)(2,1)S(1)}, bf16[3072,128]{1,0:T(8,128)(2,1)S(1)}, u32[]{:S(2)}, u32[]{:S(2)}) collective-permute-start(bf16[3072,128]{1,0:T(8,128)(2,1)S(1)} %bitcast.30), channel_id=1, source_target_pairs={{0,16},{16,0},{1,17},{17,1},{2,18},{18,2},{3,19},{19,3},{4,20},{20... | collective-permute-start | bytes 2359304 | tf_op jit(solution)/shard_map/ppermute | solution.py:362
  128.3 0.9 copy-start.5
  134.9 38.7 %copy-start.2 = (bf16[6,4096]{1,0:T(8,128)(2,1)S(1)}, bf16[6,4096]{1,0:T(8,128)(2,1)}, u32[]{:S(2)}) copy-start(bf16[6,4096]{1,0:T(8,128)(2,1)} %state.1) | copy-start | bytes 147460
  150.2 4.6 %collective-permute-start.3 = (bf16[1536,128]{1,0:T(8,128)(2,1)S(1)}, bf16[1536,128]{1,0:T(8,128)(2,1)S(1)}, u32[]{:S(2)}, u32[]{:S(2)}) collective-permute-start(bf16[1536,128]{1,0:T(8,128)(2,1)S(1)} %bitcast.32), channel_id=1, source_target_pairs={{0,16},{16,0},{1,17},{17,1},{2,18},{18,2},{3,19},{19,3},{4,20},{20... | collective-permute-start | bytes 1179656 | tf_op jit(solution)/shard_map/ppermute | solution.py:362
Sparse Core Ops, SparseCore 0:
  10.1 80.8 all-gather.1

commit v7 on v6

--- a/solution.py
+++ b/solution.py
@@ -49,7 +49,7 @@
     return copies
 
 
-def call(kernel, out_shape, n_scalar, *args, scratch=(), vmem_mib=20):
+def call(kernel, out_shape, n_scalar, *args, scratch=(), vmem_mib=20, n_hbm=0):
     in_specs = [pl.BlockSpec(memory_space=pltpu.SMEM)] * n_scalar
     for a in args[n_scalar:]:
         if isinstance(a, tuple):
@@ -59,11 +59,12 @@
     flat = [a[0] if isinstance(a, tuple) else a for a in args]
     multi = isinstance(out_shape, (tuple, list))
     vmem = pl.BlockSpec(memory_space=pltpu.VMEM)
+    hbm = pl.BlockSpec(memory_space=pltpu.HBM)
     return pl.pallas_call(
         kernel,
         out_shape=out_shape,
         in_specs=in_specs,
-        out_specs=[vmem] * len(out_shape) if multi else vmem,
+        out_specs=[vmem] * (len(out_shape) - n_hbm) + [hbm] * n_hbm if multi else vmem,
         scratch_shapes=scratch,
         compiler_params=pltpu.CompilerParams(vmem_limit_bytes=vmem_mib * 1024 * 1024),
     )(*flat)
@@ -131,8 +132,11 @@
     return dot(probs, val).astype(BF), dot(d_probs.astype(BF), val) + dot(probs, dv)
 
 
-def pack_kernel(state_hbm, probe_hbm, state_ref, probe_ref, state, probe, sem):
-    copies = fetch(sem, (state_hbm, state), (probe_hbm, probe))
+def pack_kernel(
+    meta, state_hbm, probe_hbm, out_map, state_ref, probe_ref, s0, s1, s2, s3, state, probe, sem
+):
+    shifted = [(out_map.at[:, (meta[2] + k) & 3], to) for k, to in enumerate((s0, s1, s2, s3))]
+    copies = fetch(sem, (state_hbm, state), (probe_hbm, probe), *shifted)
     for i, (source, write) in enumerate(((state, None), (probe, probe_ref))):
         copies[i].wait()
         main = source[:, :3072]
@@ -145,6 +149,8 @@
         else:
             write[:, :3072] = whole
             write[:, 3072:] = whole
+    for copy in copies[2:]:
+        copy.wait()
 
 
 def core_order(core):
@@ -203,6 +209,9 @@
                 yield side, y * 4 + z, z * 8 + y * 2 + c
 
 
+SHIFTS = (0, 1, 3, 2)
+
+
 def plane_products(core, own, oth, rows):
     left = []
     for z in range(4):
@@ -210,19 +219,21 @@
         first = jnp.where(core == 0, mine, other)
         second = jnp.where(core == 0, other, mine)
         left.append(jnp.concatenate([first, second], axis=1))
-    for y in range(4):
+    for i in range(4):
         mapped = None
         for z in range(4):
-            right = jnp.concatenate([rows[y, z * 2], rows[y, z * 2 + 1]], axis=0)
+            right = jnp.concatenate([rows[i, z * 2], rows[i, z * 2 + 1]], axis=0)
             part = dot(left[z], right)
             mapped = part if mapped is None else mapped + part
-        yield y, mapped
-
-
-def plane_kernel(meta, own, oth, rows_hbm, part_ref, rows, sem):
-    fetch(sem, (rows_hbm, rows))[0].wait()
-    for y, mapped in plane_products(meta[0], own, oth, rows):
-        part_ref[y] = mapped
+        yield i, mapped
+
+
+def plane_kernel(meta, own, oth, r0, r1, r2, r3, part_ref, rows, sem):
+    copies = fetch(sem, *[(r, rows.at[i]) for i, r in enumerate((r0, r1, r2, r3))])
+    for copy in copies:
+        copy.wait()
+    for i, mapped in plane_products(meta[0], own, oth, rows):
+        part_ref[(meta[2] - SHIFTS[i]) & 3] = mapped
 
 
 def middle_kernel(meta, parts, gates, col, vel_ref, mid_ref):
@@ -303,10 +314,18 @@
         both_ref[i, TOK:] = d_both
 
 
-def last_kernel(meta, own, oth, rows_hbm, gates, vel_hbm, probe_hbm, out_ref, rows, vel1, probe, sem):
-    core, plane, slab = meta[0], meta[2], meta[3]
-    columns = [(probe_hbm.at[slab * 8 + y * 2 + core], probe.at[y]) for y in range(4)]
-    copies = fetch(sem, (rows_hbm, rows), (vel_hbm, vel1), *columns)
+def last_kernel(
+    meta, own, oth, r0, r1, r2, r3, gates, vel_hbm, probe_hbm, out_ref, rows, vel1, probe, sem
+):
+    core, slab = meta[0], meta[3]
+    place_y = [(meta[2] - shift) & 3 for shift in SHIFTS]
+    columns = [slab * 8 + y * 2 + core for y in place_y]
+    copies = fetch(
+        sem,
+        *[(r, rows.at[i]) for i, r in enumerate((r0, r1, r2, r3))],
+        (vel_hbm, vel1),
+        *[(probe_hbm.at[column], probe.at[i]) for i, column in enumerate(columns)],
+    )
     row = lax.broadcasted_iota(jnp.int32, (256, TOK), 0)
     token = lax.broadcasted_iota(jnp.int32, (256, TOK), 1)
     hit = (token == (row >> 3) * 6 + (row & 7)) & ((row & 7) < 6)
@@ -315,13 +334,13 @@
         copy.wait()
     trace = jnp.zeros((1, 128), F32)
     laid = []
-    for y, mapped in plane_products(core, own, oth, rows):
-        column = slab * 8 + y * 2 + core
-        mapped = mapped * gates[column]
-        terms = mapped[TOK:] * probe[y].astype(F32)
+    for i, mapped in plane_products(core, own, oth, rows):
+        mapped = mapped * gates[columns[i]]
+        terms = mapped[TOK:] * probe[i].astype(F32)
         trace = trace + jnp.sum(terms, axis=0, keepdims=True)
-        vel = vel1[...].astype(F32)
-        part = mapped[:TOK] + jnp.where(plane == y, vel, jnp.zeros_like(vel))
+        part = mapped[:TOK]
+        if i == 0:
+            part = part + vel1[...].astype(F32)
         laid.append(dot(lay, part.astype(BF)))
     trace = row_sum(trace)
     high = trace.astype(BF).astype(F32)
@@ -330,20 +349,20 @@
     lane = lax.broadcasted_iota(jnp.int32, (1, 128), 1)
     coded = jnp.where(lane == 0, high, jnp.where(lane == 1, mid, jnp.where(lane == 2, low, 0.0)))
     slot = lax.broadcasted_iota(jnp.int32, (256, 128), 0) & 7
-    for y in range(4):
-        block = jnp.where(slot == 6, coded, laid[y]) if y == 0 else laid[y]
-        out_ref[:, y * 128 : (y + 1) * 128] = block.astype(BF)
+    for i in range(4):
+        block = jnp.where(slot == 6, coded, laid[i]) if i == 0 else laid[i]
+        out_ref[:, pl.ds(pl.multiple_of(place_y[i] * 128, 128), 128)] = block.astype(BF)
 
 
 def land_kernel(got, state, next_ref, change_ref):
-    total = jnp.zeros((8, 128), F32)
+    total = jnp.zeros((8, 512), F32)
     for z in range(4):
         for c in range(2):
             sums = jnp.zeros((8, 512), F32)
             for y in range(4):
                 block = got[z * 8 + y * 2 + c].astype(F32)
-                total = total + block[:, :128]
                 sums = sums + block
+            total = total + sums
             for y in range(4):
                 j = z * 8 + y * 2 + c
                 cols = slice(j * 128, (j + 1) * 128)
@@ -370,28 +389,29 @@
     maps = head_maps.reshape(32, 128, 384)
     gain = norm_gain.reshape(32, 1, 128)
 
-    packed_state, packed_probe = call(
-        pack_kernel, [shape((4, 8, 3072)), shape((8, 6144))], 0, (state,), (probe,),
-        scratch=[pltpu.VMEM((6, 4096), BF), pltpu.VMEM((6, 4096), BF), sems(2)], vmem_mib=FULL,
+    packed_state, packed_probe, *sends = call(
+        pack_kernel, [shape((4, 8, 3072)), shape((8, 6144))] + [shape((4, 256, 128))] * 4,
+        1, meta, (state,), (probe,), (out_map.reshape(4, 4, 256, 128),),
+        scratch=[pltpu.VMEM((6, 4096), BF), pltpu.VMEM((6, 4096), BF), sems(6)],
+        vmem_mib=FULL, n_hbm=4,
     )
     probe_all = lax.all_gather(packed_probe, SEQ, axis=0, tiled=True)
     _, own = spread(packed_state)
-    by_plane = out_map.reshape(4, 4, 256, 128).transpose(1, 0, 2, 3).reshape(4096, 128)
-    by_plane, own = lax.optimization_barrier((by_plane, own))
-    plane_outs = lax.all_to_all(by_plane, "y", 0, 0, tiled=True)
+    plane_outs = [sends[0]]
+    for k in (1, 3, 2):
+        plane_outs.append(lax.ppermute(sends[k], "y", [(y, (y + k) % 4) for y in range(4)]))
+    plane_outs = [(piece.reshape(8, 128, 128),) for piece in plane_outs]
     oth = swap(own)
     att1, col = call(
         first_kernel, [shape((4, TOK, 128)), shape((TOK, 128))],
-        1, meta, own, oth, (maps,), gain, query_gain, key_gain, scratch=[HELD, MAPS, sems(1)],
-    )
-    att1, plane_outs = lax.optimization_barrier((att1, plane_outs))
-    plane_outs = plane_outs.reshape(4, 8, 128, 128)
+        1, meta, own, oth, (maps,), gain, query_gain, key_gain, scratch=[HELD, MAPS, sems(1)], vmem_mib=51,
+    )
     own1 = lax.all_to_all(att1.reshape(4 * TOK, 128), "z", 0, 0, tiled=True)
     oth1 = swap(own1)
     parts = call(
         plane_kernel, shape((4, TOK, 128), F32),
-        1, meta, own1.reshape(4, TOK, 128), oth1.reshape(4, TOK, 128), (plane_outs,),
-        scratch=[ROWS, sems(1)], vmem_mib=MIDDLE,
+        1, meta, own1.reshape(4, TOK, 128), oth1.reshape(4, TOK, 128), *plane_outs,
+        scratch=[ROWS, sems(4)], vmem_mib=MIDDLE,
     )
     parts = lax.all_to_all(parts.reshape(4 * TOK, 128), "y", 0, 0, tiled=True)
     vel1, mid = call(
@@ -421,10 +441,10 @@
     columns = call(
         last_kernel, shape((256, 512)),
         1, meta, own2.reshape(4, 2 * TOK, 128), oth2.reshape(4, 2 * TOK, 128),
-        (plane_outs,), gates, (vel1,), (probe_blocks,),
+        *plane_outs, gates, (vel1,), (probe_blocks,),
         scratch=[
             ROWS, pltpu.VMEM((TOK, 128), BF),
-            pltpu.VMEM((4, TOK, 128), BF), sems(6),
+            pltpu.VMEM((4, TOK, 128), BF), sems(9),
         ],
         vmem_mib=LAST,
     )

time: 182 us -> 205 us (1.13)
  Pallas kernels: 26.1 us -> 58.7 us
  waiting for transfers between devices: 27.8 us -> 15 us
  blocking collectives: 70.9 us -> 74.8 us
  local copies, waits for them, and re-layouts: 5.24 us -> 2.01 us
    pallas_call x8, Pallas kernels: 26.1 us -> 58.7 us  [call(): pl.pallas_call(kernel, out_shape=out_shape, in_specs=in_specs, out_specs=...]
    all_to_all x1, waiting for transfers between devices: 15.6 us -> 0.01 us  [per_device(): own1 = lax.all_to_all(att1.reshape(4 * TOK, 128), 'z', 0, 0, tiled=True)]
    ppermute x0 -> x3, waiting for transfers between devices: none -> 8.79 us  [per_device(): lax.ppermute(sends[k], 'y', [(y, (y + k) % 4) for y in range(4)])]
    ppermute x0 -> x3, starting transfers between devices: none -> 8.53 us  [per_device(): lax.ppermute(sends[k], 'y', [(y, (y + k) % 4) for y in range(4)])]
    all_to_all x2 -> x1, waiting for transfers between devices: 7.96 us -> 1.05 us  [spread(): return (a, lax.all_to_all(jnp.tile(a, (4, 1)), 'y', 0, 0, tiled=True))]
    all_to_all x2 -> x1, starting transfers between devices: 8.01 us -> 3.49 us  [spread(): return (a, lax.all_to_all(jnp.tile(a, (4, 1)), 'y', 0, 0, tiled=True))]
    all_to_all x1, blocking collectives: 10.5 us -> 13.2 us  [spread(): return (a, lax.all_to_all(jnp.tile(a, (4, 1)), 'y', 0, 0, tiled=True))]
    all_to_all x1, blocking collectives: 10.2 us -> 12.7 us  [per_device(): parts = lax.all_to_all(parts.reshape(4 * TOK, 128), 'y', 0, 0, tiled=True)]
  transfers between devices with their start and end apart: 8 -> 10, of which waited for: 6 -> 6; matrix products, arithmetic and copies ran while one was open for 2% -> 1% of each run, Pallas kernels for 8% -> 7%
where the time goes in v7:
time: 205 us; the launch traced here: 204 us
  blocking collectives  74.8 us (36%)
  Pallas kernels  58.7 us (29%)
  starting transfers between devices  38.1 us (19%)
  waiting for transfers between devices  15 us (7%)
  between operations  14.4 us (7%)
    pallas_call x8, Pallas kernels, call(): pl.pallas_call(kernel, out_shape=out_shape, in_specs=in_specs, out_specs=...  58.7 us
    ppermute x4, starting transfers between devices, swap(): return lax.ppermute(block, 'c', [(0, 1), (1, 0)])  22.5 us
    all_to_all x2, blocking collectives, spread(): a = lax.all_to_all(copies.reshape(n * rows, lanes), 'z', 0, 0, tiled=True)  20.1 us
    all_to_all x1, blocking collectives, per_device(): got = lax.all_to_all(columns, SEQ, 0, 0, tiled=True).reshape(32, 8, 512)  14.9 us
    all_to_all x1, blocking collectives, per_device(): own2 = lax.all_to_all(both.reshape(8 * TOK, 128), 'z', 0, 0, tiled=True)  13.9 us
    all_to_all x1, blocking collectives, spread(): return (a, lax.all_to_all(jnp.tile(a, (4, 1)), 'y', 0, 0, tiled=True))  13.2 us
    all_to_all x1, blocking collectives, per_device(): parts = lax.all_to_all(parts.reshape(4 * TOK, 128), 'y', 0, 0, tiled=True)  12.7 us
    ppermute x3, waiting for transfers between devices, per_device(): lax.ppermute(sends[k], 'y', [(y, (y + k) % 4) for y in range(4)])  8.79 us
  transfers between devices with their start and end apart: 10, of which 6 were waited for; matrix products, arithmetic and copies ran while one was open for 1% of the time, Pallas kernels for 7%

profile of v7, /device:TPU:1, one launch (start us, length us, event | category | flops | bytes accessed | tf_op | source)
XLA Modules:
  0.0 203.6 jit_solution(11595352019687157140)
XLA Ops:
  7.3 0.7 pad_add_fusion.meta
  7.9 34.4 %shard_map.95 = (bf16[4,8,3072]{2,1,0:T(8,128)(2,1)}, bf16[8,6144]{1,0:T(8,128)(2,1)}, bf16[4,256,128]{2,1,0:T(8,128)(2,1)}, bf16[4,256,128]{2,1,0:T(8,128)(2,1)...) custom-call(s32[4]{0:T(128)} %pad_add_fusion.meta, bf16[6,4096]{1,0:T(8,128)(2,1)} %state.1, ...), custom_call_target="tpu_custom_call" | custom-call | tf_op jit(solution)/shard_map/pallas_call | solution.py:63
  42.4 12.1 %all_to_all.62 = bf16[4,8,3072]{2,1,0:T(8,128)(2,1)S(1)} all-to-all(bf16[4,8,3072]{2,1,0:T(8,128)(2,1)} %get-tuple-element.18), channel_id=1, replica_groups=mesh['z'=4,'y'=4,'c'=2,'w'=4,'x'=4] {'z'}, dimensions={0} | all-to-all | bytes 393216 | tf_op jit(solution)/shard_map/all_to_all | solution.py:376
  54.6 13.2 %all_to_all.63 = bf16[4,32,3072]{2,1,0:T(8,128)(2,1)S(1)} all-to-all(bf16[4,32,3072]{2,1,0:T(8,128)(2,1)S(1)} %tile.9), channel_id=1, replica_groups=mesh['z'=4,'y'=4,'c'=2,'w'=4,'x'=4] {'y'}, dimensions={0} | all-to-all | bytes 1572864 | tf_op jit(solution)/shard_map/all_to_all | solution.py:377
  67.8 8.3 %collective-permute-start = (bf16[128,3072]{1,0:T(8,128)(2,1)S(1)}, bf16[128,3072]{1,0:T(8,128)(2,1)S(1)}, u32[]{:S(2)}, u32[]{:S(2)}) collective-permute-start(bf16[128,3072]{1,0:T(8,128)(2,1)S(1)} %bitcast.25), channel_id=1, source_target_pairs={{0,16},{16,0},{1,17},{17,1},{2,18},{18,2},{3,19},{19,3},{4,20},{20... | collective-permute-start | bytes 2359304 | tf_op jit(solution)/shard_map/ppermute | solution.py:381
  76.2 1.9 collective-permute-done.xb.xb_hbm
  78.1 5.1 %shard_map.96 = (bf16[4,192,128]{2,1,0:T(8,128)(2,1)}, bf16[192,128]{1,0:T(8,128)(2,1)S(1)}) custom-call(s32[4]{0:T(128)S(1)} %copy-done.9, bf16[128,3072]{1,0:T(8,128)(2,1)S(1)} %bitcast.26, bf16[128,3072]{1,0:T(8,128)(2,1)S(1)} %collective-permute-done.xb.xb_hbm, bf16[32,128,384]{2,1,0:T(8,128)(2,1)} %bitcast.49, f32[32,1,128]{2,1,0:T(1,128)S(1)} %bitcast.45, ...), custom_call_target="tpu_custom_call" | custom-call | tf_op jit(solution)/shard_map/pallas_call | solution.py:63
  83.2 3.5 %all-to-all-start.2 = ((bf16[4,192,128]{2,1,0:T(8,128)(2,1)}), bf16[4,192,128]{2,1,0:T(8,128)(2,1)S(1)}, u32[]{:S(2)}, u32[]{:S(2)}) async-start(bf16[4,192,128]{2,1,0:T(8,128)(2,1)} %get-tuple-element.19), calls=%async_computation.2 | async-start | bytes 393216 | tf_op jit(solution)/shard_map/all_to_all | solution.py:409
  86.7 2.9 %collective-permute-start.2 = (bf16[4,256,128]{2,1,0:T(8,128)(2,1)}, bf16[4,256,128]{2,1,0:T(8,128)(2,1)S(1)}, u32[]{:S(2)}, u32[]{:S(2)}) collective-permute-start(bf16[4,256,128]{2,1,0:T(8,128)(2,1)} %get-tuple-element.21), channel_id=1, source_target_pairs={{0,32},{32,64},{64,96},{96,0},{1,33},{33,65},{65,97},{97,1},{2,34}... | collective-permute-start | bytes 786440 | tf_op jit(solution)/shard_map/ppermute | solution.py:402
  89.7 3.6 %collective-permute-start.3 = (bf16[4,256,128]{2,1,0:T(8,128)(2,1)S(1)}, bf16[4,256,128]{2,1,0:T(8,128)(2,1)S(1)}, u32[]{:S(2)}, u32[]{:S(2)}) collective-permute-start(bf16[4,256,128]{2,1,0:T(8,128)(2,1)S(1)} %copy-done.16), channel_id=1, source_target_pairs={{0,96},{32,0},{64,32},{96,64},{1,97},{33,1},{65,33},{97,65},{2,98}... | collective-permute-start | bytes 786440 | tf_op jit(solution)/shard_map/ppermute | solution.py:402
  93.3 2.1 %collective-permute-start.4 = (bf16[4,256,128]{2,1,0:T(8,128)(2,1)S(1)}, bf16[4,256,128]{2,1,0:T(8,128)(2,1)S(1)}, u32[]{:S(2)}, u32[]{:S(2)}) collective-permute-start(bf16[4,256,128]{2,1,0:T(8,128)(2,1)S(1)} %copy-done.15), channel_id=1, source_target_pairs={{0,64},{32,96},{64,0},{96,32},{1,65},{33,97},{65,1},{97,33},{2,66}... | collective-permute-start | bytes 786440 | tf_op jit(solution)/shard_map/ppermute | solution.py:402
  95.3 3.7 %collective-permute-start.1 = (bf16[768,128]{1,0:T(8,128)(2,1)S(1)}, bf16[768,128]{1,0:T(8,128)(2,1)S(1)}, u32[]{:S(2)}, u32[]{:S(2)}) collective-permute-start(bf16[768,128]{1,0:T(8,128)(2,1)S(1)} %bitcast.41), channel_id=1, source_target_pairs={{0,16},{16,0},{1,17},{17,1},{2,18},{18,2},{3,19},{19,3},{4,20},{20... | collective-permute-start | bytes 589832 | tf_op jit(solution)/shard_map/ppermute | solution.py:381
  99.1 2.2 %collective-permute-done.3 = bf16[4,256,128]{2,1,0:T(8,128)(2,1)S(1)} collective-permute-done((bf16[4,256,128]{2,1,0:T(8,128)(2,1)S(1)}, bf16[4,256,128]{2,1,0:T(8,128)(2,1)S(1)}, u32[]{:S(2)}, u32[]{:S(2)}) %collective-permute-start.3) | collective-permute-done | bytes 262176 | tf_op jit(solution)/shard_map/ppermute | solution.py:402
  101.3 6.5 %collective-permute-done.4 = bf16[4,256,128]{2,1,0:T(8,128)(2,1)S(1)} collective-permute-done((bf16[4,256,128]{2,1,0:T(8,128)(2,1)S(1)}, bf16[4,256,128]{2,1,0:T(8,128)(2,1)S(1)}, u32[]{:S(2)}, u32[]{:S(2)}) %collective-permute-start.4) | collective-permute-done | bytes 262176 | tf_op jit(solution)/shard_map/ppermute | solution.py:402
  107.8 1.2 shard_map.97
  109.1 12.7 %all_to_all.64.parts = f32[4,192,128]{2,1,0:T(8,128)S(1)} all-to-all(f32[4,192,128]{2,1,0:T(8,128)S(1)} %shard_map.97), channel_id=1, replica_groups=mesh['z'=4,'y'=4,'c'=2,'w'=4,'x'=4] {'y'}, dimensions={0} | all-to-all | bytes 786432 | tf_op jit(solution)/shard_map/all_to_all | solution.py:416
  121.8 0.6 shard_map.98
  122.4 8.0 %all_to_all.65 = bf16[4,192,128]{2,1,0:T(8,128)(2,1)S(1)} all-to-all(bf16[4,192,128]{2,1,0:T(8,128)(2,1)S(1)} %get-tuple-element.25.after), channel_id=1, replica_groups=mesh['z'=4,'y'=4,'c'=2,'w'=4,'x'=4] {'z'}, dimensions={0} | all-to-all | bytes 393216 | tf_op jit(solution)/shard_map/all_to_all | solution.py:376
  130.4 1.0 tile.21
  131.4 3.5 %all-to-all-start.5 = ((bf16[4,768,128]{2,1,0:T(8,128)(2,1)}), bf16[4,768,128]{2,1,0:T(8,128)(2,1)S(1)}, u32[]{:S(2)}, u32[]{:S(2)}) async-start(bf16[4,768,128]{2,1,0:T(8,128)(2,1)} %tile.21), calls=%async_computation.5 | async-start | bytes 1572864 | tf_op jit(solution)/shard_map/all_to_all | solution.py:377
  134.9 7.2 %shard_map.99 = (bf16[32,192,128]{2,1,0:T(8,128)(2,1)}, f32[192,128]{1,0:T(8,128)}) custom-call(s32[4]{0:T(128)} %pad_add_fusion.meta, bf16[128,3072]{1,0:T(8,128)(2,1)} %bitcast.27, bf16[128,3072]{1,0:T(8,128)(2,1)} %copy-done.1, bf16[256,6144]{1,0:T(8,128)(2,1)} %all-gather.2.cloned.1.call-done.packed_hbm, bf16[32,128,384]{2,1,0:T(8,128)(2,1)} %bitcast.50, ...), custom_call_target="tpu_custom_call" | custom-call | tf_op jit(solution)/shard_map/pallas_call | solution.py:63
  142.1 1.0 all-to-all-done.5
  143.2 7.3 %collective-permute-start.5 = (bf16[3072,128]{1,0:T(8,128)(2,1)S(1)}, bf16[3072,128]{1,0:T(8,128)(2,1)S(1)}, u32[]{:S(2)}, u32[]{:S(2)}) collective-permute-start(bf16[3072,128]{1,0:T(8,128)(2,1)S(1)} %bitcast.28), channel_id=1, source_target_pairs={{0,16},{16,0},{1,17},{17,1},{2,18},{18,2},{3,19},{19,3},{4,20},{20... | collective-permute-start | bytes 2359304 | tf_op jit(solution)/shard_map/ppermute | solution.py:381
  150.5 1.9 collective-permute-done.5
  152.4 0.9 copy-done.7
  153.3 5.7 %shard_map.100 = bf16[4,384,128]{2,1,0:T(8,128)(2,1)S(1)} custom-call(s32[4]{0:T(128)S(1)} %copy-done.10, bf16[16,192,128]{2,1,0:T(8,128)(2,1)S(1)} %bitcast.29, bf16[16,192,128]{2,1,0:T(8,128)(2,1)S(1)} %bitcast.40, bf16[32,192,128]{2,1,0:T(8,128)(2,1)} %get-tuple-element.29.probe.probe_hbm, bf16[32,128,384]{2,1,0:T(8,128)(2,1)} %bitcast.51, ...), custom_call_target="tpu_custom_call" | custom-call | tf_op jit(solution)/shard_map/pallas_call | solution.py:63
  159.0 13.9 %all_to_all.66.own = bf16[4,384,128]{2,1,0:T(8,128)(2,1)S(1)} all-to-all(bf16[4,384,128]{2,1,0:T(8,128)(2,1)S(1)} %shard_map.100), channel_id=1, replica_groups=mesh['z'=4,'y'=4,'c'=2,'w'=4,'x'=4] {'z'}, dimensions={0} | all-to-all | bytes 786432 | tf_op jit(solution)/shard_map/all_to_all | solution.py:439
  172.9 3.1 %collective-permute-start.6 = (bf16[1536,128]{1,0:T(8,128)(2,1)S(1)}, bf16[1536,128]{1,0:T(8,128)(2,1)S(1)}, u32[]{:S(2)}, u32[]{:S(2)}) collective-permute-start(bf16[1536,128]{1,0:T(8,128)(2,1)S(1)} %bitcast.30), channel_id=1, source_target_pairs={{0,16},{16,0},{1,17},{17,1},{2,18},{18,2},{3,19},{19,3},{4,20},{20... | collective-permute-start | bytes 1179656 | tf_op jit(solution)/shard_map/ppermute | solution.py:381
  176.1 1.3 collective-permute-done.6
  177.4 3.8 %shard_map.101 = bf16[256,512]{1,0:T(8,128)(2,1)S(1)} custom-call(s32[4]{0:T(128)S(1)} %copy-done.10, bf16[4,384,128]{2,1,0:T(8,128)(2,1)S(1)} %all_to_all.66.own, bf16[4,384,128]{2,1,0:T(8,128)(2,1)S(1)} %bitcast.42, bf16[8,128,128]{2,1,0:T(8,128)(2,1)S(1)} %bitcast.33, bf16[8,128,128]{2,1,0:T(8,128)(2,1)S(1)} %bitcast.35, ...), custom_call_target="tpu_custom_call" | custom-call | tf_op jit(solution)/shard_map/pallas_call | solution.py:63
  181.2 14.9 %all_to_all.67.got = bf16[32,8,512]{2,1,0:T(8,128)(2,1)S(1)} all-to-all(bf16[32,8,512]{2,1,0:T(8,128)(2,1)S(1)} %bitcast.31), channel_id=1, replica_groups=mesh['z'=4,'y'=4,'c'=2,'w'=4,'x'=4] {'z','y','c'}, dimensions={0} | all-to-all | bytes 524288 | tf_op jit(solution)/shard_map/all_to_all | solution.py:451
  196.1 0.7 shard_map.102
  (40 shorter events, 0.2 us)
Async XLA Ops:
  7.2 70.9 %copy-start.13 = (f32[1,128]{1,0:T(1,128)S(1)}, f32[1,128]{1,0:T(1,128)}, u32[]{:S(2)}) copy-start(f32[1,128]{1,0:T(1,128)} %k_gain.5) | copy-start | bytes 1540
  7.2 70.9 %copy-start.11 = (f32[1,128]{1,0:T(1,128)S(1)}, f32[1,128]{1,0:T(1,128)}, u32[]{:S(2)}) copy-start(f32[1,128]{1,0:T(1,128)} %q_gain.5) | copy-start | bytes 1540
  7.2 70.9 %copy-start.5 = (f32[4096]{0:T(1024)S(1)}, f32[4096]{0:T(1024)}, u32[]{:S(2)}) copy-start(f32[4096]{0:T(1024)} %param.10) | copy-start | bytes 49156
  7.2 127.7 %all-gather.2.cloned.1.call-start = ((), (), s32[]{:S(2)}) async-start(), calls=%async_computation.8 | async-start | bytes 3244032 | tf_op jit(solution)/shard_map/all_gather | solution.py:398
  7.9 70.2 %copy-start.9 = (s32[4]{0:T(128)S(1)}, s32[4]{0:T(128)}, u32[]{:S(2)}) copy-start(s32[4]{0:T(128)} %pad_add_fusion.meta) | copy-start | bytes 52
  54.6 35.1 %copy-start.16 = (bf16[4,256,128]{2,1,0:T(8,128)(2,1)S(1)}, bf16[4,256,128]{2,1,0:T(8,128)(2,1)}, u32[]{:S(2)}) copy-start(bf16[4,256,128]{2,1,0:T(8,128)(2,1)} %get-tuple-element.22) | copy-start | bytes 786436
  54.6 38.7 %copy-start.15 = (bf16[4,256,128]{2,1,0:T(8,128)(2,1)S(1)}, bf16[4,256,128]{2,1,0:T(8,128)(2,1)}, u32[]{:S(2)}) copy-start(bf16[4,256,128]{2,1,0:T(8,128)(2,1)} %get-tuple-element.23) | copy-start | bytes 786436
  54.6 53.2 %copy-start.2 = (bf16[4,256,128]{2,1,0:T(8,128)(2,1)S(1)}, bf16[4,256,128]{2,1,0:T(8,128)(2,1)}, u32[]{:S(2)}) copy-start(bf16[4,256,128]{2,1,0:T(8,128)(2,1)} %get-tuple-element.20) | copy-start | bytes 786436
  67.8 41.3 %copy-start = (bf16[4,32,3072]{2,1,0:T(8,128)(2,1)}, bf16[4,32,3072]{2,1,0:T(8,128)(2,1)S(1)}, u32[]{:S(2)}) copy-start(bf16[4,32,3072]{2,1,0:T(8,128)(2,1)S(1)} %all_to_all.63) | copy-start | bytes 2359300
  67.8 10.3 %collective-permute-start = (bf16[128,3072]{1,0:T(8,128)(2,1)S(1)}, bf16[128,3072]{1,0:T(8,128)(2,1)S(1)}, u32[]{:S(2)}, u32[]{:S(2)}) collective-permute-start(bf16[128,3072]{1,0:T(8,128)(2,1)S(1)} %bitcast.25), channel_id=1, source_target_pairs={{0,16},{16,0},{1,17},{17,1},{2,18},{18,2},{3,19},{19,3},{4,20},{20... | collective-permute-start | bytes 2359304 | tf_op jit(solution)/shard_map/ppermute | solution.py:381
  78.1 31.0 %copy-start.1 = (bf16[128,3072]{1,0:T(8,128)(2,1)}, bf16[128,3072]{1,0:T(8,128)(2,1)S(1)}, u32[]{:S(2)}) copy-start(bf16[128,3072]{1,0:T(8,128)(2,1)S(1)} %collective-permute-done.xb.xb_hbm) | copy-start | bytes 2359300
  78.1 43.6 %copy-start.8 = (f32[4096]{0:T(1024)S(1)}, f32[4096]{0:T(1024)}, u32[]{:S(2)}) copy-start(f32[4096]{0:T(1024)} %param.15) | copy-start | bytes 49156
  83.2 12.1 %all-to-all-start.2 = ((bf16[4,192,128]{2,1,0:T(8,128)(2,1)}), bf16[4,192,128]{2,1,0:T(8,128)(2,1)S(1)}, u32[]{:S(2)}, u32[]{:S(2)}) async-start(bf16[4,192,128]{2,1,0:T(8,128)(2,1)} %get-tuple-element.19), calls=%async_computation.2 | async-start | bytes 393216 | tf_op jit(solution)/shard_map/all_to_all | solution.py:409
  86.7 12.3 %collective-permute-start.2 = (bf16[4,256,128]{2,1,0:T(8,128)(2,1)}, bf16[4,256,128]{2,1,0:T(8,128)(2,1)S(1)}, u32[]{:S(2)}, u32[]{:S(2)}) collective-permute-start(bf16[4,256,128]{2,1,0:T(8,128)(2,1)} %get-tuple-element.21), channel_id=1, source_target_pairs={{0,32},{32,64},{64,96},{96,0},{1,33},{33,65},{65,97},{97,1},{2,34}... | collective-permute-start | bytes 786440 | tf_op jit(solution)/shard_map/ppermute | solution.py:402
  89.7 11.6 %collective-permute-start.3 = (bf16[4,256,128]{2,1,0:T(8,128)(2,1)S(1)}, bf16[4,256,128]{2,1,0:T(8,128)(2,1)S(1)}, u32[]{:S(2)}, u32[]{:S(2)}) collective-permute-start(bf16[4,256,128]{2,1,0:T(8,128)(2,1)S(1)} %copy-done.16), channel_id=1, source_target_pairs={{0,96},{32,0},{64,32},{96,64},{1,97},{33,1},{65,33},{97,65},{2,98}... | collective-permute-start | bytes 786440 | tf_op jit(solution)/shard_map/ppermute | solution.py:402
  93.3 14.6 %collective-permute-start.4 = (bf16[4,256,128]{2,1,0:T(8,128)(2,1)S(1)}, bf16[4,256,128]{2,1,0:T(8,128)(2,1)S(1)}, u32[]{:S(2)}, u32[]{:S(2)}) collective-permute-start(bf16[4,256,128]{2,1,0:T(8,128)(2,1)S(1)} %copy-done.15), channel_id=1, source_target_pairs={{0,64},{32,96},{64,0},{96,32},{1,65},{33,97},{65,1},{97,33},{2,66}... | collective-permute-start | bytes 786440 | tf_op jit(solution)/shard_map/ppermute | solution.py:402
  95.3 12.5 %collective-permute-start.1 = (bf16[768,128]{1,0:T(8,128)(2,1)S(1)}, bf16[768,128]{1,0:T(8,128)(2,1)S(1)}, u32[]{:S(2)}, u32[]{:S(2)}) collective-permute-start(bf16[768,128]{1,0:T(8,128)(2,1)S(1)} %bitcast.41), channel_id=1, source_target_pairs={{0,16},{16,0},{1,17},{17,1},{2,18},{18,2},{3,19},{19,3},{4,20},{20... | collective-permute-start | bytes 589832 | tf_op jit(solution)/shard_map/ppermute | solution.py:381
  122.3 12.6 %copy-start.3 = (bf16[4,192,128]{2,1,0:T(8,128)(2,1)}, bf16[4,192,128]{2,1,0:T(8,128)(2,1)S(1)}, u32[]{:S(2)}) copy-start(bf16[4,192,128]{2,1,0:T(8,128)(2,1)S(1)} %get-tuple-element.25.after) | copy-start | bytes 589828
  131.4 11.8 %all-to-all-start.5 = ((bf16[4,768,128]{2,1,0:T(8,128)(2,1)}), bf16[4,768,128]{2,1,0:T(8,128)(2,1)S(1)}, u32[]{:S(2)}, u32[]{:S(2)}) async-start(bf16[4,768,128]{2,1,0:T(8,128)(2,1)} %tile.21), calls=%async_computation.5 | async-start | bytes 1572864 | tf_op jit(solution)/shard_map/all_to_all | solution.py:377
  134.9 17.5 %copy-start.6 = (f32[4096]{0:T(1024)S(1)}, f32[4096]{0:T(1024)}, u32[]{:S(2)}) copy-start(f32[4096]{0:T(1024)} %param.10) | copy-start | bytes 49156
  134.9 17.5 %copy-start.10 = (s32[4]{0:T(128)S(1)}, s32[4]{0:T(128)}, u32[]{:S(2)}) copy-start(s32[4]{0:T(128)} %pad_add_fusion.meta) | copy-start | bytes 52
  134.9 17.5 %copy-start.12 = (f32[1,128]{1,0:T(1,128)S(1)}, f32[1,128]{1,0:T(1,128)}, u32[]{:S(2)}) copy-start(f32[1,128]{1,0:T(1,128)} %q_gain.5) | copy-start | bytes 1540
  134.9 17.5 %copy-start.14 = (f32[1,128]{1,0:T(1,128)S(1)}, f32[1,128]{1,0:T(1,128)}, u32[]{:S(2)}) copy-start(f32[1,128]{1,0:T(1,128)} %k_gain.5) | copy-start | bytes 1540
  143.2 9.2 %collective-permute-start.5 = (bf16[3072,128]{1,0:T(8,128)(2,1)S(1)}, bf16[3072,128]{1,0:T(8,128)(2,1)S(1)}, u32[]{:S(2)}, u32[]{:S(2)}) collective-permute-start(bf16[3072,128]{1,0:T(8,128)(2,1)S(1)} %bitcast.28), channel_id=1, source_target_pairs={{0,16},{16,0},{1,17},{17,1},{2,18},{18,2},{3,19},{19,3},{4,20},{20... | collective-permute-start | bytes 2359304 | tf_op jit(solution)/shard_map/ppermute | solution.py:381
  152.4 0.9 copy-start.7
  159.0 37.1 %copy-start.4 = (bf16[6,4096]{1,0:T(8,128)(2,1)S(1)}, bf16[6,4096]{1,0:T(8,128)(2,1)}, u32[]{:S(2)}) copy-start(bf16[6,4096]{1,0:T(8,128)(2,1)} %state.1) | copy-start | bytes 147460
  172.9 4.5 %collective-permute-start.6 = (bf16[1536,128]{1,0:T(8,128)(2,1)S(1)}, bf16[1536,128]{1,0:T(8,128)(2,1)S(1)}, u32[]{:S(2)}, u32[]{:S(2)}) collective-permute-start(bf16[1536,128]{1,0:T(8,128)(2,1)S(1)} %bitcast.30), channel_id=1, source_target_pairs={{0,16},{16,0},{1,17},{17,1},{2,18},{18,2},{3,19},{19,3},{4,20},{20... | collective-permute-start | bytes 1179656 | tf_op jit(solution)/shard_map/ppermute | solution.py:381
Sparse Core Ops, SparseCore 0:
  42.5 80.3 all-gather.1

commit v8 on v7

--- a/solution.py
+++ b/solution.py
@@ -371,10 +371,13 @@
     change_ref[...] = jnp.broadcast_to(-0.5 * STEP * row_sum(total[6:7, :]) / TOK, (1, 128))
 
 
-def spread(copies):
+def along_z(copies):
     n, rows, lanes = copies.shape
-    a = lax.all_to_all(copies.reshape(n * rows, lanes), "z", 0, 0, tiled=True)
-    return a, lax.all_to_all(jnp.tile(a, (4, 1)), "y", 0, 0, tiled=True)
+    return lax.all_to_all(copies.reshape(n * rows, lanes), "z", 0, 0, tiled=True)
+
+
+def along_y(block):
+    return lax.all_to_all(jnp.tile(block, (4, 1)), "y", 0, 0, tiled=True)
 
 
 def swap(block):
@@ -393,20 +396,22 @@
         pack_kernel, [shape((4, 8, 3072)), shape((8, 6144))] + [shape((4, 256, 128))] * 4,
         1, meta, (state,), (probe,), (out_map.reshape(4, 4, 256, 128),),
         scratch=[pltpu.VMEM((6, 4096), BF), pltpu.VMEM((6, 4096), BF), sems(6)],
-        vmem_mib=FULL, n_hbm=4,
+        vmem_mib=FULL,
     )
     probe_all = lax.all_gather(packed_probe, SEQ, axis=0, tiled=True)
-    _, own = spread(packed_state)
-    plane_outs = [sends[0]]
-    for k in (1, 3, 2):
-        plane_outs.append(lax.ppermute(sends[k], "y", [(y, (y + k) % 4) for y in range(4)]))
-    plane_outs = [(piece.reshape(8, 128, 128),) for piece in plane_outs]
+    lines = along_z(packed_state)
+    moved = [
+        lax.ppermute(sends[k], "y", [(y, (y + k) % 4) for y in range(4)]) for k in (1, 3, 2)
+    ]
+    lines, moved[0], moved[1] = lax.optimization_barrier((lines, moved[0], moved[1]))
+    plane_outs = [(piece.reshape(8, 128, 128),) for piece in (sends[0], *moved)]
+    own = along_y(lines)
     oth = swap(own)
     att1, col = call(
         first_kernel, [shape((4, TOK, 128)), shape((TOK, 128))],
         1, meta, own, oth, (maps,), gain, query_gain, key_gain, scratch=[HELD, MAPS, sems(1)], vmem_mib=51,
     )
-    own1 = lax.all_to_all(att1.reshape(4 * TOK, 128), "z", 0, 0, tiled=True)
+    own1 = along_z(att1)
     oth1 = swap(own1)
     parts = call(
         plane_kernel, shape((4, TOK, 128), F32),
@@ -418,7 +423,7 @@
         middle_kernel, [shape((TOK, 128)), shape((4, TOK, 128))],
         1, meta, parts.reshape(4, TOK, 128), gates, col, vmem_mib=MIDDLE,
     )
-    _, own_m = spread(mid)
+    own_m = along_y(along_z(mid))
     probe_blocks, datt1 = call(
         tangent_kernel, [shape((32, TOK, 128)), shape((TOK, 128), F32)],
         1, meta, (own,), (oth,), (probe_all,), (maps,), gain, query_gain, key_gain, (mid,),

time: 205 us -> 172 us (0.84)
  Pallas kernels: 58.7 us -> 27.4 us
  blocking collectives: 74.8 us -> 62.9 us
  starting transfers between devices: 38.1 us -> 46.7 us
    pallas_call x8, Pallas kernels: 58.7 us -> 27.4 us  [call(): pl.pallas_call(kernel, out_shape=out_shape, in_specs=in_specs, out_specs=...]
    all_to_all x3 -> x2, blocking collectives: 33.3 us -> 25.4 us  [the longest x1 15.5 us: along_y(): return lax.all_to_all(jnp.tile(block, (4, 1)), 'y', 0, 0, tiled=True)]
    all_to_all x2 -> x3, starting transfers between devices: 7 us -> 14.4 us  [the longest x2 10.9 us: along_z(): lax.all_to_all(copies.reshape(n * rows, lanes), 'z', 0, 0, tiled=True)]
    all_to_all x2 -> x3, waiting for transfers between devices: 1.05 us -> 6.07 us  [the longest x2 5.02 us: along_z(): lax.all_to_all(copies.reshape(n * rows, lanes), 'z', 0, 0, tiled=True)]
    all_to_all x1, blocking collectives: 12.7 us -> 8.68 us  [per_device(): parts = lax.all_to_all(parts.reshape(4 * TOK, 128), 'y', 0, 0, tiled=True)]
    ppermute x3, waiting for transfers between devices: 8.79 us -> 4.87 us  [per_device(): lax.ppermute(sends[k], 'y', [(y, (y + k) % 4) for y in range(4)])]
  transfers between devices with their start and end apart: 10 -> 11, of which waited for: 6 -> 9; matrix products, arithmetic and copies ran while one was open for 1% -> 1% of each run, Pallas kernels for 7% -> 8%
where the time goes in v8:
time: 172 us; the launch traced here: 170 us
  blocking collectives  62.9 us (37%)
  starting transfers between devices  46.7 us (27%)
  Pallas kernels  27.4 us (16%)
  waiting for transfers between devices  16.5 us (10%)
  between operations  14.3 us (8%)
  local copies, waits for them, and re-layouts  2.02 us (1%)
    pallas_call x8, Pallas kernels, call(): pl.pallas_call(kernel, out_shape=out_shape, in_specs=in_specs, out_specs=...  27.4 us
    ppermute x4, starting transfers between devices, swap(): return lax.ppermute(block, 'c', [(0, 1), (1, 0)])  23 us
    all_to_all x1, blocking collectives, along_y(): return lax.all_to_all(jnp.tile(block, (4, 1)), 'y', 0, 0, tiled=True)  15.5 us
    all_to_all x1, blocking collectives, per_device(): got = lax.all_to_all(columns, SEQ, 0, 0, tiled=True).reshape(32, 8, 512)  14.9 us
    all_to_all x1, blocking collectives, per_device(): own2 = lax.all_to_all(both.reshape(8 * TOK, 128), 'z', 0, 0, tiled=True)  14 us
    all_to_all x2, starting transfers between devices, along_z(): lax.all_to_all(copies.reshape(n * rows, lanes), 'z', 0, 0, tiled=True)  10.9 us
    all_to_all x1, blocking collectives, along_z(): lax.all_to_all(copies.reshape(n * rows, lanes), 'z', 0, 0, tiled=True)  9.9 us
    ppermute x3, starting transfers between devices, per_device(): lax.ppermute(sends[k], 'y', [(y, (y + k) % 4) for y in range(4)])  9.27 us
  transfers between devices with their start and end apart: 11, of which 9 were waited for; matrix products, arithmetic and copies ran while one was open for 1% of the time, Pallas kernels for 8%

profile of v8, /device:TPU:1, one launch (start us, length us, event | category | flops | bytes accessed | tf_op | source)
XLA Modules:
  0.0 170.4 jit_solution(12645602537921063324)
XLA Ops:
  7.3 0.7 pad_add_fusion.meta
  7.9 3.1 %shard_map.95 = (bf16[4,8,3072]{2,1,0:T(8,128)(2,1)}, bf16[8,6144]{1,0:T(8,128)(2,1)}, bf16[4,256,128]{2,1,0:T(8,128)(2,1)}, bf16[4,256,128]{2,1,0:T(8,128)(2,1)...) custom-call(s32[4]{0:T(128)} %pad_add_fusion.meta, bf16[6,4096]{1,0:T(8,128)(2,1)} %state.1, ...), custom_call_target="tpu_custom_call" | custom-call | tf_op jit(solution)/shard_map/pallas_call | solution.py:63
  11.1 6.5 %all-to-all-start = ((bf16[4,8,3072]{2,1,0:T(8,128)(2,1)}), bf16[4,8,3072]{2,1,0:T(8,128)(2,1)S(1)}, u32[]{:S(2)}, u32[]{:S(2)}) async-start(bf16[4,8,3072]{2,1,0:T(8,128)(2,1)} %get-tuple-element.21), calls=%async_computation | async-start | bytes 393216 | tf_op jit(solution)/shard_map/all_to_all | solution.py:376
  17.5 3.2 %collective-permute-start = (bf16[4,256,128]{2,1,0:T(8,128)(2,1)}, bf16[4,256,128]{2,1,0:T(8,128)(2,1)S(1)}, u32[]{:S(2)}, u32[]{:S(2)}) collective-permute-start(bf16[4,256,128]{2,1,0:T(8,128)(2,1)} %get-tuple-element.22), channel_id=1, source_target_pairs={{0,32},{32,64},{64,96},{96,0},{1,33},{33,65},{65,97},{97,1},{2,34}... | collective-permute-start | bytes 786440 | tf_op jit(solution)/shard_map/ppermute | solution.py:404
  20.7 3.4 %collective-permute-start.1 = (bf16[4,256,128]{2,1,0:T(8,128)(2,1)}, bf16[4,256,128]{2,1,0:T(8,128)(2,1)S(1)}, u32[]{:S(2)}, u32[]{:S(2)}) collective-permute-start(bf16[4,256,128]{2,1,0:T(8,128)(2,1)} %get-tuple-element.23), channel_id=1, source_target_pairs={{0,96},{32,0},{64,32},{96,64},{1,97},{33,1},{65,33},{97,65},{2,98}... | collective-permute-start | bytes 786440 | tf_op jit(solution)/shard_map/ppermute | solution.py:404
  24.1 2.2 %collective-permute-done = bf16[4,256,128]{2,1,0:T(8,128)(2,1)S(1)} collective-permute-done((bf16[4,256,128]{2,1,0:T(8,128)(2,1)}, bf16[4,256,128]{2,1,0:T(8,128)(2,1)S(1)}, u32[]{:S(2)}, u32[]{:S(2)}) %collective-permute-start) | collective-permute-done | bytes 262176 | tf_op jit(solution)/shard_map/ppermute | solution.py:404
  26.2 2.1 %collective-permute-done.1 = bf16[4,256,128]{2,1,0:T(8,128)(2,1)S(1)} collective-permute-done((bf16[4,256,128]{2,1,0:T(8,128)(2,1)}, bf16[4,256,128]{2,1,0:T(8,128)(2,1)S(1)}, u32[]{:S(2)}, u32[]{:S(2)}) %collective-permute-start.1) | collective-permute-done | bytes 262176 | tf_op jit(solution)/shard_map/ppermute | solution.py:404
  28.4 15.5 %all_to_all.65 = bf16[4,32,3072]{2,1,0:T(8,128)(2,1)S(1)} all-to-all(bf16[4,32,3072]{2,1,0:T(8,128)(2,1)S(1)} %tile.6), channel_id=1, replica_groups=mesh['z'=4,'y'=4,'c'=2,'w'=4,'x'=4] {'y'}, dimensions={0} | all-to-all | bytes 1572864 | tf_op jit(solution)/shard_map/all_to_all | solution.py:380
  43.9 8.0 %collective-permute-start.2 = (bf16[128,3072]{1,0:T(8,128)(2,1)S(1)}, bf16[128,3072]{1,0:T(8,128)(2,1)S(1)}, u32[]{:S(2)}, u32[]{:S(2)}) collective-permute-start(bf16[128,3072]{1,0:T(8,128)(2,1)S(1)} %bitcast.25), channel_id=1, source_target_pairs={{0,16},{16,0},{1,17},{17,1},{2,18},{18,2},{3,19},{19,3},{4,20},{20... | collective-permute-start | bytes 2359304 | tf_op jit(solution)/shard_map/ppermute | solution.py:384
  51.9 1.9 %collective-permute-done.2.xb.xb_hbm = bf16[128,3072]{1,0:T(8,128)(2,1)S(1)} collective-permute-done((bf16[128,3072]{1,0:T(8,128)(2,1)S(1)}, bf16[128,3072]{1,0:T(8,128)(2,1)S(1)}, u32[]{:S(2)}, u32[]{:S(2)}) %collective-permute-start.2) | collective-permute-done | bytes 786464 | tf_op jit(solution)/shard_map/ppermute | solution.py:384
  53.8 5.1 %shard_map.96 = (bf16[4,192,128]{2,1,0:T(8,128)(2,1)}, bf16[192,128]{1,0:T(8,128)(2,1)S(1)}) custom-call(s32[4]{0:T(128)S(1)} %copy-done.9, bf16[128,3072]{1,0:T(8,128)(2,1)S(1)} %bitcast.26, bf16[128,3072]{1,0:T(8,128)(2,1)S(1)} %collective-permute-done.2.xb.xb_hbm, bf16[32,128,384]{2,1,0:T(8,128)(2,1)} %bitcast.49, f32[32,1,128]{2,1,0:T(1,128)S(1)} %bitcast.45, ...), custom_call_target="tpu_custom_call" | custom-call | tf_op jit(solution)/shard_map/pallas_call | solution.py:63
  58.9 4.4 %all-to-all-start.2 = ((bf16[4,192,128]{2,1,0:T(8,128)(2,1)}), bf16[4,192,128]{2,1,0:T(8,128)(2,1)S(1)}, u32[]{:S(2)}, u32[]{:S(2)}) async-start(bf16[4,192,128]{2,1,0:T(8,128)(2,1)} %get-tuple-element.25), calls=%async_computation.2 | async-start | bytes 393216 | tf_op jit(solution)/shard_map/all_to_all | solution.py:376
  63.3 2.7 %collective-permute-start.4 = (bf16[4,256,128]{2,1,0:T(8,128)(2,1)S(1)}, bf16[4,256,128]{2,1,0:T(8,128)(2,1)S(1)}, u32[]{:S(2)}, u32[]{:S(2)}) collective-permute-start(bf16[4,256,128]{2,1,0:T(8,128)(2,1)S(1)} %copy-done.15), channel_id=1, source_target_pairs={{0,64},{32,96},{64,0},{96,32},{1,65},{33,97},{65,1},{97,33},{2,66}... | collective-permute-start | bytes 786440 | tf_op jit(solution)/shard_map/ppermute | solution.py:404
  66.1 5.0 %all-to-all-done.2.own = bf16[4,192,128]{2,1,0:T(8,128)(2,1)S(1)} async-done(((bf16[4,192,128]{2,1,0:T(8,128)(2,1)}), bf16[4,192,128]{2,1,0:T(8,128)(2,1)S(1)}, u32[]{:S(2)}, u32[]{:S(2)}) %all-to-all-start.2) | async-done | bytes 196640 | tf_op jit(solution)/shard_map/all_to_all | solution.py:376
  71.1 4.5 %collective-permute-start.3 = (bf16[768,128]{1,0:T(8,128)(2,1)S(1)}, bf16[768,128]{1,0:T(8,128)(2,1)S(1)}, u32[]{:S(2)}, u32[]{:S(2)}) collective-permute-start(bf16[768,128]{1,0:T(8,128)(2,1)S(1)} %bitcast.41), channel_id=1, source_target_pairs={{0,16},{16,0},{1,17},{17,1},{2,18},{18,2},{3,19},{19,3},{4,20},{20... | collective-permute-start | bytes 589832 | tf_op jit(solution)/shard_map/ppermute | solution.py:384
  76.6 1.2 shard_map.97
  77.9 8.7 %all_to_all.66.parts = f32[4,192,128]{2,1,0:T(8,128)S(1)} all-to-all(f32[4,192,128]{2,1,0:T(8,128)S(1)} %shard_map.97), channel_id=1, replica_groups=mesh['z'=4,'y'=4,'c'=2,'w'=4,'x'=4] {'y'}, dimensions={0} | all-to-all | bytes 786432 | tf_op jit(solution)/shard_map/all_to_all | solution.py:421
  87.2 9.9 %all_to_all.67 = bf16[4,192,128]{2,1,0:T(8,128)(2,1)S(1)} all-to-all(bf16[4,192,128]{2,1,0:T(8,128)(2,1)S(1)} %get-tuple-element.31.after), channel_id=1, replica_groups=mesh['z'=4,'y'=4,'c'=2,'w'=4,'x'=4] {'z'}, dimensions={0} | all-to-all | bytes 393216 | tf_op jit(solution)/shard_map/all_to_all | solution.py:376
  97.1 1.0 tile.8
  98.1 3.5 %all-to-all-start.5 = ((bf16[4,768,128]{2,1,0:T(8,128)(2,1)}), bf16[4,768,128]{2,1,0:T(8,128)(2,1)S(1)}, u32[]{:S(2)}, u32[]{:S(2)}) async-start(bf16[4,768,128]{2,1,0:T(8,128)(2,1)} %tile.8), calls=%async_computation.5 | async-start | bytes 1572864 | tf_op jit(solution)/shard_map/all_to_all | solution.py:380
  101.6 7.2 %shard_map.99 = (bf16[32,192,128]{2,1,0:T(8,128)(2,1)}, f32[192,128]{1,0:T(8,128)}) custom-call(s32[4]{0:T(128)} %pad_add_fusion.meta, bf16[128,3072]{1,0:T(8,128)(2,1)} %bitcast.27, bf16[128,3072]{1,0:T(8,128)(2,1)} %copy-done.1, bf16[256,6144]{1,0:T(8,128)(2,1)} %all-gather.2.cloned.1.call-done.packed_hbm, bf16[32,128,384]{2,1,0:T(8,128)(2,1)} %bitcast.50, ...), custom_call_target="tpu_custom_call" | custom-call | tf_op jit(solution)/shard_map/pallas_call | solution.py:63
  108.8 1.1 all-to-all-done.5
  109.9 7.4 %collective-permute-start.5 = (bf16[3072,128]{1,0:T(8,128)(2,1)S(1)}, bf16[3072,128]{1,0:T(8,128)(2,1)S(1)}, u32[]{:S(2)}, u32[]{:S(2)}) collective-permute-start(bf16[3072,128]{1,0:T(8,128)(2,1)S(1)} %bitcast.28), channel_id=1, source_target_pairs={{0,16},{16,0},{1,17},{17,1},{2,18},{18,2},{3,19},{19,3},{4,20},{20... | collective-permute-start | bytes 2359304 | tf_op jit(solution)/shard_map/ppermute | solution.py:384
  117.3 1.9 %collective-permute-done.5 = bf16[3072,128]{1,0:T(8,128)(2,1)S(1)} collective-permute-done((bf16[3072,128]{1,0:T(8,128)(2,1)S(1)}, bf16[3072,128]{1,0:T(8,128)(2,1)S(1)}, u32[]{:S(2)}, u32[]{:S(2)}) %collective-permute-start.5) | collective-permute-done | bytes 786464 | tf_op jit(solution)/shard_map/ppermute | solution.py:384
  119.2 0.9 copy-done.7
  120.1 5.7 %shard_map.100 = bf16[4,384,128]{2,1,0:T(8,128)(2,1)S(1)} custom-call(s32[4]{0:T(128)S(1)} %copy-done.10, bf16[16,192,128]{2,1,0:T(8,128)(2,1)S(1)} %bitcast.29, bf16[16,192,128]{2,1,0:T(8,128)(2,1)S(1)} %bitcast.40, bf16[32,192,128]{2,1,0:T(8,128)(2,1)} %get-tuple-element.35.probe.probe_hbm, bf16[32,128,384]{2,1,0:T(8,128)(2,1)} %bitcast.51, ...), custom_call_target="tpu_custom_call" | custom-call | tf_op jit(solution)/shard_map/pallas_call | solution.py:63
  125.8 14.0 %all_to_all.68.own = bf16[4,384,128]{2,1,0:T(8,128)(2,1)S(1)} all-to-all(bf16[4,384,128]{2,1,0:T(8,128)(2,1)S(1)} %shard_map.100), channel_id=1, replica_groups=mesh['z'=4,'y'=4,'c'=2,'w'=4,'x'=4] {'z'}, dimensions={0} | all-to-all | bytes 786432 | tf_op jit(solution)/shard_map/all_to_all | solution.py:444
  139.7 3.1 %collective-permute-start.6 = (bf16[1536,128]{1,0:T(8,128)(2,1)S(1)}, bf16[1536,128]{1,0:T(8,128)(2,1)S(1)}, u32[]{:S(2)}, u32[]{:S(2)}) collective-permute-start(bf16[1536,128]{1,0:T(8,128)(2,1)S(1)} %bitcast.30), channel_id=1, source_target_pairs={{0,16},{16,0},{1,17},{17,1},{2,18},{18,2},{3,19},{19,3},{4,20},{20... | collective-permute-start | bytes 1179656 | tf_op jit(solution)/shard_map/ppermute | solution.py:384
  142.9 1.3 collective-permute-done.6
  144.2 3.8 %shard_map.101 = bf16[256,512]{1,0:T(8,128)(2,1)S(1)} custom-call(s32[4]{0:T(128)S(1)} %copy-done.10, bf16[4,384,128]{2,1,0:T(8,128)(2,1)S(1)} %all_to_all.68.own, bf16[4,384,128]{2,1,0:T(8,128)(2,1)S(1)} %bitcast.42, bf16[8,128,128]{2,1,0:T(8,128)(2,1)S(1)} %bitcast.33, bf16[8,128,128]{2,1,0:T(8,128)(2,1)S(1)} %bitcast.35, ...), custom_call_target="tpu_custom_call" | custom-call | tf_op jit(solution)/shard_map/pallas_call | solution.py:63
  148.0 14.9 %all_to_all.69.got = bf16[32,8,512]{2,1,0:T(8,128)(2,1)S(1)} all-to-all(bf16[32,8,512]{2,1,0:T(8,128)(2,1)S(1)} %bitcast.31), channel_id=1, replica_groups=mesh['z'=4,'y'=4,'c'=2,'w'=4,'x'=4] {'z','y','c'}, dimensions={0} | all-to-all | bytes 524288 | tf_op jit(solution)/shard_map/all_to_all | solution.py:456
  162.9 0.7 shard_map.102
  (39 shorter events, 1.9 us)
Async XLA Ops:
  7.2 46.6 %copy-start.13 = (f32[1,128]{1,0:T(1,128)S(1)}, f32[1,128]{1,0:T(1,128)}, u32[]{:S(2)}) copy-start(f32[1,128]{1,0:T(1,128)} %k_gain.5) | copy-start | bytes 1540
  7.2 46.6 %copy-start.11 = (f32[1,128]{1,0:T(1,128)S(1)}, f32[1,128]{1,0:T(1,128)}, u32[]{:S(2)}) copy-start(f32[1,128]{1,0:T(1,128)} %q_gain.5) | copy-start | bytes 1540
  7.2 46.6 %copy-start.5 = (f32[4096]{0:T(1024)S(1)}, f32[4096]{0:T(1024)}, u32[]{:S(2)}) copy-start(f32[4096]{0:T(1024)} %param.10) | copy-start | bytes 49156
  7.2 94.4 %all-gather.2.cloned.1.call-start = ((), (), s32[]{:S(2)}) async-start(), calls=%async_computation.8 | async-start | bytes 3244032 | tf_op jit(solution)/shard_map/all_gather | solution.py:401
  7.9 45.9 %copy-start.9 = (s32[4]{0:T(128)S(1)}, s32[4]{0:T(128)}, u32[]{:S(2)}) copy-start(s32[4]{0:T(128)} %pad_add_fusion.meta) | copy-start | bytes 52
  11.1 17.3 %all-to-all-start = ((bf16[4,8,3072]{2,1,0:T(8,128)(2,1)}), bf16[4,8,3072]{2,1,0:T(8,128)(2,1)S(1)}, u32[]{:S(2)}, u32[]{:S(2)}) async-start(bf16[4,8,3072]{2,1,0:T(8,128)(2,1)} %get-tuple-element.21), calls=%async_computation | async-start | bytes 393216 | tf_op jit(solution)/shard_map/all_to_all | solution.py:376
  17.5 8.7 %collective-permute-start = (bf16[4,256,128]{2,1,0:T(8,128)(2,1)}, bf16[4,256,128]{2,1,0:T(8,128)(2,1)S(1)}, u32[]{:S(2)}, u32[]{:S(2)}) collective-permute-start(bf16[4,256,128]{2,1,0:T(8,128)(2,1)} %get-tuple-element.22), channel_id=1, source_target_pairs={{0,32},{32,64},{64,96},{96,0},{1,33},{33,65},{65,97},{97,1},{2,34}... | collective-permute-start | bytes 786440 | tf_op jit(solution)/shard_map/ppermute | solution.py:404
  20.7 7.6 %collective-permute-start.1 = (bf16[4,256,128]{2,1,0:T(8,128)(2,1)}, bf16[4,256,128]{2,1,0:T(8,128)(2,1)S(1)}, u32[]{:S(2)}, u32[]{:S(2)}) collective-permute-start(bf16[4,256,128]{2,1,0:T(8,128)(2,1)} %get-tuple-element.23), channel_id=1, source_target_pairs={{0,96},{32,0},{64,32},{96,64},{1,97},{33,1},{65,33},{97,65},{2,98}... | collective-permute-start | bytes 786440 | tf_op jit(solution)/shard_map/ppermute | solution.py:404
  28.4 34.9 %copy-start.15 = (bf16[4,256,128]{2,1,0:T(8,128)(2,1)S(1)}, bf16[4,256,128]{2,1,0:T(8,128)(2,1)}, u32[]{:S(2)}) copy-start(bf16[4,256,128]{2,1,0:T(8,128)(2,1)} %get-tuple-element.29) | copy-start | bytes 786436
  28.4 48.2 %copy-start.2 = (bf16[4,256,128]{2,1,0:T(8,128)(2,1)S(1)}, bf16[4,256,128]{2,1,0:T(8,128)(2,1)}, u32[]{:S(2)}) copy-start(bf16[4,256,128]{2,1,0:T(8,128)(2,1)} %get-tuple-element.26) | copy-start | bytes 786436
  43.9 34.0 %copy-start = (bf16[4,32,3072]{2,1,0:T(8,128)(2,1)}, bf16[4,32,3072]{2,1,0:T(8,128)(2,1)S(1)}, u32[]{:S(2)}) copy-start(bf16[4,32,3072]{2,1,0:T(8,128)(2,1)S(1)} %all_to_all.65) | copy-start | bytes 2359300
  43.9 9.9 %collective-permute-start.2 = (bf16[128,3072]{1,0:T(8,128)(2,1)S(1)}, bf16[128,3072]{1,0:T(8,128)(2,1)S(1)}, u32[]{:S(2)}, u32[]{:S(2)}) collective-permute-start(bf16[128,3072]{1,0:T(8,128)(2,1)S(1)} %bitcast.25), channel_id=1, source_target_pairs={{0,16},{16,0},{1,17},{17,1},{2,18},{18,2},{3,19},{19,3},{4,20},{20... | collective-permute-start | bytes 2359304 | tf_op jit(solution)/shard_map/ppermute | solution.py:384
  53.8 24.1 %copy-start.1 = (bf16[128,3072]{1,0:T(8,128)(2,1)}, bf16[128,3072]{1,0:T(8,128)(2,1)S(1)}, u32[]{:S(2)}) copy-start(bf16[128,3072]{1,0:T(8,128)(2,1)S(1)} %collective-permute-done.2.xb.xb_hbm) | copy-start | bytes 2359300
  53.8 32.8 %copy-start.8 = (f32[4096]{0:T(1024)S(1)}, f32[4096]{0:T(1024)}, u32[]{:S(2)}) copy-start(f32[4096]{0:T(1024)} %param.15) | copy-start | bytes 49156
  58.9 12.2 %all-to-all-start.2 = ((bf16[4,192,128]{2,1,0:T(8,128)(2,1)}), bf16[4,192,128]{2,1,0:T(8,128)(2,1)S(1)}, u32[]{:S(2)}, u32[]{:S(2)}) async-start(bf16[4,192,128]{2,1,0:T(8,128)(2,1)} %get-tuple-element.25), calls=%async_computation.2 | async-start | bytes 393216 | tf_op jit(solution)/shard_map/all_to_all | solution.py:376
  63.3 12.9 %collective-permute-start.4 = (bf16[4,256,128]{2,1,0:T(8,128)(2,1)S(1)}, bf16[4,256,128]{2,1,0:T(8,128)(2,1)S(1)}, u32[]{:S(2)}, u32[]{:S(2)}) collective-permute-start(bf16[4,256,128]{2,1,0:T(8,128)(2,1)S(1)} %copy-done.15), channel_id=1, source_target_pairs={{0,64},{32,96},{64,0},{96,32},{1,65},{33,97},{65,1},{97,33},{2,66}... | collective-permute-start | bytes 786440 | tf_op jit(solution)/shard_map/ppermute | solution.py:404
  71.1 5.5 %collective-permute-start.3 = (bf16[768,128]{1,0:T(8,128)(2,1)S(1)}, bf16[768,128]{1,0:T(8,128)(2,1)S(1)}, u32[]{:S(2)}, u32[]{:S(2)}) collective-permute-start(bf16[768,128]{1,0:T(8,128)(2,1)S(1)} %bitcast.41), channel_id=1, source_target_pairs={{0,16},{16,0},{1,17},{17,1},{2,18},{18,2},{3,19},{19,3},{4,20},{20... | collective-permute-start | bytes 589832 | tf_op jit(solution)/shard_map/ppermute | solution.py:384
  87.2 14.5 %copy-start.3 = (bf16[4,192,128]{2,1,0:T(8,128)(2,1)}, bf16[4,192,128]{2,1,0:T(8,128)(2,1)S(1)}, u32[]{:S(2)}) copy-start(bf16[4,192,128]{2,1,0:T(8,128)(2,1)S(1)} %get-tuple-element.31.after) | copy-start | bytes 589828
  98.1 11.8 %all-to-all-start.5 = ((bf16[4,768,128]{2,1,0:T(8,128)(2,1)}), bf16[4,768,128]{2,1,0:T(8,128)(2,1)S(1)}, u32[]{:S(2)}, u32[]{:S(2)}) async-start(bf16[4,768,128]{2,1,0:T(8,128)(2,1)} %tile.8), calls=%async_computation.5 | async-start | bytes 1572864 | tf_op jit(solution)/shard_map/all_to_all | solution.py:380
  101.6 17.6 %copy-start.6 = (f32[4096]{0:T(1024)S(1)}, f32[4096]{0:T(1024)}, u32[]{:S(2)}) copy-start(f32[4096]{0:T(1024)} %param.10) | copy-start | bytes 49156
  101.6 17.6 %copy-start.10 = (s32[4]{0:T(128)S(1)}, s32[4]{0:T(128)}, u32[]{:S(2)}) copy-start(s32[4]{0:T(128)} %pad_add_fusion.meta) | copy-start | bytes 52
  101.6 17.6 %copy-start.12 = (f32[1,128]{1,0:T(1,128)S(1)}, f32[1,128]{1,0:T(1,128)}, u32[]{:S(2)}) copy-start(f32[1,128]{1,0:T(1,128)} %q_gain.5) | copy-start | bytes 1540
  101.6 17.6 %copy-start.14 = (f32[1,128]{1,0:T(1,128)S(1)}, f32[1,128]{1,0:T(1,128)}, u32[]{:S(2)}) copy-start(f32[1,128]{1,0:T(1,128)} %k_gain.5) | copy-start | bytes 1540
  109.9 9.3 %collective-permute-start.5 = (bf16[3072,128]{1,0:T(8,128)(2,1)S(1)}, bf16[3072,128]{1,0:T(8,128)(2,1)S(1)}, u32[]{:S(2)}, u32[]{:S(2)}) collective-permute-start(bf16[3072,128]{1,0:T(8,128)(2,1)S(1)} %bitcast.28), channel_id=1, source_target_pairs={{0,16},{16,0},{1,17},{17,1},{2,18},{18,2},{3,19},{19,3},{4,20},{20... | collective-permute-start | bytes 2359304 | tf_op jit(solution)/shard_map/ppermute | solution.py:384
  119.2 0.9 copy-start.7
  125.8 37.1 %copy-start.4 = (bf16[6,4096]{1,0:T(8,128)(2,1)S(1)}, bf16[6,4096]{1,0:T(8,128)(2,1)}, u32[]{:S(2)}) copy-start(bf16[6,4096]{1,0:T(8,128)(2,1)} %state.1) | copy-start | bytes 147460
  139.7 4.4 %collective-permute-start.6 = (bf16[1536,128]{1,0:T(8,128)(2,1)S(1)}, bf16[1536,128]{1,0:T(8,128)(2,1)S(1)}, u32[]{:S(2)}, u32[]{:S(2)}) collective-permute-start(bf16[1536,128]{1,0:T(8,128)(2,1)S(1)} %bitcast.30), channel_id=1, source_target_pairs={{0,16},{16,0},{1,17},{17,1},{2,18},{18,2},{3,19},{19,3},{4,20},{20... | collective-permute-start | bytes 1179656 | tf_op jit(solution)/shard_map/ppermute | solution.py:384
Sparse Core Ops, SparseCore 0:
  11.2 75.6 all-gather.1

commit v9 on v8

--- a/solution.py
+++ b/solution.py
@@ -49,9 +49,16 @@
     return copies
 
 
-def call(kernel, out_shape, n_scalar, *args, scratch=(), vmem_mib=20, n_hbm=0):
-    in_specs = [pl.BlockSpec(memory_space=pltpu.SMEM)] * n_scalar
-    for a in args[n_scalar:]:
+def call(kernel, out_shape, placed, *args, scratch=(), vmem_mib=20, n_hbm=0):
+    body = kernel
+    if placed:
+
+        def body(*refs):
+            c, y, z = lax.axis_index("c"), lax.axis_index("y"), lax.axis_index("z")
+            return kernel((c, z * 8 + y * 2 + c, y, z), *refs)
+
+    in_specs = []
+    for a in args:
         if isinstance(a, tuple):
             in_specs.append(pl.BlockSpec(memory_space=pltpu.HBM))
         else:
@@ -61,7 +68,7 @@
     vmem = pl.BlockSpec(memory_space=pltpu.VMEM)
     hbm = pl.BlockSpec(memory_space=pltpu.HBM)
     return pl.pallas_call(
-        kernel,
+        body,
         out_shape=out_shape,
         in_specs=in_specs,
         out_specs=[vmem] * (len(out_shape) - n_hbm) + [hbm] * n_hbm if multi else vmem,
@@ -148,7 +155,7 @@
                 state_ref[n] = whole
         else:
             write[:, :3072] = whole
-            write[:, 3072:] = whole
+            write[:, 3072:] = whole[:, :1024]
     for copy in copies[2:]:
         copy.wait()
 
@@ -283,10 +290,10 @@
 
 
 def second_kernel(
-    meta, own, oth, probe, maps_hbm, gain, q_gain, k_gain, datt1, both_ref, maps, sem
+    meta, own, oth, probe, maps_hbm, gain, q_gain, k_gain, datt_hbm, both_ref, maps, datt1, sem
 ):
     core = meta[0]
-    copies = fetch(sem, (maps_hbm, maps))
+    copies = fetch(sem, (maps_hbm, maps), (datt_hbm, datt1))
     squares = jnp.zeros((TOK, 128), F32)
     dots = jnp.zeros((TOK, 128), F32)
     for side, b, h in blocks(core, own, oth):
@@ -308,6 +315,7 @@
         rows = jnp.concatenate([maps[h], maps[h + 8]], axis=0)
         proj = proj + dot(jnp.concatenate(pair, axis=1), rows)
     att, d_att = attend_tangent(proj[:TOK], proj[TOK:], q_gain[...], k_gain[...])
+    copies[1].wait()
     d_both = (d_att + datt1[...]).astype(BF)
     for i in range(4):
         both_ref[i, :TOK] = att
@@ -385,16 +393,13 @@
 
 
 def per_device(state, probe, norm_gain, head_maps, query_gain, key_gain, out_map, out_gate):
-    place = lax.axis_index(SEQ)
-    meta = [lax.axis_index("c"), place, lax.axis_index("y"), lax.axis_index("z")]
-    meta = jnp.stack(meta).astype(jnp.int32)
     gates = out_gate.reshape(32, 1, 128)
     maps = head_maps.reshape(32, 128, 384)
     gain = norm_gain.reshape(32, 1, 128)
 
     packed_state, packed_probe, *sends = call(
-        pack_kernel, [shape((4, 8, 3072)), shape((8, 6144))] + [shape((4, 256, 128))] * 4,
-        1, meta, (state,), (probe,), (out_map.reshape(4, 4, 256, 128),),
+        pack_kernel, [shape((4, 8, 3072)), shape((8, 4096))] + [shape((4, 256, 128))] * 4,
+        True, (state,), (probe,), (out_map.reshape(4, 4, 256, 128),),
         scratch=[pltpu.VMEM((6, 4096), BF), pltpu.VMEM((6, 4096), BF), sems(6)],
         vmem_mib=FULL,
     )
@@ -403,30 +408,31 @@
     moved = [
         lax.ppermute(sends[k], "y", [(y, (y + k) % 4) for y in range(4)]) for k in (1, 3, 2)
     ]
-    lines, moved[0], moved[1] = lax.optimization_barrier((lines, moved[0], moved[1]))
-    plane_outs = [(piece.reshape(8, 128, 128),) for piece in (sends[0], *moved)]
+    lines, moved[0] = lax.optimization_barrier((lines, moved[0]))
     own = along_y(lines)
     oth = swap(own)
     att1, col = call(
         first_kernel, [shape((4, TOK, 128)), shape((TOK, 128))],
-        1, meta, own, oth, (maps,), gain, query_gain, key_gain, scratch=[HELD, MAPS, sems(1)], vmem_mib=51,
-    )
+        True, own, oth, (maps,), gain, query_gain, key_gain, scratch=[HELD, MAPS, sems(1)], vmem_mib=51,
+    )
+    att1, moved[1] = lax.optimization_barrier((att1, moved[1]))
+    plane_outs = [(piece.reshape(8, 128, 128),) for piece in (sends[0], *moved)]
     own1 = along_z(att1)
     oth1 = swap(own1)
     parts = call(
         plane_kernel, shape((4, TOK, 128), F32),
-        1, meta, own1.reshape(4, TOK, 128), oth1.reshape(4, TOK, 128), *plane_outs,
+        True, own1.reshape(4, TOK, 128), oth1.reshape(4, TOK, 128), *plane_outs,
         scratch=[ROWS, sems(4)], vmem_mib=MIDDLE,
     )
     parts = lax.all_to_all(parts.reshape(4 * TOK, 128), "y", 0, 0, tiled=True)
     vel1, mid = call(
         middle_kernel, [shape((TOK, 128)), shape((4, TOK, 128))],
-        1, meta, parts.reshape(4, TOK, 128), gates, col, vmem_mib=MIDDLE,
+        True, parts.reshape(4, TOK, 128), gates, col, vmem_mib=MIDDLE,
     )
     own_m = along_y(along_z(mid))
     probe_blocks, datt1 = call(
         tangent_kernel, [shape((32, TOK, 128)), shape((TOK, 128), F32)],
-        1, meta, (own,), (oth,), (probe_all,), (maps,), gain, query_gain, key_gain, (mid,),
+        True, (own,), (oth,), (probe_all,), (maps,), gain, query_gain, key_gain, (mid,),
         scratch=[
             HELD, pltpu.VMEM((128, 3072), BF), pltpu.VMEM((128, 3072), BF),
             pltpu.VMEM((256, 3072), BF), MAPS, sems(4),
@@ -438,14 +444,14 @@
     own_m = own_m.reshape(16, TOK, 128)
     both = call(
         second_kernel, shape((4, 2 * TOK, 128)),
-        1, meta, own_m, oth_m, probe_blocks, (maps,), gain, query_gain, key_gain, datt1,
-        scratch=[MAPS, sems(1)], vmem_mib=SECOND,
+        True, own_m, oth_m, probe_blocks, (maps,), gain, query_gain, key_gain, (datt1,),
+        scratch=[MAPS, pltpu.VMEM((TOK, 128), F32), sems(2)], vmem_mib=SECOND,
     )
     own2 = lax.all_to_all(both.reshape(8 * TOK, 128), "z", 0, 0, tiled=True)
     oth2 = swap(own2)
     columns = call(
         last_kernel, shape((256, 512)),
-        1, meta, own2.reshape(4, 2 * TOK, 128), oth2.reshape(4, 2 * TOK, 128),
+        True, own2.reshape(4, 2 * TOK, 128), oth2.reshape(4, 2 * TOK, 128),
         *plane_outs, gates, (vel1,), (probe_blocks,),
         scratch=[
             ROWS, pltpu.VMEM((TOK, 128), BF),
@@ -455,7 +461,7 @@
     )
     got = lax.all_to_all(columns, SEQ, 0, 0, tiled=True).reshape(32, 8, 512)
     next_state, change = call(
-        land_kernel, [shape((6, 4096)), shape((1, 128), F32)], 0, got, state
+        land_kernel, [shape((6, 4096)), shape((1, 128), F32)], False, got, state
     )
     return next_state, change[0, :1]
 

time: 172 us -> 167 us (0.971)
  waiting for transfers between devices: 16.5 us -> 20.2 us
  Pallas kernels: 27.4 us -> 24.4 us
  starting transfers between devices: 46.7 us -> 43.8 us
  blocking collectives: 62.9 us -> 60.8 us
    ppermute x3, waiting for transfers between devices: 4.87 us -> 9.78 us  [per_device(): lax.ppermute(sends[k], 'y', [(y, (y + k) % 4) for y in range(4)])]
    pallas_call x8, Pallas kernels: 27.4 us -> 24.4 us  [call(): pl.pallas_call(body, out_shape=out_shape, in_specs=in_specs, out_specs=[v...]
    ppermute x4, starting transfers between devices: 23 us -> 20.7 us  [swap(): return lax.ppermute(block, 'c', [(0, 1), (1, 0)])]
    all_to_all x1, blocking collectives: 15.5 us -> 13.5 us  [along_y(): return lax.all_to_all(jnp.tile(block, (4, 1)), 'y', 0, 0, tiled=True)]
  transfers between devices with their start and end apart: 11 -> 11, of which waited for: 9 -> 7; matrix products, arithmetic and copies ran while one was open for 1% -> 1% of each run, Pallas kernels for 8% -> 7%
where the time goes in v9:
time: 167 us; the launch traced here: 166 us
  blocking collectives  60.8 us (36%)
  starting transfers between devices  43.8 us (26%)
  Pallas kernels  24.4 us (15%)
  waiting for transfers between devices  20.2 us (12%)
  between operations  14.3 us (9%)
  local copies, waits for them, and re-layouts  2.04 us (1%)
    pallas_call x8, Pallas kernels, call(): pl.pallas_call(body, out_shape=out_shape, in_specs=in_specs, out_specs=[v...  24.4 us
    ppermute x4, starting transfers between devices, swap(): return lax.ppermute(block, 'c', [(0, 1), (1, 0)])  20.7 us
    all_to_all x1, blocking collectives, per_device(): got = lax.all_to_all(columns, SEQ, 0, 0, tiled=True).reshape(32, 8, 512)  14.8 us
    all_to_all x1, blocking collectives, per_device(): own2 = lax.all_to_all(both.reshape(8 * TOK, 128), 'z', 0, 0, tiled=True)  13.8 us
    all_to_all x1, blocking collectives, along_y(): return lax.all_to_all(jnp.tile(block, (4, 1)), 'y', 0, 0, tiled=True)  13.5 us
    all_to_all x2, starting transfers between devices, along_z(): lax.all_to_all(copies.reshape(n * rows, lanes), 'z', 0, 0, tiled=True)  10.4 us
    all_to_all x1, blocking collectives, per_device(): parts = lax.all_to_all(parts.reshape(4 * TOK, 128), 'y', 0, 0, tiled=True)  10 us
    ppermute x3, waiting for transfers between devices, per_device(): lax.ppermute(sends[k], 'y', [(y, (y + k) % 4) for y in range(4)])  9.78 us
  transfers between devices with their start and end apart: 11, of which 7 were waited for; matrix products, arithmetic and copies ran while one was open for 1% of the time, Pallas kernels for 7%

profile of v9, /device:TPU:1, one launch (start us, length us, event | category | flops | bytes accessed | tf_op | source)
XLA Modules:
  0.0 165.5 jit_solution(8925177102038715328)
XLA Ops:
  7.2 2.4 %shard_map.95 = (bf16[4,8,3072]{2,1,0:T(8,128)(2,1)}, bf16[8,4096]{1,0:T(8,128)(2,1)}, bf16[4,256,128]{2,1,0:T(8,128)(2,1)}, bf16[4,256,128]{2,1,0:T(8,128)(2,1)...) custom-call(bf16[6,4096]{1,0:T(8,128)(2,1)} %state.1, bf16[6,4096]{1,0:T(8,128)(2,1)} %refs_1_.1, ...), custom_call_target="tpu_custom_call" | custom-call | tf_op jit(solution)/shard_map/pallas_call | solution.py:70
  9.6 6.6 %all-to-all-start = ((bf16[4,8,3072]{2,1,0:T(8,128)(2,1)}), bf16[4,8,3072]{2,1,0:T(8,128)(2,1)S(1)}, u32[]{:S(2)}, u32[]{:S(2)}) async-start(bf16[4,8,3072]{2,1,0:T(8,128)(2,1)} %get-tuple-element.22), calls=%async_computation | async-start | bytes 393216 | tf_op jit(solution)/shard_map/all_to_all | solution.py:384
  16.2 0.7 all-gather.2.cloned.1.call-update
  16.9 3.2 %collective-permute-start = (bf16[4,256,128]{2,1,0:T(8,128)(2,1)}, bf16[4,256,128]{2,1,0:T(8,128)(2,1)S(1)}, u32[]{:S(2)}, u32[]{:S(2)}) collective-permute-start(bf16[4,256,128]{2,1,0:T(8,128)(2,1)} %get-tuple-element.23), channel_id=1, source_target_pairs={{0,32},{32,64},{64,96},{96,0},{1,33},{33,65},{65,97},{97,1},{2,34}... | collective-permute-start | bytes 786440 | tf_op jit(solution)/shard_map/ppermute | solution.py:409
  20.1 5.5 %collective-permute-done = bf16[4,256,128]{2,1,0:T(8,128)(2,1)S(1)} collective-permute-done((bf16[4,256,128]{2,1,0:T(8,128)(2,1)}, bf16[4,256,128]{2,1,0:T(8,128)(2,1)S(1)}, u32[]{:S(2)}, u32[]{:S(2)}) %collective-permute-start) | collective-permute-done | bytes 262176 | tf_op jit(solution)/shard_map/ppermute | solution.py:409
  25.7 13.5 %all_to_all.65 = bf16[4,32,3072]{2,1,0:T(8,128)(2,1)S(1)} all-to-all(bf16[4,32,3072]{2,1,0:T(8,128)(2,1)S(1)} %tile.6), channel_id=1, replica_groups=mesh['z'=4,'y'=4,'c'=2,'w'=4,'x'=4] {'y'}, dimensions={0} | all-to-all | bytes 1572864 | tf_op jit(solution)/shard_map/all_to_all | solution.py:388
  39.2 5.8 %collective-permute-start.1 = (bf16[128,3072]{1,0:T(8,128)(2,1)S(1)}, bf16[128,3072]{1,0:T(8,128)(2,1)S(1)}, u32[]{:S(2)}, u32[]{:S(2)}) collective-permute-start(bf16[128,3072]{1,0:T(8,128)(2,1)S(1)} %bitcast.21), channel_id=1, source_target_pairs={{0,16},{16,0},{1,17},{17,1},{2,18},{18,2},{3,19},{19,3},{4,20},{20... | collective-permute-start | bytes 2359304 | tf_op jit(solution)/shard_map/ppermute | solution.py:392
  45.1 2.8 %collective-permute-start.2 = (bf16[4,256,128]{2,1,0:T(8,128)(2,1)S(1)}, bf16[4,256,128]{2,1,0:T(8,128)(2,1)S(1)}, u32[]{:S(2)}, u32[]{:S(2)}) collective-permute-start(bf16[4,256,128]{2,1,0:T(8,128)(2,1)S(1)} %copy-done.14), channel_id=1, source_target_pairs={{0,96},{32,0},{64,32},{96,64},{1,97},{33,1},{65,33},{97,65},{2,98}... | collective-permute-start | bytes 786440 | tf_op jit(solution)/shard_map/ppermute | solution.py:409
  47.9 4.5 %shard_map.96 = (bf16[4,192,128]{2,1,0:T(8,128)(2,1)}, bf16[192,128]{1,0:T(8,128)(2,1)S(1)}) custom-call(bf16[128,3072]{1,0:T(8,128)(2,1)S(1)} %bitcast.22, bf16[128,3072]{1,0:T(8,128)(2,1)S(1)} %collective-permute-done.1.refs_1_, bf16[32,128,384]{2,1,0:T(8,128)(2,1)} %bitcast.45, f32[32,1,128]{2,1,0:T(1,128)S(1)} %bitcast.41, f32[1,128]{1,0:T(1,128)S(1)} %copy-done.9, ...), custom_call_target="tpu_custom_call" | custom-call | tf_op jit(solution)/shard_map/pallas_call | solution.py:70
  52.5 4.2 %collective-permute-done.2 = bf16[4,256,128]{2,1,0:T(8,128)(2,1)S(1)} collective-permute-done((bf16[4,256,128]{2,1,0:T(8,128)(2,1)S(1)}, bf16[4,256,128]{2,1,0:T(8,128)(2,1)S(1)}, u32[]{:S(2)}, u32[]{:S(2)}) %collective-permute-start.2) | collective-permute-done | bytes 262176 | tf_op jit(solution)/shard_map/ppermute | solution.py:409
  56.8 3.8 %all-to-all-start.2 = ((bf16[4,192,128]{2,1,0:T(8,128)(2,1)}), bf16[4,192,128]{2,1,0:T(8,128)(2,1)S(1)}, u32[]{:S(2)}, u32[]{:S(2)}) async-start(bf16[4,192,128]{2,1,0:T(8,128)(2,1)} %get-tuple-element.27), calls=%async_computation.2 | async-start | bytes 393216 | tf_op jit(solution)/shard_map/all_to_all | solution.py:384
  60.6 3.2 %collective-permute-start.4 = (bf16[4,256,128]{2,1,0:T(8,128)(2,1)S(1)}, bf16[4,256,128]{2,1,0:T(8,128)(2,1)S(1)}, u32[]{:S(2)}, u32[]{:S(2)}) collective-permute-start(bf16[4,256,128]{2,1,0:T(8,128)(2,1)S(1)} %copy-done.13), channel_id=1, source_target_pairs={{0,64},{32,96},{64,0},{96,32},{1,65},{33,97},{65,1},{97,33},{2,66}... | collective-permute-start | bytes 786440 | tf_op jit(solution)/shard_map/ppermute | solution.py:409
  63.9 4.3 %all-to-all-done.2.refs_0_ = bf16[4,192,128]{2,1,0:T(8,128)(2,1)S(1)} async-done(((bf16[4,192,128]{2,1,0:T(8,128)(2,1)}), bf16[4,192,128]{2,1,0:T(8,128)(2,1)S(1)}, u32[]{:S(2)}, u32[]{:S(2)}) %all-to-all-start.2) | async-done | bytes 196640 | tf_op jit(solution)/shard_map/all_to_all | solution.py:384
  68.1 4.1 %collective-permute-start.3 = (bf16[768,128]{1,0:T(8,128)(2,1)S(1)}, bf16[768,128]{1,0:T(8,128)(2,1)S(1)}, u32[]{:S(2)}, u32[]{:S(2)}) collective-permute-start(bf16[768,128]{1,0:T(8,128)(2,1)S(1)} %bitcast.36), channel_id=1, source_target_pairs={{0,16},{16,0},{1,17},{17,1},{2,18},{18,2},{3,19},{19,3},{4,20},{20... | collective-permute-start | bytes 589832 | tf_op jit(solution)/shard_map/ppermute | solution.py:392
  72.3 1.0 collective-permute-done.3
  73.3 0.7 shard_map.97
  74.0 10.0 %all_to_all.66.refs_0_ = f32[4,192,128]{2,1,0:T(8,128)S(1)} all-to-all(f32[4,192,128]{2,1,0:T(8,128)S(1)} %shard_map.97), channel_id=1, replica_groups=mesh['z'=4,'y'=4,'c'=2,'w'=4,'x'=4] {'y'}, dimensions={0} | all-to-all | bytes 786432 | tf_op jit(solution)/shard_map/all_to_all | solution.py:427
  84.1 8.6 %all_to_all.67 = bf16[4,192,128]{2,1,0:T(8,128)(2,1)S(1)} all-to-all(bf16[4,192,128]{2,1,0:T(8,128)(2,1)S(1)} %get-tuple-element.33.refs_7_), channel_id=1, replica_groups=mesh['z'=4,'y'=4,'c'=2,'w'=4,'x'=4] {'z'}, dimensions={0} | all-to-all | bytes 393216 | tf_op jit(solution)/shard_map/all_to_all | solution.py:384
  92.7 1.0 tile.8
  93.7 3.5 %all-to-all-start.5 = ((bf16[4,768,128]{2,1,0:T(8,128)(2,1)}), bf16[4,768,128]{2,1,0:T(8,128)(2,1)S(1)}, u32[]{:S(2)}, u32[]{:S(2)}) async-start(bf16[4,768,128]{2,1,0:T(8,128)(2,1)} %tile.8), calls=%async_computation.5 | async-start | bytes 1572864 | tf_op jit(solution)/shard_map/all_to_all | solution.py:388
  97.3 7.1 %shard_map.99 = (bf16[32,192,128]{2,1,0:T(8,128)(2,1)}, f32[192,128]{1,0:T(8,128)}) custom-call(bf16[128,3072]{1,0:T(8,128)(2,1)} %bitcast.23, bf16[128,3072]{1,0:T(8,128)(2,1)} %copy-done.1, bf16[256,4096]{1,0:T(8,128)(2,1)} %all-gather.2.cloned.1.call-done.refs_2_, bf16[32,128,384]{2,1,0:T(8,128)(2,1)} %bitcast.46, f32[32,1,128]{2,1,0:T(1,128)} %bitcast.40, ...), custom_call_target="tpu_custom_call" | custom-call | tf_op jit(solution)/shard_map/pallas_call | solution.py:70
  104.4 1.1 all-to-all-done.5
  105.5 7.6 %collective-permute-start.5 = (bf16[3072,128]{1,0:T(8,128)(2,1)S(1)}, bf16[3072,128]{1,0:T(8,128)(2,1)S(1)}, u32[]{:S(2)}, u32[]{:S(2)}) collective-permute-start(bf16[3072,128]{1,0:T(8,128)(2,1)S(1)} %bitcast.24), channel_id=1, source_target_pairs={{0,16},{16,0},{1,17},{17,1},{2,18},{18,2},{3,19},{19,3},{4,20},{20... | collective-permute-start | bytes 2359304 | tf_op jit(solution)/shard_map/ppermute | solution.py:392
  113.1 1.9 %collective-permute-done.5 = bf16[3072,128]{1,0:T(8,128)(2,1)S(1)} collective-permute-done((bf16[3072,128]{1,0:T(8,128)(2,1)S(1)}, bf16[3072,128]{1,0:T(8,128)(2,1)S(1)}, u32[]{:S(2)}, u32[]{:S(2)}) %collective-permute-start.5) | collective-permute-done | bytes 786464 | tf_op jit(solution)/shard_map/ppermute | solution.py:392
  115.1 0.9 copy-done.7
  115.9 5.7 %shard_map.100 = bf16[4,384,128]{2,1,0:T(8,128)(2,1)S(1)} custom-call(bf16[16,192,128]{2,1,0:T(8,128)(2,1)S(1)} %bitcast.25, bf16[16,192,128]{2,1,0:T(8,128)(2,1)S(1)} %bitcast.37, bf16[32,192,128]{2,1,0:T(8,128)(2,1)} %get-tuple-element.37.refs_2_.refs_8_, bf16[32,128,384]{2,1,0:T(8,128)(2,1)} %bitcast.47, f32[32,1,128]{2,1,0:T(1,128)S(1)} %bitcast.42, ...), custom_call_target="tpu_custom_call" | custom-call | tf_op jit(solution)/shard_map/pallas_call | solution.py:70
  121.6 13.8 %all_to_all.68.refs_0_ = bf16[4,384,128]{2,1,0:T(8,128)(2,1)S(1)} all-to-all(bf16[4,384,128]{2,1,0:T(8,128)(2,1)S(1)} %shard_map.100), channel_id=1, replica_groups=mesh['z'=4,'y'=4,'c'=2,'w'=4,'x'=4] {'z'}, dimensions={0} | all-to-all | bytes 786432 | tf_op jit(solution)/shard_map/all_to_all | solution.py:450
  135.5 3.1 %collective-permute-start.6 = (bf16[1536,128]{1,0:T(8,128)(2,1)S(1)}, bf16[1536,128]{1,0:T(8,128)(2,1)S(1)}, u32[]{:S(2)}, u32[]{:S(2)}) collective-permute-start(bf16[1536,128]{1,0:T(8,128)(2,1)S(1)} %bitcast.26), channel_id=1, source_target_pairs={{0,16},{16,0},{1,17},{17,1},{2,18},{18,2},{3,19},{19,3},{4,20},{20... | collective-permute-start | bytes 1179656 | tf_op jit(solution)/shard_map/ppermute | solution.py:392
  138.6 1.3 collective-permute-done.6
  139.9 3.3 %shard_map.101 = bf16[256,512]{1,0:T(8,128)(2,1)S(1)} custom-call(bf16[4,384,128]{2,1,0:T(8,128)(2,1)S(1)} %all_to_all.68.refs_0_, bf16[4,384,128]{2,1,0:T(8,128)(2,1)S(1)} %bitcast.38, bf16[8,128,128]{2,1,0:T(8,128)(2,1)S(1)} %bitcast.28, bf16[8,128,128]{2,1,0:T(8,128)(2,1)S(1)} %bitcast.30, bf16[8,128,128]{2,1,0:T(8,128)(2,1)S(1)} %bitcast.32, ...), custom_call_target="tpu_custom_call" | custom-call | tf_op jit(solution)/shard_map/pallas_call | solution.py:70
  143.2 14.8 %all_to_all.69.got = bf16[32,8,512]{2,1,0:T(8,128)(2,1)S(1)} all-to-all(bf16[32,8,512]{2,1,0:T(8,128)(2,1)S(1)} %bitcast.35), channel_id=1, replica_groups=mesh['z'=4,'y'=4,'c'=2,'w'=4,'x'=4] {'z','y','c'}, dimensions={0} | all-to-all | bytes 524288 | tf_op jit(solution)/shard_map/all_to_all | solution.py:462
  158.0 0.7 shard_map.102
  (36 shorter events, 0.2 us)
Async XLA Ops:
  7.2 40.7 %copy-start.5 = (f32[4096]{0:T(1024)S(1)}, f32[4096]{0:T(1024)}, u32[]{:S(2)}) copy-start(f32[4096]{0:T(1024)} %param.10) | copy-start | bytes 49156
  7.2 40.7 %copy-start.9 = (f32[1,128]{1,0:T(1,128)S(1)}, f32[1,128]{1,0:T(1,128)}, u32[]{:S(2)}) copy-start(f32[1,128]{1,0:T(1,128)} %refs_5_.5) | copy-start | bytes 1540
  7.2 40.7 %copy-start.11 = (f32[1,128]{1,0:T(1,128)S(1)}, f32[1,128]{1,0:T(1,128)}, u32[]{:S(2)}) copy-start(f32[1,128]{1,0:T(1,128)} %refs_6_.3) | copy-start | bytes 1540
  9.6 35.5 %copy-start.14 = (bf16[4,256,128]{2,1,0:T(8,128)(2,1)S(1)}, bf16[4,256,128]{2,1,0:T(8,128)(2,1)}, u32[]{:S(2)}) copy-start(bf16[4,256,128]{2,1,0:T(8,128)(2,1)} %get-tuple-element.26) | copy-start | bytes 786436
  9.6 16.1 %all-to-all-start = ((bf16[4,8,3072]{2,1,0:T(8,128)(2,1)}), bf16[4,8,3072]{2,1,0:T(8,128)(2,1)S(1)}, u32[]{:S(2)}, u32[]{:S(2)}) async-start(bf16[4,8,3072]{2,1,0:T(8,128)(2,1)} %get-tuple-element.22), calls=%async_computation | async-start | bytes 393216 | tf_op jit(solution)/shard_map/all_to_all | solution.py:384
  16.2 81.1 %all-gather.2.cloned.1.call-start = ((), (), s32[]{:S(2)}) async-start(), calls=%async_computation.8 | async-start | bytes 2162688 | tf_op jit(solution)/shard_map/all_gather | solution.py:406
  16.9 8.8 %collective-permute-start = (bf16[4,256,128]{2,1,0:T(8,128)(2,1)}, bf16[4,256,128]{2,1,0:T(8,128)(2,1)S(1)}, u32[]{:S(2)}, u32[]{:S(2)}) collective-permute-start(bf16[4,256,128]{2,1,0:T(8,128)(2,1)} %get-tuple-element.23), channel_id=1, source_target_pairs={{0,32},{32,64},{64,96},{96,0},{1,33},{33,65},{65,97},{97,1},{2,34}... | collective-permute-start | bytes 786440 | tf_op jit(solution)/shard_map/ppermute | solution.py:409
  39.2 13.3 %copy-start = (bf16[4,32,3072]{2,1,0:T(8,128)(2,1)}, bf16[4,32,3072]{2,1,0:T(8,128)(2,1)S(1)}, u32[]{:S(2)}) copy-start(bf16[4,32,3072]{2,1,0:T(8,128)(2,1)S(1)} %all_to_all.65) | copy-start | bytes 2359300
  39.2 8.6 %collective-permute-start.1 = (bf16[128,3072]{1,0:T(8,128)(2,1)S(1)}, bf16[128,3072]{1,0:T(8,128)(2,1)S(1)}, u32[]{:S(2)}, u32[]{:S(2)}) collective-permute-start(bf16[128,3072]{1,0:T(8,128)(2,1)S(1)} %bitcast.21), channel_id=1, source_target_pairs={{0,16},{16,0},{1,17},{17,1},{2,18},{18,2},{3,19},{19,3},{4,20},{20... | collective-permute-start | bytes 2359304 | tf_op jit(solution)/shard_map/ppermute | solution.py:392
  45.1 11.7 %collective-permute-start.2 = (bf16[4,256,128]{2,1,0:T(8,128)(2,1)S(1)}, bf16[4,256,128]{2,1,0:T(8,128)(2,1)S(1)}, u32[]{:S(2)}, u32[]{:S(2)}) collective-permute-start(bf16[4,256,128]{2,1,0:T(8,128)(2,1)S(1)} %copy-done.14), channel_id=1, source_target_pairs={{0,96},{32,0},{64,32},{96,64},{1,97},{33,1},{65,33},{97,65},{2,98}... | collective-permute-start | bytes 786440 | tf_op jit(solution)/shard_map/ppermute | solution.py:409
  47.9 4.6 %copy-start.1 = (bf16[128,3072]{1,0:T(8,128)(2,1)}, bf16[128,3072]{1,0:T(8,128)(2,1)S(1)}, u32[]{:S(2)}) copy-start(bf16[128,3072]{1,0:T(8,128)(2,1)S(1)} %collective-permute-done.1.refs_1_) | copy-start | bytes 2359300
  47.9 12.7 %copy-start.13 = (bf16[4,256,128]{2,1,0:T(8,128)(2,1)S(1)}, bf16[4,256,128]{2,1,0:T(8,128)(2,1)}, u32[]{:S(2)}) copy-start(bf16[4,256,128]{2,1,0:T(8,128)(2,1)} %get-tuple-element.31) | copy-start | bytes 786436
  47.9 25.4 %copy-start.2 = (bf16[4,256,128]{2,1,0:T(8,128)(2,1)S(1)}, bf16[4,256,128]{2,1,0:T(8,128)(2,1)}, u32[]{:S(2)}) copy-start(bf16[4,256,128]{2,1,0:T(8,128)(2,1)} %get-tuple-element.28) | copy-start | bytes 786436
  52.5 31.5 %copy-start.8 = (f32[4096]{0:T(1024)S(1)}, f32[4096]{0:T(1024)}, u32[]{:S(2)}) copy-start(f32[4096]{0:T(1024)} %param.15) | copy-start | bytes 49156
  56.8 11.4 %all-to-all-start.2 = ((bf16[4,192,128]{2,1,0:T(8,128)(2,1)}), bf16[4,192,128]{2,1,0:T(8,128)(2,1)S(1)}, u32[]{:S(2)}, u32[]{:S(2)}) async-start(bf16[4,192,128]{2,1,0:T(8,128)(2,1)} %get-tuple-element.27), calls=%async_computation.2 | async-start | bytes 393216 | tf_op jit(solution)/shard_map/all_to_all | solution.py:384
  60.6 11.6 %collective-permute-start.4 = (bf16[4,256,128]{2,1,0:T(8,128)(2,1)S(1)}, bf16[4,256,128]{2,1,0:T(8,128)(2,1)S(1)}, u32[]{:S(2)}, u32[]{:S(2)}) collective-permute-start(bf16[4,256,128]{2,1,0:T(8,128)(2,1)S(1)} %copy-done.13), channel_id=1, source_target_pairs={{0,64},{32,96},{64,0},{96,32},{1,65},{33,97},{65,1},{97,33},{2,66}... | collective-permute-start | bytes 786440 | tf_op jit(solution)/shard_map/ppermute | solution.py:409
  68.1 5.2 %collective-permute-start.3 = (bf16[768,128]{1,0:T(8,128)(2,1)S(1)}, bf16[768,128]{1,0:T(8,128)(2,1)S(1)}, u32[]{:S(2)}, u32[]{:S(2)}) collective-permute-start(bf16[768,128]{1,0:T(8,128)(2,1)S(1)} %bitcast.36), channel_id=1, source_target_pairs={{0,16},{16,0},{1,17},{17,1},{2,18},{18,2},{3,19},{19,3},{4,20},{20... | collective-permute-start | bytes 589832 | tf_op jit(solution)/shard_map/ppermute | solution.py:392
  84.1 13.2 %copy-start.3 = (bf16[4,192,128]{2,1,0:T(8,128)(2,1)}, bf16[4,192,128]{2,1,0:T(8,128)(2,1)S(1)}, u32[]{:S(2)}) copy-start(bf16[4,192,128]{2,1,0:T(8,128)(2,1)S(1)} %get-tuple-element.33.refs_7_) | copy-start | bytes 589828
  93.7 11.8 %all-to-all-start.5 = ((bf16[4,768,128]{2,1,0:T(8,128)(2,1)}), bf16[4,768,128]{2,1,0:T(8,128)(2,1)S(1)}, u32[]{:S(2)}, u32[]{:S(2)}) async-start(bf16[4,768,128]{2,1,0:T(8,128)(2,1)} %tile.8), calls=%async_computation.5 | async-start | bytes 1572864 | tf_op jit(solution)/shard_map/all_to_all | solution.py:388
  97.2 17.8 %copy-start.6 = (f32[4096]{0:T(1024)S(1)}, f32[4096]{0:T(1024)}, u32[]{:S(2)}) copy-start(f32[4096]{0:T(1024)} %param.10) | copy-start | bytes 49156
  97.2 17.8 %copy-start.10 = (f32[1,128]{1,0:T(1,128)S(1)}, f32[1,128]{1,0:T(1,128)}, u32[]{:S(2)}) copy-start(f32[1,128]{1,0:T(1,128)} %refs_5_.5) | copy-start | bytes 1540
  97.2 17.8 %copy-start.12 = (f32[1,128]{1,0:T(1,128)S(1)}, f32[1,128]{1,0:T(1,128)}, u32[]{:S(2)}) copy-start(f32[1,128]{1,0:T(1,128)} %refs_6_.3) | copy-start | bytes 1540
  105.5 9.5 %collective-permute-start.5 = (bf16[3072,128]{1,0:T(8,128)(2,1)S(1)}, bf16[3072,128]{1,0:T(8,128)(2,1)S(1)}, u32[]{:S(2)}, u32[]{:S(2)}) collective-permute-start(bf16[3072,128]{1,0:T(8,128)(2,1)S(1)} %bitcast.24), channel_id=1, source_target_pairs={{0,16},{16,0},{1,17},{17,1},{2,18},{18,2},{3,19},{19,3},{4,20},{20... | collective-permute-start | bytes 2359304 | tf_op jit(solution)/shard_map/ppermute | solution.py:392
  115.0 0.9 copy-start.7
  135.5 4.4 %collective-permute-start.6 = (bf16[1536,128]{1,0:T(8,128)(2,1)S(1)}, bf16[1536,128]{1,0:T(8,128)(2,1)S(1)}, u32[]{:S(2)}, u32[]{:S(2)}) collective-permute-start(bf16[1536,128]{1,0:T(8,128)(2,1)S(1)} %bitcast.26), channel_id=1, source_target_pairs={{0,16},{16,0},{1,17},{17,1},{2,18},{18,2},{3,19},{19,3},{4,20},{20... | collective-permute-start | bytes 1179656 | tf_op jit(solution)/shard_map/ppermute | solution.py:392
  139.9 18.1 %copy-start.4 = (bf16[6,4096]{1,0:T(8,128)(2,1)S(1)}, bf16[6,4096]{1,0:T(8,128)(2,1)}, u32[]{:S(2)}) copy-start(bf16[6,4096]{1,0:T(8,128)(2,1)} %state.1) | copy-start | bytes 147460
Sparse Core Ops, SparseCore 0:
  19.7 71.7 all-gather.1

commit v10 on v9

--- a/solution.py
+++ b/solution.py
@@ -259,7 +259,7 @@
 
 
 def tangent_kernel(
-    meta, xa_hbm, xb_hbm, packed_hbm, maps_hbm, gain, q_gain, k_gain, after, probe_ref, datt_ref,
+    meta, xa_hbm, xb_hbm, packed_hbm, maps_hbm, gain, q_gain, k_gain, after, probe_ref,
     held, xa, xb, packed, maps, sem,
 ):
     copies = fetch(
@@ -286,24 +286,30 @@
         ]
         rows = jnp.concatenate([maps[h], maps[h + 1]], axis=0)
         proj = proj + dot(jnp.concatenate(pair, axis=1), rows)
-    datt_ref[...] = attend_tangent(proj[:TOK], proj[TOK:], q_gain[...], k_gain[...])[1]
+    d_att = attend_tangent(proj[:TOK], proj[TOK:], q_gain[...], k_gain[...])[1]
+    high = d_att.astype(BF)
+    probe_ref[32] = high
+    probe_ref[33] = (d_att - high.astype(F32)).astype(BF)
 
 
 def second_kernel(
-    meta, own, oth, probe, maps_hbm, gain, q_gain, k_gain, datt_hbm, both_ref, maps, datt1, sem
+    meta, own, oth, probe_hbm, maps_hbm, gain, q_gain, k_gain, both_ref, probe, maps, sem
 ):
     core = meta[0]
-    copies = fetch(sem, (maps_hbm, maps), (datt_hbm, datt1))
+    copies = fetch(sem, (probe_hbm, probe), (maps_hbm, maps))
     squares = jnp.zeros((TOK, 128), F32)
     dots = jnp.zeros((TOK, 128), F32)
     for side, b, h in blocks(core, own, oth):
         for i in range(2):
             x = side[b + i].astype(F32)
             squares = squares + x * x
-            dots = dots + x * probe[h + 8 * i].astype(F32)
+    copies[0].wait()
+    for side, b, h in blocks(core, own, oth):
+        for i in range(2):
+            dots = dots + side[b + i].astype(F32) * probe[h + 8 * i].astype(F32)
     recip = lax.rsqrt(row_sum(squares) * (1.0 / 4096) + EPS)
     d_recip = -(recip * recip * recip) * (row_sum(dots) * (1.0 / 4096))
-    copies[0].wait()
+    copies[1].wait()
     proj = jnp.zeros((2 * TOK, 384), F32)
     for side, b, h in blocks(core, own, oth):
         pair = [
@@ -315,8 +321,8 @@
         rows = jnp.concatenate([maps[h], maps[h + 8]], axis=0)
         proj = proj + dot(jnp.concatenate(pair, axis=1), rows)
     att, d_att = attend_tangent(proj[:TOK], proj[TOK:], q_gain[...], k_gain[...])
-    copies[1].wait()
-    d_both = (d_att + datt1[...]).astype(BF)
+    d_first = probe[32].astype(F32) + probe[33].astype(F32)
+    d_both = (d_att + d_first).astype(BF)
     for i in range(4):
         both_ref[i, :TOK] = att
         both_ref[i, TOK:] = d_both
@@ -408,14 +414,13 @@
     moved = [
         lax.ppermute(sends[k], "y", [(y, (y + k) % 4) for y in range(4)]) for k in (1, 3, 2)
     ]
-    lines, moved[0] = lax.optimization_barrier((lines, moved[0]))
+    lines, moved[0], moved[1] = lax.optimization_barrier((lines, moved[0], moved[1]))
     own = along_y(lines)
     oth = swap(own)
     att1, col = call(
         first_kernel, [shape((4, TOK, 128)), shape((TOK, 128))],
         True, own, oth, (maps,), gain, query_gain, key_gain, scratch=[HELD, MAPS, sems(1)], vmem_mib=51,
     )
-    att1, moved[1] = lax.optimization_barrier((att1, moved[1]))
     plane_outs = [(piece.reshape(8, 128, 128),) for piece in (sends[0], *moved)]
     own1 = along_z(att1)
     oth1 = swap(own1)
@@ -430,8 +435,8 @@
         True, parts.reshape(4, TOK, 128), gates, col, vmem_mib=MIDDLE,
     )
     own_m = along_y(along_z(mid))
-    probe_blocks, datt1 = call(
-        tangent_kernel, [shape((32, TOK, 128)), shape((TOK, 128), F32)],
+    probe_blocks = call(
+        tangent_kernel, shape((34, TOK, 128)),
         True, (own,), (oth,), (probe_all,), (maps,), gain, query_gain, key_gain, (mid,),
         scratch=[
             HELD, pltpu.VMEM((128, 3072), BF), pltpu.VMEM((128, 3072), BF),
@@ -439,13 +444,13 @@
         ],
         vmem_mib=FULL,
     )
-    own_m, datt1 = lax.optimization_barrier((own_m, datt1))
+    own_m, probe_blocks = lax.optimization_barrier((own_m, probe_blocks))
     oth_m = swap(own_m).reshape(16, TOK, 128)
     own_m = own_m.reshape(16, TOK, 128)
     both = call(
         second_kernel, shape((4, 2 * TOK, 128)),
-        True, own_m, oth_m, probe_blocks, (maps,), gain, query_gain, key_gain, (datt1,),
-        scratch=[MAPS, pltpu.VMEM((TOK, 128), F32), sems(2)], vmem_mib=SECOND,
+        True, own_m, oth_m, (probe_blocks,), (maps,), gain, query_gain, key_gain,
+        scratch=[pltpu.VMEM((34, TOK, 128), BF), MAPS, sems(2)], vmem_mib=SECOND,
     )
     own2 = lax.all_to_all(both.reshape(8 * TOK, 128), "z", 0, 0, tiled=True)
     oth2 = swap(own2)

time: 167 us -> 165 us (0.988)
  starting transfers between devices: 43.8 us -> 49.6 us
  waiting for transfers between devices: 20.2 us -> 14.8 us
    ppermute x3, waiting for transfers between devices: 9.78 us -> 4.56 us  [per_device(): lax.ppermute(sends[k], 'y', [(y, (y + k) % 4) for y in range(4)])]
    ppermute x4, starting transfers between devices: 20.7 us -> 25.8 us  [swap(): return lax.ppermute(block, 'c', [(0, 1), (1, 0)])]
  transfers between devices with their start and end apart: 11 -> 11, of which waited for: 7 -> 9; matrix products, arithmetic and copies ran while one was open for 1% -> 1% of each run, Pallas kernels for 7% -> 8%
where the time goes in v10:
time: 165 us; the launch traced here: 164 us
  blocking collectives  60.4 us (37%)
  starting transfers between devices  49.6 us (30%)
  Pallas kernels  24 us (15%)
  waiting for transfers between devices  14.8 us (9%)
  between operations  14.3 us (9%)
    ppermute x4, starting transfers between devices, swap(): return lax.ppermute(block, 'c', [(0, 1), (1, 0)])  25.8 us
    pallas_call x8, Pallas kernels, call(): pl.pallas_call(body, out_shape=out_shape, in_specs=in_specs, out_specs=[v...  24 us
    all_to_all x1, blocking collectives, per_device(): got = lax.all_to_all(columns, SEQ, 0, 0, tiled=True).reshape(32, 8, 512)  15.4 us
    all_to_all x1, blocking collectives, per_device(): own2 = lax.all_to_all(both.reshape(8 * TOK, 128), 'z', 0, 0, tiled=True)  13.8 us
    all_to_all x1, blocking collectives, along_y(): return lax.all_to_all(jnp.tile(block, (4, 1)), 'y', 0, 0, tiled=True)  11.9 us
    all_to_all x2, starting transfers between devices, along_z(): lax.all_to_all(copies.reshape(n * rows, lanes), 'z', 0, 0, tiled=True)  11.3 us
    all_to_all x1, blocking collectives, per_device(): parts = lax.all_to_all(parts.reshape(4 * TOK, 128), 'y', 0, 0, tiled=True)  9.96 us
    all_to_all x1, blocking collectives, along_z(): lax.all_to_all(copies.reshape(n * rows, lanes), 'z', 0, 0, tiled=True)  9.36 us
  transfers between devices with their start and end apart: 11, of which 9 were waited for; matrix products, arithmetic and copies ran while one was open for 1% of the time, Pallas kernels for 8%

profile of v10, /device:TPU:1, one launch (start us, length us, event | category | flops | bytes accessed | tf_op | source)
XLA Modules:
  0.0 164.2 jit_solution(10269786847979706251)
XLA Ops:
  7.2 2.4 %shard_map.95 = (bf16[4,8,3072]{2,1,0:T(8,128)(2,1)}, bf16[8,4096]{1,0:T(8,128)(2,1)}, bf16[4,256,128]{2,1,0:T(8,128)(2,1)}, bf16[4,256,128]{2,1,0:T(8,128)(2,1)...) custom-call(bf16[6,4096]{1,0:T(8,128)(2,1)} %state.1, bf16[6,4096]{1,0:T(8,128)(2,1)} %refs_1_.1, ...), custom_call_target="tpu_custom_call" | custom-call | tf_op jit(solution)/shard_map/pallas_call | solution.py:70
  9.6 6.5 %all-to-all-start = ((bf16[4,8,3072]{2,1,0:T(8,128)(2,1)}), bf16[4,8,3072]{2,1,0:T(8,128)(2,1)S(1)}, u32[]{:S(2)}, u32[]{:S(2)}) async-start(bf16[4,8,3072]{2,1,0:T(8,128)(2,1)} %get-tuple-element.19), calls=%async_computation | async-start | bytes 393216 | tf_op jit(solution)/shard_map/all_to_all | solution.py:390
  16.0 0.7 all-gather.2.cloned.1.call-update
  16.8 3.2 %collective-permute-start = (bf16[4,256,128]{2,1,0:T(8,128)(2,1)}, bf16[4,256,128]{2,1,0:T(8,128)(2,1)S(1)}, u32[]{:S(2)}, u32[]{:S(2)}) collective-permute-start(bf16[4,256,128]{2,1,0:T(8,128)(2,1)} %get-tuple-element.20), channel_id=1, source_target_pairs={{0,32},{32,64},{64,96},{96,0},{1,33},{33,65},{65,97},{97,1},{2,34}... | collective-permute-start | bytes 786440 | tf_op jit(solution)/shard_map/ppermute | solution.py:415
  20.0 3.4 %collective-permute-start.1 = (bf16[4,256,128]{2,1,0:T(8,128)(2,1)}, bf16[4,256,128]{2,1,0:T(8,128)(2,1)S(1)}, u32[]{:S(2)}, u32[]{:S(2)}) collective-permute-start(bf16[4,256,128]{2,1,0:T(8,128)(2,1)} %get-tuple-element.21), channel_id=1, source_target_pairs={{0,96},{32,0},{64,32},{96,64},{1,97},{33,1},{65,33},{97,65},{2,98}... | collective-permute-start | bytes 786440 | tf_op jit(solution)/shard_map/ppermute | solution.py:415
  23.3 2.2 %collective-permute-done = bf16[4,256,128]{2,1,0:T(8,128)(2,1)S(1)} collective-permute-done((bf16[4,256,128]{2,1,0:T(8,128)(2,1)}, bf16[4,256,128]{2,1,0:T(8,128)(2,1)S(1)}, u32[]{:S(2)}, u32[]{:S(2)}) %collective-permute-start) | collective-permute-done | bytes 262176 | tf_op jit(solution)/shard_map/ppermute | solution.py:415
  25.5 2.1 %collective-permute-done.1 = bf16[4,256,128]{2,1,0:T(8,128)(2,1)S(1)} collective-permute-done((bf16[4,256,128]{2,1,0:T(8,128)(2,1)}, bf16[4,256,128]{2,1,0:T(8,128)(2,1)S(1)}, u32[]{:S(2)}, u32[]{:S(2)}) %collective-permute-start.1) | collective-permute-done | bytes 262176 | tf_op jit(solution)/shard_map/ppermute | solution.py:415
  27.7 11.9 %all_to_all.65 = bf16[4,32,3072]{2,1,0:T(8,128)(2,1)S(1)} all-to-all(bf16[4,32,3072]{2,1,0:T(8,128)(2,1)S(1)} %tile.6), channel_id=1, replica_groups=mesh['z'=4,'y'=4,'c'=2,'w'=4,'x'=4] {'y'}, dimensions={0} | all-to-all | bytes 1572864 | tf_op jit(solution)/shard_map/all_to_all | solution.py:394
  39.6 9.8 %collective-permute-start.2 = (bf16[128,3072]{1,0:T(8,128)(2,1)S(1)}, bf16[128,3072]{1,0:T(8,128)(2,1)S(1)}, u32[]{:S(2)}, u32[]{:S(2)}) collective-permute-start(bf16[128,3072]{1,0:T(8,128)(2,1)S(1)} %bitcast.21), channel_id=1, source_target_pairs={{0,16},{16,0},{1,17},{17,1},{2,18},{18,2},{3,19},{19,3},{4,20},{20... | collective-permute-start | bytes 2359304 | tf_op jit(solution)/shard_map/ppermute | solution.py:398
  49.4 1.9 %collective-permute-done.2.refs_1_ = bf16[128,3072]{1,0:T(8,128)(2,1)S(1)} collective-permute-done((bf16[128,3072]{1,0:T(8,128)(2,1)S(1)}, bf16[128,3072]{1,0:T(8,128)(2,1)S(1)}, u32[]{:S(2)}, u32[]{:S(2)}) %collective-permute-start.2) | collective-permute-done | bytes 786464 | tf_op jit(solution)/shard_map/ppermute | solution.py:398
  51.3 4.6 %shard_map.96 = (bf16[4,192,128]{2,1,0:T(8,128)(2,1)}, bf16[192,128]{1,0:T(8,128)(2,1)S(1)}) custom-call(bf16[128,3072]{1,0:T(8,128)(2,1)S(1)} %bitcast.22, bf16[128,3072]{1,0:T(8,128)(2,1)S(1)} %collective-permute-done.2.refs_1_, bf16[32,128,384]{2,1,0:T(8,128)(2,1)} %bitcast.45, f32[32,1,128]{2,1,0:T(1,128)S(1)} %bitcast.41, f32[1,128]{1,0:T(1,128)S(1)} %copy-done.8, ...), custom_call_target="tpu_custom_call" | custom-call | tf_op jit(solution)/shard_map/pallas_call | solution.py:70
  55.9 4.8 %all-to-all-start.2 = ((bf16[4,192,128]{2,1,0:T(8,128)(2,1)}), bf16[4,192,128]{2,1,0:T(8,128)(2,1)S(1)}, u32[]{:S(2)}, u32[]{:S(2)}) async-start(bf16[4,192,128]{2,1,0:T(8,128)(2,1)} %get-tuple-element.23), calls=%async_computation.2 | async-start | bytes 393216 | tf_op jit(solution)/shard_map/all_to_all | solution.py:390
  60.7 2.5 %collective-permute-start.4 = (bf16[4,256,128]{2,1,0:T(8,128)(2,1)S(1)}, bf16[4,256,128]{2,1,0:T(8,128)(2,1)S(1)}, u32[]{:S(2)}, u32[]{:S(2)}) collective-permute-start(bf16[4,256,128]{2,1,0:T(8,128)(2,1)S(1)} %copy-done.12), channel_id=1, source_target_pairs={{0,64},{32,96},{64,0},{96,32},{1,65},{33,97},{65,1},{97,33},{2,66}... | collective-permute-start | bytes 786440 | tf_op jit(solution)/shard_map/ppermute | solution.py:415
  63.2 3.0 %all-to-all-done.2.refs_0_ = bf16[4,192,128]{2,1,0:T(8,128)(2,1)S(1)} async-done(((bf16[4,192,128]{2,1,0:T(8,128)(2,1)}), bf16[4,192,128]{2,1,0:T(8,128)(2,1)S(1)}, u32[]{:S(2)}, u32[]{:S(2)}) %all-to-all-start.2) | async-done | bytes 196640 | tf_op jit(solution)/shard_map/all_to_all | solution.py:390
  66.2 5.9 %collective-permute-start.3 = (bf16[768,128]{1,0:T(8,128)(2,1)S(1)}, bf16[768,128]{1,0:T(8,128)(2,1)S(1)}, u32[]{:S(2)}, u32[]{:S(2)}) collective-permute-start(bf16[768,128]{1,0:T(8,128)(2,1)S(1)} %bitcast.36), channel_id=1, source_target_pairs={{0,16},{16,0},{1,17},{17,1},{2,18},{18,2},{3,19},{19,3},{4,20},{20... | collective-permute-start | bytes 589832 | tf_op jit(solution)/shard_map/ppermute | solution.py:398
  72.4 0.7 collective-permute-done.3
  73.2 0.7 shard_map.97
  73.9 10.0 %all_to_all.66.refs_0_ = f32[4,192,128]{2,1,0:T(8,128)S(1)} all-to-all(f32[4,192,128]{2,1,0:T(8,128)S(1)} %shard_map.97), channel_id=1, replica_groups=mesh['z'=4,'y'=4,'c'=2,'w'=4,'x'=4] {'y'}, dimensions={0} | all-to-all | bytes 786432 | tf_op jit(solution)/shard_map/all_to_all | solution.py:432
  83.9 9.4 %all_to_all.67 = bf16[4,192,128]{2,1,0:T(8,128)(2,1)S(1)} all-to-all(bf16[4,192,128]{2,1,0:T(8,128)(2,1)S(1)} %get-tuple-element.29.refs_7_), channel_id=1, replica_groups=mesh['z'=4,'y'=4,'c'=2,'w'=4,'x'=4] {'z'}, dimensions={0} | all-to-all | bytes 393216 | tf_op jit(solution)/shard_map/all_to_all | solution.py:390
  93.2 1.0 tile.8
  94.2 3.5 %all-to-all-start.5 = ((bf16[4,768,128]{2,1,0:T(8,128)(2,1)}), bf16[4,768,128]{2,1,0:T(8,128)(2,1)S(1)}, u32[]{:S(2)}, u32[]{:S(2)}) async-start(bf16[4,768,128]{2,1,0:T(8,128)(2,1)} %tile.8), calls=%async_computation.5 | async-start | bytes 1572864 | tf_op jit(solution)/shard_map/all_to_all | solution.py:394
  97.8 7.6 %shard_map.99.refs_2_.refs_8_ = bf16[34,192,128]{2,1,0:T(8,128)(2,1)} custom-call(bf16[128,3072]{1,0:T(8,128)(2,1)} %bitcast.23, bf16[128,3072]{1,0:T(8,128)(2,1)} %copy-done.1, bf16[256,4096]{1,0:T(8,128)(2,1)} %all-gather.2.cloned.1.call-done.refs_2_, bf16[32,128,384]{2,1,0:T(8,128)(2,1)} %bitcast.46, f32[32,1,128]{2,1,0:T(1,128)} %bitcast.40, ...), custom_call_target="tpu_custom_call" | custom-call | tf_op jit(solution)/shard_map/pallas_call | solution.py:70
  105.5 0.6 all-to-all-done.5
  106.0 7.0 %collective-permute-start.5 = (bf16[3072,128]{1,0:T(8,128)(2,1)S(1)}, bf16[3072,128]{1,0:T(8,128)(2,1)S(1)}, u32[]{:S(2)}, u32[]{:S(2)}) collective-permute-start(bf16[3072,128]{1,0:T(8,128)(2,1)S(1)} %bitcast.24), channel_id=1, source_target_pairs={{0,16},{16,0},{1,17},{17,1},{2,18},{18,2},{3,19},{19,3},{4,20},{20... | collective-permute-start | bytes 2359304 | tf_op jit(solution)/shard_map/ppermute | solution.py:398
  113.1 1.9 %collective-permute-done.5 = bf16[3072,128]{1,0:T(8,128)(2,1)S(1)} collective-permute-done((bf16[3072,128]{1,0:T(8,128)(2,1)S(1)}, bf16[3072,128]{1,0:T(8,128)(2,1)S(1)}, u32[]{:S(2)}, u32[]{:S(2)}) %collective-permute-start.5) | collective-permute-done | bytes 786464 | tf_op jit(solution)/shard_map/ppermute | solution.py:398
  115.0 4.8 %shard_map.100 = bf16[4,384,128]{2,1,0:T(8,128)(2,1)S(1)} custom-call(bf16[16,192,128]{2,1,0:T(8,128)(2,1)S(1)} %bitcast.25, bf16[16,192,128]{2,1,0:T(8,128)(2,1)S(1)} %bitcast.37, bf16[34,192,128]{2,1,0:T(8,128)(2,1)} %shard_map.99.refs_2_.refs_8_, bf16[32,128,384]{2,1,0:T(8,128)(2,1)} %bitcast.47, f32[32,1,128]{2,1,0:T(1,128)S(1)} %bitcast.42, ...), custom_call_target="tpu_custom_call" | custom-call | tf_op jit(solution)/shard_map/pallas_call | solution.py:70
  119.7 13.8 %all_to_all.68.refs_0_ = bf16[4,384,128]{2,1,0:T(8,128)(2,1)S(1)} all-to-all(bf16[4,384,128]{2,1,0:T(8,128)(2,1)S(1)} %shard_map.100), channel_id=1, replica_groups=mesh['z'=4,'y'=4,'c'=2,'w'=4,'x'=4] {'z'}, dimensions={0} | all-to-all | bytes 786432 | tf_op jit(solution)/shard_map/all_to_all | solution.py:455
  133.6 3.1 %collective-permute-start.6 = (bf16[1536,128]{1,0:T(8,128)(2,1)S(1)}, bf16[1536,128]{1,0:T(8,128)(2,1)S(1)}, u32[]{:S(2)}, u32[]{:S(2)}) collective-permute-start(bf16[1536,128]{1,0:T(8,128)(2,1)S(1)} %bitcast.26), channel_id=1, source_target_pairs={{0,16},{16,0},{1,17},{17,1},{2,18},{18,2},{3,19},{19,3},{4,20},{20... | collective-permute-start | bytes 1179656 | tf_op jit(solution)/shard_map/ppermute | solution.py:398
  136.7 1.3 collective-permute-done.6
  138.0 3.3 %shard_map.101 = bf16[256,512]{1,0:T(8,128)(2,1)S(1)} custom-call(bf16[4,384,128]{2,1,0:T(8,128)(2,1)S(1)} %all_to_all.68.refs_0_, bf16[4,384,128]{2,1,0:T(8,128)(2,1)S(1)} %bitcast.38, bf16[8,128,128]{2,1,0:T(8,128)(2,1)S(1)} %bitcast.28, bf16[8,128,128]{2,1,0:T(8,128)(2,1)S(1)} %bitcast.30, bf16[8,128,128]{2,1,0:T(8,128)(2,1)S(1)} %bitcast.32, ...), custom_call_target="tpu_custom_call" | custom-call | tf_op jit(solution)/shard_map/pallas_call | solution.py:70
  141.3 15.4 %all_to_all.69.got = bf16[32,8,512]{2,1,0:T(8,128)(2,1)S(1)} all-to-all(bf16[32,8,512]{2,1,0:T(8,128)(2,1)S(1)} %bitcast.35), channel_id=1, replica_groups=mesh['z'=4,'y'=4,'c'=2,'w'=4,'x'=4] {'z','y','c'}, dimensions={0} | all-to-all | bytes 524288 | tf_op jit(solution)/shard_map/all_to_all | solution.py:467
  156.7 0.7 shard_map.102
  (32 shorter events, 0.5 us)
Async XLA Ops:
  7.2 44.1 %copy-start.5 = (f32[4096]{0:T(1024)S(1)}, f32[4096]{0:T(1024)}, u32[]{:S(2)}) copy-start(f32[4096]{0:T(1024)} %param.10) | copy-start | bytes 49156
  7.2 44.1 %copy-start.8 = (f32[1,128]{1,0:T(1,128)S(1)}, f32[1,128]{1,0:T(1,128)}, u32[]{:S(2)}) copy-start(f32[1,128]{1,0:T(1,128)} %refs_5_.5) | copy-start | bytes 1540
  7.2 44.1 %copy-start.10 = (f32[1,128]{1,0:T(1,128)S(1)}, f32[1,128]{1,0:T(1,128)}, u32[]{:S(2)}) copy-start(f32[1,128]{1,0:T(1,128)} %refs_6_.3) | copy-start | bytes 1540
  9.6 18.0 %all-to-all-start = ((bf16[4,8,3072]{2,1,0:T(8,128)(2,1)}), bf16[4,8,3072]{2,1,0:T(8,128)(2,1)S(1)}, u32[]{:S(2)}, u32[]{:S(2)}) async-start(bf16[4,8,3072]{2,1,0:T(8,128)(2,1)} %get-tuple-element.19), calls=%async_computation | async-start | bytes 393216 | tf_op jit(solution)/shard_map/all_to_all | solution.py:390
  16.0 81.7 %all-gather.2.cloned.1.call-start = ((), (), s32[]{:S(2)}) async-start(), calls=%async_computation.8 | async-start | bytes 2162688 | tf_op jit(solution)/shard_map/all_gather | solution.py:412
  16.8 8.8 %collective-permute-start = (bf16[4,256,128]{2,1,0:T(8,128)(2,1)}, bf16[4,256,128]{2,1,0:T(8,128)(2,1)S(1)}, u32[]{:S(2)}, u32[]{:S(2)}) collective-permute-start(bf16[4,256,128]{2,1,0:T(8,128)(2,1)} %get-tuple-element.20), channel_id=1, source_target_pairs={{0,32},{32,64},{64,96},{96,0},{1,33},{33,65},{65,97},{97,1},{2,34}... | collective-permute-start | bytes 786440 | tf_op jit(solution)/shard_map/ppermute | solution.py:415
  20.0 7.6 %collective-permute-start.1 = (bf16[4,256,128]{2,1,0:T(8,128)(2,1)}, bf16[4,256,128]{2,1,0:T(8,128)(2,1)S(1)}, u32[]{:S(2)}, u32[]{:S(2)}) collective-permute-start(bf16[4,256,128]{2,1,0:T(8,128)(2,1)} %get-tuple-element.21), channel_id=1, source_target_pairs={{0,96},{32,0},{64,32},{96,64},{1,97},{33,1},{65,33},{97,65},{2,98}... | collective-permute-start | bytes 786440 | tf_op jit(solution)/shard_map/ppermute | solution.py:415
  39.6 16.3 %copy-start = (bf16[4,32,3072]{2,1,0:T(8,128)(2,1)}, bf16[4,32,3072]{2,1,0:T(8,128)(2,1)S(1)}, u32[]{:S(2)}) copy-start(bf16[4,32,3072]{2,1,0:T(8,128)(2,1)S(1)} %all_to_all.65) | copy-start | bytes 2359300
  39.6 11.7 %collective-permute-start.2 = (bf16[128,3072]{1,0:T(8,128)(2,1)S(1)}, bf16[128,3072]{1,0:T(8,128)(2,1)S(1)}, u32[]{:S(2)}, u32[]{:S(2)}) collective-permute-start(bf16[128,3072]{1,0:T(8,128)(2,1)S(1)} %bitcast.21), channel_id=1, source_target_pairs={{0,16},{16,0},{1,17},{17,1},{2,18},{18,2},{3,19},{19,3},{4,20},{20... | collective-permute-start | bytes 2359304 | tf_op jit(solution)/shard_map/ppermute | solution.py:398
  51.3 4.6 %copy-start.1 = (bf16[128,3072]{1,0:T(8,128)(2,1)}, bf16[128,3072]{1,0:T(8,128)(2,1)S(1)}, u32[]{:S(2)}) copy-start(bf16[128,3072]{1,0:T(8,128)(2,1)S(1)} %collective-permute-done.2.refs_1_) | copy-start | bytes 2359300
  51.3 9.4 %copy-start.12 = (bf16[4,256,128]{2,1,0:T(8,128)(2,1)S(1)}, bf16[4,256,128]{2,1,0:T(8,128)(2,1)}, u32[]{:S(2)}) copy-start(bf16[4,256,128]{2,1,0:T(8,128)(2,1)} %get-tuple-element.27) | copy-start | bytes 786436
  51.3 21.9 %copy-start.2 = (bf16[4,256,128]{2,1,0:T(8,128)(2,1)S(1)}, bf16[4,256,128]{2,1,0:T(8,128)(2,1)}, u32[]{:S(2)}) copy-start(bf16[4,256,128]{2,1,0:T(8,128)(2,1)} %get-tuple-element.24) | copy-start | bytes 786436
  55.9 27.9 %copy-start.7 = (f32[4096]{0:T(1024)S(1)}, f32[4096]{0:T(1024)}, u32[]{:S(2)}) copy-start(f32[4096]{0:T(1024)} %param.15) | copy-start | bytes 49156
  55.9 10.3 %all-to-all-start.2 = ((bf16[4,192,128]{2,1,0:T(8,128)(2,1)}), bf16[4,192,128]{2,1,0:T(8,128)(2,1)S(1)}, u32[]{:S(2)}, u32[]{:S(2)}) async-start(bf16[4,192,128]{2,1,0:T(8,128)(2,1)} %get-tuple-element.23), calls=%async_computation.2 | async-start | bytes 393216 | tf_op jit(solution)/shard_map/all_to_all | solution.py:390
  60.7 11.7 %collective-permute-start.4 = (bf16[4,256,128]{2,1,0:T(8,128)(2,1)S(1)}, bf16[4,256,128]{2,1,0:T(8,128)(2,1)S(1)}, u32[]{:S(2)}, u32[]{:S(2)}) collective-permute-start(bf16[4,256,128]{2,1,0:T(8,128)(2,1)S(1)} %copy-done.12), channel_id=1, source_target_pairs={{0,64},{32,96},{64,0},{96,32},{1,65},{33,97},{65,1},{97,33},{2,66}... | collective-permute-start | bytes 786440 | tf_op jit(solution)/shard_map/ppermute | solution.py:415
  66.2 7.0 %collective-permute-start.3 = (bf16[768,128]{1,0:T(8,128)(2,1)S(1)}, bf16[768,128]{1,0:T(8,128)(2,1)S(1)}, u32[]{:S(2)}, u32[]{:S(2)}) collective-permute-start(bf16[768,128]{1,0:T(8,128)(2,1)S(1)} %bitcast.36), channel_id=1, source_target_pairs={{0,16},{16,0},{1,17},{17,1},{2,18},{18,2},{3,19},{19,3},{4,20},{20... | collective-permute-start | bytes 589832 | tf_op jit(solution)/shard_map/ppermute | solution.py:398
  83.9 13.9 %copy-start.3 = (bf16[4,192,128]{2,1,0:T(8,128)(2,1)}, bf16[4,192,128]{2,1,0:T(8,128)(2,1)S(1)}, u32[]{:S(2)}) copy-start(bf16[4,192,128]{2,1,0:T(8,128)(2,1)S(1)} %get-tuple-element.29.refs_7_) | copy-start | bytes 589828
  94.2 11.8 %all-to-all-start.5 = ((bf16[4,768,128]{2,1,0:T(8,128)(2,1)}), bf16[4,768,128]{2,1,0:T(8,128)(2,1)S(1)}, u32[]{:S(2)}, u32[]{:S(2)}) async-start(bf16[4,768,128]{2,1,0:T(8,128)(2,1)} %tile.8), calls=%async_computation.5 | async-start | bytes 1572864 | tf_op jit(solution)/shard_map/all_to_all | solution.py:394
  97.7 17.2 %copy-start.6 = (f32[4096]{0:T(1024)S(1)}, f32[4096]{0:T(1024)}, u32[]{:S(2)}) copy-start(f32[4096]{0:T(1024)} %param.10) | copy-start | bytes 49156
  97.7 17.2 %copy-start.9 = (f32[1,128]{1,0:T(1,128)S(1)}, f32[1,128]{1,0:T(1,128)}, u32[]{:S(2)}) copy-start(f32[1,128]{1,0:T(1,128)} %refs_5_.5) | copy-start | bytes 1540
  97.8 17.2 %copy-start.11 = (f32[1,128]{1,0:T(1,128)S(1)}, f32[1,128]{1,0:T(1,128)}, u32[]{:S(2)}) copy-start(f32[1,128]{1,0:T(1,128)} %refs_6_.3) | copy-start | bytes 1540
  106.0 8.9 %collective-permute-start.5 = (bf16[3072,128]{1,0:T(8,128)(2,1)S(1)}, bf16[3072,128]{1,0:T(8,128)(2,1)S(1)}, u32[]{:S(2)}, u32[]{:S(2)}) collective-permute-start(bf16[3072,128]{1,0:T(8,128)(2,1)S(1)} %bitcast.24), channel_id=1, source_target_pairs={{0,16},{16,0},{1,17},{17,1},{2,18},{18,2},{3,19},{19,3},{4,20},{20... | collective-permute-start | bytes 2359304 | tf_op jit(solution)/shard_map/ppermute | solution.py:398
  133.6 4.4 %collective-permute-start.6 = (bf16[1536,128]{1,0:T(8,128)(2,1)S(1)}, bf16[1536,128]{1,0:T(8,128)(2,1)S(1)}, u32[]{:S(2)}, u32[]{:S(2)}) collective-permute-start(bf16[1536,128]{1,0:T(8,128)(2,1)S(1)} %bitcast.26), channel_id=1, source_target_pairs={{0,16},{16,0},{1,17},{17,1},{2,18},{18,2},{3,19},{19,3},{4,20},{20... | collective-permute-start | bytes 1179656 | tf_op jit(solution)/shard_map/ppermute | solution.py:398
  138.0 18.6 %copy-start.4 = (bf16[6,4096]{1,0:T(8,128)(2,1)S(1)}, bf16[6,4096]{1,0:T(8,128)(2,1)}, u32[]{:S(2)}) copy-start(bf16[6,4096]{1,0:T(8,128)(2,1)} %state.1) | copy-start | bytes 147460
Sparse Core Ops, SparseCore 0:
  19.6 71.5 all-gather.1

commit v11 on v10

--- a/solution.py
+++ b/solution.py
@@ -219,7 +219,7 @@
 SHIFTS = (0, 1, 3, 2)
 
 
-def plane_products(core, own, oth, rows):
+def plane_products(core, own, oth, rows, copies):
     left = []
     for z in range(4):
         mine, other = own[z], oth[z]
@@ -227,6 +227,7 @@
         second = jnp.where(core == 0, other, mine)
         left.append(jnp.concatenate([first, second], axis=1))
     for i in range(4):
+        copies[i].wait()
         mapped = None
         for z in range(4):
             right = jnp.concatenate([rows[i, z * 2], rows[i, z * 2 + 1]], axis=0)
@@ -237,9 +238,7 @@
 
 def plane_kernel(meta, own, oth, r0, r1, r2, r3, part_ref, rows, sem):
     copies = fetch(sem, *[(r, rows.at[i]) for i, r in enumerate((r0, r1, r2, r3))])
-    for copy in copies:
-        copy.wait()
-    for i, mapped in plane_products(meta[0], own, oth, rows):
+    for i, mapped in plane_products(meta[0], own, oth, rows, copies):
         part_ref[(meta[2] - SHIFTS[i]) & 3] = mapped
 
 
@@ -344,16 +343,16 @@
     token = lax.broadcasted_iota(jnp.int32, (256, TOK), 1)
     hit = (token == (row >> 3) * 6 + (row & 7)) & ((row & 7) < 6)
     lay = jnp.where(hit, jnp.ones((256, TOK), F32), jnp.zeros((256, TOK), F32)).astype(BF)
-    for copy in copies:
-        copy.wait()
     trace = jnp.zeros((1, 128), F32)
     laid = []
-    for i, mapped in plane_products(core, own, oth, rows):
+    for i, mapped in plane_products(core, own, oth, rows, copies):
         mapped = mapped * gates[columns[i]]
+        copies[5 + i].wait()
         terms = mapped[TOK:] * probe[i].astype(F32)
         trace = trace + jnp.sum(terms, axis=0, keepdims=True)
         part = mapped[:TOK]
         if i == 0:
+            copies[4].wait()
             part = part + vel1[...].astype(F32)
         laid.append(dot(lay, part.astype(BF)))
     trace = row_sum(trace)

time: 165 us -> 166 us (level)
  no operation moved by 1% of the time
where the time goes in v11:
time: 166 us; the launch traced here: 165 us
  blocking collectives  60.3 us (36%)
  starting transfers between devices  49.7 us (30%)
  Pallas kernels  24.8 us (15%)
  waiting for transfers between devices  14.8 us (9%)
  between operations  14.3 us (9%)
    ppermute x4, starting transfers between devices, swap(): return lax.ppermute(block, 'c', [(0, 1), (1, 0)])  25.9 us
    pallas_call x8, Pallas kernels, call(): pl.pallas_call(body, out_shape=out_shape, in_specs=in_specs, out_specs=[v...  24.8 us
    all_to_all x1, blocking collectives, per_device(): got = lax.all_to_all(columns, SEQ, 0, 0, tiled=True).reshape(32, 8, 512)  15.4 us
    all_to_all x1, blocking collectives, per_device(): own2 = lax.all_to_all(both.reshape(8 * TOK, 128), 'z', 0, 0, tiled=True)  13.8 us
    all_to_all x1, blocking collectives, along_y(): return lax.all_to_all(jnp.tile(block, (4, 1)), 'y', 0, 0, tiled=True)  11.9 us
    all_to_all x2, starting transfers between devices, along_z(): lax.all_to_all(copies.reshape(n * rows, lanes), 'z', 0, 0, tiled=True)  11.3 us
    all_to_all x1, blocking collectives, per_device(): parts = lax.all_to_all(parts.reshape(4 * TOK, 128), 'y', 0, 0, tiled=True)  9.88 us
    all_to_all x1, blocking collectives, along_z(): lax.all_to_all(copies.reshape(n * rows, lanes), 'z', 0, 0, tiled=True)  9.27 us
  transfers between devices with their start and end apart: 11, of which 9 were waited for; matrix products, arithmetic and copies ran while one was open for 1% of the time, Pallas kernels for 8%

profile of v11, /device:TPU:1, one launch (start us, length us, event | category | flops | bytes accessed | tf_op | source)
XLA Modules:
  0.0 164.9 jit_solution(16585780417170398059)
XLA Ops:
  7.2 2.4 %shard_map.95 = (bf16[4,8,3072]{2,1,0:T(8,128)(2,1)}, bf16[8,4096]{1,0:T(8,128)(2,1)}, bf16[4,256,128]{2,1,0:T(8,128)(2,1)}, bf16[4,256,128]{2,1,0:T(8,128)(2,1)...) custom-call(bf16[6,4096]{1,0:T(8,128)(2,1)} %state.1, bf16[6,4096]{1,0:T(8,128)(2,1)} %refs_1_.1, ...), custom_call_target="tpu_custom_call" | custom-call | tf_op jit(solution)/shard_map/pallas_call | solution.py:70
  9.6 6.5 %all-to-all-start = ((bf16[4,8,3072]{2,1,0:T(8,128)(2,1)}), bf16[4,8,3072]{2,1,0:T(8,128)(2,1)S(1)}, u32[]{:S(2)}, u32[]{:S(2)}) async-start(bf16[4,8,3072]{2,1,0:T(8,128)(2,1)} %get-tuple-element.19), calls=%async_computation | async-start | bytes 393216 | tf_op jit(solution)/shard_map/all_to_all | solution.py:389
  16.0 0.7 all-gather.2.cloned.1.call-update
  16.8 3.2 %collective-permute-start = (bf16[4,256,128]{2,1,0:T(8,128)(2,1)}, bf16[4,256,128]{2,1,0:T(8,128)(2,1)S(1)}, u32[]{:S(2)}, u32[]{:S(2)}) collective-permute-start(bf16[4,256,128]{2,1,0:T(8,128)(2,1)} %get-tuple-element.20), channel_id=1, source_target_pairs={{0,32},{32,64},{64,96},{96,0},{1,33},{33,65},{65,97},{97,1},{2,34}... | collective-permute-start | bytes 786440 | tf_op jit(solution)/shard_map/ppermute | solution.py:414
  20.0 3.4 %collective-permute-start.1 = (bf16[4,256,128]{2,1,0:T(8,128)(2,1)}, bf16[4,256,128]{2,1,0:T(8,128)(2,1)S(1)}, u32[]{:S(2)}, u32[]{:S(2)}) collective-permute-start(bf16[4,256,128]{2,1,0:T(8,128)(2,1)} %get-tuple-element.21), channel_id=1, source_target_pairs={{0,96},{32,0},{64,32},{96,64},{1,97},{33,1},{65,33},{97,65},{2,98}... | collective-permute-start | bytes 786440 | tf_op jit(solution)/shard_map/ppermute | solution.py:414
  23.3 2.2 %collective-permute-done = bf16[4,256,128]{2,1,0:T(8,128)(2,1)S(1)} collective-permute-done((bf16[4,256,128]{2,1,0:T(8,128)(2,1)}, bf16[4,256,128]{2,1,0:T(8,128)(2,1)S(1)}, u32[]{:S(2)}, u32[]{:S(2)}) %collective-permute-start) | collective-permute-done | bytes 262176 | tf_op jit(solution)/shard_map/ppermute | solution.py:414
  25.5 2.1 %collective-permute-done.1 = bf16[4,256,128]{2,1,0:T(8,128)(2,1)S(1)} collective-permute-done((bf16[4,256,128]{2,1,0:T(8,128)(2,1)}, bf16[4,256,128]{2,1,0:T(8,128)(2,1)S(1)}, u32[]{:S(2)}, u32[]{:S(2)}) %collective-permute-start.1) | collective-permute-done | bytes 262176 | tf_op jit(solution)/shard_map/ppermute | solution.py:414
  27.7 11.9 %all_to_all.65 = bf16[4,32,3072]{2,1,0:T(8,128)(2,1)S(1)} all-to-all(bf16[4,32,3072]{2,1,0:T(8,128)(2,1)S(1)} %tile.6), channel_id=1, replica_groups=mesh['z'=4,'y'=4,'c'=2,'w'=4,'x'=4] {'y'}, dimensions={0} | all-to-all | bytes 1572864 | tf_op jit(solution)/shard_map/all_to_all | solution.py:393
  39.6 9.8 %collective-permute-start.2 = (bf16[128,3072]{1,0:T(8,128)(2,1)S(1)}, bf16[128,3072]{1,0:T(8,128)(2,1)S(1)}, u32[]{:S(2)}, u32[]{:S(2)}) collective-permute-start(bf16[128,3072]{1,0:T(8,128)(2,1)S(1)} %bitcast.21), channel_id=1, source_target_pairs={{0,16},{16,0},{1,17},{17,1},{2,18},{18,2},{3,19},{19,3},{4,20},{20... | collective-permute-start | bytes 2359304 | tf_op jit(solution)/shard_map/ppermute | solution.py:397
  49.4 1.9 %collective-permute-done.2.refs_1_ = bf16[128,3072]{1,0:T(8,128)(2,1)S(1)} collective-permute-done((bf16[128,3072]{1,0:T(8,128)(2,1)S(1)}, bf16[128,3072]{1,0:T(8,128)(2,1)S(1)}, u32[]{:S(2)}, u32[]{:S(2)}) %collective-permute-start.2) | collective-permute-done | bytes 786464 | tf_op jit(solution)/shard_map/ppermute | solution.py:397
  51.3 4.6 %shard_map.96 = (bf16[4,192,128]{2,1,0:T(8,128)(2,1)}, bf16[192,128]{1,0:T(8,128)(2,1)S(1)}) custom-call(bf16[128,3072]{1,0:T(8,128)(2,1)S(1)} %bitcast.22, bf16[128,3072]{1,0:T(8,128)(2,1)S(1)} %collective-permute-done.2.refs_1_, bf16[32,128,384]{2,1,0:T(8,128)(2,1)} %bitcast.45, f32[32,1,128]{2,1,0:T(1,128)S(1)} %bitcast.41, f32[1,128]{1,0:T(1,128)S(1)} %copy-done.8, ...), custom_call_target="tpu_custom_call" | custom-call | tf_op jit(solution)/shard_map/pallas_call | solution.py:70
  55.9 4.8 %all-to-all-start.2 = ((bf16[4,192,128]{2,1,0:T(8,128)(2,1)}), bf16[4,192,128]{2,1,0:T(8,128)(2,1)S(1)}, u32[]{:S(2)}, u32[]{:S(2)}) async-start(bf16[4,192,128]{2,1,0:T(8,128)(2,1)} %get-tuple-element.23), calls=%async_computation.2 | async-start | bytes 393216 | tf_op jit(solution)/shard_map/all_to_all | solution.py:389
  60.7 2.5 %collective-permute-start.4 = (bf16[4,256,128]{2,1,0:T(8,128)(2,1)S(1)}, bf16[4,256,128]{2,1,0:T(8,128)(2,1)S(1)}, u32[]{:S(2)}, u32[]{:S(2)}) collective-permute-start(bf16[4,256,128]{2,1,0:T(8,128)(2,1)S(1)} %copy-done.12), channel_id=1, source_target_pairs={{0,64},{32,96},{64,0},{96,32},{1,65},{33,97},{65,1},{97,33},{2,66}... | collective-permute-start | bytes 786440 | tf_op jit(solution)/shard_map/ppermute | solution.py:414
  63.2 3.0 %all-to-all-done.2.refs_0_ = bf16[4,192,128]{2,1,0:T(8,128)(2,1)S(1)} async-done(((bf16[4,192,128]{2,1,0:T(8,128)(2,1)}), bf16[4,192,128]{2,1,0:T(8,128)(2,1)S(1)}, u32[]{:S(2)}, u32[]{:S(2)}) %all-to-all-start.2) | async-done | bytes 196640 | tf_op jit(solution)/shard_map/all_to_all | solution.py:389
  66.2 5.9 %collective-permute-start.3 = (bf16[768,128]{1,0:T(8,128)(2,1)S(1)}, bf16[768,128]{1,0:T(8,128)(2,1)S(1)}, u32[]{:S(2)}, u32[]{:S(2)}) collective-permute-start(bf16[768,128]{1,0:T(8,128)(2,1)S(1)} %bitcast.36), channel_id=1, source_target_pairs={{0,16},{16,0},{1,17},{17,1},{2,18},{18,2},{3,19},{19,3},{4,20},{20... | collective-permute-start | bytes 589832 | tf_op jit(solution)/shard_map/ppermute | solution.py:397
  72.4 0.7 collective-permute-done.3
  73.2 1.2 shard_map.97
  74.4 9.9 %all_to_all.66.refs_0_ = f32[4,192,128]{2,1,0:T(8,128)S(1)} all-to-all(f32[4,192,128]{2,1,0:T(8,128)S(1)} %shard_map.97), channel_id=1, replica_groups=mesh['z'=4,'y'=4,'c'=2,'w'=4,'x'=4] {'y'}, dimensions={0} | all-to-all | bytes 786432 | tf_op jit(solution)/shard_map/all_to_all | solution.py:431
  84.3 9.3 %all_to_all.67 = bf16[4,192,128]{2,1,0:T(8,128)(2,1)S(1)} all-to-all(bf16[4,192,128]{2,1,0:T(8,128)(2,1)S(1)} %get-tuple-element.29.refs_7_), channel_id=1, replica_groups=mesh['z'=4,'y'=4,'c'=2,'w'=4,'x'=4] {'z'}, dimensions={0} | all-to-all | bytes 393216 | tf_op jit(solution)/shard_map/all_to_all | solution.py:389
  93.6 1.0 tile.8
  94.6 3.5 %all-to-all-start.5 = ((bf16[4,768,128]{2,1,0:T(8,128)(2,1)}), bf16[4,768,128]{2,1,0:T(8,128)(2,1)S(1)}, u32[]{:S(2)}, u32[]{:S(2)}) async-start(bf16[4,768,128]{2,1,0:T(8,128)(2,1)} %tile.8), calls=%async_computation.5 | async-start | bytes 1572864 | tf_op jit(solution)/shard_map/all_to_all | solution.py:393
  98.2 7.6 %shard_map.99.refs_2_.refs_8_ = bf16[34,192,128]{2,1,0:T(8,128)(2,1)} custom-call(bf16[128,3072]{1,0:T(8,128)(2,1)} %bitcast.23, bf16[128,3072]{1,0:T(8,128)(2,1)} %copy-done.1, bf16[256,4096]{1,0:T(8,128)(2,1)} %all-gather.2.cloned.1.call-done.refs_2_, bf16[32,128,384]{2,1,0:T(8,128)(2,1)} %bitcast.46, f32[32,1,128]{2,1,0:T(1,128)} %bitcast.40, ...), custom_call_target="tpu_custom_call" | custom-call | tf_op jit(solution)/shard_map/pallas_call | solution.py:70
  105.8 0.6 all-to-all-done.5
  106.4 7.1 %collective-permute-start.5 = (bf16[3072,128]{1,0:T(8,128)(2,1)S(1)}, bf16[3072,128]{1,0:T(8,128)(2,1)S(1)}, u32[]{:S(2)}, u32[]{:S(2)}) collective-permute-start(bf16[3072,128]{1,0:T(8,128)(2,1)S(1)} %bitcast.24), channel_id=1, source_target_pairs={{0,16},{16,0},{1,17},{17,1},{2,18},{18,2},{3,19},{19,3},{4,20},{20... | collective-permute-start | bytes 2359304 | tf_op jit(solution)/shard_map/ppermute | solution.py:397
  113.5 1.9 %collective-permute-done.5 = bf16[3072,128]{1,0:T(8,128)(2,1)S(1)} collective-permute-done((bf16[3072,128]{1,0:T(8,128)(2,1)S(1)}, bf16[3072,128]{1,0:T(8,128)(2,1)S(1)}, u32[]{:S(2)}, u32[]{:S(2)}) %collective-permute-start.5) | collective-permute-done | bytes 786464 | tf_op jit(solution)/shard_map/ppermute | solution.py:397
  115.4 4.8 %shard_map.100 = bf16[4,384,128]{2,1,0:T(8,128)(2,1)S(1)} custom-call(bf16[16,192,128]{2,1,0:T(8,128)(2,1)S(1)} %bitcast.25, bf16[16,192,128]{2,1,0:T(8,128)(2,1)S(1)} %bitcast.37, bf16[34,192,128]{2,1,0:T(8,128)(2,1)} %shard_map.99.refs_2_.refs_8_, bf16[32,128,384]{2,1,0:T(8,128)(2,1)} %bitcast.47, f32[32,1,128]{2,1,0:T(1,128)S(1)} %bitcast.42, ...), custom_call_target="tpu_custom_call" | custom-call | tf_op jit(solution)/shard_map/pallas_call | solution.py:70
  120.2 13.8 %all_to_all.68.refs_0_ = bf16[4,384,128]{2,1,0:T(8,128)(2,1)S(1)} all-to-all(bf16[4,384,128]{2,1,0:T(8,128)(2,1)S(1)} %shard_map.100), channel_id=1, replica_groups=mesh['z'=4,'y'=4,'c'=2,'w'=4,'x'=4] {'z'}, dimensions={0} | all-to-all | bytes 786432 | tf_op jit(solution)/shard_map/all_to_all | solution.py:454
  134.0 3.1 %collective-permute-start.6 = (bf16[1536,128]{1,0:T(8,128)(2,1)S(1)}, bf16[1536,128]{1,0:T(8,128)(2,1)S(1)}, u32[]{:S(2)}, u32[]{:S(2)}) collective-permute-start(bf16[1536,128]{1,0:T(8,128)(2,1)S(1)} %bitcast.26), channel_id=1, source_target_pairs={{0,16},{16,0},{1,17},{17,1},{2,18},{18,2},{3,19},{19,3},{4,20},{20... | collective-permute-start | bytes 1179656 | tf_op jit(solution)/shard_map/ppermute | solution.py:397
  137.1 1.3 collective-permute-done.6
  138.4 3.6 %shard_map.101 = bf16[256,512]{1,0:T(8,128)(2,1)S(1)} custom-call(bf16[4,384,128]{2,1,0:T(8,128)(2,1)S(1)} %all_to_all.68.refs_0_, bf16[4,384,128]{2,1,0:T(8,128)(2,1)S(1)} %bitcast.38, bf16[8,128,128]{2,1,0:T(8,128)(2,1)S(1)} %bitcast.28, bf16[8,128,128]{2,1,0:T(8,128)(2,1)S(1)} %bitcast.30, bf16[8,128,128]{2,1,0:T(8,128)(2,1)S(1)} %bitcast.32, ...), custom_call_target="tpu_custom_call" | custom-call | tf_op jit(solution)/shard_map/pallas_call | solution.py:70
  142.0 15.4 %all_to_all.69.got = bf16[32,8,512]{2,1,0:T(8,128)(2,1)S(1)} all-to-all(bf16[32,8,512]{2,1,0:T(8,128)(2,1)S(1)} %bitcast.35), channel_id=1, replica_groups=mesh['z'=4,'y'=4,'c'=2,'w'=4,'x'=4] {'z','y','c'}, dimensions={0} | all-to-all | bytes 524288 | tf_op jit(solution)/shard_map/all_to_all | solution.py:466
  157.4 0.7 shard_map.102
  (32 shorter events, 0.5 us)
Async XLA Ops:
  7.2 44.1 %copy-start.5 = (f32[4096]{0:T(1024)S(1)}, f32[4096]{0:T(1024)}, u32[]{:S(2)}) copy-start(f32[4096]{0:T(1024)} %param.10) | copy-start | bytes 49156
  7.2 44.1 %copy-start.8 = (f32[1,128]{1,0:T(1,128)S(1)}, f32[1,128]{1,0:T(1,128)}, u32[]{:S(2)}) copy-start(f32[1,128]{1,0:T(1,128)} %refs_5_.5) | copy-start | bytes 1540
  7.2 44.1 %copy-start.10 = (f32[1,128]{1,0:T(1,128)S(1)}, f32[1,128]{1,0:T(1,128)}, u32[]{:S(2)}) copy-start(f32[1,128]{1,0:T(1,128)} %refs_6_.3) | copy-start | bytes 1540
  9.6 18.0 %all-to-all-start = ((bf16[4,8,3072]{2,1,0:T(8,128)(2,1)}), bf16[4,8,3072]{2,1,0:T(8,128)(2,1)S(1)}, u32[]{:S(2)}, u32[]{:S(2)}) async-start(bf16[4,8,3072]{2,1,0:T(8,128)(2,1)} %get-tuple-element.19), calls=%async_computation | async-start | bytes 393216 | tf_op jit(solution)/shard_map/all_to_all | solution.py:389
  16.0 82.1 %all-gather.2.cloned.1.call-start = ((), (), s32[]{:S(2)}) async-start(), calls=%async_computation.8 | async-start | bytes 2162688 | tf_op jit(solution)/shard_map/all_gather | solution.py:411
  16.8 8.8 %collective-permute-start = (bf16[4,256,128]{2,1,0:T(8,128)(2,1)}, bf16[4,256,128]{2,1,0:T(8,128)(2,1)S(1)}, u32[]{:S(2)}, u32[]{:S(2)}) collective-permute-start(bf16[4,256,128]{2,1,0:T(8,128)(2,1)} %get-tuple-element.20), channel_id=1, source_target_pairs={{0,32},{32,64},{64,96},{96,0},{1,33},{33,65},{65,97},{97,1},{2,34}... | collective-permute-start | bytes 786440 | tf_op jit(solution)/shard_map/ppermute | solution.py:414
  20.0 7.6 %collective-permute-start.1 = (bf16[4,256,128]{2,1,0:T(8,128)(2,1)}, bf16[4,256,128]{2,1,0:T(8,128)(2,1)S(1)}, u32[]{:S(2)}, u32[]{:S(2)}) collective-permute-start(bf16[4,256,128]{2,1,0:T(8,128)(2,1)} %get-tuple-element.21), channel_id=1, source_target_pairs={{0,96},{32,0},{64,32},{96,64},{1,97},{33,1},{65,33},{97,65},{2,98}... | collective-permute-start | bytes 786440 | tf_op jit(solution)/shard_map/ppermute | solution.py:414
  39.6 16.3 %copy-start = (bf16[4,32,3072]{2,1,0:T(8,128)(2,1)}, bf16[4,32,3072]{2,1,0:T(8,128)(2,1)S(1)}, u32[]{:S(2)}) copy-start(bf16[4,32,3072]{2,1,0:T(8,128)(2,1)S(1)} %all_to_all.65) | copy-start | bytes 2359300
  39.6 11.7 %collective-permute-start.2 = (bf16[128,3072]{1,0:T(8,128)(2,1)S(1)}, bf16[128,3072]{1,0:T(8,128)(2,1)S(1)}, u32[]{:S(2)}, u32[]{:S(2)}) collective-permute-start(bf16[128,3072]{1,0:T(8,128)(2,1)S(1)} %bitcast.21), channel_id=1, source_target_pairs={{0,16},{16,0},{1,17},{17,1},{2,18},{18,2},{3,19},{19,3},{4,20},{20... | collective-permute-start | bytes 2359304 | tf_op jit(solution)/shard_map/ppermute | solution.py:397
  51.3 4.6 %copy-start.1 = (bf16[128,3072]{1,0:T(8,128)(2,1)}, bf16[128,3072]{1,0:T(8,128)(2,1)S(1)}, u32[]{:S(2)}) copy-start(bf16[128,3072]{1,0:T(8,128)(2,1)S(1)} %collective-permute-done.2.refs_1_) | copy-start | bytes 2359300
  51.3 9.4 %copy-start.12 = (bf16[4,256,128]{2,1,0:T(8,128)(2,1)S(1)}, bf16[4,256,128]{2,1,0:T(8,128)(2,1)}, u32[]{:S(2)}) copy-start(bf16[4,256,128]{2,1,0:T(8,128)(2,1)} %get-tuple-element.27) | copy-start | bytes 786436
  51.3 21.9 %copy-start.2 = (bf16[4,256,128]{2,1,0:T(8,128)(2,1)S(1)}, bf16[4,256,128]{2,1,0:T(8,128)(2,1)}, u32[]{:S(2)}) copy-start(bf16[4,256,128]{2,1,0:T(8,128)(2,1)} %get-tuple-element.24) | copy-start | bytes 786436
  55.9 28.4 %copy-start.7 = (f32[4096]{0:T(1024)S(1)}, f32[4096]{0:T(1024)}, u32[]{:S(2)}) copy-start(f32[4096]{0:T(1024)} %param.15) | copy-start | bytes 49156
  55.9 10.3 %all-to-all-start.2 = ((bf16[4,192,128]{2,1,0:T(8,128)(2,1)}), bf16[4,192,128]{2,1,0:T(8,128)(2,1)S(1)}, u32[]{:S(2)}, u32[]{:S(2)}) async-start(bf16[4,192,128]{2,1,0:T(8,128)(2,1)} %get-tuple-element.23), calls=%async_computation.2 | async-start | bytes 393216 | tf_op jit(solution)/shard_map/all_to_all | solution.py:389
  60.7 11.7 %collective-permute-start.4 = (bf16[4,256,128]{2,1,0:T(8,128)(2,1)S(1)}, bf16[4,256,128]{2,1,0:T(8,128)(2,1)S(1)}, u32[]{:S(2)}, u32[]{:S(2)}) collective-permute-start(bf16[4,256,128]{2,1,0:T(8,128)(2,1)S(1)} %copy-done.12), channel_id=1, source_target_pairs={{0,64},{32,96},{64,0},{96,32},{1,65},{33,97},{65,1},{97,33},{2,66}... | collective-permute-start | bytes 786440 | tf_op jit(solution)/shard_map/ppermute | solution.py:414
  66.2 7.0 %collective-permute-start.3 = (bf16[768,128]{1,0:T(8,128)(2,1)S(1)}, bf16[768,128]{1,0:T(8,128)(2,1)S(1)}, u32[]{:S(2)}, u32[]{:S(2)}) collective-permute-start(bf16[768,128]{1,0:T(8,128)(2,1)S(1)} %bitcast.36), channel_id=1, source_target_pairs={{0,16},{16,0},{1,17},{17,1},{2,18},{18,2},{3,19},{19,3},{4,20},{20... | collective-permute-start | bytes 589832 | tf_op jit(solution)/shard_map/ppermute | solution.py:397
  84.3 13.8 %copy-start.3 = (bf16[4,192,128]{2,1,0:T(8,128)(2,1)}, bf16[4,192,128]{2,1,0:T(8,128)(2,1)S(1)}, u32[]{:S(2)}) copy-start(bf16[4,192,128]{2,1,0:T(8,128)(2,1)S(1)} %get-tuple-element.29.refs_7_) | copy-start | bytes 589828
  94.6 11.8 %all-to-all-start.5 = ((bf16[4,768,128]{2,1,0:T(8,128)(2,1)}), bf16[4,768,128]{2,1,0:T(8,128)(2,1)S(1)}, u32[]{:S(2)}, u32[]{:S(2)}) async-start(bf16[4,768,128]{2,1,0:T(8,128)(2,1)} %tile.8), calls=%async_computation.5 | async-start | bytes 1572864 | tf_op jit(solution)/shard_map/all_to_all | solution.py:393
  98.1 17.3 %copy-start.6 = (f32[4096]{0:T(1024)S(1)}, f32[4096]{0:T(1024)}, u32[]{:S(2)}) copy-start(f32[4096]{0:T(1024)} %param.10) | copy-start | bytes 49156
  98.1 17.3 %copy-start.9 = (f32[1,128]{1,0:T(1,128)S(1)}, f32[1,128]{1,0:T(1,128)}, u32[]{:S(2)}) copy-start(f32[1,128]{1,0:T(1,128)} %refs_5_.5) | copy-start | bytes 1540
  98.1 17.3 %copy-start.11 = (f32[1,128]{1,0:T(1,128)S(1)}, f32[1,128]{1,0:T(1,128)}, u32[]{:S(2)}) copy-start(f32[1,128]{1,0:T(1,128)} %refs_6_.3) | copy-start | bytes 1540
  106.4 9.0 %collective-permute-start.5 = (bf16[3072,128]{1,0:T(8,128)(2,1)S(1)}, bf16[3072,128]{1,0:T(8,128)(2,1)S(1)}, u32[]{:S(2)}, u32[]{:S(2)}) collective-permute-start(bf16[3072,128]{1,0:T(8,128)(2,1)S(1)} %bitcast.24), channel_id=1, source_target_pairs={{0,16},{16,0},{1,17},{17,1},{2,18},{18,2},{3,19},{19,3},{4,20},{20... | collective-permute-start | bytes 2359304 | tf_op jit(solution)/shard_map/ppermute | solution.py:397
  134.0 4.4 %collective-permute-start.6 = (bf16[1536,128]{1,0:T(8,128)(2,1)S(1)}, bf16[1536,128]{1,0:T(8,128)(2,1)S(1)}, u32[]{:S(2)}, u32[]{:S(2)}) collective-permute-start(bf16[1536,128]{1,0:T(8,128)(2,1)S(1)} %bitcast.26), channel_id=1, source_target_pairs={{0,16},{16,0},{1,17},{17,1},{2,18},{18,2},{3,19},{19,3},{4,20},{20... | collective-permute-start | bytes 1179656 | tf_op jit(solution)/shard_map/ppermute | solution.py:397
  138.4 18.9 %copy-start.4 = (bf16[6,4096]{1,0:T(8,128)(2,1)S(1)}, bf16[6,4096]{1,0:T(8,128)(2,1)}, u32[]{:S(2)}) copy-start(bf16[6,4096]{1,0:T(8,128)(2,1)} %state.1) | copy-start | bytes 147460
Sparse Core Ops, SparseCore 0:
  19.6 71.2 all-gather.1

commit v12 on v10

--- a/solution.py
+++ b/solution.py
@@ -139,13 +139,10 @@
     return dot(probs, val).astype(BF), dot(d_probs.astype(BF), val) + dot(probs, dv)
 
 
-def pack_kernel(
-    meta, state_hbm, probe_hbm, out_map, state_ref, probe_ref, s0, s1, s2, s3, state, probe, sem
-):
+def pack_kernel(meta, state, probe, out_map, state_ref, probe_ref, s0, s1, s2, s3, sem):
     shifted = [(out_map.at[:, (meta[2] + k) & 3], to) for k, to in enumerate((s0, s1, s2, s3))]
-    copies = fetch(sem, (state_hbm, state), (probe_hbm, probe), *shifted)
-    for i, (source, write) in enumerate(((state, None), (probe, probe_ref))):
-        copies[i].wait()
+    copies = fetch(sem, *shifted)
+    for source, write in ((state, None), (probe, probe_ref)):
         main = source[:, :3072]
         sixth = jnp.concatenate([source[q : q + 1, 3072:] for q in range(3)], axis=1)
         seventh = jnp.concatenate([source[q : q + 1, 3072:] for q in range(3, 6)], axis=1)
@@ -156,7 +153,7 @@
         else:
             write[:, :3072] = whole
             write[:, 3072:] = whole[:, :1024]
-    for copy in copies[2:]:
+    for copy in copies:
         copy.wait()
 
 
@@ -405,8 +402,8 @@
 
     packed_state, packed_probe, *sends = call(
         pack_kernel, [shape((4, 8, 3072)), shape((8, 4096))] + [shape((4, 256, 128))] * 4,
-        True, (state,), (probe,), (out_map.reshape(4, 4, 256, 128),),
-        scratch=[pltpu.VMEM((6, 4096), BF), pltpu.VMEM((6, 4096), BF), sems(6)],
+        True, state, probe, (out_map.reshape(4, 4, 256, 128),),
+        scratch=[sems(4)],
         vmem_mib=FULL,
     )
     probe_all = lax.all_gather(packed_probe, SEQ, axis=0, tiled=True)

time: 165 us -> 166 us (level)
  no operation moved by 1% of the time
where the time goes in v12:
time: 166 us; the launch traced here: 165 us
  blocking collectives  60.3 us (36%)
  starting transfers between devices  49.4 us (30%)
  Pallas kernels  24.8 us (15%)
  waiting for transfers between devices  15.1 us (9%)
  between operations  14.3 us (9%)
    ppermute x4, starting transfers between devices, swap(): return lax.ppermute(block, 'c', [(0, 1), (1, 0)])  25.6 us
    pallas_call x8, Pallas kernels, call(): pl.pallas_call(body, out_shape=out_shape, in_specs=in_specs, out_specs=[v...  24.8 us
    all_to_all x1, blocking collectives, per_device(): got = lax.all_to_all(columns, SEQ, 0, 0, tiled=True).reshape(32, 8, 512)  15.4 us
    all_to_all x1, blocking collectives, per_device(): own2 = lax.all_to_all(both.reshape(8 * TOK, 128), 'z', 0, 0, tiled=True)  13.8 us
    all_to_all x1, blocking collectives, along_y(): return lax.all_to_all(jnp.tile(block, (4, 1)), 'y', 0, 0, tiled=True)  11.9 us
    all_to_all x2, starting transfers between devices, along_z(): lax.all_to_all(copies.reshape(n * rows, lanes), 'z', 0, 0, tiled=True)  11.3 us
    all_to_all x1, blocking collectives, per_device(): parts = lax.all_to_all(parts.reshape(4 * TOK, 128), 'y', 0, 0, tiled=True)  9.97 us
    all_to_all x1, blocking collectives, along_z(): lax.all_to_all(copies.reshape(n * rows, lanes), 'z', 0, 0, tiled=True)  9.23 us
  transfers between devices with their start and end apart: 11, of which 9 were waited for; matrix products, arithmetic and copies ran while one was open for 1% of the time, Pallas kernels for 8%

profile of v12, /device:TPU:1, one launch (start us, length us, event | category | flops | bytes accessed | tf_op | source)
XLA Modules:
  0.0 164.9 jit_solution(16387535378371761009)
XLA Ops:
  7.2 3.2 %shard_map.95 = (bf16[4,8,3072]{2,1,0:T(8,128)(2,1)}, bf16[8,4096]{1,0:T(8,128)(2,1)}, bf16[4,256,128]{2,1,0:T(8,128)(2,1)}, bf16[4,256,128]{2,1,0:T(8,128)(2,1)...) custom-call(bf16[6,4096]{1,0:T(8,128)(2,1)} %state.1, bf16[6,4096]{1,0:T(8,128)(2,1)} %refs_1_.1, ...), custom_call_target="tpu_custom_call" | custom-call | tf_op jit(solution)/shard_map/pallas_call | solution.py:70
  10.4 6.5 %all-to-all-start = ((bf16[4,8,3072]{2,1,0:T(8,128)(2,1)}), bf16[4,8,3072]{2,1,0:T(8,128)(2,1)S(1)}, u32[]{:S(2)}, u32[]{:S(2)}) async-start(bf16[4,8,3072]{2,1,0:T(8,128)(2,1)} %get-tuple-element.19), calls=%async_computation | async-start | bytes 393216 | tf_op jit(solution)/shard_map/all_to_all | solution.py:387
  16.8 0.7 all-gather.2.cloned.1.call-update
  17.5 3.2 %collective-permute-start = (bf16[4,256,128]{2,1,0:T(8,128)(2,1)}, bf16[4,256,128]{2,1,0:T(8,128)(2,1)S(1)}, u32[]{:S(2)}, u32[]{:S(2)}) collective-permute-start(bf16[4,256,128]{2,1,0:T(8,128)(2,1)} %get-tuple-element.20), channel_id=1, source_target_pairs={{0,32},{32,64},{64,96},{96,0},{1,33},{33,65},{65,97},{97,1},{2,34}... | collective-permute-start | bytes 786440 | tf_op jit(solution)/shard_map/ppermute | solution.py:412
  20.8 3.4 %collective-permute-start.1 = (bf16[4,256,128]{2,1,0:T(8,128)(2,1)}, bf16[4,256,128]{2,1,0:T(8,128)(2,1)S(1)}, u32[]{:S(2)}, u32[]{:S(2)}) collective-permute-start(bf16[4,256,128]{2,1,0:T(8,128)(2,1)} %get-tuple-element.21), channel_id=1, source_target_pairs={{0,96},{32,0},{64,32},{96,64},{1,97},{33,1},{65,33},{97,65},{2,98}... | collective-permute-start | bytes 786440 | tf_op jit(solution)/shard_map/ppermute | solution.py:412
  24.1 2.2 %collective-permute-done = bf16[4,256,128]{2,1,0:T(8,128)(2,1)S(1)} collective-permute-done((bf16[4,256,128]{2,1,0:T(8,128)(2,1)}, bf16[4,256,128]{2,1,0:T(8,128)(2,1)S(1)}, u32[]{:S(2)}, u32[]{:S(2)}) %collective-permute-start) | collective-permute-done | bytes 262176 | tf_op jit(solution)/shard_map/ppermute | solution.py:412
  26.3 2.1 %collective-permute-done.1 = bf16[4,256,128]{2,1,0:T(8,128)(2,1)S(1)} collective-permute-done((bf16[4,256,128]{2,1,0:T(8,128)(2,1)}, bf16[4,256,128]{2,1,0:T(8,128)(2,1)S(1)}, u32[]{:S(2)}, u32[]{:S(2)}) %collective-permute-start.1) | collective-permute-done | bytes 262176 | tf_op jit(solution)/shard_map/ppermute | solution.py:412
  28.5 11.9 %all_to_all.65 = bf16[4,32,3072]{2,1,0:T(8,128)(2,1)S(1)} all-to-all(bf16[4,32,3072]{2,1,0:T(8,128)(2,1)S(1)} %tile.6), channel_id=1, replica_groups=mesh['z'=4,'y'=4,'c'=2,'w'=4,'x'=4] {'y'}, dimensions={0} | all-to-all | bytes 1572864 | tf_op jit(solution)/shard_map/all_to_all | solution.py:391
  40.4 9.8 %collective-permute-start.2 = (bf16[128,3072]{1,0:T(8,128)(2,1)S(1)}, bf16[128,3072]{1,0:T(8,128)(2,1)S(1)}, u32[]{:S(2)}, u32[]{:S(2)}) collective-permute-start(bf16[128,3072]{1,0:T(8,128)(2,1)S(1)} %bitcast.21), channel_id=1, source_target_pairs={{0,16},{16,0},{1,17},{17,1},{2,18},{18,2},{3,19},{19,3},{4,20},{20... | collective-permute-start | bytes 2359304 | tf_op jit(solution)/shard_map/ppermute | solution.py:395
  50.2 1.9 %collective-permute-done.2.refs_1_ = bf16[128,3072]{1,0:T(8,128)(2,1)S(1)} collective-permute-done((bf16[128,3072]{1,0:T(8,128)(2,1)S(1)}, bf16[128,3072]{1,0:T(8,128)(2,1)S(1)}, u32[]{:S(2)}, u32[]{:S(2)}) %collective-permute-start.2) | collective-permute-done | bytes 786464 | tf_op jit(solution)/shard_map/ppermute | solution.py:395
  52.1 4.6 %shard_map.96 = (bf16[4,192,128]{2,1,0:T(8,128)(2,1)}, bf16[192,128]{1,0:T(8,128)(2,1)S(1)}) custom-call(bf16[128,3072]{1,0:T(8,128)(2,1)S(1)} %bitcast.22, bf16[128,3072]{1,0:T(8,128)(2,1)S(1)} %collective-permute-done.2.refs_1_, bf16[32,128,384]{2,1,0:T(8,128)(2,1)} %bitcast.45, f32[32,1,128]{2,1,0:T(1,128)S(1)} %bitcast.41, f32[1,128]{1,0:T(1,128)S(1)} %copy-done.8, ...), custom_call_target="tpu_custom_call" | custom-call | tf_op jit(solution)/shard_map/pallas_call | solution.py:70
  56.7 4.8 %all-to-all-start.2 = ((bf16[4,192,128]{2,1,0:T(8,128)(2,1)}), bf16[4,192,128]{2,1,0:T(8,128)(2,1)S(1)}, u32[]{:S(2)}, u32[]{:S(2)}) async-start(bf16[4,192,128]{2,1,0:T(8,128)(2,1)} %get-tuple-element.23), calls=%async_computation.2 | async-start | bytes 393216 | tf_op jit(solution)/shard_map/all_to_all | solution.py:387
  61.5 2.5 %collective-permute-start.4 = (bf16[4,256,128]{2,1,0:T(8,128)(2,1)S(1)}, bf16[4,256,128]{2,1,0:T(8,128)(2,1)S(1)}, u32[]{:S(2)}, u32[]{:S(2)}) collective-permute-start(bf16[4,256,128]{2,1,0:T(8,128)(2,1)S(1)} %copy-done.12), channel_id=1, source_target_pairs={{0,64},{32,96},{64,0},{96,32},{1,65},{33,97},{65,1},{97,33},{2,66}... | collective-permute-start | bytes 786440 | tf_op jit(solution)/shard_map/ppermute | solution.py:412
  64.0 3.3 %all-to-all-done.2.refs_0_ = bf16[4,192,128]{2,1,0:T(8,128)(2,1)S(1)} async-done(((bf16[4,192,128]{2,1,0:T(8,128)(2,1)}), bf16[4,192,128]{2,1,0:T(8,128)(2,1)S(1)}, u32[]{:S(2)}, u32[]{:S(2)}) %all-to-all-start.2) | async-done | bytes 196640 | tf_op jit(solution)/shard_map/all_to_all | solution.py:387
  67.3 5.7 %collective-permute-start.3 = (bf16[768,128]{1,0:T(8,128)(2,1)S(1)}, bf16[768,128]{1,0:T(8,128)(2,1)S(1)}, u32[]{:S(2)}, u32[]{:S(2)}) collective-permute-start(bf16[768,128]{1,0:T(8,128)(2,1)S(1)} %bitcast.36), channel_id=1, source_target_pairs={{0,16},{16,0},{1,17},{17,1},{2,18},{18,2},{3,19},{19,3},{4,20},{20... | collective-permute-start | bytes 589832 | tf_op jit(solution)/shard_map/ppermute | solution.py:395
  73.5 0.5 collective-permute-done.3
  74.0 0.7 shard_map.97
  74.7 10.0 %all_to_all.66.refs_0_ = f32[4,192,128]{2,1,0:T(8,128)S(1)} all-to-all(f32[4,192,128]{2,1,0:T(8,128)S(1)} %shard_map.97), channel_id=1, replica_groups=mesh['z'=4,'y'=4,'c'=2,'w'=4,'x'=4] {'y'}, dimensions={0} | all-to-all | bytes 786432 | tf_op jit(solution)/shard_map/all_to_all | solution.py:429
  84.8 9.2 %all_to_all.67 = bf16[4,192,128]{2,1,0:T(8,128)(2,1)S(1)} all-to-all(bf16[4,192,128]{2,1,0:T(8,128)(2,1)S(1)} %get-tuple-element.29.refs_7_), channel_id=1, replica_groups=mesh['z'=4,'y'=4,'c'=2,'w'=4,'x'=4] {'z'}, dimensions={0} | all-to-all | bytes 393216 | tf_op jit(solution)/shard_map/all_to_all | solution.py:387
  94.0 1.0 tile.8
  95.0 3.5 %all-to-all-start.5 = ((bf16[4,768,128]{2,1,0:T(8,128)(2,1)}), bf16[4,768,128]{2,1,0:T(8,128)(2,1)S(1)}, u32[]{:S(2)}, u32[]{:S(2)}) async-start(bf16[4,768,128]{2,1,0:T(8,128)(2,1)} %tile.8), calls=%async_computation.5 | async-start | bytes 1572864 | tf_op jit(solution)/shard_map/all_to_all | solution.py:391
  98.6 7.6 %shard_map.99.refs_2_.refs_8_ = bf16[34,192,128]{2,1,0:T(8,128)(2,1)} custom-call(bf16[128,3072]{1,0:T(8,128)(2,1)} %bitcast.23, bf16[128,3072]{1,0:T(8,128)(2,1)} %copy-done.1, bf16[256,4096]{1,0:T(8,128)(2,1)} %all-gather.2.cloned.1.call-done.refs_2_, bf16[32,128,384]{2,1,0:T(8,128)(2,1)} %bitcast.46, f32[32,1,128]{2,1,0:T(1,128)} %bitcast.40, ...), custom_call_target="tpu_custom_call" | custom-call | tf_op jit(solution)/shard_map/pallas_call | solution.py:70
  106.2 0.6 all-to-all-done.5
  106.8 7.1 %collective-permute-start.5 = (bf16[3072,128]{1,0:T(8,128)(2,1)S(1)}, bf16[3072,128]{1,0:T(8,128)(2,1)S(1)}, u32[]{:S(2)}, u32[]{:S(2)}) collective-permute-start(bf16[3072,128]{1,0:T(8,128)(2,1)S(1)} %bitcast.24), channel_id=1, source_target_pairs={{0,16},{16,0},{1,17},{17,1},{2,18},{18,2},{3,19},{19,3},{4,20},{20... | collective-permute-start | bytes 2359304 | tf_op jit(solution)/shard_map/ppermute | solution.py:395
  113.8 1.9 %collective-permute-done.5 = bf16[3072,128]{1,0:T(8,128)(2,1)S(1)} collective-permute-done((bf16[3072,128]{1,0:T(8,128)(2,1)S(1)}, bf16[3072,128]{1,0:T(8,128)(2,1)S(1)}, u32[]{:S(2)}, u32[]{:S(2)}) %collective-permute-start.5) | collective-permute-done | bytes 786464 | tf_op jit(solution)/shard_map/ppermute | solution.py:395
  115.7 4.8 %shard_map.100 = bf16[4,384,128]{2,1,0:T(8,128)(2,1)S(1)} custom-call(bf16[16,192,128]{2,1,0:T(8,128)(2,1)S(1)} %bitcast.25, bf16[16,192,128]{2,1,0:T(8,128)(2,1)S(1)} %bitcast.37, bf16[34,192,128]{2,1,0:T(8,128)(2,1)} %shard_map.99.refs_2_.refs_8_, bf16[32,128,384]{2,1,0:T(8,128)(2,1)} %bitcast.47, f32[32,1,128]{2,1,0:T(1,128)S(1)} %bitcast.42, ...), custom_call_target="tpu_custom_call" | custom-call | tf_op jit(solution)/shard_map/pallas_call | solution.py:70
  120.5 13.8 %all_to_all.68.refs_0_ = bf16[4,384,128]{2,1,0:T(8,128)(2,1)S(1)} all-to-all(bf16[4,384,128]{2,1,0:T(8,128)(2,1)S(1)} %shard_map.100), channel_id=1, replica_groups=mesh['z'=4,'y'=4,'c'=2,'w'=4,'x'=4] {'z'}, dimensions={0} | all-to-all | bytes 786432 | tf_op jit(solution)/shard_map/all_to_all | solution.py:452
  134.3 3.1 %collective-permute-start.6 = (bf16[1536,128]{1,0:T(8,128)(2,1)S(1)}, bf16[1536,128]{1,0:T(8,128)(2,1)S(1)}, u32[]{:S(2)}, u32[]{:S(2)}) collective-permute-start(bf16[1536,128]{1,0:T(8,128)(2,1)S(1)} %bitcast.26), channel_id=1, source_target_pairs={{0,16},{16,0},{1,17},{17,1},{2,18},{18,2},{3,19},{19,3},{4,20},{20... | collective-permute-start | bytes 1179656 | tf_op jit(solution)/shard_map/ppermute | solution.py:395
  137.4 1.3 collective-permute-done.6
  138.8 3.3 %shard_map.101 = bf16[256,512]{1,0:T(8,128)(2,1)S(1)} custom-call(bf16[4,384,128]{2,1,0:T(8,128)(2,1)S(1)} %all_to_all.68.refs_0_, bf16[4,384,128]{2,1,0:T(8,128)(2,1)S(1)} %bitcast.38, bf16[8,128,128]{2,1,0:T(8,128)(2,1)S(1)} %bitcast.28, bf16[8,128,128]{2,1,0:T(8,128)(2,1)S(1)} %bitcast.30, bf16[8,128,128]{2,1,0:T(8,128)(2,1)S(1)} %bitcast.32, ...), custom_call_target="tpu_custom_call" | custom-call | tf_op jit(solution)/shard_map/pallas_call | solution.py:70
  142.0 15.4 %all_to_all.69.got = bf16[32,8,512]{2,1,0:T(8,128)(2,1)S(1)} all-to-all(bf16[32,8,512]{2,1,0:T(8,128)(2,1)S(1)} %bitcast.35), channel_id=1, replica_groups=mesh['z'=4,'y'=4,'c'=2,'w'=4,'x'=4] {'z','y','c'}, dimensions={0} | all-to-all | bytes 524288 | tf_op jit(solution)/shard_map/all_to_all | solution.py:464
  157.4 0.7 shard_map.102
  (32 shorter events, 0.7 us)
Async XLA Ops:
  7.2 44.9 %copy-start.5 = (f32[4096]{0:T(1024)S(1)}, f32[4096]{0:T(1024)}, u32[]{:S(2)}) copy-start(f32[4096]{0:T(1024)} %param.10) | copy-start | bytes 49156
  7.2 44.9 %copy-start.8 = (f32[1,128]{1,0:T(1,128)S(1)}, f32[1,128]{1,0:T(1,128)}, u32[]{:S(2)}) copy-start(f32[1,128]{1,0:T(1,128)} %refs_5_.5) | copy-start | bytes 1540
  7.2 44.9 %copy-start.10 = (f32[1,128]{1,0:T(1,128)S(1)}, f32[1,128]{1,0:T(1,128)}, u32[]{:S(2)}) copy-start(f32[1,128]{1,0:T(1,128)} %refs_6_.3) | copy-start | bytes 1540
  10.4 18.0 %all-to-all-start = ((bf16[4,8,3072]{2,1,0:T(8,128)(2,1)}), bf16[4,8,3072]{2,1,0:T(8,128)(2,1)S(1)}, u32[]{:S(2)}, u32[]{:S(2)}) async-start(bf16[4,8,3072]{2,1,0:T(8,128)(2,1)} %get-tuple-element.19), calls=%async_computation | async-start | bytes 393216 | tf_op jit(solution)/shard_map/all_to_all | solution.py:387
  16.8 81.7 %all-gather.2.cloned.1.call-start = ((), (), s32[]{:S(2)}) async-start(), calls=%async_computation.8 | async-start | bytes 2162688 | tf_op jit(solution)/shard_map/all_gather | solution.py:409
  17.5 8.8 %collective-permute-start = (bf16[4,256,128]{2,1,0:T(8,128)(2,1)}, bf16[4,256,128]{2,1,0:T(8,128)(2,1)S(1)}, u32[]{:S(2)}, u32[]{:S(2)}) collective-permute-start(bf16[4,256,128]{2,1,0:T(8,128)(2,1)} %get-tuple-element.20), channel_id=1, source_target_pairs={{0,32},{32,64},{64,96},{96,0},{1,33},{33,65},{65,97},{97,1},{2,34}... | collective-permute-start | bytes 786440 | tf_op jit(solution)/shard_map/ppermute | solution.py:412
  20.8 7.6 %collective-permute-start.1 = (bf16[4,256,128]{2,1,0:T(8,128)(2,1)}, bf16[4,256,128]{2,1,0:T(8,128)(2,1)S(1)}, u32[]{:S(2)}, u32[]{:S(2)}) collective-permute-start(bf16[4,256,128]{2,1,0:T(8,128)(2,1)} %get-tuple-element.21), channel_id=1, source_target_pairs={{0,96},{32,0},{64,32},{96,64},{1,97},{33,1},{65,33},{97,65},{2,98}... | collective-permute-start | bytes 786440 | tf_op jit(solution)/shard_map/ppermute | solution.py:412
  40.4 16.3 %copy-start = (bf16[4,32,3072]{2,1,0:T(8,128)(2,1)}, bf16[4,32,3072]{2,1,0:T(8,128)(2,1)S(1)}, u32[]{:S(2)}) copy-start(bf16[4,32,3072]{2,1,0:T(8,128)(2,1)S(1)} %all_to_all.65) | copy-start | bytes 2359300
  40.4 11.7 %collective-permute-start.2 = (bf16[128,3072]{1,0:T(8,128)(2,1)S(1)}, bf16[128,3072]{1,0:T(8,128)(2,1)S(1)}, u32[]{:S(2)}, u32[]{:S(2)}) collective-permute-start(bf16[128,3072]{1,0:T(8,128)(2,1)S(1)} %bitcast.21), channel_id=1, source_target_pairs={{0,16},{16,0},{1,17},{17,1},{2,18},{18,2},{3,19},{19,3},{4,20},{20... | collective-permute-start | bytes 2359304 | tf_op jit(solution)/shard_map/ppermute | solution.py:395
  52.1 4.6 %copy-start.1 = (bf16[128,3072]{1,0:T(8,128)(2,1)}, bf16[128,3072]{1,0:T(8,128)(2,1)S(1)}, u32[]{:S(2)}) copy-start(bf16[128,3072]{1,0:T(8,128)(2,1)S(1)} %collective-permute-done.2.refs_1_) | copy-start | bytes 2359300
  52.1 9.4 %copy-start.12 = (bf16[4,256,128]{2,1,0:T(8,128)(2,1)S(1)}, bf16[4,256,128]{2,1,0:T(8,128)(2,1)}, u32[]{:S(2)}) copy-start(bf16[4,256,128]{2,1,0:T(8,128)(2,1)} %get-tuple-element.27) | copy-start | bytes 786436
  52.1 22.0 %copy-start.2 = (bf16[4,256,128]{2,1,0:T(8,128)(2,1)S(1)}, bf16[4,256,128]{2,1,0:T(8,128)(2,1)}, u32[]{:S(2)}) copy-start(bf16[4,256,128]{2,1,0:T(8,128)(2,1)} %get-tuple-element.24) | copy-start | bytes 786436
  56.7 28.0 %copy-start.7 = (f32[4096]{0:T(1024)S(1)}, f32[4096]{0:T(1024)}, u32[]{:S(2)}) copy-start(f32[4096]{0:T(1024)} %param.15) | copy-start | bytes 49156
  56.7 10.6 %all-to-all-start.2 = ((bf16[4,192,128]{2,1,0:T(8,128)(2,1)}), bf16[4,192,128]{2,1,0:T(8,128)(2,1)S(1)}, u32[]{:S(2)}, u32[]{:S(2)}) async-start(bf16[4,192,128]{2,1,0:T(8,128)(2,1)} %get-tuple-element.23), calls=%async_computation.2 | async-start | bytes 393216 | tf_op jit(solution)/shard_map/all_to_all | solution.py:387
  61.5 12.0 %collective-permute-start.4 = (bf16[4,256,128]{2,1,0:T(8,128)(2,1)S(1)}, bf16[4,256,128]{2,1,0:T(8,128)(2,1)S(1)}, u32[]{:S(2)}, u32[]{:S(2)}) collective-permute-start(bf16[4,256,128]{2,1,0:T(8,128)(2,1)S(1)} %copy-done.12), channel_id=1, source_target_pairs={{0,64},{32,96},{64,0},{96,32},{1,65},{33,97},{65,1},{97,33},{2,66}... | collective-permute-start | bytes 786440 | tf_op jit(solution)/shard_map/ppermute | solution.py:412
  67.3 6.7 %collective-permute-start.3 = (bf16[768,128]{1,0:T(8,128)(2,1)S(1)}, bf16[768,128]{1,0:T(8,128)(2,1)S(1)}, u32[]{:S(2)}, u32[]{:S(2)}) collective-permute-start(bf16[768,128]{1,0:T(8,128)(2,1)S(1)} %bitcast.36), channel_id=1, source_target_pairs={{0,16},{16,0},{1,17},{17,1},{2,18},{18,2},{3,19},{19,3},{4,20},{20... | collective-permute-start | bytes 589832 | tf_op jit(solution)/shard_map/ppermute | solution.py:395
  84.8 13.8 %copy-start.3 = (bf16[4,192,128]{2,1,0:T(8,128)(2,1)}, bf16[4,192,128]{2,1,0:T(8,128)(2,1)S(1)}, u32[]{:S(2)}) copy-start(bf16[4,192,128]{2,1,0:T(8,128)(2,1)S(1)} %get-tuple-element.29.refs_7_) | copy-start | bytes 589828
  95.0 11.8 %all-to-all-start.5 = ((bf16[4,768,128]{2,1,0:T(8,128)(2,1)}), bf16[4,768,128]{2,1,0:T(8,128)(2,1)S(1)}, u32[]{:S(2)}, u32[]{:S(2)}) async-start(bf16[4,768,128]{2,1,0:T(8,128)(2,1)} %tile.8), calls=%async_computation.5 | async-start | bytes 1572864 | tf_op jit(solution)/shard_map/all_to_all | solution.py:391
  98.5 17.3 %copy-start.6 = (f32[4096]{0:T(1024)S(1)}, f32[4096]{0:T(1024)}, u32[]{:S(2)}) copy-start(f32[4096]{0:T(1024)} %param.10) | copy-start | bytes 49156
  98.5 17.2 %copy-start.9 = (f32[1,128]{1,0:T(1,128)S(1)}, f32[1,128]{1,0:T(1,128)}, u32[]{:S(2)}) copy-start(f32[1,128]{1,0:T(1,128)} %refs_5_.5) | copy-start | bytes 1540
  98.5 17.2 %copy-start.11 = (f32[1,128]{1,0:T(1,128)S(1)}, f32[1,128]{1,0:T(1,128)}, u32[]{:S(2)}) copy-start(f32[1,128]{1,0:T(1,128)} %refs_6_.3) | copy-start | bytes 1540
  106.8 9.0 %collective-permute-start.5 = (bf16[3072,128]{1,0:T(8,128)(2,1)S(1)}, bf16[3072,128]{1,0:T(8,128)(2,1)S(1)}, u32[]{:S(2)}, u32[]{:S(2)}) collective-permute-start(bf16[3072,128]{1,0:T(8,128)(2,1)S(1)} %bitcast.24), channel_id=1, source_target_pairs={{0,16},{16,0},{1,17},{17,1},{2,18},{18,2},{3,19},{19,3},{4,20},{20... | collective-permute-start | bytes 2359304 | tf_op jit(solution)/shard_map/ppermute | solution.py:395
  134.3 4.4 %collective-permute-start.6 = (bf16[1536,128]{1,0:T(8,128)(2,1)S(1)}, bf16[1536,128]{1,0:T(8,128)(2,1)S(1)}, u32[]{:S(2)}, u32[]{:S(2)}) collective-permute-start(bf16[1536,128]{1,0:T(8,128)(2,1)S(1)} %bitcast.26), channel_id=1, source_target_pairs={{0,16},{16,0},{1,17},{17,1},{2,18},{18,2},{3,19},{19,3},{4,20},{20... | collective-permute-start | bytes 1179656 | tf_op jit(solution)/shard_map/ppermute | solution.py:395
  138.8 18.6 %copy-start.4 = (bf16[6,4096]{1,0:T(8,128)(2,1)S(1)}, bf16[6,4096]{1,0:T(8,128)(2,1)}, u32[]{:S(2)}) copy-start(bf16[6,4096]{1,0:T(8,128)(2,1)} %state.1) | copy-start | bytes 147460
Sparse Core Ops, SparseCore 0:
  20.4 71.7 all-gather.1

commit v13 on v12

--- a/solution.py
+++ b/solution.py
@@ -411,7 +411,7 @@
     moved = [
         lax.ppermute(sends[k], "y", [(y, (y + k) % 4) for y in range(4)]) for k in (1, 3, 2)
     ]
-    lines, moved[0], moved[1] = lax.optimization_barrier((lines, moved[0], moved[1]))
+    lines, moved[0], moved[2] = lax.optimization_barrier((lines, moved[0], moved[2]))
     own = along_y(lines)
     oth = swap(own)
     att1, col = call(

time: 166 us -> 169 us (1.018)
  waiting for transfers between devices: 15.1 us -> 22.1 us
  starting transfers between devices: 49.4 us -> 43.3 us
  blocking collectives: 60.3 us -> 62.8 us
    ppermute x4, starting transfers between devices: 25.6 us -> 18.8 us  [swap(): return lax.ppermute(block, 'c', [(0, 1), (1, 0)])]
    ppermute x3, waiting for transfers between devices: 4.76 us -> 9.33 us  [per_device(): lax.ppermute(sends[k], 'y', [(y, (y + k) % 4) for y in range(4)])]
    all_to_all x1, blocking collectives: 11.9 us -> 14.5 us  [along_y(): return lax.all_to_all(jnp.tile(block, (4, 1)), 'y', 0, 0, tiled=True)]
  transfers between devices with their start and end apart: 11 -> 11, of which waited for: 9 -> 8; matrix products, arithmetic and copies ran while one was open for 1% -> 1% of each run, Pallas kernels for 8% -> 8%
where the time goes in v13:
time: 169 us; the launch traced here: 168 us
  blocking collectives  62.8 us (37%)
  starting transfers between devices  43.3 us (26%)
  Pallas kernels  24.9 us (15%)
  waiting for transfers between devices  22.1 us (13%)
  between operations  14.3 us (8%)
    pallas_call x8, Pallas kernels, call(): pl.pallas_call(body, out_shape=out_shape, in_specs=in_specs, out_specs=[v...  24.9 us
    ppermute x4, starting transfers between devices, swap(): return lax.ppermute(block, 'c', [(0, 1), (1, 0)])  18.8 us
    all_to_all x1, blocking collectives, per_device(): own2 = lax.all_to_all(both.reshape(8 * TOK, 128), 'z', 0, 0, tiled=True)  14.8 us
    all_to_all x1, blocking collectives, per_device(): got = lax.all_to_all(columns, SEQ, 0, 0, tiled=True).reshape(32, 8, 512)  14.8 us
    all_to_all x1, blocking collectives, along_y(): return lax.all_to_all(jnp.tile(block, (4, 1)), 'y', 0, 0, tiled=True)  14.5 us
    all_to_all x1, blocking collectives, per_device(): parts = lax.all_to_all(parts.reshape(4 * TOK, 128), 'y', 0, 0, tiled=True)  10.7 us
    ppermute x3, starting transfers between devices, per_device(): lax.ppermute(sends[k], 'y', [(y, (y + k) % 4) for y in range(4)])  10.6 us
    all_to_all x2, starting transfers between devices, along_z(): lax.all_to_all(copies.reshape(n * rows, lanes), 'z', 0, 0, tiled=True)  10.3 us
  transfers between devices with their start and end apart: 11, of which 8 were waited for; matrix products, arithmetic and copies ran while one was open for 1% of the time, Pallas kernels for 8%

profile of v13, /device:TPU:1, one launch (start us, length us, event | category | flops | bytes accessed | tf_op | source)
XLA Modules:
  0.0 168.5 jit_solution(1117653011156990571)
XLA Ops:
  7.2 3.2 %shard_map.95 = (bf16[4,8,3072]{2,1,0:T(8,128)(2,1)}, bf16[8,4096]{1,0:T(8,128)(2,1)}, bf16[4,256,128]{2,1,0:T(8,128)(2,1)}, bf16[4,256,128]{2,1,0:T(8,128)(2,1)...) custom-call(bf16[6,4096]{1,0:T(8,128)(2,1)} %state.1, bf16[6,4096]{1,0:T(8,128)(2,1)} %refs_1_.1, ...), custom_call_target="tpu_custom_call" | custom-call | tf_op jit(solution)/shard_map/pallas_call | solution.py:70
  10.4 6.5 %all-to-all-start = ((bf16[4,8,3072]{2,1,0:T(8,128)(2,1)}), bf16[4,8,3072]{2,1,0:T(8,128)(2,1)S(1)}, u32[]{:S(2)}, u32[]{:S(2)}) async-start(bf16[4,8,3072]{2,1,0:T(8,128)(2,1)} %get-tuple-element.19), calls=%async_computation | async-start | bytes 393216 | tf_op jit(solution)/shard_map/all_to_all | solution.py:387
  16.9 0.7 all-gather.2.cloned.1.call-update
  17.6 3.2 %collective-permute-start = (bf16[4,256,128]{2,1,0:T(8,128)(2,1)}, bf16[4,256,128]{2,1,0:T(8,128)(2,1)S(1)}, u32[]{:S(2)}, u32[]{:S(2)}) collective-permute-start(bf16[4,256,128]{2,1,0:T(8,128)(2,1)} %get-tuple-element.20), channel_id=1, source_target_pairs={{0,32},{32,64},{64,96},{96,0},{1,33},{33,65},{65,97},{97,1},{2,34}... | collective-permute-start | bytes 786440 | tf_op jit(solution)/shard_map/ppermute | solution.py:412
  20.8 4.5 %collective-permute-start.1 = (bf16[4,256,128]{2,1,0:T(8,128)(2,1)}, bf16[4,256,128]{2,1,0:T(8,128)(2,1)S(1)}, u32[]{:S(2)}, u32[]{:S(2)}) collective-permute-start(bf16[4,256,128]{2,1,0:T(8,128)(2,1)} %get-tuple-element.21), channel_id=1, source_target_pairs={{0,64},{32,96},{64,0},{96,32},{1,65},{33,97},{65,1},{97,33},{2,66}... | collective-permute-start | bytes 786440 | tf_op jit(solution)/shard_map/ppermute | solution.py:412
  25.3 1.0 collective-permute-done
  26.3 8.3 %collective-permute-done.1 = bf16[4,256,128]{2,1,0:T(8,128)(2,1)S(1)} collective-permute-done((bf16[4,256,128]{2,1,0:T(8,128)(2,1)}, bf16[4,256,128]{2,1,0:T(8,128)(2,1)S(1)}, u32[]{:S(2)}, u32[]{:S(2)}) %collective-permute-start.1) | collective-permute-done | bytes 262176 | tf_op jit(solution)/shard_map/ppermute | solution.py:412
  34.7 14.5 %all_to_all.65 = bf16[4,32,3072]{2,1,0:T(8,128)(2,1)S(1)} all-to-all(bf16[4,32,3072]{2,1,0:T(8,128)(2,1)S(1)} %tile.6), channel_id=1, replica_groups=mesh['z'=4,'y'=4,'c'=2,'w'=4,'x'=4] {'y'}, dimensions={0} | all-to-all | bytes 1572864 | tf_op jit(solution)/shard_map/all_to_all | solution.py:391
  49.3 5.3 %collective-permute-start.2 = (bf16[128,3072]{1,0:T(8,128)(2,1)S(1)}, bf16[128,3072]{1,0:T(8,128)(2,1)S(1)}, u32[]{:S(2)}, u32[]{:S(2)}) collective-permute-start(bf16[128,3072]{1,0:T(8,128)(2,1)S(1)} %bitcast.21), channel_id=1, source_target_pairs={{0,16},{16,0},{1,17},{17,1},{2,18},{18,2},{3,19},{19,3},{4,20},{20... | collective-permute-start | bytes 2359304 | tf_op jit(solution)/shard_map/ppermute | solution.py:395
  54.6 1.9 %collective-permute-done.2.refs_1_ = bf16[128,3072]{1,0:T(8,128)(2,1)S(1)} collective-permute-done((bf16[128,3072]{1,0:T(8,128)(2,1)S(1)}, bf16[128,3072]{1,0:T(8,128)(2,1)S(1)}, u32[]{:S(2)}, u32[]{:S(2)}) %collective-permute-start.2) | collective-permute-done | bytes 786464 | tf_op jit(solution)/shard_map/ppermute | solution.py:395
  56.5 4.6 %shard_map.96 = (bf16[4,192,128]{2,1,0:T(8,128)(2,1)}, bf16[192,128]{1,0:T(8,128)(2,1)S(1)}) custom-call(bf16[128,3072]{1,0:T(8,128)(2,1)S(1)} %bitcast.22, bf16[128,3072]{1,0:T(8,128)(2,1)S(1)} %collective-permute-done.2.refs_1_, bf16[32,128,384]{2,1,0:T(8,128)(2,1)} %bitcast.45, f32[32,1,128]{2,1,0:T(1,128)S(1)} %bitcast.41, f32[1,128]{1,0:T(1,128)S(1)} %copy-done.8, ...), custom_call_target="tpu_custom_call" | custom-call | tf_op jit(solution)/shard_map/pallas_call | solution.py:70
  61.1 3.9 %all-to-all-start.2 = ((bf16[4,192,128]{2,1,0:T(8,128)(2,1)}), bf16[4,192,128]{2,1,0:T(8,128)(2,1)S(1)}, u32[]{:S(2)}, u32[]{:S(2)}) async-start(bf16[4,192,128]{2,1,0:T(8,128)(2,1)} %get-tuple-element.23), calls=%async_computation.2 | async-start | bytes 393216 | tf_op jit(solution)/shard_map/all_to_all | solution.py:387
  65.0 2.9 %collective-permute-start.4 = (bf16[4,256,128]{2,1,0:T(8,128)(2,1)S(1)}, bf16[4,256,128]{2,1,0:T(8,128)(2,1)S(1)}, u32[]{:S(2)}, u32[]{:S(2)}) collective-permute-start(bf16[4,256,128]{2,1,0:T(8,128)(2,1)S(1)} %copy-done.12), channel_id=1, source_target_pairs={{0,96},{32,0},{64,32},{96,64},{1,97},{33,1},{65,33},{97,65},{2,98}... | collective-permute-start | bytes 786440 | tf_op jit(solution)/shard_map/ppermute | solution.py:412
  67.9 4.4 %all-to-all-done.2.refs_0_ = bf16[4,192,128]{2,1,0:T(8,128)(2,1)S(1)} async-done(((bf16[4,192,128]{2,1,0:T(8,128)(2,1)}), bf16[4,192,128]{2,1,0:T(8,128)(2,1)S(1)}, u32[]{:S(2)}, u32[]{:S(2)}) %all-to-all-start.2) | async-done | bytes 196640 | tf_op jit(solution)/shard_map/all_to_all | solution.py:387
  72.3 4.3 %collective-permute-start.3 = (bf16[768,128]{1,0:T(8,128)(2,1)S(1)}, bf16[768,128]{1,0:T(8,128)(2,1)S(1)}, u32[]{:S(2)}, u32[]{:S(2)}) collective-permute-start(bf16[768,128]{1,0:T(8,128)(2,1)S(1)} %bitcast.36), channel_id=1, source_target_pairs={{0,16},{16,0},{1,17},{17,1},{2,18},{18,2},{3,19},{19,3},{4,20},{20... | collective-permute-start | bytes 589832 | tf_op jit(solution)/shard_map/ppermute | solution.py:395
  76.7 1.0 collective-permute-done.3
  77.7 0.7 shard_map.97
  78.4 10.7 %all_to_all.66.refs_0_ = f32[4,192,128]{2,1,0:T(8,128)S(1)} all-to-all(f32[4,192,128]{2,1,0:T(8,128)S(1)} %shard_map.97), channel_id=1, replica_groups=mesh['z'=4,'y'=4,'c'=2,'w'=4,'x'=4] {'y'}, dimensions={0} | all-to-all | bytes 786432 | tf_op jit(solution)/shard_map/all_to_all | solution.py:429
  89.2 8.0 %all_to_all.67 = bf16[4,192,128]{2,1,0:T(8,128)(2,1)S(1)} all-to-all(bf16[4,192,128]{2,1,0:T(8,128)(2,1)S(1)} %get-tuple-element.29.refs_7_), channel_id=1, replica_groups=mesh['z'=4,'y'=4,'c'=2,'w'=4,'x'=4] {'z'}, dimensions={0} | all-to-all | bytes 393216 | tf_op jit(solution)/shard_map/all_to_all | solution.py:387
  97.2 1.0 tile.8
  98.2 3.5 %all-to-all-start.5 = ((bf16[4,768,128]{2,1,0:T(8,128)(2,1)}), bf16[4,768,128]{2,1,0:T(8,128)(2,1)S(1)}, u32[]{:S(2)}, u32[]{:S(2)}) async-start(bf16[4,768,128]{2,1,0:T(8,128)(2,1)} %tile.8), calls=%async_computation.5 | async-start | bytes 1572864 | tf_op jit(solution)/shard_map/all_to_all | solution.py:391
  101.8 7.6 %shard_map.99.refs_2_.refs_8_ = bf16[34,192,128]{2,1,0:T(8,128)(2,1)} custom-call(bf16[128,3072]{1,0:T(8,128)(2,1)} %bitcast.23, bf16[128,3072]{1,0:T(8,128)(2,1)} %copy-done.1, bf16[256,4096]{1,0:T(8,128)(2,1)} %all-gather.2.cloned.1.call-done.refs_2_, bf16[32,128,384]{2,1,0:T(8,128)(2,1)} %bitcast.46, f32[32,1,128]{2,1,0:T(1,128)} %bitcast.40, ...), custom_call_target="tpu_custom_call" | custom-call | tf_op jit(solution)/shard_map/pallas_call | solution.py:70
  109.4 1.5 all-to-all-done.5
  110.9 5.9 %collective-permute-start.5 = (bf16[3072,128]{1,0:T(8,128)(2,1)S(1)}, bf16[3072,128]{1,0:T(8,128)(2,1)S(1)}, u32[]{:S(2)}, u32[]{:S(2)}) collective-permute-start(bf16[3072,128]{1,0:T(8,128)(2,1)S(1)} %bitcast.24), channel_id=1, source_target_pairs={{0,16},{16,0},{1,17},{17,1},{2,18},{18,2},{3,19},{19,3},{4,20},{20... | collective-permute-start | bytes 2359304 | tf_op jit(solution)/shard_map/ppermute | solution.py:395
  116.8 1.9 %collective-permute-done.5 = bf16[3072,128]{1,0:T(8,128)(2,1)S(1)} collective-permute-done((bf16[3072,128]{1,0:T(8,128)(2,1)S(1)}, bf16[3072,128]{1,0:T(8,128)(2,1)S(1)}, u32[]{:S(2)}, u32[]{:S(2)}) %collective-permute-start.5) | collective-permute-done | bytes 786464 | tf_op jit(solution)/shard_map/ppermute | solution.py:395
  118.7 4.8 %shard_map.100 = bf16[4,384,128]{2,1,0:T(8,128)(2,1)S(1)} custom-call(bf16[16,192,128]{2,1,0:T(8,128)(2,1)S(1)} %bitcast.25, bf16[16,192,128]{2,1,0:T(8,128)(2,1)S(1)} %bitcast.37, bf16[34,192,128]{2,1,0:T(8,128)(2,1)} %shard_map.99.refs_2_.refs_8_, bf16[32,128,384]{2,1,0:T(8,128)(2,1)} %bitcast.47, f32[32,1,128]{2,1,0:T(1,128)S(1)} %bitcast.42, ...), custom_call_target="tpu_custom_call" | custom-call | tf_op jit(solution)/shard_map/pallas_call | solution.py:70
  123.5 14.8 %all_to_all.68.refs_0_ = bf16[4,384,128]{2,1,0:T(8,128)(2,1)S(1)} all-to-all(bf16[4,384,128]{2,1,0:T(8,128)(2,1)S(1)} %shard_map.100), channel_id=1, replica_groups=mesh['z'=4,'y'=4,'c'=2,'w'=4,'x'=4] {'z'}, dimensions={0} | all-to-all | bytes 786432 | tf_op jit(solution)/shard_map/all_to_all | solution.py:452
  138.3 3.3 %collective-permute-start.6 = (bf16[1536,128]{1,0:T(8,128)(2,1)S(1)}, bf16[1536,128]{1,0:T(8,128)(2,1)S(1)}, u32[]{:S(2)}, u32[]{:S(2)}) collective-permute-start(bf16[1536,128]{1,0:T(8,128)(2,1)S(1)} %bitcast.26), channel_id=1, source_target_pairs={{0,16},{16,0},{1,17},{17,1},{2,18},{18,2},{3,19},{19,3},{4,20},{20... | collective-permute-start | bytes 1179656 | tf_op jit(solution)/shard_map/ppermute | solution.py:395
  141.6 1.3 collective-permute-done.6
  142.9 3.3 %shard_map.101 = bf16[256,512]{1,0:T(8,128)(2,1)S(1)} custom-call(bf16[4,384,128]{2,1,0:T(8,128)(2,1)S(1)} %all_to_all.68.refs_0_, bf16[4,384,128]{2,1,0:T(8,128)(2,1)S(1)} %bitcast.38, bf16[8,128,128]{2,1,0:T(8,128)(2,1)S(1)} %bitcast.28, bf16[8,128,128]{2,1,0:T(8,128)(2,1)S(1)} %bitcast.30, bf16[8,128,128]{2,1,0:T(8,128)(2,1)S(1)} %bitcast.34, ...), custom_call_target="tpu_custom_call" | custom-call | tf_op jit(solution)/shard_map/pallas_call | solution.py:70
  146.2 14.8 %all_to_all.69.got = bf16[32,8,512]{2,1,0:T(8,128)(2,1)S(1)} all-to-all(bf16[32,8,512]{2,1,0:T(8,128)(2,1)S(1)} %bitcast.35), channel_id=1, replica_groups=mesh['z'=4,'y'=4,'c'=2,'w'=4,'x'=4] {'z','y','c'}, dimensions={0} | all-to-all | bytes 524288 | tf_op jit(solution)/shard_map/all_to_all | solution.py:464
  161.0 0.7 shard_map.102
  (32 shorter events, 0.2 us)
Async XLA Ops:
  7.2 49.3 %copy-start.5 = (f32[4096]{0:T(1024)S(1)}, f32[4096]{0:T(1024)}, u32[]{:S(2)}) copy-start(f32[4096]{0:T(1024)} %param.10) | copy-start | bytes 49156
  7.2 49.3 %copy-start.8 = (f32[1,128]{1,0:T(1,128)S(1)}, f32[1,128]{1,0:T(1,128)}, u32[]{:S(2)}) copy-start(f32[1,128]{1,0:T(1,128)} %refs_5_.5) | copy-start | bytes 1540
  7.2 49.3 %copy-start.10 = (f32[1,128]{1,0:T(1,128)S(1)}, f32[1,128]{1,0:T(1,128)}, u32[]{:S(2)}) copy-start(f32[1,128]{1,0:T(1,128)} %refs_6_.3) | copy-start | bytes 1540
  10.4 24.3 %all-to-all-start = ((bf16[4,8,3072]{2,1,0:T(8,128)(2,1)}), bf16[4,8,3072]{2,1,0:T(8,128)(2,1)S(1)}, u32[]{:S(2)}, u32[]{:S(2)}) async-start(bf16[4,8,3072]{2,1,0:T(8,128)(2,1)} %get-tuple-element.19), calls=%async_computation | async-start | bytes 393216 | tf_op jit(solution)/shard_map/all_to_all | solution.py:387
  16.9 84.9 %all-gather.2.cloned.1.call-start = ((), (), s32[]{:S(2)}) async-start(), calls=%async_computation.8 | async-start | bytes 2162688 | tf_op jit(solution)/shard_map/all_gather | solution.py:409
  17.6 8.8 %collective-permute-start = (bf16[4,256,128]{2,1,0:T(8,128)(2,1)}, bf16[4,256,128]{2,1,0:T(8,128)(2,1)S(1)}, u32[]{:S(2)}, u32[]{:S(2)}) collective-permute-start(bf16[4,256,128]{2,1,0:T(8,128)(2,1)} %get-tuple-element.20), channel_id=1, source_target_pairs={{0,32},{32,64},{64,96},{96,0},{1,33},{33,65},{65,97},{97,1},{2,34}... | collective-permute-start | bytes 786440 | tf_op jit(solution)/shard_map/ppermute | solution.py:412
  20.8 13.9 %collective-permute-start.1 = (bf16[4,256,128]{2,1,0:T(8,128)(2,1)}, bf16[4,256,128]{2,1,0:T(8,128)(2,1)S(1)}, u32[]{:S(2)}, u32[]{:S(2)}) collective-permute-start(bf16[4,256,128]{2,1,0:T(8,128)(2,1)} %get-tuple-element.21), channel_id=1, source_target_pairs={{0,64},{32,96},{64,0},{96,32},{1,65},{33,97},{65,1},{97,33},{2,66}... | collective-permute-start | bytes 786440 | tf_op jit(solution)/shard_map/ppermute | solution.py:412
  49.3 11.8 %copy-start = (bf16[4,32,3072]{2,1,0:T(8,128)(2,1)}, bf16[4,32,3072]{2,1,0:T(8,128)(2,1)S(1)}, u32[]{:S(2)}) copy-start(bf16[4,32,3072]{2,1,0:T(8,128)(2,1)S(1)} %all_to_all.65) | copy-start | bytes 2359300
  49.3 7.2 %collective-permute-start.2 = (bf16[128,3072]{1,0:T(8,128)(2,1)S(1)}, bf16[128,3072]{1,0:T(8,128)(2,1)S(1)}, u32[]{:S(2)}, u32[]{:S(2)}) collective-permute-start(bf16[128,3072]{1,0:T(8,128)(2,1)S(1)} %bitcast.21), channel_id=1, source_target_pairs={{0,16},{16,0},{1,17},{17,1},{2,18},{18,2},{3,19},{19,3},{4,20},{20... | collective-permute-start | bytes 2359304 | tf_op jit(solution)/shard_map/ppermute | solution.py:395
  56.5 4.6 %copy-start.1 = (bf16[128,3072]{1,0:T(8,128)(2,1)}, bf16[128,3072]{1,0:T(8,128)(2,1)S(1)}, u32[]{:S(2)}) copy-start(bf16[128,3072]{1,0:T(8,128)(2,1)S(1)} %collective-permute-done.2.refs_1_) | copy-start | bytes 2359300
  56.5 8.5 %copy-start.12 = (bf16[4,256,128]{2,1,0:T(8,128)(2,1)S(1)}, bf16[4,256,128]{2,1,0:T(8,128)(2,1)}, u32[]{:S(2)}) copy-start(bf16[4,256,128]{2,1,0:T(8,128)(2,1)} %get-tuple-element.26) | copy-start | bytes 786436
  56.5 21.2 %copy-start.2 = (bf16[4,256,128]{2,1,0:T(8,128)(2,1)S(1)}, bf16[4,256,128]{2,1,0:T(8,128)(2,1)}, u32[]{:S(2)}) copy-start(bf16[4,256,128]{2,1,0:T(8,128)(2,1)} %get-tuple-element.24) | copy-start | bytes 786436
  61.1 28.0 %copy-start.7 = (f32[4096]{0:T(1024)S(1)}, f32[4096]{0:T(1024)}, u32[]{:S(2)}) copy-start(f32[4096]{0:T(1024)} %param.15) | copy-start | bytes 49156
  61.1 11.2 %all-to-all-start.2 = ((bf16[4,192,128]{2,1,0:T(8,128)(2,1)}), bf16[4,192,128]{2,1,0:T(8,128)(2,1)S(1)}, u32[]{:S(2)}, u32[]{:S(2)}) async-start(bf16[4,192,128]{2,1,0:T(8,128)(2,1)} %get-tuple-element.23), calls=%async_computation.2 | async-start | bytes 393216 | tf_op jit(solution)/shard_map/all_to_all | solution.py:387
  65.0 11.7 %collective-permute-start.4 = (bf16[4,256,128]{2,1,0:T(8,128)(2,1)S(1)}, bf16[4,256,128]{2,1,0:T(8,128)(2,1)S(1)}, u32[]{:S(2)}, u32[]{:S(2)}) collective-permute-start(bf16[4,256,128]{2,1,0:T(8,128)(2,1)S(1)} %copy-done.12), channel_id=1, source_target_pairs={{0,96},{32,0},{64,32},{96,64},{1,97},{33,1},{65,33},{97,65},{2,98}... | collective-permute-start | bytes 786440 | tf_op jit(solution)/shard_map/ppermute | solution.py:412
  72.3 5.4 %collective-permute-start.3 = (bf16[768,128]{1,0:T(8,128)(2,1)S(1)}, bf16[768,128]{1,0:T(8,128)(2,1)S(1)}, u32[]{:S(2)}, u32[]{:S(2)}) collective-permute-start(bf16[768,128]{1,0:T(8,128)(2,1)S(1)} %bitcast.36), channel_id=1, source_target_pairs={{0,16},{16,0},{1,17},{17,1},{2,18},{18,2},{3,19},{19,3},{4,20},{20... | collective-permute-start | bytes 589832 | tf_op jit(solution)/shard_map/ppermute | solution.py:395
  89.2 12.6 %copy-start.3 = (bf16[4,192,128]{2,1,0:T(8,128)(2,1)}, bf16[4,192,128]{2,1,0:T(8,128)(2,1)S(1)}, u32[]{:S(2)}) copy-start(bf16[4,192,128]{2,1,0:T(8,128)(2,1)S(1)} %get-tuple-element.29.refs_7_) | copy-start | bytes 589828
  98.2 12.7 %all-to-all-start.5 = ((bf16[4,768,128]{2,1,0:T(8,128)(2,1)}), bf16[4,768,128]{2,1,0:T(8,128)(2,1)S(1)}, u32[]{:S(2)}, u32[]{:S(2)}) async-start(bf16[4,768,128]{2,1,0:T(8,128)(2,1)} %tile.8), calls=%async_computation.5 | async-start | bytes 1572864 | tf_op jit(solution)/shard_map/all_to_all | solution.py:391
  101.7 17.0 %copy-start.6 = (f32[4096]{0:T(1024)S(1)}, f32[4096]{0:T(1024)}, u32[]{:S(2)}) copy-start(f32[4096]{0:T(1024)} %param.10) | copy-start | bytes 49156
  101.7 17.0 %copy-start.9 = (f32[1,128]{1,0:T(1,128)S(1)}, f32[1,128]{1,0:T(1,128)}, u32[]{:S(2)}) copy-start(f32[1,128]{1,0:T(1,128)} %refs_5_.5) | copy-start | bytes 1540
  101.7 17.0 %copy-start.11 = (f32[1,128]{1,0:T(1,128)S(1)}, f32[1,128]{1,0:T(1,128)}, u32[]{:S(2)}) copy-start(f32[1,128]{1,0:T(1,128)} %refs_6_.3) | copy-start | bytes 1540
  110.9 7.8 %collective-permute-start.5 = (bf16[3072,128]{1,0:T(8,128)(2,1)S(1)}, bf16[3072,128]{1,0:T(8,128)(2,1)S(1)}, u32[]{:S(2)}, u32[]{:S(2)}) collective-permute-start(bf16[3072,128]{1,0:T(8,128)(2,1)S(1)} %bitcast.24), channel_id=1, source_target_pairs={{0,16},{16,0},{1,17},{17,1},{2,18},{18,2},{3,19},{19,3},{4,20},{20... | collective-permute-start | bytes 2359304 | tf_op jit(solution)/shard_map/ppermute | solution.py:395
  138.3 4.6 %collective-permute-start.6 = (bf16[1536,128]{1,0:T(8,128)(2,1)S(1)}, bf16[1536,128]{1,0:T(8,128)(2,1)S(1)}, u32[]{:S(2)}, u32[]{:S(2)}) collective-permute-start(bf16[1536,128]{1,0:T(8,128)(2,1)S(1)} %bitcast.26), channel_id=1, source_target_pairs={{0,16},{16,0},{1,17},{17,1},{2,18},{18,2},{3,19},{19,3},{4,20},{20... | collective-permute-start | bytes 1179656 | tf_op jit(solution)/shard_map/ppermute | solution.py:395
  142.9 18.1 %copy-start.4 = (bf16[6,4096]{1,0:T(8,128)(2,1)S(1)}, bf16[6,4096]{1,0:T(8,128)(2,1)}, u32[]{:S(2)}) copy-start(bf16[6,4096]{1,0:T(8,128)(2,1)} %state.1) | copy-start | bytes 147460
Sparse Core Ops, SparseCore 0:
  20.4 71.3 all-gather.1
